TPU v7x, 128 devices: a whole 4x4x4 slice. The times are simulated.
128 devices in a mesh: outer: 8 (over x, core), inner: 16 (over y, z).
Axes of the slice: x: 4, y: 4, z: 4, core: 2. Of those that a mesh axis runs over, the one named last changes fastest.
Arguments:
- rhs: float32 [262144, 128], P(('outer', 'inner')), may hold values from -6 to 6
- near_blocks: bfloat16 [1024, 8, 256, 256], P(('outer', 'inner')), may hold values from -0.125 to 0.125
- near_index: int32 [1024, 8], P(('outer', 'inner')), may hold values from 0 to 11
- near_mask: int32 [1024, 8], P(('outer', 'inner')), may hold values 0 or 1
- basis: bfloat16 [1024, 64, 256], P(('outer', 'inner')), may hold values from -0.375 to 0.375
- far_blocks: bfloat16 [1024, 48, 64, 64], P(('outer', 'inner')), may hold values from -0.109375 to 0.109375
- far_slot: int32 [1024, 48], P(('outer', 'inner')), may hold values from 0 to 63
- far_mask: int32 [1024, 48], P(('outer', 'inner')), may hold values 0 or 1
- send_slot: int32 [128, 16, 4], P(('outer', 'inner')), may hold values from 0 to 7, as said below
- transfer: bfloat16 [1024, 64, 64], P(('outer', 'inner')), may hold values from -0.25 to 0.25
- top_blocks: bfloat16 [8, 8, 64, 64], P('outer'), may hold values from -0.25 to 0.25
Outputs:
- krylov: float32 [5, 262144, 128], P(None, ('outer', 'inner'))
- hessenberg: float32 [5, 4, 128], replicated
Inputs may be any that keep to these rules, and one draw needn't show every extreme that they name: `send_slot`: for each sender subtree and receiver of its branch, the 4 entries are distinct local leaves of the sender.
All inputs are finite; a program needn't handle non-finite values. No bound on the sum of `near_mask` or of `far_mask` on one device may be relied on, other than what follows from the above.
Results may differ from a plain program's by a relative error of at most 0.028.
Values may be sent and summed in bfloat16 or wider, within the bound.
No kernel may reach another device: no remote copies, remote signals or barrier semaphores. Data moves between devices by JAX's collectives and lax.ppermute only.
A program may use at most 128 MiB of HBM per device.

v0:
```python
import jax
import jax.numpy as jnp
from jax import lax
from jax.sharding import PartitionSpec as P

HW = 2
STEPS = 4


def extended(array, sides, width):
    for axis, dim in sides:
        count, length = (lax.axis_size(axis), array.shape[dim])
        up = [(i, (i + 1) % count) for i in range(count - 1)]
        down = [(j, i) for i, j in up]
        last = lax.slice_in_dim(array, length - width, length, axis=dim)
        initial = lax.slice_in_dim(array, 0, width, axis=dim)
        before = lax.ppermute(last, axis, up)
        after = lax.ppermute(initial, axis, down)
        array = jnp.concatenate([before, array, after], axis=dim)
    return array


def shards(
    rhs,
    near_blocks,
    near_index,
    near_mask,
    basis,
    far_blocks,
    far_slot,
    far_mask,
    send_slot,
    transfer,
    top_blocks,
):
    leaf_count = basis.shape[0]
    leaf_size = basis.shape[2]
    columns = rhs.shape[1]
    points_all = lax.axis_size(("outer", "inner")) * rhs.shape[0]
    near_weight = near_mask.astype(jnp.bfloat16)[:, :, None, None]
    far_weight = far_mask.astype(jnp.bfloat16)[:, :, None, None]
    branch = lax.axis_index("outer")
    branches_all = top_blocks.shape[1]
    off_diagonal = (jnp.arange(branches_all) != branch).astype(jnp.bfloat16)
    top_rows = top_blocks[0] * off_diagonal[:, None, None]
    requested = lax.all_to_all(send_slot, "inner", split_axis=1, concat_axis=1, tiled=True)
    sources = requested.shape[1]
    leaf_ids = (jnp.arange(sources, dtype=jnp.int32)[:, None] * leaf_count + requested[0]).reshape(
        -1
    )
    far_rows = leaf_ids[far_slot]

    def lengths(values):
        return lax.psum(jnp.sum(values * values, axis=0), ("outer", "inner"))

    scale = jnp.sqrt(lengths(rhs) / points_all + 1e-06)
    vectors = [rhs / scale]
    hessenberg = jnp.zeros((STEPS + 1, STEPS, columns), jnp.float32)
    for iteration in range(STEPS):
        vector = vectors[-1]
        coarse = vector.astype(jnp.bfloat16).reshape(leaf_count, leaf_size, columns)
        padded = extended(coarse, (("inner", 0),), HW)
        neighbours = padded[near_index] * near_weight
        near_part = jnp.einsum(
            "lnij,lnjr->lir", near_blocks, neighbours, preferred_element_type=jnp.float32
        )
        skeleton = jnp.einsum(
            "lki,lir->lkr", basis, coarse, preferred_element_type=jnp.float32
        ).astype(jnp.bfloat16)
        branch_skeletons = lax.all_gather(skeleton, "inner", axis=0, tiled=True)
        remote = branch_skeletons[far_rows] * far_weight
        local_far = jnp.einsum(
            "lfab,lfbr->lar", far_blocks, remote, preferred_element_type=jnp.float32
        )
        partial_up = jnp.einsum(
            "lab,lar->br", transfer, skeleton, preferred_element_type=jnp.float32
        )
        summed = lax.psum(partial_up.astype(jnp.bfloat16), "inner")
        coeffs = lax.all_gather(summed[None], "outer", axis=0, tiled=True)
        incoming = jnp.einsum("cab,cbr->ar", top_rows, coeffs, preferred_element_type=jnp.float32)
        downward = jnp.einsum(
            "lab,br->lar",
            transfer,
            incoming.astype(jnp.bfloat16),
            preferred_element_type=jnp.float32,
        )
        combined = (local_far + downward).astype(jnp.bfloat16)
        far_part = jnp.einsum("lki,lkr->lir", basis, combined, preferred_element_type=jnp.float32)
        image = vector + (near_part + far_part).reshape(-1, columns)
        stacked = jnp.stack(vectors)
        project = lax.psum(jnp.sum(stacked * image[None], axis=1), ("outer", "inner")) / points_all
        image = image - jnp.sum(project[:, None, :] * stacked, axis=0)
        height = jnp.sqrt(lengths(image) / points_all + 1e-06)
        hessenberg = hessenberg.at[: iteration + 1, iteration].set(project)
        hessenberg = hessenberg.at[iteration + 1, iteration].set(height)
        vectors.append(image / height)
    return (jnp.stack(vectors), hessenberg)


def solution(mesh):
    return jax.shard_map(
        shards,
        mesh=mesh,
        in_specs=(
            P(("outer", "inner"), None),
            P(("outer", "inner"), None, None, None),
            P(("outer", "inner"), None),
            P(("outer", "inner"), None),
            P(("outer", "inner"), None, None),
            P(("outer", "inner"), None, None, None),
            P(("outer", "inner"), None),
            P(("outer", "inner"), None),
            P(("outer", "inner"), None, None),
            P(("outer", "inner"), None, None),
            P("outer", None, None, None),
        ),
        out_specs=(P(None, ("outer", "inner"), None), P()),
        check_vma=False,
    )
```

profile of v0, /device:TPU:1, one launch (start us, length us, event | category | flops | bytes accessed | tf_op | source)
XLA Modules:
  0.0 1212.6 jit_solution(6008338441533722482)
XLA Ops:
  9.0 68.7 %psum.91 = f32[128]{0:T(128)S(1)} all-reduce(f32[128]{0:T(128)S(1)} %multiply_reduce_fusion.11), channel_id=1, replica_groups=mesh['outer'=8,'inner'=16] {'outer','inner'}, use_global_device_ids=true, to_apply=%region_1.0 | all-reduce | flops 128 | bytes 1024 | tf_op jit(solution)/shard_map/psum | solution.py:54
  83.5 7.1 all-to-all-start
  92.0 60.8 %psum.92 = bf16[1,64,128]{2,1,0:T(8,128)(2,1)S(1)} all-reduce(bf16[1,64,128]{2,1,0:T(8,128)(2,1)S(1)} %fusion.79), channel_id=1, replica_groups=mesh['outer'=8,'inner'=16] {'inner'}, use_global_device_ids=true, to_apply=%region_2.0 | all-reduce | flops 8192 | bytes 32768 | tf_op jit(solution)/shard_map/psum | solution.py:78
  152.8 28.5 %all_gather.25 = bf16[8,64,128]{2,1,0:T(8,128)(2,1)S(1)} all-gather(bf16[1,64,128]{2,1,0:T(8,128)(2,1)S(1)} %psum.92), channel_id=1, replica_groups=mesh['outer'=8,'inner'=16] {'outer'}, dimensions={0}, use_global_device_ids=true | all-gather | bytes 147456 | tf_op jit(solution)/shard_map/all_gather | solution.py:79
  184.2 2.7 gather_fusion.1
  187.2 3.1 gather_fusion
  190.3 6.4 copy.35
  196.7 7.5 fusion.24
  204.2 5.6 gather_fusion.2
  209.9 7.8 fusion.44
  222.0 63.2 %psum.93 = f32[1,128]{1,0:T(1,128)} all-reduce(f32[1,128]{1,0:T(1,128)S(1)} %bitcast.298), channel_id=1, replica_groups=mesh['outer'=8,'inner'=16] {'outer','inner'}, use_global_device_ids=true, to_apply=%region_4.0 | all-reduce | flops 128 | bytes 1024 | tf_op jit(solution)/shard_map/psum | solution.py:91
  287.2 62.6 %psum.94 = f32[128]{0:T(128)} all-reduce(f32[128]{0:T(128)} %multiply_reduce_fusion.9), channel_id=1, replica_groups=mesh['outer'=8,'inner'=16] {'outer','inner'}, use_global_device_ids=true, to_apply=%region_6.0 | all-reduce | flops 128 | bytes 1024 | tf_op jit(solution)/shard_map/psum | solution.py:54
  356.0 3.4 collective-permute-start.2
  362.4 59.6 %psum.95 = bf16[1,64,128]{2,1,0:T(8,128)(2,1)} all-reduce(bf16[1,64,128]{2,1,0:T(8,128)(2,1)} %fusion.77), channel_id=1, replica_groups=mesh['outer'=8,'inner'=16] {'inner'}, use_global_device_ids=true, to_apply=%region_7.0 | all-reduce | flops 8192 | bytes 32768 | tf_op jit(solution)/shard_map/psum | solution.py:78
  422.0 27.5 %all_gather.27 = bf16[8,64,128]{2,1,0:T(8,128)(2,1)S(1)} all-gather(bf16[1,64,128]{2,1,0:T(8,128)(2,1)} %psum.95), channel_id=1, replica_groups=mesh['outer'=8,'inner'=16] {'outer'}, dimensions={0}, use_global_device_ids=true | all-gather | bytes 147456 | tf_op jit(solution)/shard_map/all_gather | solution.py:79
  453.4 4.2 gather_fusion.3
  457.7 6.4 copy.39
  464.1 8.5 fusion.27
  472.5 5.6 gather_fusion.4
  478.2 7.8 fusion.47
  485.9 2.8 fusion.38
  494.0 64.0 %psum.96 = f32[2,128]{1,0:T(2,128)} all-reduce(f32[2,128]{1,0:T(2,128)S(1)} %multiply_reduce_fusion.5), channel_id=1, replica_groups=mesh['outer'=8,'inner'=16] {'outer','inner'}, use_global_device_ids=true, to_apply=%region_9.0 | all-reduce | flops 256 | bytes 2048 | tf_op jit(solution)/shard_map/psum | solution.py:91
  558.9 3.0 multiply_reduce_fusion.8
  561.8 62.5 %psum.97 = f32[128]{0:T(128)} all-reduce(f32[128]{0:T(128)} %get-tuple-element.102), channel_id=1, replica_groups=mesh['outer'=8,'inner'=16] {'outer','inner'}, use_global_device_ids=true, to_apply=%region_12.0 | all-reduce | flops 128 | bytes 1024 | tf_op jit(solution)/shard_map/psum | solution.py:54
  632.7 3.5 collective-permute-start.4
  639.2 59.1 %psum.98 = bf16[1,64,128]{2,1,0:T(8,128)(2,1)} all-reduce(bf16[1,64,128]{2,1,0:T(8,128)(2,1)} %fusion.75), channel_id=1, replica_groups=mesh['outer'=8,'inner'=16] {'inner'}, use_global_device_ids=true, to_apply=%region_13.0 | all-reduce | flops 8192 | bytes 32768 | tf_op jit(solution)/shard_map/psum | solution.py:78
  698.3 28.4 %all_gather.29 = bf16[8,64,128]{2,1,0:T(8,128)(2,1)S(1)} all-gather(bf16[1,64,128]{2,1,0:T(8,128)(2,1)} %psum.98), channel_id=1, replica_groups=mesh['outer'=8,'inner'=16] {'outer'}, dimensions={0}, use_global_device_ids=true | all-gather | bytes 147456 | tf_op jit(solution)/shard_map/all_gather | solution.py:79
  730.7 4.2 gather_fusion.5
  734.9 6.4 copy.42
  741.3 8.5 fusion.30
  749.8 5.6 gather_fusion.6
  755.4 7.8 fusion.50
  763.2 2.8 fusion.37
  772.1 63.0 %psum.99 = f32[3,128]{1,0:T(4,128)} all-reduce(f32[3,128]{1,0:T(4,128)S(1)} %multiply_reduce_fusion.3), channel_id=1, replica_groups=mesh['outer'=8,'inner'=16] {'outer','inner'}, use_global_device_ids=true, to_apply=%region_15.0 | all-reduce | flops 384 | bytes 3072 | tf_op jit(solution)/shard_map/psum | solution.py:91
  839.1 62.6 %psum.100 = f32[128]{0:T(128)} all-reduce(f32[128]{0:T(128)} %get-tuple-element.100), channel_id=1, replica_groups=mesh['outer'=8,'inner'=16] {'outer','inner'}, use_global_device_ids=true, to_apply=%region_18.0 | all-reduce | flops 128 | bytes 1024 | tf_op jit(solution)/shard_map/psum | solution.py:54
  923.1 3.5 collective-permute-start.6
  929.5 59.5 %psum.101 = bf16[1,64,128]{2,1,0:T(8,128)(2,1)} all-reduce(bf16[1,64,128]{2,1,0:T(8,128)(2,1)} %fusion.73), channel_id=1, replica_groups=mesh['outer'=8,'inner'=16] {'inner'}, use_global_device_ids=true, to_apply=%region_19.0 | all-reduce | flops 8192 | bytes 32768 | tf_op jit(solution)/shard_map/psum | solution.py:78
  993.2 27.8 %all_gather.31 = bf16[8,64,128]{2,1,0:T(8,128)(2,1)S(1)} all-gather(bf16[1,64,128]{2,1,0:T(8,128)(2,1)} %psum.101), channel_id=1, replica_groups=mesh['outer'=8,'inner'=16] {'outer'}, dimensions={0}, use_global_device_ids=true | all-gather | bytes 147456 | tf_op jit(solution)/shard_map/all_gather | solution.py:79
  1027.7 3.1 gather_fusion.7
  1030.8 6.4 copy.45
  1037.2 8.5 fusion.33
  1045.8 5.6 gather_fusion.8
  1051.4 7.8 fusion.53
  1059.2 2.9 fusion.36
  1068.1 63.2 %psum.102 = f32[4,128]{1,0:T(4,128)S(1)} all-reduce(f32[4,128]{1,0:T(4,128)S(1)} %multiply_reduce_fusion.1), channel_id=1, replica_groups=mesh['outer'=8,'inner'=16] {'outer','inner'}, use_global_device_ids=true, to_apply=%region_21.0 | all-reduce | flops 512 | bytes 4096 | tf_op jit(solution)/shard_map/psum | solution.py:91
  1131.4 2.7 multiply_reduce_fusion
  1134.0 2.6 broadcast_select_fusion
  1141.0 62.6 %psum.103 = f32[128]{0:T(128)S(1)} all-reduce(f32[128]{0:T(128)S(1)} %get-tuple-element.98), channel_id=1, replica_groups=mesh['outer'=8,'inner'=16] {'outer','inner'}, use_global_device_ids=true, to_apply=%region_24.0 | all-reduce | flops 128 | bytes 1024 | tf_op jit(solution)/shard_map/psum | solution.py:54
  (190 shorter events, 111.1 us)
Async XLA Ops:
  7.2 71.9 %copy-start = (bf16[8,64,256]{2,1,0:T(8,128)(2,1)S(1)}, bf16[8,64,256]{2,1,0:T(8,128)(2,1)}, u32[]{:S(2)}) copy-start(bf16[8,64,256]{2,1,0:T(8,128)(2,1)} %param.31) | copy-start | bytes 786436
  7.2 75.6 %copy-start.25 = (s32[1,16,4]{1,2,0:T(4,128)S(1)}, s32[1,16,4]{1,2,0:T(4,128)}, u32[]{:S(2)}) copy-start(s32[1,16,4]{1,2,0:T(4,128)} %param.35) | copy-start | bytes 772
  7.2 83.5 %copy-start.23 = (s32[8,8]{1,0:T(8,128)S(1)}, s32[8,8]{1,0:T(8,128)}, u32[]{:S(2)}) copy-start(s32[8,8]{1,0:T(8,128)} %param.29) | copy-start | bytes 772
  7.2 83.6 %copy-start.21 = (s32[8,8]{1,0:T(8,128)S(1)}, s32[8,8]{1,0:T(8,128)}, u32[]{:S(2)}) copy-start(s32[8,8]{1,0:T(8,128)} %param.30) | copy-start | bytes 772
  7.2 83.6 %copy-start.24 = (s32[8,48]{1,0:T(8,128)S(1)}, s32[8,48]{1,0:T(8,128)}, u32[]{:S(2)}) copy-start(s32[8,48]{1,0:T(8,128)} %param.33) | copy-start | bytes 4612
  7.2 83.7 %copy-start.11 = (bf16[8,64,64]{2,1,0:T(8,128)(2,1)S(1)}, bf16[8,64,64]{2,1,0:T(8,128)(2,1)}, u32[]{:S(2)}) copy-start(bf16[8,64,64]{2,1,0:T(8,128)(2,1)} %param.36) | copy-start | bytes 196612
  7.2 174.6 %copy-start.33 = (bf16[1,8,64,64]{3,2,1,0:T(8,128)(2,1)S(1)}, bf16[1,8,64,64]{3,2,1,0:T(8,128)(2,1)}, u32[]{:S(2)}) copy-start(bf16[1,8,64,64]{3,2,1,0:T(8,128)(2,1)} %param.37) | copy-start | bytes 196612
  7.2 175.6 %copy-start.22 = (s32[8,48]{1,0:T(8,128)S(1)}, s32[8,48]{1,0:T(8,128)}, u32[]{:S(2)}) copy-start(s32[8,48]{1,0:T(8,128)} %param.34) | copy-start | bytes 4612
  7.3 197.0 %all-gather.5.cloned.1.call-start = ((), (), s32[]{:S(2)}) async-start(), calls=%async_computation.1 | async-start | bytes 2228224 | tf_op jit(solution)/shard_map/all_gather | solution.py:70
  80.0 107.1 %collective-permute-start = (bf16[2,256,128]{2,1,0:T(8,128)(2,1)S(1)}, bf16[2,256,128]{2,1,0:T(8,128)(2,1)S(1)}, u32[]{:S(2)}, u32[]{:S(2)}) collective-permute-start(bf16[2,256,128]{2,1,0:T(8,128)(2,1)S(1)} %bitcast.295), channel_id=1, source_target_pairs={{0,1},{1,2},{2,3},{3,4},{4,5},{5,6},{6,7},{7,8},{8,9},{9,10},{10,1... | collective-permute-start | bytes 393224 | tf_op jit(solution)/shard_map/ppermute | solution.py:17
  81.5 105.6 %collective-permute-start.1 = (bf16[2,256,128]{2,1,0:T(8,128)(2,1)S(1)}, bf16[2,256,128]{2,1,0:T(8,128)(2,1)S(1)}, u32[]{:S(2)}, u32[]{:S(2)}) collective-permute-start(bf16[2,256,128]{2,1,0:T(8,128)(2,1)S(1)} %bitcast.294), channel_id=1, source_target_pairs={{1,0},{2,1},{3,2},{4,3},{5,4},{6,5},{7,6},{8,7},{9,8},{10,9},{11,1... | collective-permute-start | bytes 393224 | tf_op jit(solution)/shard_map/ppermute | solution.py:18
  83.5 99.4 %all-to-all-start = ((s32[1,16,4]{2,0,1:T(1,128)}), s32[1,16,4]{2,0,1:T(1,128)S(1)}, u32[]{:S(2)}, u32[]{:S(2)}) async-start(s32[1,16,4]{2,0,1:T(1,128)} %copy.36), calls=%async_computation | async-start | bytes 16384 | tf_op jit(solution)/shard_map/all_to_all | solution.py:46
  90.6 381.9 %all-gather.7.cloned.1.call-start = ((), (), s32[]{:S(2)}) async-start(), calls=%async_computation.2 | async-start | bytes 2228224 | tf_op jit(solution)/shard_map/all_gather | solution.py:70
  90.8 105.9 %copy-start.26 = (bf16[8,8]{1,0:T(8,128)(2,1)}, bf16[8,8]{1,0:T(8,128)(2,1)S(1)}, u32[]{:S(2)}) copy-start(bf16[8,8]{1,0:T(8,128)(2,1)S(1)} %convert_element_type.98) | copy-start | bytes 388
  181.3 0.5 copy-start.34
  182.9 27.0 %copy-start.29 = (bf16[8,48]{1,0:T(8,128)(2,1)}, bf16[8,48]{1,0:T(8,128)(2,1)S(1)}, u32[]{:S(2)}) copy-start(bf16[8,48]{1,0:T(8,128)(2,1)S(1)} %convert_element_type.101) | copy-start | bytes 2308
  217.6 4.1 copy-start.1
  221.7 129.3 %copy-start.5 = (f32[8,256,128]{2,1,0:T(8,128)}, f32[8,256,128]{2,1,0:T(8,128)S(1)}, u32[]{:S(2)}) copy-start(f32[8,256,128]{2,1,0:T(8,128)S(1)} %copy.38) | copy-start | bytes 3145732
  352.5 0.8 copy-start.14
  354.2 395.6 %all-gather.9.cloned.1.call-start = ((), (), s32[]{:S(2)}) async-start(), calls=%async_computation.3 | async-start | bytes 2228224 | tf_op jit(solution)/shard_map/all_gather | solution.py:70
  356.0 95.4 %collective-permute-start.2 = (bf16[2,256,128]{2,1,0:T(8,128)(2,1)}, bf16[2,256,128]{2,1,0:T(8,128)(2,1)}, u32[]{:S(2)}, u32[]{:S(2)}) collective-permute-start(bf16[2,256,128]{2,1,0:T(8,128)(2,1)} %bitcast.24), channel_id=1, source_target_pairs={{0,1},{1,2},{2,3},{3,4},{4,5},{5,6},{6,7},{7,8},{8,9},{9,10},{10,1... | collective-permute-start | bytes 393224 | tf_op jit(solution)/shard_map/ppermute | solution.py:17
  359.4 91.9 %collective-permute-start.3 = (bf16[2,256,128]{2,1,0:T(8,128)(2,1)}, bf16[2,256,128]{2,1,0:T(8,128)(2,1)}, u32[]{:S(2)}, u32[]{:S(2)}) collective-permute-start(bf16[2,256,128]{2,1,0:T(8,128)(2,1)} %bitcast.26), channel_id=1, source_target_pairs={{1,0},{2,1},{3,2},{4,3},{5,4},{6,5},{7,6},{8,7},{9,8},{10,9},{11,1... | collective-permute-start | bytes 393224 | tf_op jit(solution)/shard_map/ppermute | solution.py:18
  457.7 6.4 copy-start.27
  472.5 5.6 copy-start.30
  492.6 1.0 copy-start.8
  558.7 70.5 %copy-start.16 = (f32[2,128]{1,0:T(2,128)}, f32[2,128]{1,0:T(2,128)S(1)}, u32[]{:S(2)}) copy-start(f32[2,128]{1,0:T(2,128)S(1)} %broadcast_multiply_fusion.2) | copy-start | bytes 3076
  625.6 0.6 copy-start.17
  627.5 0.8 copy-start.13
  629.2 416.5 %all-gather.11.cloned.1.call-start = ((), (), s32[]{:S(2)}) async-start(), calls=%async_computation.4 | async-start | bytes 2228224 | tf_op jit(solution)/shard_map/all_gather | solution.py:70
  629.3 105.6 %copy-start.20 = (s32[2]{0:T(128)}, s32[2]{0:T(128)S(1)}, u32[]{:S(2)}) copy-start(s32[2]{0:T(128)S(1)} %iota_multiply_fusion.1) | copy-start | bytes 28
  632.7 95.8 %collective-permute-start.4 = (bf16[2,256,128]{2,1,0:T(8,128)(2,1)}, bf16[2,256,128]{2,1,0:T(8,128)(2,1)}, u32[]{:S(2)}, u32[]{:S(2)}) collective-permute-start(bf16[2,256,128]{2,1,0:T(8,128)(2,1)} %bitcast.44), channel_id=1, source_target_pairs={{0,1},{1,2},{2,3},{3,4},{4,5},{5,6},{6,7},{7,8},{8,9},{9,10},{10,1... | collective-permute-start | bytes 393224 | tf_op jit(solution)/shard_map/ppermute | solution.py:17
  636.2 92.3 %collective-permute-start.5 = (bf16[2,256,128]{2,1,0:T(8,128)(2,1)}, bf16[2,256,128]{2,1,0:T(8,128)(2,1)}, u32[]{:S(2)}, u32[]{:S(2)}) collective-permute-start(bf16[2,256,128]{2,1,0:T(8,128)(2,1)} %bitcast.46), channel_id=1, source_target_pairs={{1,0},{2,1},{3,2},{4,3},{5,4},{6,5},{7,6},{8,7},{9,8},{10,9},{11,1... | collective-permute-start | bytes 393224 | tf_op jit(solution)/shard_map/ppermute | solution.py:18
  749.8 5.6 copy-start.31
  763.2 5.3 copy-start.18
  770.2 1.0 copy-start.2
  770.2 1.3 copy-start.9
  835.0 2.3 copy-start.10
  902.9 0.6 copy-start.19
  904.8 0.8 copy-start.12
  911.6 79.8 %copy-start.4 = (f32[2048,128]{1,0:T(8,128)S(1)}, f32[2048,128]{1,0:T(8,128)}, u32[]{:S(2)}) copy-start(f32[2048,128]{1,0:T(8,128)} %get-tuple-element.101) | copy-start | bytes 3145732
  923.1 103.4 %collective-permute-start.6 = (bf16[2,256,128]{2,1,0:T(8,128)(2,1)}, bf16[2,256,128]{2,1,0:T(8,128)(2,1)}, u32[]{:S(2)}, u32[]{:S(2)}) collective-permute-start(bf16[2,256,128]{2,1,0:T(8,128)(2,1)} %bitcast.64), channel_id=1, source_target_pairs={{0,1},{1,2},{2,3},{3,4},{4,5},{5,6},{6,7},{7,8},{8,9},{9,10},{10,1... | collective-permute-start | bytes 393224 | tf_op jit(solution)/shard_map/ppermute | solution.py:17
  926.5 100.0 %collective-permute-start.7 = (bf16[2,256,128]{2,1,0:T(8,128)(2,1)}, bf16[2,256,128]{2,1,0:T(8,128)(2,1)}, u32[]{:S(2)}, u32[]{:S(2)}) collective-permute-start(bf16[2,256,128]{2,1,0:T(8,128)(2,1)} %bitcast.66), channel_id=1, source_target_pairs={{1,0},{2,1},{3,2},{4,3},{5,4},{6,5},{7,6},{8,7},{9,8},{10,9},{11,1... | collective-permute-start | bytes 393224 | tf_op jit(solution)/shard_map/ppermute | solution.py:18
  1030.8 6.4 copy-start.28
  1045.8 5.6 copy-start.32
  1051.4 7.8 copy-start.15
  1059.2 8.4 copy-start.3
  1066.3 1.0 copy-start.6
  1066.3 1.3 copy-start.7
Sparse Core Ops, SparseCore 0:
  80.1 40.6 all-gather.4
  354.3 41.7 all-gather.6
  629.3 41.5 all-gather.8
  906.6 41.5 all-gather.10
where the time goes:
time: 1220 us; the launch traced here: 1210 us
  blocking collectives  923 us (76%)
  local copies, waits for them, and re-layouts  107 us (9%)
  matrix products  91 us (7%)
  other arithmetic  52.5 us (4%)
  starting transfers between devices  24.3 us (2%)
  between operations  14.5 us (1%)
    psum x5, blocking collectives, lengths(): return lax.psum(jnp.sum(values * values, axis=0), ('outer', 'inner'))  319 us
    psum x4, blocking collectives, shards(): lax.psum(jnp.sum(stacked * image[None], axis=1), ('outer', 'inner'))  253 us
    psum x4, blocking collectives, shards(): summed = lax.psum(partial_up.astype(jnp.bfloat16), 'inner')  239 us
    all_gather x4, blocking collectives, shards(): coeffs = lax.all_gather(summed[None], 'outer', axis=0, tiled=True)  112 us
    gather x8, local copies, waits for them, and re-layouts, shards(): neighbours = padded[near_index] * near_weight  40.2 us
    dot_general x4, matrix products, shards(): jnp.einsum('lnij,lnjr->lir', near_blocks, neighbours, preferred_element_t...  32.9 us
    dot_general x4, matrix products, shards(): jnp.einsum('lfab,lfbr->lar', far_blocks, remote, preferred_element_type=j...  31.1 us
  transfers between devices with their start and end apart: 13, of which 0 were waited for; matrix products, arithmetic and copies ran while one was open for 10% of the time, Pallas kernels for 0%

commit v1 on v0

v1 whole, which is shorter than its diff:
```python
import functools

import jax
import jax.numpy as jnp
from jax import lax
from jax.experimental import pallas as pl
from jax.experimental.pallas import tpu as pltpu
from jax.sharding import PartitionSpec as P

HW = 2
STEPS = 4
EPS = 1e-06
PIECES = 3
DOT_ROWS = 16
STATE_ROWS = 64
VMEM_BYTES = 60 * 1024 * 1024
BF16 = jnp.bfloat16
F32 = jnp.float32


def dot(a, b):
    return jnp.dot(a, b, preferred_element_type=F32)


def dot_first(a, b):
    return lax.dot_general(a, b, (((0,), (0,)), ((), ())), preferred_element_type=F32)


def store_split(ref, values, count):
    rest = values
    ref[...] = jnp.zeros(ref.shape, F32)
    for piece in range(PIECES):
        part = rest.astype(BF16).astype(F32)
        ref[piece * 5 : piece * 5 + count, :] = part[:count]
        rest = rest - part


def joined(rows):
    return [rows[i : i + 1] + rows[5 + i : 6 + i] + rows[10 + i : 11 + i] for i in range(5)]


def entry_row(i, l):
    low, high = min(i, l), max(i, l)
    return 20 + high * (high + 1) // 2 + low


def basis_row(i, l):
    return 32 + i * (i + 1) // 2 + l


def coefficients(m, grams, state_in, state_out):
    last = m - 1
    entry = lambda i, l: state_in[entry_row(i, l) : entry_row(i, l) + 1, :]
    expand = lambda i, l: state_in[basis_row(i, l) : basis_row(i, l) + 1, :]

    def put(row, value):
        state_out[row : row + 1, :] = value

    dots = []
    for i in range(m):
        dots.append(sum(expand(i, l) * grams[l] for l in range(i + 1)))
    weights = [dots[i] + entry(i, last) for i in range(m)]
    spread = [sum(weights[l] * entry(i, l) for l in range(m)) for i in range(m)]
    square = grams[m]
    for i in range(m):
        square = square + weights[i] * (weights[i] + spread[i] - 2.0 * dots[i])
    total = jnp.maximum(square, 0.0) + EPS
    root = jnp.sqrt(total)
    inverse = 1.0 / root
    for l in range(m):
        value = sum(weights[i] * expand(i, l) for i in range(l, m))
        put(basis_row(m, l), -inverse * value)
    put(basis_row(m, m), inverse)
    for i in range(m):
        put(i * STEPS + last, weights[i] + (1.0 if i == last else 0.0))
    if m > 0:
        put(m * STEPS + last, root)
    if m < STEPS:
        for i in range(m):
            put(entry_row(i, m), (-entry(i, last) - spread[i]) * inverse)
        put(entry_row(m, m), -EPS / total)
    return weights, inverse


def whole(a):
    zeros = (0,) * len(a.shape)
    return pl.BlockSpec(a.shape, lambda l, *_: zeros)


def by_leaf(shape):
    zeros = (0,) * (len(shape) - 1)
    return pl.BlockSpec(shape, lambda l, *_: (l,) + zeros)


def gather_sum_kernel(recv_ref, *refs, lead):
    (*_, out_ref, rows_ref, split, semaphore) = refs
    rows = rows_ref.shape[1]
    rank = rows - DOT_ROWS
    copy = pltpu.make_async_copy(recv_ref.at[:, lead : lead + rows], rows_ref, semaphore)
    copy.start()
    copy.wait()
    total = rows_ref[0].astype(F32)
    for i in range(1, rows_ref.shape[0]):
        total = total + rows_ref[i].astype(F32)
    store_split(split, jnp.concatenate(joined(total[rank:]), axis=0), 5)
    dots = split[...].astype(BF16)
    for c in range(out_ref.shape[0]):
        if rank > 0:
            out_ref[c, :rank] = total[:rank].astype(BF16)
        out_ref[c, rank:] = dots


def gather_sum(recv, lead, outer, *earlier):
    inner, rows, columns = recv.shape
    rows = rows - lead
    return pl.pallas_call(
        functools.partial(gather_sum_kernel, lead=lead),
        in_specs=[pl.BlockSpec(memory_space=pl.ANY)] * (1 + len(earlier)),
        out_specs=pl.BlockSpec(memory_space=pltpu.VMEM),
        scratch_shapes=[
            pltpu.VMEM((inner, rows, columns), BF16),
            pltpu.VMEM((DOT_ROWS, columns), F32),
            pltpu.SemaphoreType.DMA,
        ],
        out_shape=jax.ShapeDtypeStruct((outer, rows, columns), BF16),
        compiler_params=pltpu.CompilerParams(vmem_limit_bytes=VMEM_BYTES),
        cost_estimate=pl.CostEstimate(flops=1 << 20, bytes_accessed=1 << 19, transcendentals=0),
        name="gather_sum",
    )(recv, *earlier)


def from_branches(ups_ref, rank):
    rows = ups_ref[0, rank:].astype(F32)
    for c in range(1, ups_ref.shape[0]):
        rows = rows + ups_ref[c, rank:].astype(F32)
    return joined(rows)


ANY = pl.BlockSpec(memory_space=pl.ANY)
SMEM = pl.BlockSpec(memory_space=pltpu.SMEM)
CHUNKS = 4


def call(kernel, args, in_specs, out_shape, out_specs, scratch, name, flops, moved, aliases={}):
    return pl.pallas_call(
        kernel,
        in_specs=in_specs,
        out_specs=out_specs,
        out_shape=out_shape,
        scratch_shapes=scratch,
        input_output_aliases=aliases,
        compiler_params=pltpu.CompilerParams(vmem_limit_bytes=VMEM_BYTES),
        cost_estimate=pl.CostEstimate(flops=flops, bytes_accessed=moved, transcendentals=0),
        name=name,
    )(*args)


def tie_kernel(send_in, before, after, send_out):
    pass


def tie(send, before, after):
    shape = jax.ShapeDtypeStruct(send.shape, send.dtype)
    return call(
        tie_kernel, (send, before, after), [ANY] * 3, shape, ANY, [], "tie", 0, 1 << 10, {0: 0}
    )


def pack_kernel(mask_ref, far_ref, out_ref, blocks, packed, arrived, left):
    leaves, entries, rank, _ = blocks.shape
    fetch = lambda l: pltpu.make_async_copy(far_ref.at[l], blocks.at[l], arrived.at[l])
    store = lambda l: pltpu.make_async_copy(packed.at[l], out_ref.at[l], left.at[l])
    for leaf in range(leaves):
        fetch(leaf).start()

    def body(leaf, carry):
        fetch(leaf).wait()
        for pair in range(entries // 2):
            sides = []
            for f in (2 * pair, 2 * pair + 1):
                weight = mask_ref[leaf, f].astype(F32).astype(BF16)
                sides.append(blocks[leaf, f] * weight)
            columns = slice(pair * 2 * rank, (pair + 1) * 2 * rank)
            packed[leaf, :, columns] = jnp.concatenate(sides, axis=1)
        store(leaf).start()
        return carry

    lax.fori_loop(0, leaves, body, 0)
    for leaf in range(leaves):
        store(leaf).wait()


def pack_far(far_blocks, far_mask):
    leaves, entries, rank, _ = far_blocks.shape
    shape = (leaves, rank, entries * rank)
    return call(
        pack_kernel,
        (far_mask, far_blocks),
        [SMEM, ANY],
        jax.ShapeDtypeStruct(shape, BF16),
        ANY,
        [
            pltpu.VMEM(far_blocks.shape, BF16),
            pltpu.VMEM(shape, BF16),
            pltpu.SemaphoreType.DMA((leaves,)),
            pltpu.SemaphoreType.DMA((leaves,)),
        ],
        "pack_far",
        0,
        12 << 20,
    )


def near_kernel(index_ref, mask_ref, blocks_ref, before_ref, own_ref, after_ref, *refs):
    (*_, out_ref, blocks, padded, result, arrived, halo, left) = refs
    leaves, entries = blocks.shape[:2]
    width = before_ref.shape[0]
    half = entries // 2
    size = result.shape[1]

    def fetch(leaf, part):
        piece = pl.ds(part * half, half)
        return pltpu.make_async_copy(
            blocks_ref.at[leaf, piece], blocks.at[leaf, piece], arrived.at[leaf, part]
        )

    def store(leaf):
        rows = pl.ds(pl.multiple_of(leaf * size, size), size)
        return pltpu.make_async_copy(result.at[leaf], out_ref.at[rows], left.at[leaf])

    sides = [
        pltpu.make_async_copy(own_ref, padded.at[pl.ds(width, leaves)], halo.at[0]),
        pltpu.make_async_copy(before_ref, padded.at[pl.ds(0, width)], halo.at[1]),
        pltpu.make_async_copy(after_ref, padded.at[pl.ds(width + leaves, width)], halo.at[2]),
    ]
    for side in sides:
        side.start()
    for leaf in range(leaves):
        for part in range(2):
            fetch(leaf, part).start()
    for side in sides:
        side.wait()

    def body(leaf, carry):
        fetch(leaf, 0).wait()
        fetch(leaf, 1).wait()
        total = None
        for n in range(entries):
            weight = mask_ref[leaf, n].astype(F32).astype(BF16)
            term = dot(blocks[leaf, n], padded[index_ref[leaf, n]] * weight)
            total = term if total is None else total + term
        result[leaf] = total
        store(leaf).start()
        return carry

    lax.fori_loop(0, leaves, body, 0)
    for leaf in range(leaves):
        store(leaf).wait()


def near_field(near_index, near_mask, near_blocks, before, own, after, *earlier):
    leaves, entries, size, _ = near_blocks.shape
    width, columns = before.shape[0], own.shape[2]
    return call(
        near_kernel,
        (near_index, near_mask, near_blocks, before, own, after) + earlier,
        [SMEM, SMEM] + [ANY] * (4 + len(earlier)),
        jax.ShapeDtypeStruct((leaves * size, columns), F32),
        ANY,
        [
            pltpu.VMEM(near_blocks.shape, BF16),
            pltpu.VMEM((leaves + 2 * width, size, columns), BF16),
            pltpu.VMEM((leaves, size, columns), F32),
            pltpu.SemaphoreType.DMA((leaves, 2)),
            pltpu.SemaphoreType.DMA((3,)),
            pltpu.SemaphoreType.DMA((leaves,)),
        ],
        "near_field",
        2 * near_blocks.size * columns,
        2 * near_blocks.size,
    )


def far_kernel(far_slot, recv_ref, far_ref, earlier_ref, out_ref, *scratch):
    packed, skeletons, gathered, result, arrived, came, left = scratch
    leaves, rank, depth = packed.shape
    inner, rows, _ = skeletons.shape
    slots = rows // rank
    part = inner // CHUNKS

    def get(i):
        some = pl.ds(i * part, part)
        return pltpu.make_async_copy(
            recv_ref.at[some, pl.ds(0, rows)], skeletons.at[some], came.at[i]
        )

    fetch = lambda l: pltpu.make_async_copy(far_ref.at[l], packed.at[l], arrived.at[l])
    store = lambda l: pltpu.make_async_copy(result.at[l], out_ref.at[l], left.at[l])
    for i in range(CHUNKS):
        get(i).start()
    for leaf in range(leaves):
        fetch(leaf).start()
    for i in range(CHUNKS):
        get(i).wait()

    def body(leaf, carry):
        fetch(leaf).wait()
        for f in range(depth // rank):
            slot = far_slot[leaf, f]
            start = pl.multiple_of(slot % slots * rank, rank)
            gathered[f * rank : (f + 1) * rank] = skeletons[slot // slots, pl.ds(start, rank)]
        result[leaf] = dot(packed[leaf], gathered[...])
        store(leaf).start()
        return carry

    lax.fori_loop(0, leaves, body, 0)
    for leaf in range(leaves):
        store(leaf).wait()


def far_field(far_slot, recv, packed, slots, earlier):
    leaves, rank, depth = packed.shape
    inner, _, columns = recv.shape
    shape = (leaves, rank, columns)
    return call(
        far_kernel,
        (far_slot, recv, packed, earlier),
        [SMEM, ANY, ANY, ANY],
        jax.ShapeDtypeStruct(shape, F32),
        ANY,
        [
            pltpu.VMEM(packed.shape, BF16),
            pltpu.VMEM((inner, slots * rank, columns), BF16),
            pltpu.VMEM((depth, columns), BF16),
            pltpu.VMEM(shape, F32),
            pltpu.SemaphoreType.DMA((leaves,)),
            pltpu.SemaphoreType.DMA((CHUNKS,)),
            pltpu.SemaphoreType.DMA((leaves,)),
        ],
        "far_field",
        2 * packed.size * columns,
        2 * packed.size + (1 << 20),
    )


def stage_kernel(*refs, k, points):
    refs = list(refs)
    take = lambda count: [refs.pop(0) for _ in range(count)]
    m = k - 1
    first, sends = k == 0, k < STEPS
    send_slot, branch = take(2)
    zs = take(max(k, 1))
    if not first:
        ups_any, state_any, top_any, far_any, near_any = take(5)
    basis_any, transfer_any = take(2)
    if not first:
        state_out, z_any = take(2)
    (send_any,) = take(1)
    if sends:
        coarse_any, low_any, high_any = take(3)
    basis, transfer, vectors, result, sums, send, split, sent, arrived, came, left = take(11)
    if sends:
        coarse, skeletons, upward, out = take(4)
    if not first:
        ups, state, top, far, near, coef, incoming = take(7)

    leaves, rank, size = basis.shape
    group = leaves // CHUNKS

    def rows(i):
        return pl.ds(pl.multiple_of(i * group * size, group * size), group * size)

    def some(i):
        return pl.ds(i * group, group)

    def fetches(i):
        pairs = [(z.at[rows(i)], vectors.at[l, rows(i)]) for l, z in enumerate(zs)]
        pairs.append((basis_any.at[some(i)], basis.at[some(i)]))
        pairs.append((transfer_any.at[some(i)], transfer.at[some(i)]))
        if not first:
            pairs.append((near_any.at[rows(i)], near.at[rows(i)]))
            pairs.append((far_any.at[some(i)], far.at[some(i)]))
        return [
            pltpu.make_async_copy(source, target, arrived.at[n, i])
            for n, (source, target) in enumerate(pairs)
        ]

    def stores(i):
        pairs = []
        if not first:
            pairs.append((result.at[rows(i)], z_any.at[rows(i)]))
        if sends:
            pairs.append((coarse.at[some(i)], coarse_any.at[some(i)]))
        return [
            pltpu.make_async_copy(source, target, left.at[n, i])
            for n, (source, target) in enumerate(pairs)
        ]

    if not first:
        small = [
            pltpu.make_async_copy(source, target, came.at[n])
            for n, (source, target) in enumerate(
                [(ups_any, ups), (state_any, state), (top_any, top)]
            )
        ]
        for copy in small:
            copy.start()
    for i in range(CHUNKS):
        for copy in fetches(i):
            copy.start()

    sums[...] = jnp.zeros(sums.shape, F32)
    if sends:
        upward[...] = jnp.zeros(upward.shape, F32)
    if not first:
        for copy in small:
            copy.wait()
        total = None
        for c in range(ups.shape[0]):
            weight = (branch[0] != c).astype(F32).astype(BF16)
            term = dot(top[0, c] * weight, ups[c, :rank])
            total = term if total is None else total + term
        incoming[...] = total.astype(BF16)
        grams = [row / points for row in from_branches(ups, rank)]
        state_out[...] = state[...]
        weights, inverse = coefficients(m, grams, state, state_out)
        for i, weight in enumerate(weights):
            coef[i : i + 1, :] = weight
        coef[STEPS : STEPS + 1, :] = inverse

    def one_leaf(leaf):
        own = pl.ds(pl.multiple_of(leaf * size, size), size)
        others = [vectors[l, own] for l in range(len(zs))]
        if first:
            z = others.pop()
        else:
            combined = far[leaf] + dot(transfer[leaf], incoming[...])
            z = near[own] + dot_first(basis[leaf], combined.astype(BF16))
            for i in range(m):
                z = z - coef[i : i + 1, :] * others[i + 1]
            z = z * coef[STEPS : STEPS + 1, :]
            result[own] = z
        if sends:
            rounded = z.astype(BF16)
            coarse[leaf] = rounded
            skeleton = dot(basis[leaf], rounded).astype(BF16)
            skeletons[leaf] = skeleton
            upward[...] += dot_first(transfer[leaf], skeleton)
        for i, other in enumerate(others + [z]):
            sums[i] += jnp.sum((z * other).reshape(size // 8, 8, z.shape[1]), axis=0)

    def body(i, carry):
        for copy in fetches(i):
            copy.wait()
        for j in range(group):
            one_leaf(i * group + j)
        for copy in stores(i):
            copy.start()
        return carry

    lax.fori_loop(0, CHUNKS, body, 0)

    if sends:
        halos = [
            pltpu.make_async_copy(coarse.at[pl.ds(0, HW)], low_any, out.at[0]),
            pltpu.make_async_copy(coarse.at[pl.ds(leaves - HW, HW)], high_any, out.at[1]),
        ]
        for copy in halos:
            copy.start()
    products = [jnp.sum(sums[i], axis=0, keepdims=True) for i in range(k + 1)]
    products = jnp.concatenate(products + [jnp.zeros_like(products[0])] * (7 - k), axis=0)
    store_split(split, products, k + 1)
    dots = split[...].astype(BF16)
    inner = send.shape[0]
    share = inner // sent.shape[0]

    def leave(i):
        part = pl.ds(i * share, share)
        return pltpu.make_async_copy(send.at[part], send_any.at[part], sent.at[i])

    if sends:
        lifted = upward[...].astype(BF16)
        slots = send_slot.shape[0]
        for r in range(inner):
            for s in range(slots):
                send[r, s * rank : (s + 1) * rank] = skeletons[send_slot[s, r]]
            send[r, slots * rank : (slots + 1) * rank] = lifted
            send[r, (slots + 1) * rank :] = dots
            if r % share == share - 1:
                leave(r // share).start()
    else:
        for r in range(inner):
            send[r] = dots
        for i in range(sent.shape[0]):
            leave(i).start()
    for i in range(CHUNKS):
        for copy in stores(i):
            copy.wait()
    if sends:
        for copy in halos:
            copy.wait()
    for i in range(sent.shape[0]):
        leave(i).wait()


def stage(k, points, send_slot, branch, zs, basis, transfer, later):
    leaves, rank, size = basis.shape
    first, sends = k == 0, k < STEPS
    columns = zs[0].shape[1]
    slots, inner = send_slot.shape
    tall = (leaves * size, columns)
    args = [send_slot, branch] + list(zs)
    if not first:
        ups, state, top, local_far, near = later
        args += [ups, state, top, local_far, near]
    args += [basis, transfer]
    names, shapes, out_specs = [], [], []

    def get(name, shape, dtype, spec=ANY):
        names.append(name)
        shapes.append(jax.ShapeDtypeStruct(shape, dtype))
        out_specs.append(spec)

    if not first:
        get("state", state.shape, F32, pl.BlockSpec(memory_space=pltpu.VMEM))
        get("z", tall, F32)
    sent = (inner, ((slots + 1) * rank if sends else 0) + DOT_ROWS, columns)
    get("send", sent, BF16)
    if sends:
        get("coarse", (leaves, size, columns), BF16)
        get("low", (HW, size, columns), BF16)
        get("high", (HW, size, columns), BF16)

    semaphores = pltpu.SemaphoreType.DMA
    scratch = [
        pltpu.VMEM(basis.shape, BF16),
        pltpu.VMEM(transfer.shape, BF16),
        pltpu.VMEM((len(zs),) + tall, F32),
        pltpu.VMEM(tall if not first else (8, columns), F32),
        pltpu.VMEM((STEPS + 1, 8, columns), F32),
        pltpu.VMEM(sent, BF16),
        pltpu.VMEM((DOT_ROWS, columns), F32),
        semaphores((CHUNKS if sends else 1,)),
        semaphores((len(zs) + 4, CHUNKS)),
        semaphores((3,)),
        semaphores((2, CHUNKS)),
    ]
    if sends:
        scratch += [
            pltpu.VMEM((leaves, size, columns), BF16),
            pltpu.VMEM((leaves, rank, columns), BF16),
            pltpu.VMEM((rank, columns), F32),
            semaphores((2,)),
        ]
    if not first:
        scratch += [
            pltpu.VMEM(ups.shape, BF16),
            pltpu.VMEM(state.shape, F32),
            pltpu.VMEM(top.shape, BF16),
            pltpu.VMEM(local_far.shape, F32),
            pltpu.VMEM(tall, F32),
            pltpu.VMEM((8, columns), F32),
            pltpu.VMEM((rank, columns), BF16),
        ]
    outs = call(
        functools.partial(stage_kernel, k=k, points=points),
        args,
        [SMEM, SMEM] + [ANY] * (len(args) - 2),
        shapes,
        out_specs,
        scratch,
        f"stage{k}",
        1 << 27,
        (k + 4) << 20,
    )
    return dict(zip(names, outs))


def basis_kernel(state_ref, *refs):
    zs, krylov_out = refs[:-1], refs[-1]
    values = [ref[...] for ref in zs]
    for i in range(len(zs)):
        vector = None
        for l in range(i + 1):
            row = basis_row(i, l)
            term = state_ref[row : row + 1, :] * values[l]
            vector = term if vector is None else vector + term
        krylov_out[i] = vector


def basis_vectors(state, zs, leaves):
    points, columns = zs[0].shape
    size = points // leaves
    return pl.pallas_call(
        basis_kernel,
        grid=(leaves,),
        in_specs=[whole(state)] + [by_leaf((size, columns))] * len(zs),
        out_specs=pl.BlockSpec((len(zs), size, columns), lambda l: (0, l, 0)),
        out_shape=jax.ShapeDtypeStruct((written(len(zs)), points, columns), F32),
        compiler_params=pltpu.CompilerParams(vmem_limit_bytes=VMEM_BYTES),
        cost_estimate=pl.CostEstimate(flops=1 << 23, bytes_accessed=8 << 20, transcendentals=0),
        name="basis_vectors",
    )(state, *zs)


def written(count):
    return STEPS + 1


def last_kernel(ups_any, state_any, krylov_in, *refs, points):
    zs = refs[: STEPS + 1]
    krylov_out, hess_out, ups, state_in, state_out, vectors, result = refs[STEPS + 1 : -3]
    came, arrived, left = refs[-3:]
    part = result.shape[0] // CHUNKS

    def rows(i):
        return pl.ds(pl.multiple_of(i * part, part), part)

    def fetches(i):
        return [
            pltpu.make_async_copy(z.at[rows(i)], vectors.at[l, rows(i)], arrived.at[l, i])
            for l, z in enumerate(zs)
        ]

    def store(i):
        return pltpu.make_async_copy(
            result.at[rows(i)], krylov_out.at[STEPS, rows(i)], left.at[i]
        )

    small = [
        pltpu.make_async_copy(ups_any, ups, came.at[0]),
        pltpu.make_async_copy(state_any, state_in, came.at[1]),
    ]
    for copy in small:
        copy.start()
    for i in range(CHUNKS):
        for copy in fetches(i):
            copy.start()
    for copy in small:
        copy.wait()
    grams = [row / points for row in from_branches(ups, 0)]
    state_out[...] = state_in[...]
    coefficients(STEPS, grams, state_in, state_out)
    for i in range(STEPS + 1):
        for j in range(STEPS):
            row = i * STEPS + j
            if i <= j + 1:
                hess_out[i, j : j + 1, :] = state_out[row : row + 1, :]
            else:
                hess_out[i, j : j + 1, :] = jnp.zeros((1, hess_out.shape[2]), F32)

    def body(i, carry):
        for copy in fetches(i):
            copy.wait()
        vector = None
        for l in range(STEPS + 1):
            row = basis_row(STEPS, l)
            term = state_out[row : row + 1, :] * vectors[l, rows(i)]
            vector = term if vector is None else vector + term
        result[rows(i)] = vector
        store(i).start()
        return carry

    lax.fori_loop(0, CHUNKS, body, 0)
    for i in range(CHUNKS):
        store(i).wait()


def last(points, ups, state, krylov, zs):
    columns = state.shape[1]
    hess = (STEPS + 1, STEPS, columns)
    return call(
        functools.partial(last_kernel, points=points),
        [ups, state, krylov] + list(zs),
        [ANY] * (3 + len(zs)),
        [jax.ShapeDtypeStruct(krylov.shape, F32), jax.ShapeDtypeStruct(hess, F32)],
        [ANY, pl.BlockSpec(memory_space=pltpu.VMEM)],
        [
            pltpu.VMEM(ups.shape, BF16),
            pltpu.VMEM(state.shape, F32),
            pltpu.VMEM(state.shape, F32),
            pltpu.VMEM((len(zs),) + zs[0].shape, F32),
            pltpu.VMEM(zs[0].shape, F32),
            pltpu.SemaphoreType.DMA((2,)),
            pltpu.SemaphoreType.DMA((len(zs), CHUNKS)),
            pltpu.SemaphoreType.DMA((CHUNKS,)),
        ],
        "last_vector",
        1 << 22,
        6 << 20,
        {2: 0},
    )


def shards(
    rhs,
    near_blocks,
    near_index,
    near_mask,
    basis,
    far_blocks,
    far_slot,
    far_mask,
    send_slot,
    transfer,
    top_blocks,
):
    outer, inner = lax.axis_size("outer"), lax.axis_size("inner")
    points = outer * inner * rhs.shape[0]
    leaves, rank = basis.shape[0], basis.shape[1]
    slots = send_slot.shape[2]
    branch = lax.axis_index("outer").astype(jnp.int32).reshape(1)
    up_pairs = [(i, i + 1) for i in range(inner - 1)]
    down_pairs = [(j, i) for i, j in up_pairs]
    wanted = send_slot[0].T
    packed = pack_far(far_blocks, far_mask)

    def exchange(array, axis):
        return lax.all_to_all(array, axis, split_axis=0, concat_axis=0, tiled=True)

    zs = [rhs]
    state = jnp.zeros((STATE_ROWS, rhs.shape[1]), F32)
    out = stage(0, points, wanted, branch, zs, basis, transfer, None)
    for k in range(1, STEPS + 1):
        before = lax.ppermute(out["high"], "inner", up_pairs)
        after = lax.ppermute(out["low"], "inner", down_pairs)
        recv = exchange(tie(out["send"], before, after), "inner")
        earlier = (packed,) if k == 1 else ()
        near = near_field(
            near_index, near_mask, near_blocks, before, out["coarse"], after, *earlier
        )
        summed = gather_sum(recv, slots * rank, outer, near)
        ups = exchange(summed, "outer")
        local_far = far_field(far_slot, recv, packed, slots, summed)
        later = (ups, state, top_blocks, local_far, near)
        out = stage(k, points, wanted, branch, zs, basis, transfer, later)
        state = out["state"]
        zs = zs + [out["z"]]
    krylov = basis_vectors(state, zs[:STEPS], leaves)
    recv = exchange(out["send"], "inner")
    ups = exchange(gather_sum(recv, 0, outer, krylov), "outer")
    return tuple(last(points, ups, state, krylov, zs))


def solution(mesh):
    return jax.shard_map(
        shards,
        mesh=mesh,
        in_specs=(
            P(("outer", "inner"), None),
            P(("outer", "inner"), None, None, None),
            P(("outer", "inner"), None),
            P(("outer", "inner"), None),
            P(("outer", "inner"), None, None),
            P(("outer", "inner"), None, None, None),
            P(("outer", "inner"), None),
            P(("outer", "inner"), None),
            P(("outer", "inner"), None, None),
            P(("outer", "inner"), None, None),
            P("outer", None, None, None),
        ),
        out_specs=(P(None, ("outer", "inner"), None), P()),
        check_vma=False,
    )
```

time: 1220 us -> 290 us (0.24)
  blocking collectives: 923 us -> 10.4 us
  Pallas kernels: 0 us -> 129 us
  local copies, waits for them, and re-layouts: 107 us -> 10.3 us
  matrix products: 91 us -> 0 us
  waiting for transfers between devices: 0.12 us -> 56.5 us
  starting transfers between devices: 24.3 us -> 80.2 us
  other arithmetic: 52.5 us -> 0 us
  between operations: 14.5 us -> 0.98 us
    psum x13 -> x0, blocking collectives: 811 us -> none  [the longest x5 319 us: lengths(): return lax.psum(jnp.sum(values * values, axis=0), ('outer', 'inner'))]
    pallas_call x0 -> x25, Pallas kernels: none -> 129 us  [the longest x19 114 us: call(): pl.pallas_call(kernel, in_specs=in_specs, out_specs=out_specs, out_shape=...]
    all_gather x4 -> x0, blocking collectives: 112 us -> none  [shards(): coeffs = lax.all_gather(summed[None], 'outer', axis=0, tiled=True)]
    dot_general x24 -> x0, matrix products: 91 us -> none  [the longest x4 32.9 us: shards(): jnp.einsum('lnij,lnjr->lir', near_blocks, neighbours, preferred_element_t...]
    gather x14 -> x0, local copies, waits for them, and re-layouts: 65.5 us -> none  [the longest x8 40.2 us: shards(): neighbours = padded[near_index] * near_weight]
    all_to_all x1 -> x9, starting transfers between devices: 7.11 us -> 64.1 us  [exchange(): return lax.all_to_all(array, axis, split_axis=0, concat_axis=0, tiled=True)]
    all_to_all x1 -> x9, waiting for transfers between devices: 0.01 us -> 34.5 us  [exchange(): return lax.all_to_all(array, axis, split_axis=0, concat_axis=0, tiled=True)]
    ppermute x8, waiting for transfers between devices: 0.02 us -> 22.1 us  [the longest x4 15.2 us: shards(): after = lax.ppermute(out['low'], 'inner', down_pairs)]
  transfers between devices with their start and end apart: 13 -> 17, of which waited for: 0 -> 12; matrix products, arithmetic and copies ran while one was open for 10% -> 0% of each run, Pallas kernels for 0% -> 28%
where the time goes in v1:
time: 290 us; the launch traced here: 288 us
  Pallas kernels  129 us (44%)
  starting transfers between devices  80.2 us (28%)
  waiting for transfers between devices  56.5 us (19%)
  blocking collectives  10.4 us (4%)
  local copies, waits for them, and re-layouts  10.3 us (4%)
    pallas_call x19, Pallas kernels, call(): pl.pallas_call(kernel, in_specs=in_specs, out_specs=out_specs, out_shape=...  114 us
    all_to_all x9, starting transfers between devices, exchange(): return lax.all_to_all(array, axis, split_axis=0, concat_axis=0, tiled=True)  64.1 us
    all_to_all x9, waiting for transfers between devices, exchange(): return lax.all_to_all(array, axis, split_axis=0, concat_axis=0, tiled=True)  34.5 us
    ppermute x4, waiting for transfers between devices, shards(): after = lax.ppermute(out['low'], 'inner', down_pairs)  15.2 us
    ppermute x4, starting transfers between devices, shards(): before = lax.ppermute(out['high'], 'inner', up_pairs)  11 us
    all_to_all x1, blocking collectives, exchange(): return lax.all_to_all(array, axis, split_axis=0, concat_axis=0, tiled=True)  10.4 us
    unnamed x34, local copies, waits for them, and re-layouts  9.65 us
    pallas_call x5, Pallas kernels, gather_sum(): pl.pallas_call(functools.partial(gather_sum_kernel, lead=lead), in_specs=...  8.32 us
  transfers between devices with their start and end apart: 17, of which 12 were waited for; matrix products, arithmetic and copies ran while one was open for 0% of the time, Pallas kernels for 28%

profile of v1, /device:TPU:1, one launch (start us, length us, event | category | flops | bytes accessed | tf_op | source)
XLA Modules:
  0.0 288.0 jit_solution(13099937618889637400)
XLA Ops:
  0.6 4.3 %stage0.1 = (bf16[16,336,128]{2,1,0:T(8,128)(2,1)}, bf16[8,256,128]{2,1,0:T(8,128)(2,1)}, bf16[2,256,128]{2,1,0:T(8,128)(2,1)}, bf16[2,256,128]{2,1,0:T(8,128)(2,1)}) custom-call(s32[4,16]{1,0:T(4,128)} %bitcast.4, s32[1]{0:T(128)} %bitcast.2.refs_1_, f32[2048,128]{1,0:T(8,128)} %refs_0_.3, bf16[8,64,256]{2,1,0:T(8,128)(2,1)} %refs_11_.3, ...), custom_call_target="tpu_custom_call" | custom-call | flops 134217728 | bytes 4194304 | tf_op jit(solution)/shard_map/stage0/pallas_call | solution.py:145
  4.9 4.4 %collective-permute-start = (bf16[2,256,128]{2,1,0:T(8,128)(2,1)}, bf16[2,256,128]{2,1,0:T(8,128)(2,1)S(1)}, u32[]{:S(2)}, u32[]{:S(2)}) collective-permute-start(bf16[2,256,128]{2,1,0:T(8,128)(2,1)} %get-tuple-element.28), channel_id=1, source_target_pairs={{0,1},{1,2},{2,3},{3,4},{4,5},{5,6},{6,7},{7,8},{8,9},{9,10},{10,1... | collective-permute-start | bytes 393224 | tf_op jit(solution)/shard_map/ppermute | solution.py:725
  11.8 4.1 %collective-permute-done.1.after.after_ref = bf16[2,256,128]{2,1,0:T(8,128)(2,1)S(1)} collective-permute-done((bf16[2,256,128]{2,1,0:T(8,128)(2,1)}, bf16[2,256,128]{2,1,0:T(8,128)(2,1)S(1)}, u32[]{:S(2)}, u32[]{:S(2)}) %collective-permute-start.1) | collective-permute-done | bytes 131104 | tf_op jit(solution)/shard_map/ppermute | solution.py:726
  16.5 8.2 %all-to-all-start = ((bf16[16,336,128]{2,1,0:T(8,128)(2,1)}), bf16[16,336,128]{2,1,0:T(8,128)(2,1)S(1)}, u32[]{:S(2)}, u32[]{:S(2)}) async-start(bf16[16,336,128]{2,1,0:T(8,128)(2,1)} %tie.4), calls=%async_computation | async-start | bytes 2752512 | tf_op jit(solution)/shard_map/all_to_all | solution.py:719
  24.7 5.3 %pack_far.1.refs_0_.far_ref = bf16[8,64,3072]{2,1,0:T(8,128)(2,1)} custom-call(s32[8,48]{1,0:T(8,128)} %mask_ref.5, bf16[8,48,64,64]{3,2,1,0:T(8,128)(2,1)} %far_ref.1), custom_call_target="tpu_custom_call" | custom-call | bytes 12582912 | tf_op jit(solution)/shard_map/pack_far/pallas_call | solution.py:145
  30.0 8.6 %near_field.4.refs_0_.refs_7_ = f32[2048,128]{1,0:T(8,128)} custom-call(s32[8,8]{1,0:T(8,128)} %index_ref.7, s32[8,8]{1,0:T(8,128)} %mask_ref.9, bf16[8,8,256,256]{3,2,1,0:T(8,128)(2,1)} %blocks_ref.7, bf16[2,256,128]{2,1,0:T(8,128)(2,1)} %copy-done.8, bf16[8,256,128]{2,1,0:T(8,128)(2,1)} %get-tuple-element.30.own_ref, bf16[2,256,128]{2,1,0:T(8,128)(2,1)} %copy-done.12, ...), custom_call_target="tpu_custom_call" | custom-call | flops 1073741824 | bytes 8388608 | tf_op jit(solution)/shard_map/near_field/pallas_call | solution.py:145
  38.6 4.6 %all-to-all-done.recv_ref = bf16[16,336,128]{2,1,0:T(8,128)(2,1)S(1)} async-done(((bf16[16,336,128]{2,1,0:T(8,128)(2,1)}), bf16[16,336,128]{2,1,0:T(8,128)(2,1)S(1)}, u32[]{:S(2)}, u32[]{:S(2)}) %all-to-all-start) | async-done | bytes 1376288 | tf_op jit(solution)/shard_map/all_to_all | solution.py:719
  44.3 1.7 gather_sum.5.earlier_ref
  46.0 8.1 %all-to-all-start.1 = ((bf16[8,80,128]{2,1,0:T(8,128)(2,1)}), bf16[8,80,128]{2,1,0:T(8,128)(2,1)S(1)}, u32[]{:S(2)}, u32[]{:S(2)}) async-start(bf16[8,80,128]{2,1,0:T(8,128)(2,1)} %gather_sum.5.earlier_ref), calls=%async_computation.1 | async-start | bytes 327680 | tf_op jit(solution)/shard_map/all_to_all | solution.py:719
  54.1 8.3 %far_field.4.refs_6_ = f32[8,64,128]{2,1,0:T(8,128)} custom-call(s32[8,48]{1,0:T(8,128)} %far_slot.7, bf16[16,336,128]{2,1,0:T(8,128)(2,1)} %copy-done, bf16[8,64,3072]{2,1,0:T(8,128)(2,1)} %pack_far.1.refs_0_.far_ref, bf16[8,80,128]{2,1,0:T(8,128)(2,1)} %gather_sum.5.earlier_ref), custom_call_target="tpu_custom_call" | custom-call | flops 402653184 | bytes 4194304 | tf_op jit(solution)/shard_map/far_field/pallas_call | solution.py:145
  63.1 8.2 %stage1.1 = (f32[64,128]{1,0:T(8,128)}, f32[2048,128]{1,0:T(8,128)}, bf16[16,336,128]{2,1,0:T(8,128)(2,1)}, bf16[8,256,128]{2,1,0:T(8,128)(2,1)}, bf16[2,256,128...) custom-call(s32[4,16]{1,0:T(4,128)} %bitcast.5, s32[1]{0:T(128)} %bitcast.2.refs_1_, f32[2048,128]{1,0:T(8,128)} %refs_0_.3, ...), custom_call_target="tpu_custom_call" | custom-call | flops 134217728 | bytes 5242880 | tf_op jit(solution)/shard_map/stage1/pallas_call | solution.py:145
  71.3 2.2 collective-permute-start.2
  74.8 1.9 collective-permute-done.2.before.before_ref
  76.7 3.7 %collective-permute-done.3.after.after_ref = bf16[2,256,128]{2,1,0:T(8,128)(2,1)S(1)} collective-permute-done((bf16[2,256,128]{2,1,0:T(8,128)(2,1)}, bf16[2,256,128]{2,1,0:T(8,128)(2,1)S(1)}, u32[]{:S(2)}, u32[]{:S(2)}) %collective-permute-start.3) | collective-permute-done | bytes 131104 | tf_op jit(solution)/shard_map/ppermute | solution.py:726
  81.1 7.0 %all-to-all-start.2 = ((bf16[16,336,128]{2,1,0:T(8,128)(2,1)}), bf16[16,336,128]{2,1,0:T(8,128)(2,1)S(1)}, u32[]{:S(2)}, u32[]{:S(2)}) async-start(bf16[16,336,128]{2,1,0:T(8,128)(2,1)} %tie.5), calls=%async_computation.2 | async-start | bytes 2752512 | tf_op jit(solution)/shard_map/all_to_all | solution.py:719
  88.1 8.6 %near_field.5.refs_0_.refs_8_ = f32[2048,128]{1,0:T(8,128)} custom-call(s32[8,8]{1,0:T(8,128)} %index_ref.7, s32[8,8]{1,0:T(8,128)} %mask_ref.9, bf16[8,8,256,256]{3,2,1,0:T(8,128)(2,1)} %blocks_ref.7, bf16[2,256,128]{2,1,0:T(8,128)(2,1)} %copy-done.9, bf16[8,256,128]{2,1,0:T(8,128)(2,1)} %get-tuple-element.35.own_ref, bf16[2,256,128]{2,1,0:T(8,128)(2,1)} %copy-done.13), custom_call_target="tpu_custom_call" | custom-call | flops 1073741824 | bytes 8388608 | tf_op jit(solution)/shard_map/near_field/pallas_call | solution.py:145
  96.7 10.0 %all-to-all-done.2.recv_ref = bf16[16,336,128]{2,1,0:T(8,128)(2,1)S(1)} async-done(((bf16[16,336,128]{2,1,0:T(8,128)(2,1)}), bf16[16,336,128]{2,1,0:T(8,128)(2,1)S(1)}, u32[]{:S(2)}, u32[]{:S(2)}) %all-to-all-start.2) | async-done | bytes 1376288 | tf_op jit(solution)/shard_map/all_to_all | solution.py:719
  107.7 1.7 gather_sum.6.earlier_ref
  109.5 7.8 %all-to-all-start.3 = ((bf16[8,80,128]{2,1,0:T(8,128)(2,1)}), bf16[8,80,128]{2,1,0:T(8,128)(2,1)S(1)}, u32[]{:S(2)}, u32[]{:S(2)}) async-start(bf16[8,80,128]{2,1,0:T(8,128)(2,1)} %gather_sum.6.earlier_ref), calls=%async_computation.3 | async-start | bytes 327680 | tf_op jit(solution)/shard_map/all_to_all | solution.py:719
  117.3 8.3 %far_field.5.refs_7_ = f32[8,64,128]{2,1,0:T(8,128)} custom-call(s32[8,48]{1,0:T(8,128)} %far_slot.7, bf16[16,336,128]{2,1,0:T(8,128)(2,1)} %copy-done.2, bf16[8,64,3072]{2,1,0:T(8,128)(2,1)} %pack_far.1.refs_0_.far_ref, bf16[8,80,128]{2,1,0:T(8,128)(2,1)} %gather_sum.6.earlier_ref), custom_call_target="tpu_custom_call" | custom-call | flops 402653184 | bytes 4194304 | tf_op jit(solution)/shard_map/far_field/pallas_call | solution.py:145
  126.3 8.6 %stage2.1 = (f32[64,128]{1,0:T(8,128)}, f32[2048,128]{1,0:T(8,128)}, bf16[16,336,128]{2,1,0:T(8,128)(2,1)}, bf16[8,256,128]{2,1,0:T(8,128)(2,1)}, bf16[2,256,128...) custom-call(s32[4,16]{1,0:T(4,128)} %bitcast.6, s32[1]{0:T(128)} %bitcast.2.refs_1_, f32[2048,128]{1,0:T(8,128)} %refs_0_.3, ...), custom_call_target="tpu_custom_call" | custom-call | flops 134217728 | bytes 6291456 | tf_op jit(solution)/shard_map/stage2/pallas_call | solution.py:145
  134.9 2.2 collective-permute-start.4
  137.1 1.3 collective-permute-start.5
  138.4 1.9 collective-permute-done.4.before.before_ref
  140.3 3.7 %collective-permute-done.5.after.after_ref = bf16[2,256,128]{2,1,0:T(8,128)(2,1)S(1)} collective-permute-done((bf16[2,256,128]{2,1,0:T(8,128)(2,1)}, bf16[2,256,128]{2,1,0:T(8,128)(2,1)S(1)}, u32[]{:S(2)}, u32[]{:S(2)}) %collective-permute-start.5) | collective-permute-done | bytes 131104 | tf_op jit(solution)/shard_map/ppermute | solution.py:726
  144.7 7.0 %all-to-all-start.4 = ((bf16[16,336,128]{2,1,0:T(8,128)(2,1)}), bf16[16,336,128]{2,1,0:T(8,128)(2,1)S(1)}, u32[]{:S(2)}, u32[]{:S(2)}) async-start(bf16[16,336,128]{2,1,0:T(8,128)(2,1)} %tie.6), calls=%async_computation.4 | async-start | bytes 2752512 | tf_op jit(solution)/shard_map/all_to_all | solution.py:719
  151.7 8.6 %near_field.6.refs_0_.refs_9_ = f32[2048,128]{1,0:T(8,128)} custom-call(s32[8,8]{1,0:T(8,128)} %index_ref.7, s32[8,8]{1,0:T(8,128)} %mask_ref.9, bf16[8,8,256,256]{3,2,1,0:T(8,128)(2,1)} %blocks_ref.7, bf16[2,256,128]{2,1,0:T(8,128)(2,1)} %copy-done.10, bf16[8,256,128]{2,1,0:T(8,128)(2,1)} %get-tuple-element.41.own_ref, bf16[2,256,128]{2,1,0:T(8,128)(2,1)} %copy-done.14), custom_call_target="tpu_custom_call" | custom-call | flops 1073741824 | bytes 8388608 | tf_op jit(solution)/shard_map/near_field/pallas_call | solution.py:145
  160.3 10.0 %all-to-all-done.4.recv_ref = bf16[16,336,128]{2,1,0:T(8,128)(2,1)S(1)} async-done(((bf16[16,336,128]{2,1,0:T(8,128)(2,1)}), bf16[16,336,128]{2,1,0:T(8,128)(2,1)S(1)}, u32[]{:S(2)}, u32[]{:S(2)}) %all-to-all-start.4) | async-done | bytes 1376288 | tf_op jit(solution)/shard_map/all_to_all | solution.py:719
  171.3 1.7 gather_sum.7.earlier_ref
  173.1 7.8 %all-to-all-start.5 = ((bf16[8,80,128]{2,1,0:T(8,128)(2,1)}), bf16[8,80,128]{2,1,0:T(8,128)(2,1)S(1)}, u32[]{:S(2)}, u32[]{:S(2)}) async-start(bf16[8,80,128]{2,1,0:T(8,128)(2,1)} %gather_sum.7.earlier_ref), calls=%async_computation.5 | async-start | bytes 327680 | tf_op jit(solution)/shard_map/all_to_all | solution.py:719
  180.9 8.3 %far_field.6.refs_8_ = f32[8,64,128]{2,1,0:T(8,128)} custom-call(s32[8,48]{1,0:T(8,128)} %far_slot.7, bf16[16,336,128]{2,1,0:T(8,128)(2,1)} %copy-done.3, bf16[8,64,3072]{2,1,0:T(8,128)(2,1)} %pack_far.1.refs_0_.far_ref, bf16[8,80,128]{2,1,0:T(8,128)(2,1)} %gather_sum.7.earlier_ref), custom_call_target="tpu_custom_call" | custom-call | flops 402653184 | bytes 4194304 | tf_op jit(solution)/shard_map/far_field/pallas_call | solution.py:145
  189.8 9.1 %stage3.1 = (f32[64,128]{1,0:T(8,128)}, f32[2048,128]{1,0:T(8,128)}, bf16[16,336,128]{2,1,0:T(8,128)(2,1)}, bf16[8,256,128]{2,1,0:T(8,128)(2,1)}, bf16[2,256,128...) custom-call(s32[4,16]{1,0:T(4,128)} %bitcast.7, s32[1]{0:T(128)} %bitcast.2.refs_1_, f32[2048,128]{1,0:T(8,128)} %refs_0_.3, ...), custom_call_target="tpu_custom_call" | custom-call | flops 134217728 | bytes 7340032 | tf_op jit(solution)/shard_map/stage3/pallas_call | solution.py:145
  199.0 2.2 collective-permute-start.6
  201.2 1.3 collective-permute-start.7
  202.5 1.9 collective-permute-done.6.before.before_ref
  204.4 3.7 %collective-permute-done.7.after.after_ref = bf16[2,256,128]{2,1,0:T(8,128)(2,1)S(1)} collective-permute-done((bf16[2,256,128]{2,1,0:T(8,128)(2,1)}, bf16[2,256,128]{2,1,0:T(8,128)(2,1)S(1)}, u32[]{:S(2)}, u32[]{:S(2)}) %collective-permute-start.7) | collective-permute-done | bytes 131104 | tf_op jit(solution)/shard_map/ppermute | solution.py:726
  208.7 7.0 %all-to-all-start.6 = ((bf16[16,336,128]{2,1,0:T(8,128)(2,1)}), bf16[16,336,128]{2,1,0:T(8,128)(2,1)S(1)}, u32[]{:S(2)}, u32[]{:S(2)}) async-start(bf16[16,336,128]{2,1,0:T(8,128)(2,1)} %tie.7), calls=%async_computation.6 | async-start | bytes 2752512 | tf_op jit(solution)/shard_map/all_to_all | solution.py:719
  215.7 8.6 %near_field.7.refs_0_.refs_10_ = f32[2048,128]{1,0:T(8,128)} custom-call(s32[8,8]{1,0:T(8,128)} %index_ref.7, s32[8,8]{1,0:T(8,128)} %mask_ref.9, bf16[8,8,256,256]{3,2,1,0:T(8,128)(2,1)} %blocks_ref.7, bf16[2,256,128]{2,1,0:T(8,128)(2,1)} %copy-done.11, bf16[8,256,128]{2,1,0:T(8,128)(2,1)} %get-tuple-element.47.own_ref, bf16[2,256,128]{2,1,0:T(8,128)(2,1)} %copy-done.15), custom_call_target="tpu_custom_call" | custom-call | flops 1073741824 | bytes 8388608 | tf_op jit(solution)/shard_map/near_field/pallas_call | solution.py:145
  224.3 10.0 %all-to-all-done.6.recv_ref = bf16[16,336,128]{2,1,0:T(8,128)(2,1)S(1)} async-done(((bf16[16,336,128]{2,1,0:T(8,128)(2,1)}), bf16[16,336,128]{2,1,0:T(8,128)(2,1)S(1)}, u32[]{:S(2)}, u32[]{:S(2)}) %all-to-all-start.6) | async-done | bytes 1376288 | tf_op jit(solution)/shard_map/all_to_all | solution.py:719
  235.4 1.7 gather_sum.8.earlier_ref
  237.1 7.8 %all-to-all-start.7 = ((bf16[8,80,128]{2,1,0:T(8,128)(2,1)}), bf16[8,80,128]{2,1,0:T(8,128)(2,1)S(1)}, u32[]{:S(2)}, u32[]{:S(2)}) async-start(bf16[8,80,128]{2,1,0:T(8,128)(2,1)} %gather_sum.8.earlier_ref), calls=%async_computation.7 | async-start | bytes 327680 | tf_op jit(solution)/shard_map/all_to_all | solution.py:719
  244.9 8.3 %far_field.7.refs_9_ = f32[8,64,128]{2,1,0:T(8,128)} custom-call(s32[8,48]{1,0:T(8,128)} %far_slot.7, bf16[16,336,128]{2,1,0:T(8,128)(2,1)} %copy-done.1, bf16[8,64,3072]{2,1,0:T(8,128)(2,1)} %pack_far.1.refs_0_.far_ref, bf16[8,80,128]{2,1,0:T(8,128)(2,1)} %gather_sum.8.earlier_ref), custom_call_target="tpu_custom_call" | custom-call | flops 402653184 | bytes 4194304 | tf_op jit(solution)/shard_map/far_field/pallas_call | solution.py:145
  253.9 7.0 %stage4.1 = (f32[64,128]{1,0:T(8,128)}, f32[2048,128]{1,0:T(8,128)}, bf16[16,16,128]{2,1,0:T(8,128)(2,1)}) custom-call(s32[4,16]{1,0:T(4,128)} %bitcast.8, s32[1]{0:T(128)} %bitcast.2.refs_1_, f32[2048,128]{1,0:T(8,128)} %refs_0_.3, f32[2048,128]{1,0:T(8,128)} %get-tuple-element.31.refs_3_.refs_1_, f32[2048,128]{1,0:T(8,128)} %get-tuple-element.37.refs_4_.refs_2_, ...), custom_call_target="tpu_custom_call" | custom-call | flops 134217728 | bytes 8388608 | tf_op jit(solution)/shard_map/stage4/pallas_call | solution.py:145
  260.9 3.5 %all-to-all-start.8 = ((bf16[16,16,128]{2,1,0:T(8,128)(2,1)}), bf16[16,16,128]{2,1,0:T(8,128)(2,1)S(1)}, u32[]{:S(2)}, u32[]{:S(2)}) async-start(bf16[16,16,128]{2,1,0:T(8,128)(2,1)} %get-tuple-element.49), calls=%async_computation.8 | async-start | bytes 131072 | tf_op jit(solution)/shard_map/all_to_all | solution.py:719
  264.4 6.8 %basis_vectors.1.refs_0_.krylov_in = f32[5,2048,128]{2,1,0:T(8,128)} custom-call(f32[64,128]{1,0:T(8,128)} %get-tuple-element.50.state_ref.state_any, f32[2048,128]{1,0:T(8,128)} %refs_0_.3, f32[2048,128]{1,0:T(8,128)} %get-tuple-element.31.refs_3_.refs_1_, f32[2048,128]{1,0:T(8,128)} %get-tuple-element.37.refs_4_.refs_2_, ...), custom_call_target="tpu_custom_call" | custom-call | flops 8388608 | bytes 8388608 | tf_op jit(solution)/shard_map/basis_vectors/pallas_call | solution.py:594
  271.9 1.5 gather_sum.9
  273.4 10.4 %all_to_all.50.ups_any = bf16[8,16,128]{2,1,0:T(8,128)(2,1)} all-to-all(bf16[8,16,128]{2,1,0:T(8,128)(2,1)} %gather_sum.9), channel_id=1, replica_groups=mesh['outer'=8,'inner'=16] {'outer'}, dimensions={0} | all-to-all | bytes 65536 | tf_op jit(solution)/shard_map/all_to_all | solution.py:719
  283.8 4.2 %last_vector.1 = (f32[5,2048,128]{2,1,0:T(8,128)}, f32[5,4,128]{2,1,0:T(4,128)}) custom-call(bf16[8,16,128]{2,1,0:T(8,128)(2,1)} %all_to_all.50.ups_any, f32[64,128]{1,0:T(8,128)} %get-tuple-element.50.state_ref.state_any, f32[5,2048,128]{2,1,0:T(8,128)} %basis_vectors.1.refs_0_.krylov_in, f32[2048,128]{1,0:T(8,128)} %refs_0_.3, ...), custom_call_target="tpu_custom_call", output_to_operand_aliasing={{0}: (2, {})} | custom-call | flops 4194304 | bytes 6291456 | tf_op jit(solution)/shard_map/last_vector/pallas_call | solution.py:145
  (47 shorter events, 14.1 us)
Async XLA Ops:
  4.9 6.8 %collective-permute-start = (bf16[2,256,128]{2,1,0:T(8,128)(2,1)}, bf16[2,256,128]{2,1,0:T(8,128)(2,1)S(1)}, u32[]{:S(2)}, u32[]{:S(2)}) collective-permute-start(bf16[2,256,128]{2,1,0:T(8,128)(2,1)} %get-tuple-element.28), channel_id=1, source_target_pairs={{0,1},{1,2},{2,3},{3,4},{4,5},{5,6},{6,7},{7,8},{8,9},{9,10},{10,1... | collective-permute-start | bytes 393224 | tf_op jit(solution)/shard_map/ppermute | solution.py:725
  9.3 6.5 %collective-permute-start.1 = (bf16[2,256,128]{2,1,0:T(8,128)(2,1)}, bf16[2,256,128]{2,1,0:T(8,128)(2,1)S(1)}, u32[]{:S(2)}, u32[]{:S(2)}) collective-permute-start(bf16[2,256,128]{2,1,0:T(8,128)(2,1)} %get-tuple-element.29), channel_id=1, source_target_pairs={{1,0},{2,1},{3,2},{4,3},{5,4},{6,5},{7,6},{8,7},{9,8},{10,9},{11,1... | collective-permute-start | bytes 393224 | tf_op jit(solution)/shard_map/ppermute | solution.py:726
  11.8 4.1 %copy-start.8 = (bf16[2,256,128]{2,1,0:T(8,128)(2,1)}, bf16[2,256,128]{2,1,0:T(8,128)(2,1)S(1)}, u32[]{:S(2)}) copy-start(bf16[2,256,128]{2,1,0:T(8,128)(2,1)S(1)} %collective-permute-done.before.before_ref) | copy-start | bytes 393220
  15.9 0.7 copy-start.12
  16.5 26.7 %all-to-all-start = ((bf16[16,336,128]{2,1,0:T(8,128)(2,1)}), bf16[16,336,128]{2,1,0:T(8,128)(2,1)S(1)}, u32[]{:S(2)}, u32[]{:S(2)}) async-start(bf16[16,336,128]{2,1,0:T(8,128)(2,1)} %tie.4), calls=%async_computation | async-start | bytes 2752512 | tf_op jit(solution)/shard_map/all_to_all | solution.py:719
  43.2 1.1 copy-start
  46.0 16.4 %all-to-all-start.1 = ((bf16[8,80,128]{2,1,0:T(8,128)(2,1)}), bf16[8,80,128]{2,1,0:T(8,128)(2,1)S(1)}, u32[]{:S(2)}, u32[]{:S(2)}) async-start(bf16[8,80,128]{2,1,0:T(8,128)(2,1)} %gather_sum.5.earlier_ref), calls=%async_computation.1 | async-start | bytes 327680 | tf_op jit(solution)/shard_map/all_to_all | solution.py:719
  62.5 0.7 copy-start.4
  71.3 5.4 %collective-permute-start.2 = (bf16[2,256,128]{2,1,0:T(8,128)(2,1)}, bf16[2,256,128]{2,1,0:T(8,128)(2,1)S(1)}, u32[]{:S(2)}, u32[]{:S(2)}) collective-permute-start(bf16[2,256,128]{2,1,0:T(8,128)(2,1)} %get-tuple-element.33), channel_id=1, source_target_pairs={{0,1},{1,2},{2,3},{3,4},{4,5},{5,6},{6,7},{7,8},{8,9},{9,10},{10,1... | collective-permute-start | bytes 393224 | tf_op jit(solution)/shard_map/ppermute | solution.py:725
  73.5 6.9 %collective-permute-start.3 = (bf16[2,256,128]{2,1,0:T(8,128)(2,1)}, bf16[2,256,128]{2,1,0:T(8,128)(2,1)S(1)}, u32[]{:S(2)}, u32[]{:S(2)}) collective-permute-start(bf16[2,256,128]{2,1,0:T(8,128)(2,1)} %get-tuple-element.34), channel_id=1, source_target_pairs={{1,0},{2,1},{3,2},{4,3},{5,4},{6,5},{7,6},{8,7},{9,8},{10,9},{11,1... | collective-permute-start | bytes 393224 | tf_op jit(solution)/shard_map/ppermute | solution.py:726
  76.7 3.7 %copy-start.9 = (bf16[2,256,128]{2,1,0:T(8,128)(2,1)}, bf16[2,256,128]{2,1,0:T(8,128)(2,1)S(1)}, u32[]{:S(2)}) copy-start(bf16[2,256,128]{2,1,0:T(8,128)(2,1)S(1)} %collective-permute-done.2.before.before_ref) | copy-start | bytes 393220
  80.4 0.6 copy-start.13
  81.1 25.5 %all-to-all-start.2 = ((bf16[16,336,128]{2,1,0:T(8,128)(2,1)}), bf16[16,336,128]{2,1,0:T(8,128)(2,1)S(1)}, u32[]{:S(2)}, u32[]{:S(2)}) async-start(bf16[16,336,128]{2,1,0:T(8,128)(2,1)} %tie.5), calls=%async_computation.2 | async-start | bytes 2752512 | tf_op jit(solution)/shard_map/all_to_all | solution.py:719
  106.6 1.1 copy-start.2
  109.5 16.1 %all-to-all-start.3 = ((bf16[8,80,128]{2,1,0:T(8,128)(2,1)}), bf16[8,80,128]{2,1,0:T(8,128)(2,1)S(1)}, u32[]{:S(2)}, u32[]{:S(2)}) async-start(bf16[8,80,128]{2,1,0:T(8,128)(2,1)} %gather_sum.6.earlier_ref), calls=%async_computation.3 | async-start | bytes 327680 | tf_op jit(solution)/shard_map/all_to_all | solution.py:719
  125.6 0.7 copy-start.5
  134.9 5.4 %collective-permute-start.4 = (bf16[2,256,128]{2,1,0:T(8,128)(2,1)}, bf16[2,256,128]{2,1,0:T(8,128)(2,1)S(1)}, u32[]{:S(2)}, u32[]{:S(2)}) collective-permute-start(bf16[2,256,128]{2,1,0:T(8,128)(2,1)} %get-tuple-element.39), channel_id=1, source_target_pairs={{0,1},{1,2},{2,3},{3,4},{4,5},{5,6},{6,7},{7,8},{8,9},{9,10},{10,1... | collective-permute-start | bytes 393224 | tf_op jit(solution)/shard_map/ppermute | solution.py:725
  137.1 6.9 %collective-permute-start.5 = (bf16[2,256,128]{2,1,0:T(8,128)(2,1)}, bf16[2,256,128]{2,1,0:T(8,128)(2,1)S(1)}, u32[]{:S(2)}, u32[]{:S(2)}) collective-permute-start(bf16[2,256,128]{2,1,0:T(8,128)(2,1)} %get-tuple-element.40), channel_id=1, source_target_pairs={{1,0},{2,1},{3,2},{4,3},{5,4},{6,5},{7,6},{8,7},{9,8},{10,9},{11,1... | collective-permute-start | bytes 393224 | tf_op jit(solution)/shard_map/ppermute | solution.py:726
  140.3 3.7 %copy-start.10 = (bf16[2,256,128]{2,1,0:T(8,128)(2,1)}, bf16[2,256,128]{2,1,0:T(8,128)(2,1)S(1)}, u32[]{:S(2)}) copy-start(bf16[2,256,128]{2,1,0:T(8,128)(2,1)S(1)} %collective-permute-done.4.before.before_ref) | copy-start | bytes 393220
  144.0 0.7 copy-start.14
  144.7 25.5 %all-to-all-start.4 = ((bf16[16,336,128]{2,1,0:T(8,128)(2,1)}), bf16[16,336,128]{2,1,0:T(8,128)(2,1)S(1)}, u32[]{:S(2)}, u32[]{:S(2)}) async-start(bf16[16,336,128]{2,1,0:T(8,128)(2,1)} %tie.6), calls=%async_computation.4 | async-start | bytes 2752512 | tf_op jit(solution)/shard_map/all_to_all | solution.py:719
  170.2 1.1 copy-start.3
  173.1 16.1 %all-to-all-start.5 = ((bf16[8,80,128]{2,1,0:T(8,128)(2,1)}), bf16[8,80,128]{2,1,0:T(8,128)(2,1)S(1)}, u32[]{:S(2)}, u32[]{:S(2)}) async-start(bf16[8,80,128]{2,1,0:T(8,128)(2,1)} %gather_sum.7.earlier_ref), calls=%async_computation.5 | async-start | bytes 327680 | tf_op jit(solution)/shard_map/all_to_all | solution.py:719
  189.2 0.7 copy-start.6
  199.0 5.4 %collective-permute-start.6 = (bf16[2,256,128]{2,1,0:T(8,128)(2,1)}, bf16[2,256,128]{2,1,0:T(8,128)(2,1)S(1)}, u32[]{:S(2)}, u32[]{:S(2)}) collective-permute-start(bf16[2,256,128]{2,1,0:T(8,128)(2,1)} %get-tuple-element.45), channel_id=1, source_target_pairs={{0,1},{1,2},{2,3},{3,4},{4,5},{5,6},{6,7},{7,8},{8,9},{9,10},{10,1... | collective-permute-start | bytes 393224 | tf_op jit(solution)/shard_map/ppermute | solution.py:725
  201.2 6.9 %collective-permute-start.7 = (bf16[2,256,128]{2,1,0:T(8,128)(2,1)}, bf16[2,256,128]{2,1,0:T(8,128)(2,1)S(1)}, u32[]{:S(2)}, u32[]{:S(2)}) collective-permute-start(bf16[2,256,128]{2,1,0:T(8,128)(2,1)} %get-tuple-element.46), channel_id=1, source_target_pairs={{1,0},{2,1},{3,2},{4,3},{5,4},{6,5},{7,6},{8,7},{9,8},{10,9},{11,1... | collective-permute-start | bytes 393224 | tf_op jit(solution)/shard_map/ppermute | solution.py:726
  204.4 3.7 %copy-start.11 = (bf16[2,256,128]{2,1,0:T(8,128)(2,1)}, bf16[2,256,128]{2,1,0:T(8,128)(2,1)S(1)}, u32[]{:S(2)}) copy-start(bf16[2,256,128]{2,1,0:T(8,128)(2,1)S(1)} %collective-permute-done.6.before.before_ref) | copy-start | bytes 393220
  208.1 0.6 copy-start.15
  208.7 25.5 %all-to-all-start.6 = ((bf16[16,336,128]{2,1,0:T(8,128)(2,1)}), bf16[16,336,128]{2,1,0:T(8,128)(2,1)S(1)}, u32[]{:S(2)}, u32[]{:S(2)}) async-start(bf16[16,336,128]{2,1,0:T(8,128)(2,1)} %tie.7), calls=%async_computation.6 | async-start | bytes 2752512 | tf_op jit(solution)/shard_map/all_to_all | solution.py:719
  234.3 1.1 copy-start.1
  237.1 16.1 %all-to-all-start.7 = ((bf16[8,80,128]{2,1,0:T(8,128)(2,1)}), bf16[8,80,128]{2,1,0:T(8,128)(2,1)S(1)}, u32[]{:S(2)}, u32[]{:S(2)}) async-start(bf16[8,80,128]{2,1,0:T(8,128)(2,1)} %gather_sum.8.earlier_ref), calls=%async_computation.7 | async-start | bytes 327680 | tf_op jit(solution)/shard_map/all_to_all | solution.py:719
  253.2 0.7 copy-start.7
  260.9 10.3 %all-to-all-start.8 = ((bf16[16,16,128]{2,1,0:T(8,128)(2,1)}), bf16[16,16,128]{2,1,0:T(8,128)(2,1)S(1)}, u32[]{:S(2)}, u32[]{:S(2)}) async-start(bf16[16,16,128]{2,1,0:T(8,128)(2,1)} %get-tuple-element.49), calls=%async_computation.8 | async-start | bytes 131072 | tf_op jit(solution)/shard_map/all_to_all | solution.py:719
  271.2 0.6 copy-start.16

commit v2 on v0

v2 whole, which is shorter than its diff:
```python
import functools

import jax
import jax.numpy as jnp
from jax import lax
from jax.experimental import pallas as pl
from jax.experimental.pallas import tpu as pltpu
from jax.sharding import PartitionSpec as P

HW = 2
STEPS = 4
EPS = 1e-06
PIECES = 3
DOT_ROWS = 16
STATE_ROWS = 64
VMEM_BYTES = 32 * 1024 * 1024
BF16 = jnp.bfloat16
F32 = jnp.float32


def dot(a, b):
    return jnp.dot(a, b, preferred_element_type=F32)


def dot_first(a, b):
    return lax.dot_general(a, b, (((0,), (0,)), ((), ())), preferred_element_type=F32)


def store_split(ref, values, count):
    rest = values
    ref[...] = jnp.zeros(ref.shape, F32)
    for piece in range(PIECES):
        part = rest.astype(BF16).astype(F32)
        ref[piece * 5 : piece * 5 + count, :] = part[:count]
        rest = rest - part


def joined(rows):
    return [rows[i : i + 1] + rows[5 + i : 6 + i] + rows[10 + i : 11 + i] for i in range(5)]


def entry_row(i, l):
    low, high = min(i, l), max(i, l)
    return 20 + high * (high + 1) // 2 + low


def basis_row(i, l):
    return 32 + i * (i + 1) // 2 + l


def coefficients(m, grams, state_in, state_out):
    last = m - 1
    entry = lambda i, l: state_in[entry_row(i, l) : entry_row(i, l) + 1, :]
    expand = lambda i, l: state_in[basis_row(i, l) : basis_row(i, l) + 1, :]

    def put(row, value):
        state_out[row : row + 1, :] = value

    dots = []
    for i in range(m):
        dots.append(sum(expand(i, l) * grams[l] for l in range(i + 1)))
    weights = [dots[i] + entry(i, last) for i in range(m)]
    spread = [sum(weights[l] * entry(i, l) for l in range(m)) for i in range(m)]
    square = grams[m]
    for i in range(m):
        square = square + weights[i] * (weights[i] + spread[i] - 2.0 * dots[i])
    total = jnp.maximum(square, 0.0) + EPS
    root = jnp.sqrt(total)
    inverse = 1.0 / root
    for l in range(m):
        value = sum(weights[i] * expand(i, l) for i in range(l, m))
        put(basis_row(m, l), -inverse * value)
    put(basis_row(m, m), inverse)
    for i in range(m):
        put(i * STEPS + last, weights[i] + (1.0 if i == last else 0.0))
    if m > 0:
        put(m * STEPS + last, root)
    if m < STEPS:
        for i in range(m):
            put(entry_row(i, m), (-entry(i, last) - spread[i]) * inverse)
        put(entry_row(m, m), -EPS / total)
    return weights, inverse


def from_branches(ups_ref, rank):
    rows = ups_ref[0, rank:].astype(F32)
    for c in range(1, ups_ref.shape[0]):
        rows = rows + ups_ref[c, rank:].astype(F32)
    return joined(rows)


SMEM = pl.BlockSpec(memory_space=pltpu.SMEM)
VMEM = pl.BlockSpec(memory_space=pltpu.VMEM)
HBM = pl.BlockSpec(memory_space=pl.ANY)
AFTER = pl.BlockSpec(memory_space=pl.ANY)
AFTER_VMEM = pl.BlockSpec(memory_space=pl.ANY)
LOOSE = pl.BlockSpec(memory_space=pl.ANY)
FREE = pl.BlockSpec(memory_space=pltpu.VMEM)
AHEAD = 3
PIN = True


def call(kernel, args, in_specs, outs, scratch, name, flops, moved, aliases={}):
    def pinned(array, spec):
        if not PIN or not any(spec is one for one in (VMEM, HBM, AFTER, AFTER_VMEM)):
            return array
        in_vmem = spec is VMEM or spec is AFTER_VMEM
        return pltpu.with_memory_space_constraint(array, pltpu.VMEM if in_vmem else pltpu.HBM)

    def shape_of(shape, dtype, spec):
        if not PIN or not (spec is VMEM or spec is HBM):
            return jax.ShapeDtypeStruct(shape, dtype)
        return (pltpu.VMEM if spec is VMEM else pltpu.HBM)(shape, dtype)

    return pl.pallas_call(
        kernel,
        in_specs=list(in_specs),
        out_specs=[spec for _, _, spec in outs],
        out_shape=[shape_of(*out) for out in outs],
        scratch_shapes=scratch,
        input_output_aliases=aliases,
        compiler_params=pltpu.CompilerParams(vmem_limit_bytes=VMEM_BYTES),
        cost_estimate=pl.CostEstimate(flops=flops, bytes_accessed=moved, transcendentals=0),
        name=name,
    )(*[pinned(array, spec) for array, spec in zip(args, in_specs)])


def semaphores(*shape):
    return pltpu.SemaphoreType.DMA(shape)


def windowed(count, ahead, fetch, work):
    def start(i):
        for j, copy in enumerate(fetch(i)):
            copy.start(priority=j % 2)

    def body(i, carry):
        @pl.when(i + ahead < count)
        def _():
            start(i + ahead)

        for copy in fetch(i):
            copy.wait()
        work(i)
        return carry

    def begin():
        for i in range(min(ahead, count)):
            start(i)

    return begin, lambda: lax.fori_loop(0, count, body, 0)


def slab(i, size):
    return pl.ds(pl.multiple_of(i * size, size), size)


def pack_kernel(mask_ref, slot_ref, far_ref, out_ref, blocks, total, packed, arrived, left):
    leaves, entries, rank, _ = blocks.shape
    sources, _, width = packed.shape
    slots = width // rank

    def fetch(leaf):
        halves = [pl.ds(j * (entries // 2), entries // 2) for j in range(2)]
        return [
            pltpu.make_async_copy(far_ref.at[leaf, half], blocks.at[leaf, half], arrived.at[leaf, j])
            for j, half in enumerate(halves)
        ]

    def store(leaf):
        rows = slab(leaf, rank)
        return pltpu.make_async_copy(packed.at[:, rows], out_ref.at[:, rows], left.at[leaf])

    def work(leaf):
        total[...] = jnp.zeros(total.shape, F32)
        for f in range(entries):
            weight = mask_ref[leaf, f].astype(F32)
            total[slot_ref[leaf, f]] += blocks[leaf, f].astype(F32) * weight
        rows = slab(leaf, rank)
        for source in range(sources):
            sides = [total[source * slots + s] for s in range(slots)]
            packed[source, rows] = jnp.concatenate(sides, axis=1).astype(BF16)
        store(leaf).start()

    begin, run = windowed(leaves, AHEAD, fetch, work)
    begin()
    run()
    for leaf in range(leaves):
        store(leaf).wait()


def pack_far(far_blocks, far_mask, far_slot, inner, slots):
    leaves, entries, rank, _ = far_blocks.shape
    shape = (inner, leaves * rank, slots * rank)
    return call(
        pack_kernel,
        (far_mask, far_slot, far_blocks),
        (SMEM, SMEM, HBM),
        [(shape, BF16, HBM)],
        [
            pltpu.VMEM(far_blocks.shape, BF16),
            pltpu.VMEM((inner * slots, rank, rank), F32),
            pltpu.VMEM(shape, BF16),
            semaphores(leaves, 2),
            semaphores(leaves),
        ],
        "pack_far",
        0,
        10 << 20,
    )[0]


def near_kernel(index_ref, mask_ref, blocks_ref, own_ref, *refs):
    out_ref, blocks, own, result, arrived, came, left = refs[-7:]
    leaves, entries, size, _ = blocks.shape
    half = entries // 2

    def fetch(i):
        leaf, pairs = i // 2, [pl.ds(i % 2 * half + j * half // 2, half // 2) for j in range(2)]
        return [
            pltpu.make_async_copy(
                blocks_ref.at[leaf, pair], blocks.at[leaf, pair], arrived.at[i, j]
            )
            for j, pair in enumerate(pairs)
        ]

    def store(leaf):
        return pltpu.make_async_copy(
            result.at[leaf], out_ref.at[slab(leaf, size)], left.at[leaf]
        )

    def work(i):
        leaf, part = i // 2, i % 2
        total = None
        for j in range(half):
            n = part * half + j
            place = index_ref[leaf, n] - HW
            inside = (place >= 0) & (place < leaves)
            weight = jnp.where(inside, mask_ref[leaf, n], 0).astype(F32).astype(BF16)
            values = own[jnp.clip(place, 0, leaves - 1)] * weight
            term = dot(blocks[leaf, n], values)
            total = term if total is None else total + term

        @pl.when(part == 0)
        def _():
            result[leaf] = total

        @pl.when(part == 1)
        def _():
            result[leaf] += total
            store(leaf).start()

    begin, run = windowed(2 * leaves, 2 * AHEAD, fetch, work)
    copy = pltpu.make_async_copy(own_ref, own, came)
    copy.start()
    begin()
    copy.wait()
    run()
    for leaf in range(leaves):
        store(leaf).wait()


def near_field(near_index, near_mask, near_blocks, own, *earlier):
    leaves, _, size, _ = near_blocks.shape
    columns = own.shape[2]
    return call(
        near_kernel,
        (near_index, near_mask, near_blocks, own) + earlier,
        (SMEM, SMEM, HBM, HBM) + (AFTER,) * len(earlier),
        [((leaves * size, columns), F32, HBM)],
        [
            pltpu.VMEM(near_blocks.shape, BF16),
            pltpu.VMEM(own.shape, BF16),
            pltpu.VMEM((leaves, size, columns), F32),
            semaphores(2 * leaves, 2),
            semaphores(),
            semaphores(leaves),
        ],
        "near_field",
        2 * near_blocks.size * columns,
        2 * near_blocks.size,
    )[0]


def gather_sum_kernel(recv, *refs, lead):
    out_ref, split = refs[-2:]
    rank = out_ref.shape[1] - DOT_ROWS
    total = recv[0, lead:].astype(F32)
    for i in range(1, recv.shape[0]):
        total = total + recv[i, lead:].astype(F32)
    store_split(split, jnp.concatenate(joined(total[rank:]), axis=0), 5)
    dots = split[...].astype(BF16)
    for c in range(out_ref.shape[0]):
        if rank > 0:
            out_ref[c, :rank] = total[:rank].astype(BF16)
        out_ref[c, rank:] = dots


def gather_sum(recv, lead, outer, earlier):
    _, rows, columns = recv.shape
    return call(
        functools.partial(gather_sum_kernel, lead=lead),
        (recv, earlier),
        (VMEM, AFTER),
        [((outer, rows - lead, columns), BF16, VMEM)],
        [pltpu.VMEM((DOT_ROWS, columns), F32)],
        "gather_sum",
        1 << 20,
        1 << 19,
    )[0]


def late_kernel(index_ref, mask_ref, recv, packed_ref, blocks_ref, before, after, near_ref, *refs):
    out_ref, far_ref, packed, blocks, halo, near, far = refs[1:8]
    arrived, came, fetched, near_came, left, far_left = refs[8:]
    leaves, entries, size, _ = blocks.shape
    sources, _, width = packed.shape
    reach = before.shape[0]

    rows = packed.shape[1] // 2

    def fetch(i):
        halves = [pl.ds(j * rows, rows) for j in range(2)]
        return [
            pltpu.make_async_copy(packed_ref.at[i, half], packed.at[i, half], arrived.at[i, j])
            for j, half in enumerate(halves)
        ]

    sides = [
        pltpu.make_async_copy(before, halo.at[pl.ds(0, reach)], came.at[0]),
        pltpu.make_async_copy(after, halo.at[pl.ds(reach, reach)], came.at[1]),
    ]

    def get(leaf):
        return pltpu.make_async_copy(
            near_ref.at[slab(leaf, size)], near.at[leaf], near_came.at[leaf]
        )

    def store(leaf):
        return pltpu.make_async_copy(near.at[leaf], out_ref.at[slab(leaf, size)], left.at[leaf])

    def for_halo(leaf, do):
        for n in range(entries):
            place = index_ref[leaf, n]
            low = place < reach

            @pl.when((mask_ref[leaf, n] != 0) & (low | (place >= reach + leaves)))
            def _():
                block = pltpu.make_async_copy(
                    blocks_ref.at[leaf, n], blocks.at[leaf, n], fetched.at[leaf, n]
                )
                do(n, jnp.where(low, place, place - leaves), block)

    def ask(leaf, carry):
        for_halo(leaf, lambda n, place, block: block.start(priority=n % 2))
        return carry

    def work(i):
        term = dot(packed[i], recv[i, :width])

        @pl.when(i == 0)
        def _():
            far[...] = term

        @pl.when(i > 0)
        def _():
            far[...] += term

    def add(leaf, carry):
        get(leaf).wait()

        def one(n, place, block):
            block.wait()
            near[leaf] += dot(blocks[leaf, n], halo[place])

        for_halo(leaf, one)
        store(leaf).start()
        return carry

    begin, run = windowed(sources, 2 * AHEAD, fetch, work)
    begin()
    for side in sides:
        side.start()
    lax.fori_loop(0, leaves, ask, 0)
    for leaf in range(leaves):
        get(leaf).start(priority=leaf % 2)
    run()
    out = pltpu.make_async_copy(far, far_ref, far_left)
    out.start()
    for side in sides:
        side.wait()
    lax.fori_loop(0, leaves, add, 0)
    for leaf in range(leaves):
        store(leaf).wait()
    out.wait()


def late_fields(near_index, near_mask, recv, packed, near_blocks, before, after, near, earlier):
    leaves, _, size, _ = near_blocks.shape
    sources, rows, _ = packed.shape
    columns = recv.shape[2]
    halo = (2 * before.shape[0],) + before.shape[1:]
    return call(
        late_kernel,
        (near_index, near_mask, recv, packed, near_blocks, before, after, near, earlier),
        (SMEM, SMEM, VMEM, HBM, HBM, LOOSE, LOOSE, HBM, AFTER_VMEM),
        [(near.shape, F32, HBM), ((rows, columns), F32, HBM)],
        [
            pltpu.VMEM(packed.shape, BF16),
            pltpu.VMEM(near_blocks.shape, BF16),
            pltpu.VMEM(halo, BF16),
            pltpu.VMEM((leaves, size, columns), F32),
            pltpu.VMEM((rows, columns), F32),
            semaphores(sources, 2),
            semaphores(2),
            semaphores(leaves, near_blocks.shape[1]),
            semaphores(leaves),
            semaphores(leaves),
            semaphores(),
        ],
        "late_fields",
        2 * packed.size * columns,
        2 * packed.size + (1 << 20),
    )


def stage_kernel(*refs, k, points):
    refs = list(refs)
    take = lambda count: [refs.pop(0) for _ in range(count)]
    m = k - 1
    first, sends = k == 0, k < STEPS
    send_slot, branch = take(2)
    zs = take(max(k, 1))
    if not first:
        ups, state, top_any, far_any, near_any = take(5)
    basis_any, transfer_any = take(2)
    if not first:
        (z_any,) = take(1)
    state_out, send = take(2)
    if sends:
        coarse_any, low_any, high_any = take(3)
    basis, transfer, vectors, sums, split, arrived, came, left = take(8)
    if sends:
        coarse, skeletons, upward, out = take(4)
    if not first:
        top, far, near, result, coef, incoming = take(6)

    leaves, rank, size = basis.shape

    def fetch(i):
        pairs = [(z.at[slab(i, size)], vectors.at[l, i]) for l, z in enumerate(zs)]
        if first:
            half = size // 2
            rows = [pl.ds(pl.multiple_of(i * size + j * half, half), half) for j in range(2)]
            pairs = [(zs[0].at[rows[j]], vectors.at[0, i, pl.ds(j * half, half)]) for j in range(2)]
        else:
            pairs.append((near_any.at[slab(i, size)], near.at[i]))
            pairs.append((far_any.at[slab(i, rank)], far.at[i]))
        return [
            pltpu.make_async_copy(source, target, arrived.at[n, i])
            for n, (source, target) in enumerate(pairs)
        ]

    def stores(i):
        pairs = []
        if not first:
            pairs.append((result.at[i], z_any.at[slab(i, size)]))
        if sends:
            pairs.append((coarse.at[i], coarse_any.at[i]))
        return [
            pltpu.make_async_copy(source, target, left.at[n, i])
            for n, (source, target) in enumerate(pairs)
        ]

    def one_leaf(leaf):
        others = [vectors[l, leaf] for l in range(len(zs))]
        if first:
            z = others.pop()
        else:
            combined = far[leaf] + dot(transfer[leaf], incoming[...])
            z = near[leaf] + dot_first(basis[leaf], combined.astype(BF16))
            for i in range(m):
                z = z - coef[i : i + 1, :] * others[i + 1]
            z = z * coef[STEPS : STEPS + 1, :]
            result[leaf] = z
        if sends:
            rounded = z.astype(BF16)
            coarse[leaf] = rounded
        for j, copy in enumerate(stores(leaf)):
            copy.start(priority=j)
        if sends:
            skeleton = dot(basis[leaf], rounded).astype(BF16)
            skeletons[leaf] = skeleton
            upward[...] += dot_first(transfer[leaf], skeleton)
        for i, other in enumerate(others + [z]):
            sums[i] += jnp.sum((z * other).reshape(size // 8, 8, z.shape[1]), axis=0)

    begin, run = windowed(leaves, AHEAD, fetch, one_leaf)
    small = [
        pltpu.make_async_copy(basis_any, basis, came.at[0]),
        pltpu.make_async_copy(transfer_any, transfer, came.at[1]),
    ]
    if not first:
        small.insert(0, pltpu.make_async_copy(top_any, top, came.at[2]))
    for j, copy in enumerate(small):
        copy.start(priority=(j + 1) % 2)
    begin()
    sums[...] = jnp.zeros(sums.shape, F32)
    if sends:
        upward[...] = jnp.zeros(upward.shape, F32)
    if first:
        state_out[...] = jnp.zeros(state_out.shape, F32)
    else:
        grams = [row / points for row in from_branches(ups, rank)]
        state_out[...] = state[...]
        weights, inverse = coefficients(m, grams, state, state_out)
        for i, weight in enumerate(weights):
            coef[i : i + 1, :] = weight
        coef[STEPS : STEPS + 1, :] = inverse
        small.pop(0).wait()
        total = None
        for c in range(ups.shape[0]):
            weight = (branch[0] != c).astype(F32).astype(BF16)
            term = dot(top[0, c] * weight, ups[c, :rank])
            total = term if total is None else total + term
        incoming[...] = total.astype(BF16)
    for copy in small:
        copy.wait()
    run()

    if sends:
        halos = [
            pltpu.make_async_copy(coarse.at[pl.ds(0, HW)], low_any, out.at[0]),
            pltpu.make_async_copy(coarse.at[pl.ds(leaves - HW, HW)], high_any, out.at[1]),
        ]
        for j, copy in enumerate(halos):
            copy.start(priority=j)
    products = [jnp.sum(sums[i], axis=0, keepdims=True) for i in range(k + 1)]
    products = jnp.concatenate(products + [jnp.zeros_like(products[0])] * (7 - k), axis=0)
    store_split(split, products, k + 1)
    dots = split[...].astype(BF16)
    inner = send.shape[0]
    if sends:
        lifted = upward[...].astype(BF16)
        slots = send_slot.shape[0]
        for r in range(inner):
            for s in range(slots):
                send[r, s * rank : (s + 1) * rank] = skeletons[send_slot[s, r]]
            send[r, slots * rank : (slots + 1) * rank] = lifted
            send[r, (slots + 1) * rank :] = dots
    else:
        for r in range(inner):
            send[r] = dots
    for i in range(leaves):
        for copy in stores(i):
            copy.wait()
    if sends:
        for copy in halos:
            copy.wait()


def stage(k, points, send_slot, branch, zs, basis, transfer, later):
    leaves, rank, size = basis.shape
    first, sends = k == 0, k < STEPS
    columns = zs[0].shape[1]
    slots, inner = send_slot.shape
    tall = (leaves, size, columns)
    names, outs = [], []

    def get(name, shape, dtype, spec):
        names.append(name)
        outs.append((shape, dtype, spec))

    args = [send_slot, branch] + list(zs)
    specs = [SMEM, SMEM] + [HBM] * len(zs)
    if not first:
        args += list(later)
        specs += [VMEM, VMEM, HBM, HBM, HBM]
    args += [basis, transfer]
    specs += [HBM, HBM]
    if not first:
        get("z", (leaves * size, columns), F32, HBM)
    get("state", (STATE_ROWS, columns), F32, VMEM)
    rows = ((slots + 1) * rank if sends else 0) + DOT_ROWS
    get("send", (inner, rows, columns), BF16, VMEM)
    if sends:
        get("coarse", tall, BF16, HBM)
        get("low", (HW, size, columns), BF16, LOOSE)
        get("high", (HW, size, columns), BF16, LOOSE)

    scratch = [
        pltpu.VMEM(basis.shape, BF16),
        pltpu.VMEM(transfer.shape, BF16),
        pltpu.VMEM((len(zs),) + tall, F32),
        pltpu.VMEM((STEPS + 1, 8, columns), F32),
        pltpu.VMEM((DOT_ROWS, columns), F32),
        semaphores(len(zs) + 2, leaves),
        semaphores(3),
        semaphores(2, leaves),
    ]
    if sends:
        scratch += [
            pltpu.VMEM(tall, BF16),
            pltpu.VMEM((leaves, rank, columns), BF16),
            pltpu.VMEM((rank, columns), F32),
            semaphores(2),
        ]
    if not first:
        scratch += [
            pltpu.VMEM(later[2].shape, BF16),
            pltpu.VMEM((leaves, rank, columns), F32),
            pltpu.VMEM(tall, F32),
            pltpu.VMEM(tall, F32),
            pltpu.VMEM((8, columns), F32),
            pltpu.VMEM((rank, columns), BF16),
        ]
    results = call(
        functools.partial(stage_kernel, k=k, points=points),
        args,
        specs,
        outs,
        scratch,
        f"stage{k}",
        1 << 27,
        (k + 4) << 20,
    )
    return dict(zip(names, results))


def vectors_kernel(*refs, known, points):
    refs = list(refs)
    take = lambda count: [refs.pop(0) for _ in range(count)]
    (state,) = take(1)
    if not known:
        (ups,) = take(1)
    zs = take(known if known else STEPS + 1)
    if known:
        (krylov,) = take(1)
    else:
        _, krylov, hess_out = take(3)
    vectors, result, arrived, left = take(4)
    (after,) = take(1) if not known else (state,)
    parts = arrived.shape[1]
    part = result.shape[1] // parts
    wanted = range(known) if known else [STEPS]

    def fetch(i):
        return [
            pltpu.make_async_copy(
                z.at[slab(i, part)], vectors.at[l, slab(i, part)], arrived.at[l, i]
            )
            for l, z in enumerate(zs)
        ]

    def store(n, i):
        return pltpu.make_async_copy(
            result.at[n, slab(i, part)], krylov.at[wanted[n], slab(i, part)], left.at[n, i]
        )

    def work(i):
        for n, j in enumerate(wanted):
            vector = None
            for l in range(j + 1):
                row = basis_row(j, l)
                term = after[row : row + 1, :] * vectors[l, slab(i, part)]
                vector = term if vector is None else vector + term
            result[n, slab(i, part)] = vector
            store(n, i).start()

    begin, run = windowed(parts, AHEAD, fetch, work)
    begin()
    if not known:
        grams = [row / points for row in from_branches(ups, 0)]
        after[...] = state[...]
        coefficients(STEPS, grams, state, after)
    run()
    if not known:
        for i in range(STEPS + 1):
            for j in range(STEPS):
                row = i * STEPS + j
                if i <= j + 1:
                    hess_out[i, j : j + 1, :] = after[row : row + 1, :]
                else:
                    hess_out[i, j : j + 1, :] = jnp.zeros((1, hess_out.shape[2]), F32)
    for n in range(len(wanted)):
        for i in range(parts):
            store(n, i).wait()


def basis_vectors(state, zs, parts):
    known = len(zs)
    tall = zs[0].shape
    return call(
        functools.partial(vectors_kernel, known=known, points=0),
        [state] + zs,
        [VMEM] + [HBM] * known,
        [((STEPS + 1,) + tall, F32, HBM)],
        [
            pltpu.VMEM((known,) + tall, F32),
            pltpu.VMEM((known,) + tall, F32),
            semaphores(known, parts),
            semaphores(known, parts),
        ],
        "basis_vectors",
        1 << 23,
        8 << 20,
    )[0]


def last(points, ups, state, krylov, zs, parts):
    tall = zs[0].shape
    return call(
        functools.partial(vectors_kernel, known=0, points=points),
        [state, ups] + list(zs) + [krylov],
        [VMEM, VMEM] + [HBM] * len(zs) + [HBM],
        [(krylov.shape, F32, HBM), ((STEPS + 1, STEPS, tall[1]), F32, FREE)],
        [
            pltpu.VMEM((len(zs),) + tall, F32),
            pltpu.VMEM((1,) + tall, F32),
            semaphores(len(zs), parts),
            semaphores(1, parts),
            pltpu.VMEM(state.shape, F32),
        ],
        "last_vector",
        1 << 22,
        6 << 20,
        {2 + len(zs): 0},
    )


def shards(
    rhs,
    near_blocks,
    near_index,
    near_mask,
    basis,
    far_blocks,
    far_slot,
    far_mask,
    send_slot,
    transfer,
    top_blocks,
):
    outer, inner = lax.axis_size("outer"), lax.axis_size("inner")
    points = outer * inner * rhs.shape[0]
    leaves, rank = basis.shape[:2]
    slots = send_slot.shape[2]
    branch = lax.axis_index("outer").astype(jnp.int32).reshape(1)
    up_pairs = [(i, i + 1) for i in range(inner - 1)]
    down_pairs = [(j, i) for i, j in up_pairs]
    wanted = send_slot[0].T

    def exchange(array, axis):
        return lax.all_to_all(array, axis, split_axis=0, concat_axis=0, tiled=True)

    out = stage(0, points, wanted, branch, [rhs], basis, transfer, None)
    packed = pack_far(far_blocks, far_mask, far_slot, inner, slots)
    zs, state = [rhs], out["state"]
    for k in range(1, STEPS + 1):
        recv = exchange(out["send"], "inner")
        before = lax.ppermute(out["high"], "inner", up_pairs)
        after = lax.ppermute(out["low"], "inner", down_pairs)
        earlier = (packed,) if k == 1 else ()
        near = near_field(near_index, near_mask, near_blocks, out["coarse"], *earlier)
        summed = gather_sum(recv, slots * rank, outer, near)
        ups = exchange(summed, "outer")
        near, local_far = late_fields(
            near_index, near_mask, recv, packed, near_blocks, before, after, near, summed
        )
        later = (ups, state, top_blocks, local_far, near)
        out = stage(k, points, wanted, branch, zs, basis, transfer, later)
        state = out["state"]
        zs = zs + [out["z"]]
    krylov = basis_vectors(state, zs[:STEPS], leaves)
    recv = exchange(out["send"], "inner")
    ups = exchange(gather_sum(recv, 0, outer, krylov), "outer")
    return tuple(last(points, ups, state, krylov, zs, leaves))


def solution(mesh):
    return jax.shard_map(
        shards,
        mesh=mesh,
        in_specs=(
            P(("outer", "inner"), None),
            P(("outer", "inner"), None, None, None),
            P(("outer", "inner"), None),
            P(("outer", "inner"), None),
            P(("outer", "inner"), None, None),
            P(("outer", "inner"), None, None, None),
            P(("outer", "inner"), None),
            P(("outer", "inner"), None),
            P(("outer", "inner"), None, None),
            P(("outer", "inner"), None, None),
            P("outer", None, None, None),
        ),
        out_specs=(P(None, ("outer", "inner"), None), P()),
        check_vma=False,
    )
```

time: 1220 us -> 251 us (0.21)
  blocking collectives: 923 us -> 9.57 us
  Pallas kernels: 0 us -> 138 us
  local copies, waits for them, and re-layouts: 107 us -> 0.71 us
  matrix products: 91 us -> 0 us
  other arithmetic: 52.5 us -> 0 us
  starting transfers between devices: 24.3 us -> 73.8 us
  waiting for transfers between devices: 0.12 us -> 26.6 us
  between operations: 14.5 us -> 1 us
    psum x13 -> x0, blocking collectives: 811 us -> none  [the longest x5 319 us: lengths(): return lax.psum(jnp.sum(values * values, axis=0), ('outer', 'inner'))]
    pallas_call x0 -> x21, Pallas kernels: none -> 138 us  [call(): pl.pallas_call(kernel, in_specs=list(in_specs), out_specs=[spec for _, _,...]
    all_gather x4 -> x0, blocking collectives: 112 us -> none  [shards(): coeffs = lax.all_gather(summed[None], 'outer', axis=0, tiled=True)]
    dot_general x24 -> x0, matrix products: 91 us -> none  [the longest x4 32.9 us: shards(): jnp.einsum('lnij,lnjr->lir', near_blocks, neighbours, preferred_element_t...]
    gather x14 -> x0, local copies, waits for them, and re-layouts: 65.5 us -> none  [the longest x8 40.2 us: shards(): neighbours = padded[near_index] * near_weight]
    all_to_all x1 -> x9, starting transfers between devices: 7.11 us -> 55.6 us  [exchange(): return lax.all_to_all(array, axis, split_axis=0, concat_axis=0, tiled=True)]
    all_to_all x1 -> x9, waiting for transfers between devices: 0.01 us -> 26.5 us  [exchange(): return lax.all_to_all(array, axis, split_axis=0, concat_axis=0, tiled=True)]
    another operation x15 -> x0, other arithmetic: 19.1 us -> none
  transfers between devices with their start and end apart: 13 -> 17, of which waited for: 0 -> 4; matrix products, arithmetic and copies ran while one was open for 10% -> 0% of each run, Pallas kernels for 0% -> 37%
where the time goes in v2:
time: 251 us; the launch traced here: 250 us
  Pallas kernels  138 us (55%)
  starting transfers between devices  73.8 us (29%)
  waiting for transfers between devices  26.6 us (11%)
  blocking collectives  9.57 us (4%)
    pallas_call x21, Pallas kernels, call(): pl.pallas_call(kernel, in_specs=list(in_specs), out_specs=[spec for _, _,...  138 us
    all_to_all x9, starting transfers between devices, exchange(): return lax.all_to_all(array, axis, split_axis=0, concat_axis=0, tiled=True)  55.6 us
    all_to_all x9, waiting for transfers between devices, exchange(): return lax.all_to_all(array, axis, split_axis=0, concat_axis=0, tiled=True)  26.5 us
    ppermute x4, starting transfers between devices, shards(): before = lax.ppermute(out['high'], 'inner', up_pairs)  13.1 us
    all_to_all x1, blocking collectives, exchange(): return lax.all_to_all(array, axis, split_axis=0, concat_axis=0, tiled=True)  9.57 us
    ppermute x4, starting transfers between devices, shards(): after = lax.ppermute(out['low'], 'inner', down_pairs)  5.17 us
  transfers between devices with their start and end apart: 17, of which 4 were waited for; matrix products, arithmetic and copies ran while one was open for 0% of the time, Pallas kernels for 37%

profile of v2, /device:TPU:1, one launch (start us, length us, event | category | flops | bytes accessed | tf_op | source)
XLA Modules:
  0.0 249.7 jit_solution(1724284772838236805)
XLA Ops:
  0.6 0.0 copy-start.2
  0.6 0.7 copy-done.2
  1.3 6.0 %stage0.1 = (f32[64,128]{1,0:T(8,128)S(1)}, bf16[16,336,128]{2,1,0:T(8,128)(2,1)}, bf16[8,256,128]{2,1,0:T(8,128)(2,1)}, bf16[2,256,128]{2,1,0:T(8,128)(2,1)S(1)}, bf16[2,256,128]{2,1,0:T(8,128)(2,1)S(1)}) custom-call(s32[4,16]{1,0:T(4,128)S(1)} %bitcast.4, s32[1]{0:T(128)} %bitcast.2.refs_1_, f32[2048,128]{1,0:T(8,128)} %refs_2_.11, ...), custom_call_target="tpu_custom_call" | custom-call | flops 134217728 | bytes 4194304 | tf_op jit(solution)/shard_map/stage0/pallas_call | solution.py:115
  7.3 0.0 copy-start.4
  7.3 0.0 copy-start.5
  7.3 8.6 %all-to-all-start = ((bf16[16,336,128]{2,1,0:T(8,128)(2,1)}), bf16[16,336,128]{2,1,0:T(8,128)(2,1)S(1)}, u32[]{:S(2)}, u32[]{:S(2)}) async-start(bf16[16,336,128]{2,1,0:T(8,128)(2,1)} %get-tuple-element.36), calls=%async_computation | async-start | bytes 2752512 | tf_op jit(solution)/shard_map/all_to_all | solution.py:754
  16.0 3.3 %collective-permute-start = (bf16[2,256,128]{2,1,0:T(8,128)(2,1)S(1)}, bf16[2,256,128]{2,1,0:T(8,128)(2,1)S(1)}, u32[]{:S(2)}, u32[]{:S(2)}) collective-permute-start(bf16[2,256,128]{2,1,0:T(8,128)(2,1)S(1)} %get-tuple-element.39), channel_id=1, source_target_pairs={{0,1},{1,2},{2,3},{3,4},{4,5},{5,6},{6,7},{7,8},{8,9},{9,10},{10,1... | collective-permute-start | bytes 393224 | tf_op jit(solution)/shard_map/ppermute | solution.py:761
  19.2 0.0 copy-start
  19.2 0.0 copy-start.1
  19.3 1.3 collective-permute-start.1
  20.6 8.4 %pack_far.1.refs_0_.packed_ref = bf16[16,512,256]{2,1,0:T(8,128)(2,1)} custom-call(s32[8,48]{1,0:T(8,128)S(1)} %copy-done.4, s32[8,48]{1,0:T(8,128)S(1)} %copy-done.5, bf16[8,48,64,64]{3,2,1,0:T(8,128)(2,1)} %far_ref.1), custom_call_target="tpu_custom_call" | custom-call | bytes 10485760 | tf_op jit(solution)/shard_map/pack_far/pallas_call | solution.py:115
  29.0 8.6 %near_field.4.refs_0_.near_ref = f32[2048,128]{1,0:T(8,128)} custom-call(s32[8,8]{1,0:T(8,128)S(1)} %copy-done, s32[8,8]{1,0:T(8,128)S(1)} %copy-done.1, bf16[8,8,256,256]{3,2,1,0:T(8,128)(2,1)} %blocks_ref.15, bf16[8,256,128]{2,1,0:T(8,128)(2,1)} %get-tuple-element.37.own_ref, bf16[16,512,256]{2,1,0:T(8,128)(2,1)} %pack_far.1.refs_0_.packed_ref), custom_call_target="tpu_custom_call" | custom-call | flops 1073741824 | bytes 8388608 | tf_op jit(solution)/shard_map/near_field/pallas_call | solution.py:115
  37.6 0.7 gather_sum.5.refs_0_
  38.3 5.8 %all-to-all-start.1 = ((bf16[8,80,128]{2,1,0:T(8,128)(2,1)}), bf16[8,80,128]{2,1,0:T(8,128)(2,1)S(1)}, u32[]{:S(2)}, u32[]{:S(2)}) async-start(bf16[8,80,128]{2,1,0:T(8,128)(2,1)} %gather_sum.5.refs_0_), calls=%async_computation.1 | async-start | bytes 327680 | tf_op jit(solution)/shard_map/all_to_all | solution.py:754
  44.1 10.6 %late_fields.4 = (f32[2048,128]{1,0:T(8,128)}, f32[512,128]{1,0:T(8,128)}) custom-call(s32[8,8]{1,0:T(8,128)S(1)} %copy-done, s32[8,8]{1,0:T(8,128)S(1)} %copy-done.1, bf16[16,336,128]{2,1,0:T(8,128)(2,1)S(1)} %all-to-all-done.recv, bf16[16,512,256]{2,1,0:T(8,128)(2,1)} %pack_far.1.refs_0_.packed_ref, bf16[8,8,256,256]{3,2,1,0:T(8,128)(2,1)} %blocks_ref.15, ...), custom_call_target="tpu_custom_call" | custom-call | flops 536870912 | bytes 5242880 | tf_op jit(solution)/shard_map/late_fields/pallas_call | solution.py:115
  54.7 8.4 %stage1.1 = (f32[2048,128]{1,0:T(8,128)}, f32[64,128]{1,0:T(8,128)S(1)}, bf16[16,336,128]{2,1,0:T(8,128)(2,1)}, bf16[8,256,128]{2,1,0:T(8,128)(2,1)}, bf16[2,256...) custom-call(s32[4,16]{1,0:T(4,128)S(1)} %bitcast.5, s32[1]{0:T(128)} %bitcast.2.refs_1_, f32[2048,128]{1,0:T(8,128)} %refs_2_.11, ...), custom_call_target="tpu_custom_call" | custom-call | flops 134217728 | bytes 5242880 | tf_op jit(solution)/shard_map/stage1/pallas_call | solution.py:115
  63.1 8.4 %all-to-all-start.2 = ((bf16[16,336,128]{2,1,0:T(8,128)(2,1)}), bf16[16,336,128]{2,1,0:T(8,128)(2,1)S(1)}, u32[]{:S(2)}, u32[]{:S(2)}) async-start(bf16[16,336,128]{2,1,0:T(8,128)(2,1)} %get-tuple-element.44), calls=%async_computation.2 | async-start | bytes 2752512 | tf_op jit(solution)/shard_map/all_to_all | solution.py:754
  71.6 3.3 %collective-permute-start.2 = (bf16[2,256,128]{2,1,0:T(8,128)(2,1)S(1)}, bf16[2,256,128]{2,1,0:T(8,128)(2,1)S(1)}, u32[]{:S(2)}, u32[]{:S(2)}) collective-permute-start(bf16[2,256,128]{2,1,0:T(8,128)(2,1)S(1)} %get-tuple-element.47), channel_id=1, source_target_pairs={{0,1},{1,2},{2,3},{3,4},{4,5},{5,6},{6,7},{7,8},{8,9},{9,10},{10,1... | collective-permute-start | bytes 393224 | tf_op jit(solution)/shard_map/ppermute | solution.py:761
  74.9 1.3 collective-permute-start.3
  76.2 8.6 %near_field.5.refs_0_.near_ref = f32[2048,128]{1,0:T(8,128)} custom-call(s32[8,8]{1,0:T(8,128)S(1)} %copy-done, s32[8,8]{1,0:T(8,128)S(1)} %copy-done.1, bf16[8,8,256,256]{3,2,1,0:T(8,128)(2,1)} %blocks_ref.15, bf16[8,256,128]{2,1,0:T(8,128)(2,1)} %get-tuple-element.45.own_ref), custom_call_target="tpu_custom_call" | custom-call | flops 1073741824 | bytes 8388608 | tf_op jit(solution)/shard_map/near_field/pallas_call | solution.py:115
  84.7 8.5 %all-to-all-done.2.recv = bf16[16,336,128]{2,1,0:T(8,128)(2,1)S(1)} async-done(((bf16[16,336,128]{2,1,0:T(8,128)(2,1)}), bf16[16,336,128]{2,1,0:T(8,128)(2,1)S(1)}, u32[]{:S(2)}, u32[]{:S(2)}) %all-to-all-start.2) | async-done | bytes 1376288 | tf_op jit(solution)/shard_map/all_to_all | solution.py:754
  93.2 0.7 gather_sum.6.refs_0_
  94.0 5.5 %all-to-all-start.3 = ((bf16[8,80,128]{2,1,0:T(8,128)(2,1)}), bf16[8,80,128]{2,1,0:T(8,128)(2,1)S(1)}, u32[]{:S(2)}, u32[]{:S(2)}) async-start(bf16[8,80,128]{2,1,0:T(8,128)(2,1)} %gather_sum.6.refs_0_), calls=%async_computation.3 | async-start | bytes 327680 | tf_op jit(solution)/shard_map/all_to_all | solution.py:754
  99.5 10.6 %late_fields.5 = (f32[2048,128]{1,0:T(8,128)}, f32[512,128]{1,0:T(8,128)}) custom-call(s32[8,8]{1,0:T(8,128)S(1)} %copy-done, s32[8,8]{1,0:T(8,128)S(1)} %copy-done.1, bf16[16,336,128]{2,1,0:T(8,128)(2,1)S(1)} %all-to-all-done.2.recv, bf16[16,512,256]{2,1,0:T(8,128)(2,1)} %pack_far.1.refs_0_.packed_ref, bf16[8,8,256,256]{3,2,1,0:T(8,128)(2,1)} %blocks_ref.15, ...), custom_call_target="tpu_custom_call" | custom-call | flops 536870912 | bytes 5242880 | tf_op jit(solution)/shard_map/late_fields/pallas_call | solution.py:115
  110.1 8.7 %stage2.1 = (f32[2048,128]{1,0:T(8,128)}, f32[64,128]{1,0:T(8,128)S(1)}, bf16[16,336,128]{2,1,0:T(8,128)(2,1)}, bf16[8,256,128]{2,1,0:T(8,128)(2,1)}, bf16[2,256...) custom-call(s32[4,16]{1,0:T(4,128)S(1)} %bitcast.6, s32[1]{0:T(128)} %bitcast.2.refs_1_, f32[2048,128]{1,0:T(8,128)} %refs_2_.11, ...), custom_call_target="tpu_custom_call" | custom-call | flops 134217728 | bytes 6291456 | tf_op jit(solution)/shard_map/stage2/pallas_call | solution.py:115
  118.8 6.1 %all-to-all-start.4 = ((bf16[16,336,128]{2,1,0:T(8,128)(2,1)}), bf16[16,336,128]{2,1,0:T(8,128)(2,1)S(1)}, u32[]{:S(2)}, u32[]{:S(2)}) async-start(bf16[16,336,128]{2,1,0:T(8,128)(2,1)} %get-tuple-element.52), calls=%async_computation.4 | async-start | bytes 2752512 | tf_op jit(solution)/shard_map/all_to_all | solution.py:754
  124.8 3.3 %collective-permute-start.4 = (bf16[2,256,128]{2,1,0:T(8,128)(2,1)S(1)}, bf16[2,256,128]{2,1,0:T(8,128)(2,1)S(1)}, u32[]{:S(2)}, u32[]{:S(2)}) collective-permute-start(bf16[2,256,128]{2,1,0:T(8,128)(2,1)S(1)} %get-tuple-element.55), channel_id=1, source_target_pairs={{0,1},{1,2},{2,3},{3,4},{4,5},{5,6},{6,7},{7,8},{8,9},{9,10},{10,1... | collective-permute-start | bytes 393224 | tf_op jit(solution)/shard_map/ppermute | solution.py:761
  128.1 1.3 collective-permute-start.5
  129.4 8.6 %near_field.6.refs_0_.near_ref = f32[2048,128]{1,0:T(8,128)} custom-call(s32[8,8]{1,0:T(8,128)S(1)} %copy-done, s32[8,8]{1,0:T(8,128)S(1)} %copy-done.1, bf16[8,8,256,256]{3,2,1,0:T(8,128)(2,1)} %blocks_ref.15, bf16[8,256,128]{2,1,0:T(8,128)(2,1)} %get-tuple-element.53.own_ref), custom_call_target="tpu_custom_call" | custom-call | flops 1073741824 | bytes 8388608 | tf_op jit(solution)/shard_map/near_field/pallas_call | solution.py:115
  138.0 8.4 %all-to-all-done.4.recv = bf16[16,336,128]{2,1,0:T(8,128)(2,1)S(1)} async-done(((bf16[16,336,128]{2,1,0:T(8,128)(2,1)}), bf16[16,336,128]{2,1,0:T(8,128)(2,1)S(1)}, u32[]{:S(2)}, u32[]{:S(2)}) %all-to-all-start.4) | async-done | bytes 1376288 | tf_op jit(solution)/shard_map/all_to_all | solution.py:754
  146.4 0.7 gather_sum.7.refs_0_
  147.1 5.5 %all-to-all-start.5 = ((bf16[8,80,128]{2,1,0:T(8,128)(2,1)}), bf16[8,80,128]{2,1,0:T(8,128)(2,1)S(1)}, u32[]{:S(2)}, u32[]{:S(2)}) async-start(bf16[8,80,128]{2,1,0:T(8,128)(2,1)} %gather_sum.7.refs_0_), calls=%async_computation.5 | async-start | bytes 327680 | tf_op jit(solution)/shard_map/all_to_all | solution.py:754
  152.6 10.6 %late_fields.6 = (f32[2048,128]{1,0:T(8,128)}, f32[512,128]{1,0:T(8,128)}) custom-call(s32[8,8]{1,0:T(8,128)S(1)} %copy-done, s32[8,8]{1,0:T(8,128)S(1)} %copy-done.1, bf16[16,336,128]{2,1,0:T(8,128)(2,1)S(1)} %all-to-all-done.4.recv, bf16[16,512,256]{2,1,0:T(8,128)(2,1)} %pack_far.1.refs_0_.packed_ref, bf16[8,8,256,256]{3,2,1,0:T(8,128)(2,1)} %blocks_ref.15, ...), custom_call_target="tpu_custom_call" | custom-call | flops 536870912 | bytes 5242880 | tf_op jit(solution)/shard_map/late_fields/pallas_call | solution.py:115
  163.2 9.1 %stage3.1 = (f32[2048,128]{1,0:T(8,128)}, f32[64,128]{1,0:T(8,128)S(1)}, bf16[16,336,128]{2,1,0:T(8,128)(2,1)}, bf16[8,256,128]{2,1,0:T(8,128)(2,1)}, bf16[2,256...) custom-call(s32[4,16]{1,0:T(4,128)S(1)} %bitcast.7, s32[1]{0:T(128)} %bitcast.2.refs_1_, f32[2048,128]{1,0:T(8,128)} %refs_2_.11, ...), custom_call_target="tpu_custom_call" | custom-call | flops 134217728 | bytes 7340032 | tf_op jit(solution)/shard_map/stage3/pallas_call | solution.py:115
  172.3 5.1 %all-to-all-start.6 = ((bf16[16,336,128]{2,1,0:T(8,128)(2,1)}), bf16[16,336,128]{2,1,0:T(8,128)(2,1)S(1)}, u32[]{:S(2)}, u32[]{:S(2)}) async-start(bf16[16,336,128]{2,1,0:T(8,128)(2,1)} %get-tuple-element.60), calls=%async_computation.6 | async-start | bytes 2752512 | tf_op jit(solution)/shard_map/all_to_all | solution.py:754
  177.5 3.3 %collective-permute-start.6 = (bf16[2,256,128]{2,1,0:T(8,128)(2,1)S(1)}, bf16[2,256,128]{2,1,0:T(8,128)(2,1)S(1)}, u32[]{:S(2)}, u32[]{:S(2)}) collective-permute-start(bf16[2,256,128]{2,1,0:T(8,128)(2,1)S(1)} %get-tuple-element.63), channel_id=1, source_target_pairs={{0,1},{1,2},{2,3},{3,4},{4,5},{5,6},{6,7},{7,8},{8,9},{9,10},{10,1... | collective-permute-start | bytes 393224 | tf_op jit(solution)/shard_map/ppermute | solution.py:761
  180.7 1.3 collective-permute-start.7
  182.0 8.6 %near_field.7.refs_0_.near_ref = f32[2048,128]{1,0:T(8,128)} custom-call(s32[8,8]{1,0:T(8,128)S(1)} %copy-done, s32[8,8]{1,0:T(8,128)S(1)} %copy-done.1, bf16[8,8,256,256]{3,2,1,0:T(8,128)(2,1)} %blocks_ref.15, bf16[8,256,128]{2,1,0:T(8,128)(2,1)} %get-tuple-element.61.own_ref), custom_call_target="tpu_custom_call" | custom-call | flops 1073741824 | bytes 8388608 | tf_op jit(solution)/shard_map/near_field/pallas_call | solution.py:115
  190.6 8.4 %all-to-all-done.6.recv = bf16[16,336,128]{2,1,0:T(8,128)(2,1)S(1)} async-done(((bf16[16,336,128]{2,1,0:T(8,128)(2,1)}), bf16[16,336,128]{2,1,0:T(8,128)(2,1)S(1)}, u32[]{:S(2)}, u32[]{:S(2)}) %all-to-all-start.6) | async-done | bytes 1376288 | tf_op jit(solution)/shard_map/all_to_all | solution.py:754
  199.0 0.7 gather_sum.8.refs_0_
  199.7 4.7 %all-to-all-start.7 = ((bf16[8,80,128]{2,1,0:T(8,128)(2,1)}), bf16[8,80,128]{2,1,0:T(8,128)(2,1)S(1)}, u32[]{:S(2)}, u32[]{:S(2)}) async-start(bf16[8,80,128]{2,1,0:T(8,128)(2,1)} %gather_sum.8.refs_0_), calls=%async_computation.7 | async-start | bytes 327680 | tf_op jit(solution)/shard_map/all_to_all | solution.py:754
  204.4 10.6 %late_fields.7 = (f32[2048,128]{1,0:T(8,128)}, f32[512,128]{1,0:T(8,128)}) custom-call(s32[8,8]{1,0:T(8,128)S(1)} %copy-done, s32[8,8]{1,0:T(8,128)S(1)} %copy-done.1, bf16[16,336,128]{2,1,0:T(8,128)(2,1)S(1)} %all-to-all-done.6.recv, bf16[16,512,256]{2,1,0:T(8,128)(2,1)} %pack_far.1.refs_0_.packed_ref, bf16[8,8,256,256]{3,2,1,0:T(8,128)(2,1)} %blocks_ref.15, ...), custom_call_target="tpu_custom_call" | custom-call | flops 536870912 | bytes 5242880 | tf_op jit(solution)/shard_map/late_fields/pallas_call | solution.py:115
  215.0 7.4 %stage4.1 = (f32[2048,128]{1,0:T(8,128)}, f32[64,128]{1,0:T(8,128)S(1)}, bf16[16,16,128]{2,1,0:T(8,128)(2,1)}) custom-call(s32[4,16]{1,0:T(4,128)S(1)} %bitcast.8, s32[1]{0:T(128)} %bitcast.2.refs_1_, f32[2048,128]{1,0:T(8,128)} %refs_2_.11, f32[2048,128]{1,0:T(8,128)} %get-tuple-element.43.refs_3_.refs_2_, f32[2048,128]{1,0:T(8,128)} %get-tuple-element.51.refs_4_.refs_3_, ...), custom_call_target="tpu_custom_call" | custom-call | flops 134217728 | bytes 8388608 | tf_op jit(solution)/shard_map/stage4/pallas_call | solution.py:115
  222.4 5.9 %all-to-all-start.8 = ((bf16[16,16,128]{2,1,0:T(8,128)(2,1)}), bf16[16,16,128]{2,1,0:T(8,128)(2,1)S(1)}, u32[]{:S(2)}, u32[]{:S(2)}) async-start(bf16[16,16,128]{2,1,0:T(8,128)(2,1)} %get-tuple-element.68), calls=%async_computation.8 | async-start | bytes 131072 | tf_op jit(solution)/shard_map/all_to_all | solution.py:754
  228.3 5.2 %basis_vectors.1.refs_0_.refs_7_ = f32[5,2048,128]{2,1,0:T(8,128)} custom-call(f32[64,128]{1,0:T(8,128)S(1)} %get-tuple-element.67.refs_0_, f32[2048,128]{1,0:T(8,128)} %refs_2_.11, f32[2048,128]{1,0:T(8,128)} %get-tuple-element.43.refs_3_.refs_2_, f32[2048,128]{1,0:T(8,128)} %get-tuple-element.51.refs_4_.refs_3_, f32[2048,128]{1,0:T(8,128)} %get-tuple-element.59.refs_5_.refs_4_), custom_call_target="tpu_custom_call" | custom-call | flops 8388608 | bytes 8388608 | tf_op jit(solution)/shard_map/basis_vectors/pallas_call | solution.py:115
  233.5 1.3 all-to-all-done.8.recv
  234.9 9.6 %all_to_all.50.refs_1_ = bf16[8,16,128]{2,1,0:T(8,128)(2,1)S(1)} all-to-all(bf16[8,16,128]{2,1,0:T(8,128)(2,1)S(1)} %gather_sum.9), channel_id=1, replica_groups=mesh['outer'=8,'inner'=16] {'outer'}, dimensions={0} | all-to-all | bytes 65536 | tf_op jit(solution)/shard_map/all_to_all | solution.py:754
  244.4 5.2 %last_vector.1 = (f32[5,2048,128]{2,1,0:T(8,128)}, f32[5,4,128]{2,1,0:T(4,128)}) custom-call(f32[64,128]{1,0:T(8,128)S(1)} %get-tuple-element.67.refs_0_, bf16[8,16,128]{2,1,0:T(8,128)(2,1)S(1)} %all_to_all.50.refs_1_, f32[2048,128]{1,0:T(8,128)} %refs_2_.11, f32[2048,128]{1,0:T(8,128)} %get-tuple-element.43.refs_3_.refs_2_, ...), custom_call_target="tpu_custom_call", output_to_operand_aliasing={{0}: (7, {})} | custom-call | flops 4194304 | bytes 6291456 | tf_op jit(solution)/shard_map/last_vector/pallas_call | solution.py:115
  (20 shorter events, 0.1 us)
Async XLA Ops:
  0.6 0.7 copy-start.2
  7.3 13.2 %copy-start.4 = (s32[8,48]{1,0:T(8,128)S(1)}, s32[8,48]{1,0:T(8,128)}, u32[]{:S(2)}) copy-start(s32[8,48]{1,0:T(8,128)} %mask_ref.9) | copy-start | bytes 4612
  7.3 13.2 %copy-start.5 = (s32[8,48]{1,0:T(8,128)S(1)}, s32[8,48]{1,0:T(8,128)}, u32[]{:S(2)}) copy-start(s32[8,48]{1,0:T(8,128)} %slot_ref.1) | copy-start | bytes 4612
  7.3 30.2 %all-to-all-start = ((bf16[16,336,128]{2,1,0:T(8,128)(2,1)}), bf16[16,336,128]{2,1,0:T(8,128)(2,1)S(1)}, u32[]{:S(2)}, u32[]{:S(2)}) async-start(bf16[16,336,128]{2,1,0:T(8,128)(2,1)} %get-tuple-element.36), calls=%async_computation | async-start | bytes 2752512 | tf_op jit(solution)/shard_map/all_to_all | solution.py:754
  16.0 28.1 %collective-permute-start = (bf16[2,256,128]{2,1,0:T(8,128)(2,1)S(1)}, bf16[2,256,128]{2,1,0:T(8,128)(2,1)S(1)}, u32[]{:S(2)}, u32[]{:S(2)}) collective-permute-start(bf16[2,256,128]{2,1,0:T(8,128)(2,1)S(1)} %get-tuple-element.39), channel_id=1, source_target_pairs={{0,1},{1,2},{2,3},{3,4},{4,5},{5,6},{6,7},{7,8},{8,9},{9,10},{10,1... | collective-permute-start | bytes 393224 | tf_op jit(solution)/shard_map/ppermute | solution.py:761
  19.2 9.7 %copy-start = (s32[8,8]{1,0:T(8,128)S(1)}, s32[8,8]{1,0:T(8,128)}, u32[]{:S(2)}) copy-start(s32[8,8]{1,0:T(8,128)} %index_ref.15) | copy-start | bytes 772
  19.2 9.7 %copy-start.1 = (s32[8,8]{1,0:T(8,128)S(1)}, s32[8,8]{1,0:T(8,128)}, u32[]{:S(2)}) copy-start(s32[8,8]{1,0:T(8,128)} %mask_ref.17) | copy-start | bytes 772
  19.3 24.9 %collective-permute-start.1 = (bf16[2,256,128]{2,1,0:T(8,128)(2,1)S(1)}, bf16[2,256,128]{2,1,0:T(8,128)(2,1)S(1)}, u32[]{:S(2)}, u32[]{:S(2)}) collective-permute-start(bf16[2,256,128]{2,1,0:T(8,128)(2,1)S(1)} %get-tuple-element.40), channel_id=1, source_target_pairs={{1,0},{2,1},{3,2},{4,3},{5,4},{6,5},{7,6},{8,7},{9,8},{10,9},{11,1... | collective-permute-start | bytes 393224 | tf_op jit(solution)/shard_map/ppermute | solution.py:762
  38.3 16.4 %all-to-all-start.1 = ((bf16[8,80,128]{2,1,0:T(8,128)(2,1)}), bf16[8,80,128]{2,1,0:T(8,128)(2,1)S(1)}, u32[]{:S(2)}, u32[]{:S(2)}) async-start(bf16[8,80,128]{2,1,0:T(8,128)(2,1)} %gather_sum.5.refs_0_), calls=%async_computation.1 | async-start | bytes 327680 | tf_op jit(solution)/shard_map/all_to_all | solution.py:754
  44.1 10.6 %copy-start.3 = (s32[1,16,4]{1,2,0:T(4,128)S(1)}, s32[1,16,4]{1,2,0:T(4,128)}, u32[]{:S(2)}) copy-start(s32[1,16,4]{1,2,0:T(4,128)} %param.19) | copy-start | bytes 772
  63.1 30.1 %all-to-all-start.2 = ((bf16[16,336,128]{2,1,0:T(8,128)(2,1)}), bf16[16,336,128]{2,1,0:T(8,128)(2,1)S(1)}, u32[]{:S(2)}, u32[]{:S(2)}) async-start(bf16[16,336,128]{2,1,0:T(8,128)(2,1)} %get-tuple-element.44), calls=%async_computation.2 | async-start | bytes 2752512 | tf_op jit(solution)/shard_map/all_to_all | solution.py:754
  71.6 27.9 %collective-permute-start.2 = (bf16[2,256,128]{2,1,0:T(8,128)(2,1)S(1)}, bf16[2,256,128]{2,1,0:T(8,128)(2,1)S(1)}, u32[]{:S(2)}, u32[]{:S(2)}) collective-permute-start(bf16[2,256,128]{2,1,0:T(8,128)(2,1)S(1)} %get-tuple-element.47), channel_id=1, source_target_pairs={{0,1},{1,2},{2,3},{3,4},{4,5},{5,6},{6,7},{7,8},{8,9},{9,10},{10,1... | collective-permute-start | bytes 393224 | tf_op jit(solution)/shard_map/ppermute | solution.py:761
  74.9 24.6 %collective-permute-start.3 = (bf16[2,256,128]{2,1,0:T(8,128)(2,1)S(1)}, bf16[2,256,128]{2,1,0:T(8,128)(2,1)S(1)}, u32[]{:S(2)}, u32[]{:S(2)}) collective-permute-start(bf16[2,256,128]{2,1,0:T(8,128)(2,1)S(1)} %get-tuple-element.48), channel_id=1, source_target_pairs={{1,0},{2,1},{3,2},{4,3},{5,4},{6,5},{7,6},{8,7},{9,8},{10,9},{11,1... | collective-permute-start | bytes 393224 | tf_op jit(solution)/shard_map/ppermute | solution.py:762
  94.0 16.1 %all-to-all-start.3 = ((bf16[8,80,128]{2,1,0:T(8,128)(2,1)}), bf16[8,80,128]{2,1,0:T(8,128)(2,1)S(1)}, u32[]{:S(2)}, u32[]{:S(2)}) async-start(bf16[8,80,128]{2,1,0:T(8,128)(2,1)} %gather_sum.6.refs_0_), calls=%async_computation.3 | async-start | bytes 327680 | tf_op jit(solution)/shard_map/all_to_all | solution.py:754
  118.8 27.6 %all-to-all-start.4 = ((bf16[16,336,128]{2,1,0:T(8,128)(2,1)}), bf16[16,336,128]{2,1,0:T(8,128)(2,1)S(1)}, u32[]{:S(2)}, u32[]{:S(2)}) async-start(bf16[16,336,128]{2,1,0:T(8,128)(2,1)} %get-tuple-element.52), calls=%async_computation.4 | async-start | bytes 2752512 | tf_op jit(solution)/shard_map/all_to_all | solution.py:754
  124.8 27.8 %collective-permute-start.4 = (bf16[2,256,128]{2,1,0:T(8,128)(2,1)S(1)}, bf16[2,256,128]{2,1,0:T(8,128)(2,1)S(1)}, u32[]{:S(2)}, u32[]{:S(2)}) collective-permute-start(bf16[2,256,128]{2,1,0:T(8,128)(2,1)S(1)} %get-tuple-element.55), channel_id=1, source_target_pairs={{0,1},{1,2},{2,3},{3,4},{4,5},{5,6},{6,7},{7,8},{8,9},{9,10},{10,1... | collective-permute-start | bytes 393224 | tf_op jit(solution)/shard_map/ppermute | solution.py:761
  128.1 24.5 %collective-permute-start.5 = (bf16[2,256,128]{2,1,0:T(8,128)(2,1)S(1)}, bf16[2,256,128]{2,1,0:T(8,128)(2,1)S(1)}, u32[]{:S(2)}, u32[]{:S(2)}) collective-permute-start(bf16[2,256,128]{2,1,0:T(8,128)(2,1)S(1)} %get-tuple-element.56), channel_id=1, source_target_pairs={{1,0},{2,1},{3,2},{4,3},{5,4},{6,5},{7,6},{8,7},{9,8},{10,9},{11,1... | collective-permute-start | bytes 393224 | tf_op jit(solution)/shard_map/ppermute | solution.py:762
  147.1 16.1 %all-to-all-start.5 = ((bf16[8,80,128]{2,1,0:T(8,128)(2,1)}), bf16[8,80,128]{2,1,0:T(8,128)(2,1)S(1)}, u32[]{:S(2)}, u32[]{:S(2)}) async-start(bf16[8,80,128]{2,1,0:T(8,128)(2,1)} %gather_sum.7.refs_0_), calls=%async_computation.5 | async-start | bytes 327680 | tf_op jit(solution)/shard_map/all_to_all | solution.py:754
  172.3 26.7 %all-to-all-start.6 = ((bf16[16,336,128]{2,1,0:T(8,128)(2,1)}), bf16[16,336,128]{2,1,0:T(8,128)(2,1)S(1)}, u32[]{:S(2)}, u32[]{:S(2)}) async-start(bf16[16,336,128]{2,1,0:T(8,128)(2,1)} %get-tuple-element.60), calls=%async_computation.6 | async-start | bytes 2752512 | tf_op jit(solution)/shard_map/all_to_all | solution.py:754
  177.5 26.9 %collective-permute-start.6 = (bf16[2,256,128]{2,1,0:T(8,128)(2,1)S(1)}, bf16[2,256,128]{2,1,0:T(8,128)(2,1)S(1)}, u32[]{:S(2)}, u32[]{:S(2)}) collective-permute-start(bf16[2,256,128]{2,1,0:T(8,128)(2,1)S(1)} %get-tuple-element.63), channel_id=1, source_target_pairs={{0,1},{1,2},{2,3},{3,4},{4,5},{5,6},{6,7},{7,8},{8,9},{9,10},{10,1... | collective-permute-start | bytes 393224 | tf_op jit(solution)/shard_map/ppermute | solution.py:761
  180.7 23.7 %collective-permute-start.7 = (bf16[2,256,128]{2,1,0:T(8,128)(2,1)S(1)}, bf16[2,256,128]{2,1,0:T(8,128)(2,1)S(1)}, u32[]{:S(2)}, u32[]{:S(2)}) collective-permute-start(bf16[2,256,128]{2,1,0:T(8,128)(2,1)S(1)} %get-tuple-element.64), channel_id=1, source_target_pairs={{1,0},{2,1},{3,2},{4,3},{5,4},{6,5},{7,6},{8,7},{9,8},{10,9},{11,1... | collective-permute-start | bytes 393224 | tf_op jit(solution)/shard_map/ppermute | solution.py:762
  199.7 15.3 %all-to-all-start.7 = ((bf16[8,80,128]{2,1,0:T(8,128)(2,1)}), bf16[8,80,128]{2,1,0:T(8,128)(2,1)S(1)}, u32[]{:S(2)}, u32[]{:S(2)}) async-start(bf16[8,80,128]{2,1,0:T(8,128)(2,1)} %gather_sum.8.refs_0_), calls=%async_computation.7 | async-start | bytes 327680 | tf_op jit(solution)/shard_map/all_to_all | solution.py:754
  222.4 12.4 %all-to-all-start.8 = ((bf16[16,16,128]{2,1,0:T(8,128)(2,1)}), bf16[16,16,128]{2,1,0:T(8,128)(2,1)S(1)}, u32[]{:S(2)}, u32[]{:S(2)}) async-start(bf16[16,16,128]{2,1,0:T(8,128)(2,1)} %get-tuple-element.68), calls=%async_computation.8 | async-start | bytes 131072 | tf_op jit(solution)/shard_map/all_to_all | solution.py:754

commit v3 on v2

v3 whole, which is shorter than its diff:
```python
import functools

import jax
import jax.numpy as jnp
from jax import lax
from jax.experimental import pallas as pl
from jax.experimental.pallas import tpu as pltpu
from jax.sharding import PartitionSpec as P

HW = 2
STEPS = 4
EPS = 1e-06
PIECES = 3
DOT_ROWS = 16
STATE_ROWS = 64
VMEM_BYTES = 32 * 1024 * 1024
BF16 = jnp.bfloat16
F32 = jnp.float32


def dot(a, b):
    return jnp.dot(a, b, preferred_element_type=F32)


def dot_first(a, b):
    return lax.dot_general(a, b, (((0,), (0,)), ((), ())), preferred_element_type=F32)


def store_split(ref, values, count):
    rest = values
    ref[...] = jnp.zeros(ref.shape, F32)
    for piece in range(PIECES):
        part = rest.astype(BF16).astype(F32)
        ref[piece * 5 : piece * 5 + count, :] = part[:count]
        rest = rest - part


def joined(rows):
    return [rows[i : i + 1] + rows[5 + i : 6 + i] + rows[10 + i : 11 + i] for i in range(5)]


def entry_row(i, l):
    low, high = min(i, l), max(i, l)
    return 20 + high * (high + 1) // 2 + low


def basis_row(i, l):
    return 32 + i * (i + 1) // 2 + l


def coefficients(m, grams, state_in, state_out):
    last = m - 1
    entry = lambda i, l: state_in[entry_row(i, l) : entry_row(i, l) + 1, :]
    expand = lambda i, l: state_in[basis_row(i, l) : basis_row(i, l) + 1, :]

    def put(row, value):
        state_out[row : row + 1, :] = value

    dots = []
    for i in range(m):
        dots.append(sum(expand(i, l) * grams[l] for l in range(i + 1)))
    weights = [dots[i] + entry(i, last) for i in range(m)]
    spread = [sum(weights[l] * entry(i, l) for l in range(m)) for i in range(m)]
    square = grams[m]
    for i in range(m):
        square = square + weights[i] * (weights[i] + spread[i] - 2.0 * dots[i])
    total = jnp.maximum(square, 0.0) + EPS
    root = jnp.sqrt(total)
    inverse = 1.0 / root
    for l in range(m):
        value = sum(weights[i] * expand(i, l) for i in range(l, m))
        put(basis_row(m, l), -inverse * value)
    put(basis_row(m, m), inverse)
    for i in range(m):
        put(i * STEPS + last, weights[i] + (1.0 if i == last else 0.0))
    if m > 0:
        put(m * STEPS + last, root)
    if m < STEPS:
        for i in range(m):
            put(entry_row(i, m), (-entry(i, last) - spread[i]) * inverse)
        put(entry_row(m, m), -EPS / total)
    return weights, inverse


def from_branches(ups_ref, rank):
    rows = ups_ref[0, rank:].astype(F32)
    for c in range(1, ups_ref.shape[0]):
        rows = rows + ups_ref[c, rank:].astype(F32)
    return joined(rows)


SMEM = pl.BlockSpec(memory_space=pltpu.SMEM)
VMEM = pl.BlockSpec(memory_space=pltpu.VMEM)
HBM = pl.BlockSpec(memory_space=pl.ANY)
AFTER = pl.BlockSpec(memory_space=pl.ANY)
AFTER_VMEM = pl.BlockSpec(memory_space=pl.ANY)
LOOSE = pl.BlockSpec(memory_space=pl.ANY)
FREE = pl.BlockSpec(memory_space=pltpu.VMEM)
AHEAD = 3
CHUNKS = 4
PIN = True


def call(kernel, args, in_specs, outs, scratch, name, flops, moved, aliases={}):
    def pinned(array, spec):
        if not PIN or not any(spec is one for one in (VMEM, HBM, AFTER, AFTER_VMEM)):
            return array
        in_vmem = spec is VMEM or spec is AFTER_VMEM
        return pltpu.with_memory_space_constraint(array, pltpu.VMEM if in_vmem else pltpu.HBM)

    def shape_of(shape, dtype, spec):
        if not PIN or not (spec is VMEM or spec is HBM):
            return jax.ShapeDtypeStruct(shape, dtype)
        return (pltpu.VMEM if spec is VMEM else pltpu.HBM)(shape, dtype)

    return pl.pallas_call(
        kernel,
        in_specs=list(in_specs),
        out_specs=[spec for _, _, spec in outs],
        out_shape=[shape_of(*out) for out in outs],
        scratch_shapes=scratch,
        input_output_aliases=aliases,
        compiler_params=pltpu.CompilerParams(vmem_limit_bytes=VMEM_BYTES),
        cost_estimate=pl.CostEstimate(flops=flops, bytes_accessed=moved, transcendentals=0),
        name=name,
    )(*[pinned(array, spec) for array, spec in zip(args, in_specs)])


def semaphores(*shape):
    return pltpu.SemaphoreType.DMA(shape)


def windowed(count, ahead, fetch, work):
    def start(i):
        for j, copy in enumerate(fetch(i)):
            copy.start(priority=j % 2)

    def body(i, carry):
        @pl.when(i + ahead < count)
        def _():
            start(i + ahead)

        for copy in fetch(i):
            copy.wait()
        work(i)
        return carry

    def begin():
        for i in range(min(ahead, count)):
            start(i)

    return begin, lambda: lax.fori_loop(0, count, body, 0)


def slab(i, size):
    return pl.ds(pl.multiple_of(i * size, size), size)


def pack_kernel(branch, mask_ref, slot_ref, index_ref, near_mask_ref, far_ref, *refs):
    basis_ref, transfer_ref, top_ref = refs[:3]
    out_ref, count_ref, list_ref, basis_out, transfer_out, top_out = refs[3:9]
    blocks, total, packed, basis, transfer, top, turned, lifting, row, arrived, left, came = refs[9:]
    leaves, entries, rank, _ = blocks.shape
    sources, _, width = packed.shape
    slots = width // rank
    near_entries = index_ref.shape[1]

    def fetch(leaf):
        return [pltpu.make_async_copy(far_ref.at[leaf], blocks.at[leaf], arrived.at[leaf])]

    def store(leaf):
        rows = slab(leaf, rank)
        return pltpu.make_async_copy(packed.at[:, rows], out_ref.at[:, rows], left.at[leaf])

    def work(leaf):
        total[...] = jnp.zeros(total.shape, F32)
        for f in range(entries):
            weight = mask_ref[leaf, f].astype(F32)
            total[slot_ref[leaf, f]] += blocks[leaf, f].astype(F32) * weight
        rows = slab(leaf, rank)
        for source in range(sources):
            sides = [total[source * slots + s] for s in range(slots)]
            packed[source, rows] = jnp.concatenate(sides, axis=1).astype(BF16)
        store(leaf).start()

    def list_one(i, count):
        leaf, n = i // near_entries, i % near_entries
        place = index_ref[leaf, n]
        hit = (near_mask_ref[leaf, n] != 0) & ((place < HW) | (place >= HW + leaves))
        list_ref[i] = 0

        @pl.when(hit)
        def _():
            list_ref[count] = i

        return count + hit.astype(jnp.int32)

    small = [
        pltpu.make_async_copy(basis_ref, basis, came.at[0]),
        pltpu.make_async_copy(transfer_ref, transfer, came.at[1]),
        pltpu.make_async_copy(top_ref, top, came.at[2]),
    ]
    for copy in small:
        copy.start()
    begin, run = windowed(leaves, AHEAD, fetch, work)
    begin()
    count_ref[0] = lax.fori_loop(0, list_ref.shape[0], list_one, 0)
    for copy in small:
        copy.wait()
    turn = lambda a: a.astype(F32).T.astype(BF16)
    for leaf in range(leaves):
        turned[leaf] = turn(basis[leaf])
    for pair in range(leaves // 2):
        columns = slice(pair * 2 * rank, (pair + 1) * 2 * rank)
        sides = [turn(transfer[2 * pair + j]) for j in range(2)]
        lifting[:, columns] = jnp.concatenate(sides, axis=1)
    for pair in range(top.shape[1] // 2):
        columns = slice(pair * 2 * rank, (pair + 1) * 2 * rank)
        sides = []
        for c in (2 * pair, 2 * pair + 1):
            sides.append(top[0, c] * (branch[0] != c).astype(F32).astype(BF16))
        row[:, columns] = jnp.concatenate(sides, axis=1)
    results = [
        pltpu.make_async_copy(turned, basis_out, came.at[0]),
        pltpu.make_async_copy(lifting, transfer_out, came.at[1]),
        pltpu.make_async_copy(row, top_out, came.at[2]),
    ]
    for copy in results:
        copy.start()
    run()
    for leaf in range(leaves):
        store(leaf).wait()
    for copy in results:
        copy.wait()


def pack(branch, basis, transfer, top_blocks, far_blocks, far_mask, far_slot, near_index, near_mask, inner, slots):
    leaves, entries, rank, _ = far_blocks.shape
    shape = (inner, leaves * rank, slots * rank)
    turned = (leaves, basis.shape[2], rank)
    lifting = (rank, leaves * rank)
    row = (rank, top_blocks.shape[1] * rank)
    return call(
        pack_kernel,
        (branch, far_mask, far_slot, near_index, near_mask, far_blocks, basis, transfer, top_blocks),
        (SMEM,) * 5 + (HBM,) * 4,
        [
            (shape, BF16, HBM),
            ((1,), jnp.int32, SMEM),
            ((near_index.size,), jnp.int32, SMEM),
            (turned, BF16, HBM),
            (lifting, BF16, HBM),
            (row, BF16, HBM),
        ],
        [
            pltpu.VMEM(far_blocks.shape, BF16),
            pltpu.VMEM((inner * slots, rank, rank), F32),
            pltpu.VMEM(shape, BF16),
            pltpu.VMEM(basis.shape, BF16),
            pltpu.VMEM(transfer.shape, BF16),
            pltpu.VMEM(top_blocks.shape, BF16),
            pltpu.VMEM(turned, BF16),
            pltpu.VMEM(lifting, BF16),
            pltpu.VMEM(row, BF16),
            semaphores(leaves),
            semaphores(leaves),
            semaphores(3),
        ],
        "pack",
        0,
        10 << 20,
    )


def near_kernel(index_ref, mask_ref, blocks_ref, own_ref, *refs):
    out_ref, blocks, own, result, arrived, came, left = refs[-7:]
    leaves, entries, size, _ = blocks.shape

    def fetch(leaf):
        halves = [pl.ds(j * (entries // 2), entries // 2) for j in range(2)]
        return [
            pltpu.make_async_copy(
                blocks_ref.at[leaf, half], blocks.at[leaf, half], arrived.at[leaf, j]
            )
            for j, half in enumerate(halves)
        ]

    def store(leaf):
        return pltpu.make_async_copy(
            result.at[leaf], out_ref.at[leaf], left.at[leaf]
        )

    def work(leaf):
        total = None
        for n in range(entries):
            place = index_ref[leaf, n] - HW
            inside = (place >= 0) & (place < leaves)
            weight = jnp.where(inside, mask_ref[leaf, n], 0).astype(F32).astype(BF16)
            values = own[jnp.clip(place, 0, leaves - 1)] * weight
            term = dot(blocks[leaf, n], values)
            total = term if total is None else total + term
        result[leaf] = total
        store(leaf).start()

    begin, run = windowed(leaves, AHEAD, fetch, work)
    copy = pltpu.make_async_copy(own_ref, own, came)
    copy.start()
    begin()
    copy.wait()
    run()
    for leaf in range(leaves):
        store(leaf).wait()


def near_field(near_index, near_mask, near_blocks, own, *earlier):
    leaves, _, size, _ = near_blocks.shape
    columns = own.shape[2]
    return call(
        near_kernel,
        (near_index, near_mask, near_blocks, own) + earlier,
        (SMEM, SMEM, HBM, HBM) + (AFTER,) * len(earlier),
        [((leaves, size, columns), F32, HBM)],
        [
            pltpu.VMEM(near_blocks.shape, BF16),
            pltpu.VMEM(own.shape, BF16),
            pltpu.VMEM((leaves, size, columns), F32),
            semaphores(leaves, 2),
            semaphores(),
            semaphores(leaves),
        ],
        "near_field",
        2 * near_blocks.size * columns,
        2 * near_blocks.size,
    )[0]


def gather_sum_kernel(recv, *refs, lead):
    out_ref, split = refs[-2:]
    rank = out_ref.shape[0] - DOT_ROWS
    total = recv[0, lead:].astype(F32)
    for i in range(1, recv.shape[0]):
        total = total + recv[i, lead:].astype(F32)
    store_split(split, jnp.concatenate(joined(total[rank:]), axis=0), 5)
    if rank > 0:
        out_ref[:rank] = total[:rank].astype(BF16)
    out_ref[rank:] = split[...].astype(BF16)


def gather_sum(recv, lead, earlier):
    _, rows, columns = recv.shape
    return call(
        functools.partial(gather_sum_kernel, lead=lead),
        (recv, earlier),
        (VMEM, AFTER),
        [((rows - lead, columns), BF16, VMEM)],
        [pltpu.VMEM((DOT_ROWS, columns), F32)],
        "gather_sum",
        1 << 20,
        1 << 19,
    )[0]


def stack_kernel(*refs):
    for i, ref in enumerate(refs[:-2]):
        refs[-1][i] = ref[...]


def over_branches(summed, outer, earlier, between):
    shifts = [[(o, (o + 2 * j) % outer) for o in range(outer)] for j in range(1, outer // 2)]
    parts = [summed] + [lax.ppermute(summed, "outer", shift) for shift in shifts]
    column = call(
        stack_kernel,
        parts + [earlier],
        [VMEM] * len(parts) + [AFTER_VMEM],
        [((len(parts),) + summed.shape, BF16, VMEM)],
        [],
        "stack",
        0,
        1 << 18,
    )[0]
    other = lax.ppermute(column, "outer", [(o, o ^ 1) for o in range(outer)])
    return column, other, between(column)


def in_order(branch, column, other, ups):
    count = ups.shape[0]
    for j in range(count // 2):
        ups[lax.rem(branch[0] + count - 2 * j, count)] = column[j]
        mate = branch[0] + 1 - 2 * lax.rem(branch[0], 2)
        ups[lax.rem(mate + count - 2 * j, count)] = other[j]


def far_kernel(recv, packed_ref, _, far, packed, arrived):
    sources, _, width = packed.shape
    share = sources // CHUNKS

    def fetch(i):
        some = slab(i, share)
        return [pltpu.make_async_copy(packed_ref.at[some], packed.at[some], arrived.at[i])]

    def work(i):
        term = None
        for j in range(share):
            source = i * share + j
            one = dot(packed[source], recv[source, :width])
            term = one if term is None else term + one

        @pl.when(i == 0)
        def _():
            far[...] = term

        @pl.when(i > 0)
        def _():
            far[...] += term

    begin, run = windowed(CHUNKS, CHUNKS, fetch, work)
    begin()
    run()


def far_field(recv, packed, earlier):
    sources, rows, _ = packed.shape
    return call(
        far_kernel,
        (recv, packed, earlier),
        (VMEM, HBM, AFTER_VMEM),
        [((rows, recv.shape[2]), F32, VMEM)],
        [pltpu.VMEM(packed.shape, BF16), semaphores(CHUNKS)],
        "far_field",
        2 * packed.size * recv.shape[2],
        2 * packed.size,
    )[0]


def halo_kernel(count_ref, list_ref, index_ref, blocks_ref, before, after, near_ref, *refs):
    refs = list(refs)
    take = lambda count: [refs.pop(0) for _ in range(count)]
    held = (len(refs) - 8) // 2
    sources = take(held)
    take(1)
    near, *targets = take(1 + held)
    blocks, halo, came, fetched, near_came, loaded = take(6)
    leaves = near.shape[0]
    reach = before.shape[0]
    entries = blocks_ref.shape[1]
    sides = [
        pltpu.make_async_copy(before, halo.at[pl.ds(0, reach)], came.at[0]),
        pltpu.make_async_copy(after, halo.at[pl.ds(reach, reach)], came.at[1]),
    ]
    get = [
        pltpu.make_async_copy(near_ref.at[leaf], near.at[leaf], near_came.at[leaf])
        for leaf in range(leaves)
    ]
    load = [
        pltpu.make_async_copy(source, target, loaded.at[i])
        for i, (source, target) in enumerate(zip(sources, targets))
    ]

    def block(i):
        entry = list_ref[i]
        return pltpu.make_async_copy(
            blocks_ref.at[entry // entries, entry % entries], blocks.at[i], fetched.at[i]
        )

    def ask(i, carry):
        block(i).start()
        return carry

    count = count_ref[0]
    at_once = 4

    def add(group, carry):
        terms = []
        for j in range(at_once):
            i = group * at_once + j

            @pl.when(i < count)
            def _():
                block(i).wait()

        for j in range(at_once):
            i = jnp.minimum(group * at_once + j, count - 1)
            weight = (group * at_once + j < count).astype(F32).astype(BF16)
            entry = list_ref[i]
            leaf = entry // entries
            place = index_ref[leaf, entry % entries]
            values = halo[jnp.where(place < reach, place, place - leaves)] * weight
            terms.append((leaf, dot(blocks[i], values)))
        for leaf, term in terms:
            near[leaf] += term
        return carry

    for side in sides:
        side.start()
    lax.fori_loop(0, count, ask, 0)
    for copy in get + load:
        copy.start()
    for copy in sides + get:
        copy.wait()
    lax.fori_loop(0, (count + at_once - 1) // at_once, add, 0)
    for copy in load:
        copy.wait()


def halo_part(listed, near_index, near_blocks, before, after, near, held, earlier):
    leaves, entries, size, _ = near_blocks.shape
    halo = (2 * before.shape[0],) + before.shape[1:]
    return call(
        halo_kernel,
        (*listed, near_index, near_blocks, before, after, near, *held, earlier),
        (SMEM, SMEM, SMEM, HBM, LOOSE, LOOSE) + (HBM,) * (1 + len(held)) + (AFTER_VMEM,),
        [(a.shape, a.dtype, VMEM) for a in (near, *held)],
        [
            pltpu.VMEM((leaves * entries, size, size), BF16),
            pltpu.VMEM(halo, BF16),
            semaphores(2),
            semaphores(leaves * entries),
            semaphores(leaves),
            semaphores(len(held)),
        ],
        "halo_part",
        1 << 28,
        6 << 20,
    )


def load_kernel(*refs):
    count = (len(refs) - 2) // 2
    copies = [
        pltpu.make_async_copy(refs[i], refs[count + 1 + i], refs[-1].at[i]) for i in range(count)
    ]
    for copy in copies:
        copy.start()
    for copy in copies:
        copy.wait()


def load(arrays, earlier):
    return call(
        load_kernel,
        (*arrays, earlier),
        (HBM,) * len(arrays) + (AFTER_VMEM,),
        [(a.shape, a.dtype, VMEM) for a in arrays],
        [semaphores(len(arrays))],
        "load",
        0,
        5 << 20,
    )


def stage_kernel(*refs, k, points):
    refs = list(refs)
    take = lambda count: [refs.pop(0) for _ in range(count)]
    m = k - 1
    first, sends = k == 0, k < STEPS
    send_slot, branch = take(2)
    if first:
        z_any, basis_any, transfer_any = take(3)
    else:
        column, other, state, far, near, basis, turned, transfer, lifting, top = take(10)
        zs = take(k)
        (z_any,) = take(1)
    state_out, send = take(2)
    if sends:
        coarse_any, low_any, high_any = take(3)
    sums, split, arrived, left = take(4)
    if sends:
        coarse, skeletons, out = take(3)
    if first:
        basis, transfer, vectors, came = take(4)
    else:
        ups, result, coef, combined = take(4)

    leaves, rank, size = basis.shape
    group = leaves // CHUNKS

    def fetch(i):
        if not first:
            return []
        some = slab(i, group)
        return [pltpu.make_async_copy(z_any.at[some], vectors.at[some], arrived.at[i])]

    def stores(i):
        some = slab(i, group)
        pairs = []
        if not first:
            pairs.append((result.at[some], z_any.at[some]))
        if sends:
            pairs.append((coarse.at[some], coarse_any.at[some]))
        return [
            pltpu.make_async_copy(source, target, left.at[n, i])
            for n, (source, target) in enumerate(pairs)
        ]

    def work(i):
        for j in range(group):
            leaf = i * group + j
            if first:
                others = []
                z = vectors[leaf]
            else:
                others = [ref[leaf] for ref in zs]
                z = near[leaf] + dot(turned[leaf], combined[slab(leaf, rank)])
                for l in range(m):
                    z = z - coef[l : l + 1, :] * others[l + 1]
                z = z * coef[STEPS : STEPS + 1, :]
                result[leaf] = z
            if sends:
                rounded = z.astype(BF16)
                coarse[leaf] = rounded
                skeletons[slab(leaf, rank)] = dot(basis[leaf], rounded).astype(BF16)
            for l, vector in enumerate(others + [z]):
                sums[l] += jnp.sum((z * vector).reshape(size // 8, 8, z.shape[1]), axis=0)
        for copy in stores(i):
            copy.start()

    begin, run = windowed(CHUNKS, CHUNKS, fetch, work)
    if first:
        small = [
            pltpu.make_async_copy(basis_any, basis, came.at[0]),
            pltpu.make_async_copy(transfer_any, transfer, came.at[1]),
        ]
        for copy in small:
            copy.start()
    begin()
    sums[...] = jnp.zeros(sums.shape, F32)
    if first:
        state_out[...] = jnp.zeros(state_out.shape, F32)
        for copy in small:
            copy.wait()
    else:
        in_order(branch, column, other, ups)
        count, columns = ups.shape[0], ups.shape[2]
        incoming = dot(top[...], ups[:, :rank].reshape(count * rank, columns)).astype(BF16)
        down = dot(transfer[...].reshape(leaves * rank, rank), incoming)
        combined[...] = (far[...] + down).astype(BF16)
        grams = [row / points for row in from_branches(ups, rank)]
        state_out[...] = state[...]
        weights, inverse = coefficients(m, grams, state, state_out)
        for i, weight in enumerate(weights):
            coef[i : i + 1, :] = weight
        coef[STEPS : STEPS + 1, :] = inverse
    run()

    if sends:
        halos = [
            pltpu.make_async_copy(coarse.at[pl.ds(0, HW)], low_any, out.at[0]),
            pltpu.make_async_copy(coarse.at[pl.ds(leaves - HW, HW)], high_any, out.at[1]),
        ]
        for copy in halos:
            copy.start()
        if first:
            lifted = dot_first(transfer[...].reshape(leaves * rank, rank), skeletons[...])
        else:
            lifted = dot(lifting[...], skeletons[...])
        lifted = lifted.astype(BF16)
    products = [jnp.sum(sums[i], axis=0, keepdims=True) for i in range(k + 1)]
    products = jnp.concatenate(products + [jnp.zeros_like(products[0])] * (7 - k), axis=0)
    store_split(split, products, k + 1)
    dots = split[...].astype(BF16)
    inner = send.shape[0]
    if sends:
        slots = send_slot.shape[0]
        for r in range(inner):
            for s in range(slots):
                send[r, s * rank : (s + 1) * rank] = skeletons[slab(send_slot[s, r], rank)]
            send[r, slots * rank : (slots + 1) * rank] = lifted
            send[r, (slots + 1) * rank :] = dots
    else:
        for r in range(inner):
            send[r] = dots
    for i in range(CHUNKS):
        for copy in stores(i):
            copy.wait()
    if sends:
        for copy in halos:
            copy.wait()


def stage(k, points, send_slot, branch, rhs, basis, transfer, later):
    leaves, rank, size = basis.shape
    first, sends = k == 0, k < STEPS
    tall = rhs.shape
    columns = tall[2]
    slots, inner = send_slot.shape
    names, outs = [], []

    def get(name, shape, dtype, spec):
        names.append(name)
        outs.append((shape, dtype, spec))

    args, specs = [send_slot, branch], [SMEM, SMEM]
    if first:
        args += [rhs, basis, transfer]
        specs += [HBM] * 3
    else:
        args += later
        specs += [VMEM] * len(later)
        get("z", tall, F32, HBM)
    get("state", (STATE_ROWS, columns), F32, VMEM)
    rows = ((slots + 1) * rank if sends else 0) + DOT_ROWS
    get("send", (inner, rows, columns), BF16, VMEM)
    if sends:
        get("coarse", tall, BF16, HBM)
        get("low", (HW, size, columns), BF16, LOOSE)
        get("high", (HW, size, columns), BF16, LOOSE)

    scratch = [
        pltpu.VMEM((STEPS + 1, 8, columns), F32),
        pltpu.VMEM((DOT_ROWS, columns), F32),
        semaphores(CHUNKS),
        semaphores(2, CHUNKS),
    ]
    if sends:
        scratch += [
            pltpu.VMEM(tall, BF16),
            pltpu.VMEM((leaves * rank, columns), BF16),
            semaphores(2),
        ]
    if first:
        scratch += [
            pltpu.VMEM(basis.shape, BF16),
            pltpu.VMEM(transfer.shape, BF16),
            pltpu.VMEM(tall, F32),
            semaphores(2),
        ]
    else:
        column = later[0].shape
        scratch += [
            pltpu.VMEM((2 * column[0],) + column[1:], BF16),
            pltpu.VMEM(tall, F32),
            pltpu.VMEM((8, columns), F32),
            pltpu.VMEM((leaves * rank, columns), BF16),
        ]
    results = call(
        functools.partial(stage_kernel, k=k, points=points),
        args,
        specs,
        outs,
        scratch,
        f"stage{k}",
        1 << 27,
        (k + 4) << 20,
    )
    return dict(zip(names, results))


def vectors_kernel(*refs, known, points):
    refs = list(refs)
    take = lambda count: [refs.pop(0) for _ in range(count)]
    (state,) = take(1)
    if not known:
        branch, column, other = take(3)
    zs = take(known if known else STEPS + 1)
    if known:
        (krylov,) = take(1)
    else:
        _, krylov, hess_out = take(3)
    if known:
        vectors, result, arrived, left = take(4)
        after = state
    else:
        result, left, after, ups = take(4)
        vectors = zs
    parts = left.shape[1]
    group = zs[0].shape[0] // parts
    size = zs[0].shape[1]
    wanted = range(known) if known else [STEPS]

    def fetch(i):
        some = slab(i, group)
        return [
            pltpu.make_async_copy(z.at[some], vectors.at[l, some], arrived.at[l, i])
            for l, z in enumerate(zs if known else [])
        ]

    def store(n, i):
        some = slab(i, group)
        return pltpu.make_async_copy(result.at[n, some], krylov.at[wanted[n], some], left.at[n, i])

    def work(i):
        for j in range(group):
            leaf = i * group + j
            for n, which in enumerate(wanted):
                vector = None
                for l in range(which + 1):
                    row = basis_row(which, l)
                    values = vectors[l, leaf] if known else vectors[l][leaf]
                    term = after[row : row + 1, :] * values
                    vector = term if vector is None else vector + term
                result[n, leaf] = vector
        for n in range(len(wanted)):
            store(n, i).start()

    begin, run = windowed(parts, parts, fetch, work)
    begin()
    if not known:
        in_order(branch, column, other, ups)
        grams = [row / points for row in from_branches(ups, 0)]
        after[...] = state[...]
        coefficients(STEPS, grams, state, after)
    run()
    if not known:
        for i in range(STEPS + 1):
            for j in range(STEPS):
                row = i * STEPS + j
                if i <= j + 1:
                    hess_out[i, j : j + 1, :] = after[row : row + 1, :]
                else:
                    hess_out[i, j : j + 1, :] = jnp.zeros((1, hess_out.shape[2]), F32)
    for n in range(len(wanted)):
        for i in range(parts):
            store(n, i).wait()


def basis_vectors(state, zs, parts):
    known = len(zs)
    tall = zs[0].shape
    return call(
        functools.partial(vectors_kernel, known=known, points=0),
        [state] + zs,
        [VMEM] + [HBM] * known,
        [((STEPS + 1,) + tall, F32, HBM)],
        [
            pltpu.VMEM((known,) + tall, F32),
            pltpu.VMEM((known,) + tall, F32),
            semaphores(known, parts),
            semaphores(known, parts),
        ],
        "basis_vectors",
        1 << 23,
        8 << 20,
    )[0]


def last(points, branch, column, other, state, krylov, zs, parts):
    tall = zs[0].shape
    return call(
        functools.partial(vectors_kernel, known=0, points=points),
        [state, branch, column, other] + list(zs) + [krylov],
        [VMEM, SMEM, VMEM, VMEM] + [VMEM] * len(zs) + [HBM],
        [(krylov.shape, F32, HBM), ((STEPS + 1, STEPS, tall[2]), F32, FREE)],
        [
            pltpu.VMEM((1,) + tall, F32),
            semaphores(1, parts),
            pltpu.VMEM(state.shape, F32),
            pltpu.VMEM((2 * column.shape[0],) + column.shape[1:], BF16),
        ],
        "last_vector",
        1 << 22,
        6 << 20,
        {4 + len(zs): 0},
    )


def shards(
    rhs,
    near_blocks,
    near_index,
    near_mask,
    basis,
    far_blocks,
    far_slot,
    far_mask,
    send_slot,
    transfer,
    top_blocks,
):
    outer, inner = lax.axis_size("outer"), lax.axis_size("inner")
    points = outer * inner * rhs.shape[0]
    leaves, rank = basis.shape[:2]
    slots = send_slot.shape[2]
    branch = lax.axis_index("outer").astype(jnp.int32).reshape(1)
    up_pairs = [(i, i + 1) for i in range(inner - 1)]
    down_pairs = [(j, i) for i, j in up_pairs]
    wanted = send_slot[0].T

    def exchange(array, axis):
        return lax.all_to_all(array, axis, split_axis=0, concat_axis=0, tiled=True)

    zs = [rhs.reshape(leaves, -1, rhs.shape[1])]
    out = stage(0, points, wanted, branch, zs[0], basis, transfer, None)
    packed, count, entries, turned, lifting, top = pack(
        branch, basis, transfer, top_blocks, far_blocks, far_mask, far_slot, near_index, near_mask,
        inner, slots,
    )
    listed = (count, entries)
    state = out["state"]
    for k in range(1, STEPS + 1):
        recv = exchange(out["send"], "inner")
        before = lax.ppermute(out["high"], "inner", up_pairs)
        after = lax.ppermute(out["low"], "inner", down_pairs)
        earlier = (packed,) if k == 1 else ()
        near = near_field(near_index, near_mask, near_blocks, out["coarse"], *earlier)
        summed = gather_sum(recv, slots * rank, near)
        local_far = far_field(recv, packed, summed)

        def between(column):
            held = (basis, turned, transfer, lifting, top, *zs)
            return halo_part(
                listed, near_index, near_blocks, before, after, near, held, column
            )

        column, other, (near, *held) = over_branches(summed, outer, local_far, between)
        later = [column, other, state, local_far, near, *held]
        out = stage(k, points, wanted, branch, zs[0], basis, transfer, later)
        state = out["state"]
        zs = zs + [out["z"]]
    krylov = basis_vectors(state, zs[:STEPS], CHUNKS)
    recv = exchange(out["send"], "inner")
    summed = gather_sum(recv, 0, krylov)
    loaded = load(zs, summed)
    column, other, loaded = over_branches(summed, outer, loaded[0], lambda column: loaded)
    krylov, hessenberg = last(points, branch, column, other, state, krylov, loaded, CHUNKS)
    return krylov.reshape(STEPS + 1, *rhs.shape), hessenberg


def solution(mesh):
    return jax.shard_map(
        shards,
        mesh=mesh,
        in_specs=(
            P(("outer", "inner"), None),
            P(("outer", "inner"), None, None, None),
            P(("outer", "inner"), None),
            P(("outer", "inner"), None),
            P(("outer", "inner"), None, None),
            P(("outer", "inner"), None, None, None),
            P(("outer", "inner"), None),
            P(("outer", "inner"), None),
            P(("outer", "inner"), None, None),
            P(("outer", "inner"), None, None),
            P("outer", None, None, None),
        ),
        out_specs=(P(None, ("outer", "inner"), None), P()),
        check_vma=False,
    )
```

time: 251 us -> 221 us (0.88)
  Pallas kernels: 138 us -> 103 us
  blocking collectives: 9.57 us -> 0 us
  waiting for transfers between devices: 26.6 us -> 34.1 us
  starting transfers between devices: 73.8 us -> 81.2 us
    pallas_call x21 -> x31, Pallas kernels: 138 us -> 103 us  [call(): pl.pallas_call(kernel, in_specs=list(in_specs), out_specs=[spec for _, _,...]
    ppermute x0 -> x20, starting transfers between devices: none -> 29.7 us  [the longest x5 16.1 us: over_branches(): other = lax.ppermute(column, 'outer', [(o, o ^ 1) for o in range(outer)])]
    all_to_all x9 -> x5, starting transfers between devices: 55.6 us -> 33.2 us  [exchange(): return lax.all_to_all(array, axis, split_axis=0, concat_axis=0, tiled=True)]
    all_to_all x1 -> x0, blocking collectives: 9.57 us -> none  [exchange(): return lax.all_to_all(array, axis, split_axis=0, concat_axis=0, tiled=True)]
    all_to_all x9 -> x5, waiting for transfers between devices: 26.5 us -> 32.6 us  [exchange(): return lax.all_to_all(array, axis, split_axis=0, concat_axis=0, tiled=True)]
  transfers between devices with their start and end apart: 17 -> 33, of which waited for: 4 -> 8; matrix products, arithmetic and copies ran while one was open for 0% -> 0% of each run, Pallas kernels for 37% -> 36%
where the time goes in v3:
time: 221 us
  Pallas kernels  103 us (47%)
  starting transfers between devices  81.2 us (37%)
  waiting for transfers between devices  34.1 us (15%)
    pallas_call x31, Pallas kernels, call(): pl.pallas_call(kernel, in_specs=list(in_specs), out_specs=[spec for _, _,...  103 us
    all_to_all x5, starting transfers between devices, exchange(): return lax.all_to_all(array, axis, split_axis=0, concat_axis=0, tiled=True)  33.2 us
    all_to_all x5, waiting for transfers between devices, exchange(): return lax.all_to_all(array, axis, split_axis=0, concat_axis=0, tiled=True)  32.6 us
    ppermute x5, starting transfers between devices, over_branches(): other = lax.ppermute(column, 'outer', [(o, o ^ 1) for o in range(outer)])  16.1 us
    ppermute x15, starting transfers between devices, over_branches(): lax.ppermute(summed, 'outer', shift)  13.6 us
    ppermute x4, starting transfers between devices, shards(): before = lax.ppermute(out['high'], 'inner', up_pairs)  13.1 us
    ppermute x4, starting transfers between devices, shards(): after = lax.ppermute(out['low'], 'inner', down_pairs)  5.17 us
  transfers between devices with their start and end apart: 33, of which 8 were waited for; matrix products, arithmetic and copies ran while one was open for 0% of the time, Pallas kernels for 36%

profile of v3, /device:TPU:1, one launch (start us, length us, event | category | flops | bytes accessed | tf_op | source)
XLA Modules:
  0.0 220.6 jit_solution(18158573018241455874)
XLA Ops:
  1.3 4.2 %stage0.1 = (f32[64,128]{1,0:T(8,128)S(1)}, bf16[16,336,128]{2,1,0:T(8,128)(2,1)}, bf16[8,256,128]{2,1,0:T(8,128)(2,1)}, bf16[2,256,128]{2,1,0:T(8,128)(2,1)S(1)}, bf16[2,256,128]{2,1,0:T(8,128)(2,1)S(1)}) custom-call(s32[4,16]{1,0:T(4,128)S(1)} %bitcast.6, s32[1]{0:T(128)} %bitcast.2.refs_1_.branch, f32[8,256,128]{2,1,0:T(8,128)} %bitcast.11, ...), custom_call_target="tpu_custom_call" | custom-call | flops 134217728 | bytes 4194304 | tf_op jit(solution)/shard_map/stage0/pallas_call | solution.py:116
  5.6 8.7 %all-to-all-start = ((bf16[16,336,128]{2,1,0:T(8,128)(2,1)}), bf16[16,336,128]{2,1,0:T(8,128)(2,1)S(1)}, u32[]{:S(2)}, u32[]{:S(2)}) async-start(bf16[16,336,128]{2,1,0:T(8,128)(2,1)} %get-tuple-element.75), calls=%async_computation | async-start | bytes 2752512 | tf_op jit(solution)/shard_map/all_to_all | solution.py:879
  14.4 3.3 %collective-permute-start.4 = (bf16[2,256,128]{2,1,0:T(8,128)(2,1)S(1)}, bf16[2,256,128]{2,1,0:T(8,128)(2,1)S(1)}, u32[]{:S(2)}, u32[]{:S(2)}) collective-permute-start(bf16[2,256,128]{2,1,0:T(8,128)(2,1)S(1)} %get-tuple-element.81), channel_id=1, source_target_pairs={{0,1},{1,2},{2,3},{3,4},{4,5},{5,6},{6,7},{7,8},{8,9},{9,10},{10,1... | collective-permute-start | bytes 393224 | tf_op jit(solution)/shard_map/ppermute | solution.py:891
  17.6 1.3 collective-permute-start.5
  19.0 8.6 %pack.1 = (bf16[16,512,256]{2,1,0:T(8,128)(2,1)}, s32[1]{0:T(128)}, s32[64]{0:T(128)S(1)}, bf16[8,256,64]{2,1,0:T(8,128)(2,1)}, bf16[64,512]{1,0:T(8,128)(2,1)}, /*index=5*/bf16[64,512]{1,0:T(8,128)(2,1)}) custom-call(s32[1]{0:T(128)} %bitcast.2.refs_1_.branch, s32[8,48]{1,0:T(8,128)S(1)} %copy-done.4, s32[8,48]{1,0:T(8,128)S(1)} %copy-done.5, ...), custom_call_target="tpu_custom_call" | custom-call | bytes 10485760 | tf_op jit(solution)/shard_map/pack/pallas_call | solution.py:116
  27.6 6.7 %near_field.4.refs_0_.near_ref = f32[8,256,128]{2,1,0:T(8,128)} custom-call(s32[8,8]{1,0:T(8,128)S(1)} %copy-done, s32[8,8]{1,0:T(8,128)S(1)} %copy-done.1, bf16[8,8,256,256]{3,2,1,0:T(8,128)(2,1)} %blocks_ref.15, bf16[8,256,128]{2,1,0:T(8,128)(2,1)} %get-tuple-element.76.own_ref, bf16[16,512,256]{2,1,0:T(8,128)(2,1)} %get-tuple-element.77.refs_0_.packed_ref), custom_call_target="tpu_custom_call" | custom-call | flops 1073741824 | bytes 8388608 | tf_op jit(solution)/shard_map/near_field/pallas_call | solution.py:116
  34.4 2.5 %collective-permute-start.2 = (bf16[80,128]{1,0:T(8,128)(2,1)S(1)}, bf16[80,128]{1,0:T(8,128)(2,1)S(1)}, u32[]{:S(2)}, u32[]{:S(2)}) collective-permute-start(bf16[80,128]{1,0:T(8,128)(2,1)S(1)} %gather_sum.5._.refs_0_), channel_id=1, source_target_pairs={{0,96},{16,112},{32,0},{48,16},{64,32},{80,48},{96,64},{112,80},{1... | collective-permute-start | bytes 61448 | tf_op jit(solution)/shard_map/ppermute | solution.py:370
  38.1 3.1 %far_field.4.refs_4_.refs_5_ = f32[512,128]{1,0:T(8,128)S(1)} custom-call(bf16[16,336,128]{2,1,0:T(8,128)(2,1)S(1)} %all-to-all-done.recv, bf16[16,512,256]{2,1,0:T(8,128)(2,1)} %get-tuple-element.77.refs_0_.packed_ref, bf16[80,128]{1,0:T(8,128)(2,1)S(1)} %gather_sum.5._.refs_0_), custom_call_target="tpu_custom_call" | custom-call | flops 536870912 | bytes 4194304 | tf_op jit(solution)/shard_map/far_field/pallas_call | solution.py:116
  41.3 4.2 %collective-permute-start.3 = (bf16[4,80,128]{2,1,0:T(8,128)(2,1)S(1)}, bf16[4,80,128]{2,1,0:T(8,128)(2,1)S(1)}, u32[]{:S(2)}, u32[]{:S(2)}) collective-permute-start(bf16[4,80,128]{2,1,0:T(8,128)(2,1)S(1)} %stack.5.refs_6_.refs_2_), channel_id=1, source_target_pairs={{0,16},{16,0},{32,48},{48,32},{64,80},{80,64},{96,112},{112,96},{1... | collective-permute-start | bytes 245768 | tf_op jit(solution)/shard_map/ppermute | solution.py:381
  45.6 5.8 %halo_part.4 = (f32[8,256,128]{2,1,0:T(8,128)S(1)}, bf16[8,64,256]{2,1,0:T(8,128)(2,1)S(1)}, bf16[8,256,64]{2,1,0:T(8,128)(2,1)S(1)}, bf16[8,64,64]{2,1,0:T(8,12...) custom-call(s32[1]{0:T(128)} %get-tuple-element.79.count_ref, ...), custom_call_target="tpu_custom_call" | custom-call | flops 268435456 | bytes 6291456 | tf_op jit(solution)/shard_map/halo_part/pallas_call | solution.py:116
  51.4 4.7 %stage1.1 = (f32[8,256,128]{2,1,0:T(8,128)}, f32[64,128]{1,0:T(8,128)S(1)}, bf16[16,336,128]{2,1,0:T(8,128)(2,1)}, bf16[8,256,128]{2,1,0:T(8,128)(2,1)}, bf16[2,...) custom-call(s32[4,16]{1,0:T(4,128)S(1)} %bitcast.7, s32[1]{0:T(128)} %bitcast.2.refs_1_.branch, ...), custom_call_target="tpu_custom_call" | custom-call | flops 134217728 | bytes 5242880 | tf_op jit(solution)/shard_map/stage1/pallas_call | solution.py:116
  56.1 7.8 %all-to-all-start.1 = ((bf16[16,336,128]{2,1,0:T(8,128)(2,1)}), bf16[16,336,128]{2,1,0:T(8,128)(2,1)S(1)}, u32[]{:S(2)}, u32[]{:S(2)}) async-start(bf16[16,336,128]{2,1,0:T(8,128)(2,1)} %get-tuple-element.93), calls=%async_computation.1 | async-start | bytes 2752512 | tf_op jit(solution)/shard_map/all_to_all | solution.py:879
  63.9 3.3 %collective-permute-start.10 = (bf16[2,256,128]{2,1,0:T(8,128)(2,1)S(1)}, bf16[2,256,128]{2,1,0:T(8,128)(2,1)S(1)}, u32[]{:S(2)}, u32[]{:S(2)}) collective-permute-start(bf16[2,256,128]{2,1,0:T(8,128)(2,1)S(1)} %get-tuple-element.96), channel_id=1, source_target_pairs={{0,1},{1,2},{2,3},{3,4},{4,5},{5,6},{6,7},{7,8},{8,9},{9,10},{10,1... | collective-permute-start | bytes 393224 | tf_op jit(solution)/shard_map/ppermute | solution.py:891
  67.2 1.3 collective-permute-start.11
  68.5 6.7 %near_field.5.refs_0_.near_ref = f32[8,256,128]{2,1,0:T(8,128)} custom-call(s32[8,8]{1,0:T(8,128)S(1)} %copy-done, s32[8,8]{1,0:T(8,128)S(1)} %copy-done.1, bf16[8,8,256,256]{3,2,1,0:T(8,128)(2,1)} %blocks_ref.15, bf16[8,256,128]{2,1,0:T(8,128)(2,1)} %get-tuple-element.94.own_ref), custom_call_target="tpu_custom_call" | custom-call | flops 1073741824 | bytes 8388608 | tf_op jit(solution)/shard_map/near_field/pallas_call | solution.py:116
  75.2 10.0 %all-to-all-done.1.recv = bf16[16,336,128]{2,1,0:T(8,128)(2,1)S(1)} async-done(((bf16[16,336,128]{2,1,0:T(8,128)(2,1)}), bf16[16,336,128]{2,1,0:T(8,128)(2,1)S(1)}, u32[]{:S(2)}, u32[]{:S(2)}) %all-to-all-start.1) | async-done | bytes 1376288 | tf_op jit(solution)/shard_map/all_to_all | solution.py:879
  87.2 3.1 %far_field.5.refs_4_.refs_5_ = f32[512,128]{1,0:T(8,128)S(1)} custom-call(bf16[16,336,128]{2,1,0:T(8,128)(2,1)S(1)} %all-to-all-done.1.recv, bf16[16,512,256]{2,1,0:T(8,128)(2,1)} %get-tuple-element.77.refs_0_.packed_ref, bf16[80,128]{1,0:T(8,128)(2,1)S(1)} %gather_sum.6._.refs_0_), custom_call_target="tpu_custom_call" | custom-call | flops 536870912 | bytes 4194304 | tf_op jit(solution)/shard_map/far_field/pallas_call | solution.py:116
  90.4 3.4 %collective-permute-start.9 = (bf16[4,80,128]{2,1,0:T(8,128)(2,1)S(1)}, bf16[4,80,128]{2,1,0:T(8,128)(2,1)S(1)}, u32[]{:S(2)}, u32[]{:S(2)}) collective-permute-start(bf16[4,80,128]{2,1,0:T(8,128)(2,1)S(1)} %stack.6.refs_7_.refs_2_), channel_id=1, source_target_pairs={{0,16},{16,0},{32,48},{48,32},{64,80},{80,64},{96,112},{112,96},{1... | collective-permute-start | bytes 245768 | tf_op jit(solution)/shard_map/ppermute | solution.py:381
  93.9 5.9 %halo_part.5 = (f32[8,256,128]{2,1,0:T(8,128)S(1)}, bf16[8,64,256]{2,1,0:T(8,128)(2,1)S(1)}, bf16[8,256,64]{2,1,0:T(8,128)(2,1)S(1)}, bf16[8,64,64]{2,1,0:T(8,12...) custom-call(s32[1]{0:T(128)} %get-tuple-element.79.count_ref, ...), custom_call_target="tpu_custom_call" | custom-call | flops 268435456 | bytes 6291456 | tf_op jit(solution)/shard_map/halo_part/pallas_call | solution.py:116
  99.7 4.8 %stage2.1 = (f32[8,256,128]{2,1,0:T(8,128)}, f32[64,128]{1,0:T(8,128)S(1)}, bf16[16,336,128]{2,1,0:T(8,128)(2,1)}, bf16[8,256,128]{2,1,0:T(8,128)(2,1)}, bf16[2,...) custom-call(s32[4,16]{1,0:T(4,128)S(1)} %bitcast.8, s32[1]{0:T(128)} %bitcast.2.refs_1_.branch, ...), custom_call_target="tpu_custom_call" | custom-call | flops 134217728 | bytes 6291456 | tf_op jit(solution)/shard_map/stage2/pallas_call | solution.py:116
  104.5 5.3 %all-to-all-start.2 = ((bf16[16,336,128]{2,1,0:T(8,128)(2,1)}), bf16[16,336,128]{2,1,0:T(8,128)(2,1)S(1)}, u32[]{:S(2)}, u32[]{:S(2)}) async-start(bf16[16,336,128]{2,1,0:T(8,128)(2,1)} %get-tuple-element.107), calls=%async_computation.2 | async-start | bytes 2752512 | tf_op jit(solution)/shard_map/all_to_all | solution.py:879
  109.8 3.3 %collective-permute-start.16 = (bf16[2,256,128]{2,1,0:T(8,128)(2,1)S(1)}, bf16[2,256,128]{2,1,0:T(8,128)(2,1)S(1)}, u32[]{:S(2)}, u32[]{:S(2)}) collective-permute-start(bf16[2,256,128]{2,1,0:T(8,128)(2,1)S(1)} %get-tuple-element.110), channel_id=1, source_target_pairs={{0,1},{1,2},{2,3},{3,4},{4,5},{5,6},{6,7},{7,8},{8,9},{9,10},{10,1... | collective-permute-start | bytes 393224 | tf_op jit(solution)/shard_map/ppermute | solution.py:891
  113.1 1.3 collective-permute-start.17
  114.4 6.7 %near_field.6.refs_0_.near_ref = f32[8,256,128]{2,1,0:T(8,128)} custom-call(s32[8,8]{1,0:T(8,128)S(1)} %copy-done, s32[8,8]{1,0:T(8,128)S(1)} %copy-done.1, bf16[8,8,256,256]{3,2,1,0:T(8,128)(2,1)} %blocks_ref.15, bf16[8,256,128]{2,1,0:T(8,128)(2,1)} %get-tuple-element.108.own_ref), custom_call_target="tpu_custom_call" | custom-call | flops 1073741824 | bytes 8388608 | tf_op jit(solution)/shard_map/near_field/pallas_call | solution.py:116
  121.2 10.0 %all-to-all-done.2.recv = bf16[16,336,128]{2,1,0:T(8,128)(2,1)S(1)} async-done(((bf16[16,336,128]{2,1,0:T(8,128)(2,1)}), bf16[16,336,128]{2,1,0:T(8,128)(2,1)S(1)}, u32[]{:S(2)}, u32[]{:S(2)}) %all-to-all-start.2) | async-done | bytes 1376288 | tf_op jit(solution)/shard_map/all_to_all | solution.py:879
  132.1 1.5 collective-permute-start.13
  134.3 3.1 %far_field.6.refs_4_.refs_5_ = f32[512,128]{1,0:T(8,128)S(1)} custom-call(bf16[16,336,128]{2,1,0:T(8,128)(2,1)S(1)} %all-to-all-done.2.recv, bf16[16,512,256]{2,1,0:T(8,128)(2,1)} %get-tuple-element.77.refs_0_.packed_ref, bf16[80,128]{1,0:T(8,128)(2,1)S(1)} %gather_sum.7._.refs_0_), custom_call_target="tpu_custom_call" | custom-call | flops 536870912 | bytes 4194304 | tf_op jit(solution)/shard_map/far_field/pallas_call | solution.py:116
  137.5 2.8 %collective-permute-start.15 = (bf16[4,80,128]{2,1,0:T(8,128)(2,1)S(1)}, bf16[4,80,128]{2,1,0:T(8,128)(2,1)S(1)}, u32[]{:S(2)}, u32[]{:S(2)}) collective-permute-start(bf16[4,80,128]{2,1,0:T(8,128)(2,1)S(1)} %stack.7.refs_8_.refs_2_), channel_id=1, source_target_pairs={{0,16},{16,0},{32,48},{48,32},{64,80},{80,64},{96,112},{112,96},{1... | collective-permute-start | bytes 245768 | tf_op jit(solution)/shard_map/ppermute | solution.py:381
  140.3 6.4 %halo_part.6 = (f32[8,256,128]{2,1,0:T(8,128)S(1)}, bf16[8,64,256]{2,1,0:T(8,128)(2,1)S(1)}, bf16[8,256,64]{2,1,0:T(8,128)(2,1)S(1)}, bf16[8,64,64]{2,1,0:T(8,12...) custom-call(s32[1]{0:T(128)} %get-tuple-element.79.count_ref, ...), custom_call_target="tpu_custom_call" | custom-call | flops 268435456 | bytes 6291456 | tf_op jit(solution)/shard_map/halo_part/pallas_call | solution.py:116
  146.7 4.9 %stage3.1 = (f32[8,256,128]{2,1,0:T(8,128)}, f32[64,128]{1,0:T(8,128)S(1)}, bf16[16,336,128]{2,1,0:T(8,128)(2,1)}, bf16[8,256,128]{2,1,0:T(8,128)(2,1)}, bf16[2,...) custom-call(s32[4,16]{1,0:T(4,128)S(1)} %bitcast.9, s32[1]{0:T(128)} %bitcast.2.refs_1_.branch, ...), custom_call_target="tpu_custom_call" | custom-call | flops 134217728 | bytes 7340032 | tf_op jit(solution)/shard_map/stage3/pallas_call | solution.py:116
  151.6 5.7 %all-to-all-start.3 = ((bf16[16,336,128]{2,1,0:T(8,128)(2,1)}), bf16[16,336,128]{2,1,0:T(8,128)(2,1)S(1)}, u32[]{:S(2)}, u32[]{:S(2)}) async-start(bf16[16,336,128]{2,1,0:T(8,128)(2,1)} %get-tuple-element.122), calls=%async_computation.3 | async-start | bytes 2752512 | tf_op jit(solution)/shard_map/all_to_all | solution.py:879
  157.3 3.3 %collective-permute-start.22 = (bf16[2,256,128]{2,1,0:T(8,128)(2,1)S(1)}, bf16[2,256,128]{2,1,0:T(8,128)(2,1)S(1)}, u32[]{:S(2)}, u32[]{:S(2)}) collective-permute-start(bf16[2,256,128]{2,1,0:T(8,128)(2,1)S(1)} %get-tuple-element.125), channel_id=1, source_target_pairs={{0,1},{1,2},{2,3},{3,4},{4,5},{5,6},{6,7},{7,8},{8,9},{9,10},{10,1... | collective-permute-start | bytes 393224 | tf_op jit(solution)/shard_map/ppermute | solution.py:891
  160.6 1.3 collective-permute-start.23
  161.9 6.8 %near_field.7.refs_0_.near_ref = f32[8,256,128]{2,1,0:T(8,128)} custom-call(s32[8,8]{1,0:T(8,128)S(1)} %copy-done, s32[8,8]{1,0:T(8,128)S(1)} %copy-done.1, bf16[8,8,256,256]{3,2,1,0:T(8,128)(2,1)} %blocks_ref.15, bf16[8,256,128]{2,1,0:T(8,128)(2,1)} %get-tuple-element.123.own_ref), custom_call_target="tpu_custom_call" | custom-call | flops 1073741824 | bytes 8388608 | tf_op jit(solution)/shard_map/near_field/pallas_call | solution.py:116
  168.6 10.0 %all-to-all-done.3.recv = bf16[16,336,128]{2,1,0:T(8,128)(2,1)S(1)} async-done(((bf16[16,336,128]{2,1,0:T(8,128)(2,1)}), bf16[16,336,128]{2,1,0:T(8,128)(2,1)S(1)}, u32[]{:S(2)}, u32[]{:S(2)}) %all-to-all-start.3) | async-done | bytes 1376288 | tf_op jit(solution)/shard_map/all_to_all | solution.py:879
  178.8 1.4 collective-permute-start.19
  180.9 3.1 %far_field.7.refs_4_.refs_5_ = f32[512,128]{1,0:T(8,128)S(1)} custom-call(bf16[16,336,128]{2,1,0:T(8,128)(2,1)S(1)} %all-to-all-done.3.recv, bf16[16,512,256]{2,1,0:T(8,128)(2,1)} %get-tuple-element.77.refs_0_.packed_ref, bf16[80,128]{1,0:T(8,128)(2,1)S(1)} %gather_sum.8._.refs_0_), custom_call_target="tpu_custom_call" | custom-call | flops 536870912 | bytes 4194304 | tf_op jit(solution)/shard_map/far_field/pallas_call | solution.py:116
  184.1 2.8 %collective-permute-start.21 = (bf16[4,80,128]{2,1,0:T(8,128)(2,1)S(1)}, bf16[4,80,128]{2,1,0:T(8,128)(2,1)S(1)}, u32[]{:S(2)}, u32[]{:S(2)}) collective-permute-start(bf16[4,80,128]{2,1,0:T(8,128)(2,1)S(1)} %stack.8.refs_9_.refs_2_), channel_id=1, source_target_pairs={{0,16},{16,0},{32,48},{48,32},{64,80},{80,64},{96,112},{112,96},{1... | collective-permute-start | bytes 245768 | tf_op jit(solution)/shard_map/ppermute | solution.py:381
  186.9 6.5 %halo_part.7 = (f32[8,256,128]{2,1,0:T(8,128)S(1)}, bf16[8,64,256]{2,1,0:T(8,128)(2,1)S(1)}, bf16[8,256,64]{2,1,0:T(8,128)(2,1)S(1)}, bf16[8,64,64]{2,1,0:T(8,12...) custom-call(s32[1]{0:T(128)} %get-tuple-element.79.count_ref, ...), custom_call_target="tpu_custom_call" | custom-call | flops 268435456 | bytes 6291456 | tf_op jit(solution)/shard_map/halo_part/pallas_call | solution.py:116
  193.4 3.6 %stage4.1 = (f32[8,256,128]{2,1,0:T(8,128)}, f32[64,128]{1,0:T(8,128)S(1)}, bf16[16,16,128]{2,1,0:T(8,128)(2,1)}) custom-call(s32[4,16]{1,0:T(4,128)S(1)} %bitcast.10, s32[1]{0:T(128)} %bitcast.2.refs_1_.branch, bf16[4,80,128]{2,1,0:T(8,128)(2,1)S(1)} %stack.8.refs_9_.refs_2_, bf16[4,80,128]{2,1,0:T(8,128)(2,1)S(1)} %collective-permute-done.21.refs_3_, ...), custom_call_target="tpu_custom_call" | custom-call | flops 134217728 | bytes 8388608 | tf_op jit(solution)/shard_map/stage4/pallas_call | solution.py:116
  197.0 5.6 %all-to-all-start.4 = ((bf16[16,16,128]{2,1,0:T(8,128)(2,1)}), bf16[16,16,128]{2,1,0:T(8,128)(2,1)S(1)}, u32[]{:S(2)}, u32[]{:S(2)}) async-start(bf16[16,16,128]{2,1,0:T(8,128)(2,1)} %get-tuple-element.139), calls=%async_computation.4 | async-start | bytes 131072 | tf_op jit(solution)/shard_map/all_to_all | solution.py:879
  202.6 4.1 %basis_vectors.1.refs_0_.refs_9_ = f32[5,8,256,128]{3,2,1,0:T(8,128)} custom-call(f32[64,128]{1,0:T(8,128)S(1)} %get-tuple-element.138.refs_0_, f32[8,256,128]{2,1,0:T(8,128)} %bitcast.16, f32[8,256,128]{2,1,0:T(8,128)} %get-tuple-element.98.refs_6_.refs_2_.refs_1_, f32[8,256,128]{2,1,0:T(8,128)} %get-tuple-element.112.refs_7_.refs_3_.refs_2_, ...), custom_call_target="tpu_custom_call" | custom-call | flops 8388608 | bytes 8388608 | tf_op jit(solution)/shard_map/basis_vectors/pallas_call | solution.py:116
  206.7 2.5 %all-to-all-done.4.recv = bf16[16,16,128]{2,1,0:T(8,128)(2,1)S(1)} async-done(((bf16[16,16,128]{2,1,0:T(8,128)(2,1)}), bf16[16,16,128]{2,1,0:T(8,128)(2,1)S(1)}, u32[]{:S(2)}, u32[]{:S(2)}) %all-to-all-start.4) | async-done | bytes 65568 | tf_op jit(solution)/shard_map/all_to_all | solution.py:879
  209.7 1.6 collective-permute-start.25
  212.1 2.5 %load.1 = (f32[8,256,128]{2,1,0:T(8,128)S(1)}, f32[8,256,128]{2,1,0:T(8,128)S(1)}, f32[8,256,128]{2,1,0:T(8,128)S(1)}, f32[8,256,128]{2,1,0:T(8,128)S(1)}, f32[8,256,128]{2,1,0:T(8,128)S(1)}) custom-call(f32[8,256,128]{2,1,0:T(8,128)} %bitcast.17, f32[8,256,128]{2,1,0:T(8,128)} %get-tuple-element.98.refs_6_.refs_2_.refs_1_, ...), custom_call_target="tpu_custom_call" | custom-call | bytes 5242880 | tf_op jit(solution)/shard_map/load/pallas_call | solution.py:116
  215.0 2.8 %collective-permute-start.27 = (bf16[4,16,128]{2,1,0:T(8,128)(2,1)S(1)}, bf16[4,16,128]{2,1,0:T(8,128)(2,1)S(1)}, u32[]{:S(2)}, u32[]{:S(2)}) collective-permute-start(bf16[4,16,128]{2,1,0:T(8,128)(2,1)S(1)} %stack.9.refs_2_), channel_id=1, source_target_pairs={{0,16},{16,0},{32,48},{48,32},{64,80},{80,64},{96,112},{112,96},{1... | collective-permute-start | bytes 49160 | tf_op jit(solution)/shard_map/ppermute | solution.py:381
  217.9 0.8 collective-permute-done.27.refs_3_
  218.7 1.8 last_vector.1
  (61 shorter events, 8.3 us)
Async XLA Ops:
  0.6 0.7 copy-start.2
  5.6 13.4 %copy-start = (s32[8,8]{1,0:T(8,128)S(1)}, s32[8,8]{1,0:T(8,128)}, u32[]{:S(2)}) copy-start(s32[8,8]{1,0:T(8,128)} %index_ref.17) | copy-start | bytes 772
  5.6 13.4 %copy-start.1 = (s32[8,8]{1,0:T(8,128)S(1)}, s32[8,8]{1,0:T(8,128)}, u32[]{:S(2)}) copy-start(s32[8,8]{1,0:T(8,128)} %mask_ref.9) | copy-start | bytes 772
  5.6 13.4 %copy-start.4 = (s32[8,48]{1,0:T(8,128)S(1)}, s32[8,48]{1,0:T(8,128)}, u32[]{:S(2)}) copy-start(s32[8,48]{1,0:T(8,128)} %mask_ref.5) | copy-start | bytes 4612
  5.6 13.4 %copy-start.5 = (s32[8,48]{1,0:T(8,128)S(1)}, s32[8,48]{1,0:T(8,128)}, u32[]{:S(2)}) copy-start(s32[8,48]{1,0:T(8,128)} %slot_ref.1) | copy-start | bytes 4612
  5.6 28.7 %all-to-all-start = ((bf16[16,336,128]{2,1,0:T(8,128)(2,1)}), bf16[16,336,128]{2,1,0:T(8,128)(2,1)S(1)}, u32[]{:S(2)}, u32[]{:S(2)}) async-start(bf16[16,336,128]{2,1,0:T(8,128)(2,1)} %get-tuple-element.75), calls=%async_computation | async-start | bytes 2752512 | tf_op jit(solution)/shard_map/all_to_all | solution.py:879
  14.4 31.2 %collective-permute-start.4 = (bf16[2,256,128]{2,1,0:T(8,128)(2,1)S(1)}, bf16[2,256,128]{2,1,0:T(8,128)(2,1)S(1)}, u32[]{:S(2)}, u32[]{:S(2)}) collective-permute-start(bf16[2,256,128]{2,1,0:T(8,128)(2,1)S(1)} %get-tuple-element.81), channel_id=1, source_target_pairs={{0,1},{1,2},{2,3},{3,4},{4,5},{5,6},{6,7},{7,8},{8,9},{9,10},{10,1... | collective-permute-start | bytes 393224 | tf_op jit(solution)/shard_map/ppermute | solution.py:891
  17.6 27.9 %collective-permute-start.5 = (bf16[2,256,128]{2,1,0:T(8,128)(2,1)S(1)}, bf16[2,256,128]{2,1,0:T(8,128)(2,1)S(1)}, u32[]{:S(2)}, u32[]{:S(2)}) collective-permute-start(bf16[2,256,128]{2,1,0:T(8,128)(2,1)S(1)} %get-tuple-element.82), channel_id=1, source_target_pairs={{1,0},{2,1},{3,2},{4,3},{5,4},{6,5},{7,6},{8,7},{9,8},{10,9},{11,1... | collective-permute-start | bytes 393224 | tf_op jit(solution)/shard_map/ppermute | solution.py:892
  34.4 6.8 %collective-permute-start.2 = (bf16[80,128]{1,0:T(8,128)(2,1)S(1)}, bf16[80,128]{1,0:T(8,128)(2,1)S(1)}, u32[]{:S(2)}, u32[]{:S(2)}) collective-permute-start(bf16[80,128]{1,0:T(8,128)(2,1)S(1)} %gather_sum.5._.refs_0_), channel_id=1, source_target_pairs={{0,96},{16,112},{32,0},{48,16},{64,32},{80,48},{96,64},{112,80},{1... | collective-permute-start | bytes 61448 | tf_op jit(solution)/shard_map/ppermute | solution.py:370
  37.0 4.3 %collective-permute-start.1 = (bf16[80,128]{1,0:T(8,128)(2,1)S(1)}, bf16[80,128]{1,0:T(8,128)(2,1)S(1)}, u32[]{:S(2)}, u32[]{:S(2)}) collective-permute-start(bf16[80,128]{1,0:T(8,128)(2,1)S(1)} %gather_sum.5._.refs_0_), channel_id=1, source_target_pairs={{0,64},{16,80},{32,96},{48,112},{64,0},{80,16},{96,32},{112,48},{1... | collective-permute-start | bytes 61448 | tf_op jit(solution)/shard_map/ppermute | solution.py:370
  37.5 3.8 %collective-permute-start = (bf16[80,128]{1,0:T(8,128)(2,1)S(1)}, bf16[80,128]{1,0:T(8,128)(2,1)S(1)}, u32[]{:S(2)}, u32[]{:S(2)}) collective-permute-start(bf16[80,128]{1,0:T(8,128)(2,1)S(1)} %gather_sum.5._.refs_0_), channel_id=1, source_target_pairs={{0,32},{16,48},{32,64},{48,80},{64,96},{80,112},{96,0},{112,16},{1... | collective-permute-start | bytes 61448 | tf_op jit(solution)/shard_map/ppermute | solution.py:370
  41.3 10.1 %collective-permute-start.3 = (bf16[4,80,128]{2,1,0:T(8,128)(2,1)S(1)}, bf16[4,80,128]{2,1,0:T(8,128)(2,1)S(1)}, u32[]{:S(2)}, u32[]{:S(2)}) collective-permute-start(bf16[4,80,128]{2,1,0:T(8,128)(2,1)S(1)} %stack.5.refs_6_.refs_2_), channel_id=1, source_target_pairs={{0,16},{16,0},{32,48},{48,32},{64,80},{80,64},{96,112},{112,96},{1... | collective-permute-start | bytes 245768 | tf_op jit(solution)/shard_map/ppermute | solution.py:381
  45.6 5.8 %copy-start.3 = (s32[1,16,4]{1,2,0:T(4,128)S(1)}, s32[1,16,4]{1,2,0:T(4,128)}, u32[]{:S(2)}) copy-start(s32[1,16,4]{1,2,0:T(4,128)} %param.19) | copy-start | bytes 772
  56.1 29.2 %all-to-all-start.1 = ((bf16[16,336,128]{2,1,0:T(8,128)(2,1)}), bf16[16,336,128]{2,1,0:T(8,128)(2,1)S(1)}, u32[]{:S(2)}, u32[]{:S(2)}) async-start(bf16[16,336,128]{2,1,0:T(8,128)(2,1)} %get-tuple-element.93), calls=%async_computation.1 | async-start | bytes 2752512 | tf_op jit(solution)/shard_map/all_to_all | solution.py:879
  63.9 29.9 %collective-permute-start.10 = (bf16[2,256,128]{2,1,0:T(8,128)(2,1)S(1)}, bf16[2,256,128]{2,1,0:T(8,128)(2,1)S(1)}, u32[]{:S(2)}, u32[]{:S(2)}) collective-permute-start(bf16[2,256,128]{2,1,0:T(8,128)(2,1)S(1)} %get-tuple-element.96), channel_id=1, source_target_pairs={{0,1},{1,2},{2,3},{3,4},{4,5},{5,6},{6,7},{7,8},{8,9},{9,10},{10,1... | collective-permute-start | bytes 393224 | tf_op jit(solution)/shard_map/ppermute | solution.py:891
  67.2 26.7 %collective-permute-start.11 = (bf16[2,256,128]{2,1,0:T(8,128)(2,1)S(1)}, bf16[2,256,128]{2,1,0:T(8,128)(2,1)S(1)}, u32[]{:S(2)}, u32[]{:S(2)}) collective-permute-start(bf16[2,256,128]{2,1,0:T(8,128)(2,1)S(1)} %get-tuple-element.97), channel_id=1, source_target_pairs={{1,0},{2,1},{3,2},{4,3},{5,4},{6,5},{7,6},{8,7},{9,8},{10,9},{11,1... | collective-permute-start | bytes 393224 | tf_op jit(solution)/shard_map/ppermute | solution.py:892
  85.3 5.0 %collective-permute-start.8 = (bf16[80,128]{1,0:T(8,128)(2,1)S(1)}, bf16[80,128]{1,0:T(8,128)(2,1)S(1)}, u32[]{:S(2)}, u32[]{:S(2)}) collective-permute-start(bf16[80,128]{1,0:T(8,128)(2,1)S(1)} %gather_sum.6._.refs_0_), channel_id=1, source_target_pairs={{0,96},{16,112},{32,0},{48,16},{64,32},{80,48},{96,64},{112,80},{1... | collective-permute-start | bytes 61448 | tf_op jit(solution)/shard_map/ppermute | solution.py:370
  85.8 4.5 %collective-permute-start.7 = (bf16[80,128]{1,0:T(8,128)(2,1)S(1)}, bf16[80,128]{1,0:T(8,128)(2,1)S(1)}, u32[]{:S(2)}, u32[]{:S(2)}) collective-permute-start(bf16[80,128]{1,0:T(8,128)(2,1)S(1)} %gather_sum.6._.refs_0_), channel_id=1, source_target_pairs={{0,64},{16,80},{32,96},{48,112},{64,0},{80,16},{96,32},{112,48},{1... | collective-permute-start | bytes 61448 | tf_op jit(solution)/shard_map/ppermute | solution.py:370
  86.4 4.0 %collective-permute-start.6 = (bf16[80,128]{1,0:T(8,128)(2,1)S(1)}, bf16[80,128]{1,0:T(8,128)(2,1)S(1)}, u32[]{:S(2)}, u32[]{:S(2)}) collective-permute-start(bf16[80,128]{1,0:T(8,128)(2,1)S(1)} %gather_sum.6._.refs_0_), channel_id=1, source_target_pairs={{0,32},{16,48},{32,64},{48,80},{64,96},{80,112},{96,0},{112,16},{1... | collective-permute-start | bytes 61448 | tf_op jit(solution)/shard_map/ppermute | solution.py:370
  90.4 9.3 %collective-permute-start.9 = (bf16[4,80,128]{2,1,0:T(8,128)(2,1)S(1)}, bf16[4,80,128]{2,1,0:T(8,128)(2,1)S(1)}, u32[]{:S(2)}, u32[]{:S(2)}) collective-permute-start(bf16[4,80,128]{2,1,0:T(8,128)(2,1)S(1)} %stack.6.refs_7_.refs_2_), channel_id=1, source_target_pairs={{0,16},{16,0},{32,48},{48,32},{64,80},{80,64},{96,112},{112,96},{1... | collective-permute-start | bytes 245768 | tf_op jit(solution)/shard_map/ppermute | solution.py:381
  104.5 26.7 %all-to-all-start.2 = ((bf16[16,336,128]{2,1,0:T(8,128)(2,1)}), bf16[16,336,128]{2,1,0:T(8,128)(2,1)S(1)}, u32[]{:S(2)}, u32[]{:S(2)}) async-start(bf16[16,336,128]{2,1,0:T(8,128)(2,1)} %get-tuple-element.107), calls=%async_computation.2 | async-start | bytes 2752512 | tf_op jit(solution)/shard_map/all_to_all | solution.py:879
  109.8 30.4 %collective-permute-start.16 = (bf16[2,256,128]{2,1,0:T(8,128)(2,1)S(1)}, bf16[2,256,128]{2,1,0:T(8,128)(2,1)S(1)}, u32[]{:S(2)}, u32[]{:S(2)}) collective-permute-start(bf16[2,256,128]{2,1,0:T(8,128)(2,1)S(1)} %get-tuple-element.110), channel_id=1, source_target_pairs={{0,1},{1,2},{2,3},{3,4},{4,5},{5,6},{6,7},{7,8},{8,9},{9,10},{10,1... | collective-permute-start | bytes 393224 | tf_op jit(solution)/shard_map/ppermute | solution.py:891
  113.1 27.1 %collective-permute-start.17 = (bf16[2,256,128]{2,1,0:T(8,128)(2,1)S(1)}, bf16[2,256,128]{2,1,0:T(8,128)(2,1)S(1)}, u32[]{:S(2)}, u32[]{:S(2)}) collective-permute-start(bf16[2,256,128]{2,1,0:T(8,128)(2,1)S(1)} %get-tuple-element.111), channel_id=1, source_target_pairs={{1,0},{2,1},{3,2},{4,3},{5,4},{6,5},{7,6},{8,7},{9,8},{10,9},{11,1... | collective-permute-start | bytes 393224 | tf_op jit(solution)/shard_map/ppermute | solution.py:892
  131.3 6.2 %collective-permute-start.14 = (bf16[80,128]{1,0:T(8,128)(2,1)S(1)}, bf16[80,128]{1,0:T(8,128)(2,1)S(1)}, u32[]{:S(2)}, u32[]{:S(2)}) collective-permute-start(bf16[80,128]{1,0:T(8,128)(2,1)S(1)} %gather_sum.7._.refs_0_), channel_id=1, source_target_pairs={{0,96},{16,112},{32,0},{48,16},{64,32},{80,48},{96,64},{112,80},{1... | collective-permute-start | bytes 61448 | tf_op jit(solution)/shard_map/ppermute | solution.py:370
  132.1 5.3 %collective-permute-start.13 = (bf16[80,128]{1,0:T(8,128)(2,1)S(1)}, bf16[80,128]{1,0:T(8,128)(2,1)S(1)}, u32[]{:S(2)}, u32[]{:S(2)}) collective-permute-start(bf16[80,128]{1,0:T(8,128)(2,1)S(1)} %gather_sum.7._.refs_0_), channel_id=1, source_target_pairs={{0,64},{16,80},{32,96},{48,112},{64,0},{80,16},{96,32},{112,48},{1... | collective-permute-start | bytes 61448 | tf_op jit(solution)/shard_map/ppermute | solution.py:370
  133.6 3.9 %collective-permute-start.12 = (bf16[80,128]{1,0:T(8,128)(2,1)S(1)}, bf16[80,128]{1,0:T(8,128)(2,1)S(1)}, u32[]{:S(2)}, u32[]{:S(2)}) collective-permute-start(bf16[80,128]{1,0:T(8,128)(2,1)S(1)} %gather_sum.7._.refs_0_), channel_id=1, source_target_pairs={{0,32},{16,48},{32,64},{48,80},{64,96},{80,112},{96,0},{112,16},{1... | collective-permute-start | bytes 61448 | tf_op jit(solution)/shard_map/ppermute | solution.py:370
  137.5 9.2 %collective-permute-start.15 = (bf16[4,80,128]{2,1,0:T(8,128)(2,1)S(1)}, bf16[4,80,128]{2,1,0:T(8,128)(2,1)S(1)}, u32[]{:S(2)}, u32[]{:S(2)}) collective-permute-start(bf16[4,80,128]{2,1,0:T(8,128)(2,1)S(1)} %stack.7.refs_8_.refs_2_), channel_id=1, source_target_pairs={{0,16},{16,0},{32,48},{48,32},{64,80},{80,64},{96,112},{112,96},{1... | collective-permute-start | bytes 245768 | tf_op jit(solution)/shard_map/ppermute | solution.py:381
  151.6 27.0 %all-to-all-start.3 = ((bf16[16,336,128]{2,1,0:T(8,128)(2,1)}), bf16[16,336,128]{2,1,0:T(8,128)(2,1)S(1)}, u32[]{:S(2)}, u32[]{:S(2)}) async-start(bf16[16,336,128]{2,1,0:T(8,128)(2,1)} %get-tuple-element.122), calls=%async_computation.3 | async-start | bytes 2752512 | tf_op jit(solution)/shard_map/all_to_all | solution.py:879
  157.3 29.6 %collective-permute-start.22 = (bf16[2,256,128]{2,1,0:T(8,128)(2,1)S(1)}, bf16[2,256,128]{2,1,0:T(8,128)(2,1)S(1)}, u32[]{:S(2)}, u32[]{:S(2)}) collective-permute-start(bf16[2,256,128]{2,1,0:T(8,128)(2,1)S(1)} %get-tuple-element.125), channel_id=1, source_target_pairs={{0,1},{1,2},{2,3},{3,4},{4,5},{5,6},{6,7},{7,8},{8,9},{9,10},{10,1... | collective-permute-start | bytes 393224 | tf_op jit(solution)/shard_map/ppermute | solution.py:891
  160.6 26.3 %collective-permute-start.23 = (bf16[2,256,128]{2,1,0:T(8,128)(2,1)S(1)}, bf16[2,256,128]{2,1,0:T(8,128)(2,1)S(1)}, u32[]{:S(2)}, u32[]{:S(2)}) collective-permute-start(bf16[2,256,128]{2,1,0:T(8,128)(2,1)S(1)} %get-tuple-element.126), channel_id=1, source_target_pairs={{1,0},{2,1},{3,2},{4,3},{5,4},{6,5},{7,6},{8,7},{9,8},{10,9},{11,1... | collective-permute-start | bytes 393224 | tf_op jit(solution)/shard_map/ppermute | solution.py:892
  178.7 5.3 %collective-permute-start.20 = (bf16[80,128]{1,0:T(8,128)(2,1)S(1)}, bf16[80,128]{1,0:T(8,128)(2,1)S(1)}, u32[]{:S(2)}, u32[]{:S(2)}) collective-permute-start(bf16[80,128]{1,0:T(8,128)(2,1)S(1)} %gather_sum.8._.refs_0_), channel_id=1, source_target_pairs={{0,96},{16,112},{32,0},{48,16},{64,32},{80,48},{96,64},{112,80},{1... | collective-permute-start | bytes 61448 | tf_op jit(solution)/shard_map/ppermute | solution.py:370
  178.8 5.3 %collective-permute-start.19 = (bf16[80,128]{1,0:T(8,128)(2,1)S(1)}, bf16[80,128]{1,0:T(8,128)(2,1)S(1)}, u32[]{:S(2)}, u32[]{:S(2)}) collective-permute-start(bf16[80,128]{1,0:T(8,128)(2,1)S(1)} %gather_sum.8._.refs_0_), channel_id=1, source_target_pairs={{0,64},{16,80},{32,96},{48,112},{64,0},{80,16},{96,32},{112,48},{1... | collective-permute-start | bytes 61448 | tf_op jit(solution)/shard_map/ppermute | solution.py:370
  180.2 3.9 %collective-permute-start.18 = (bf16[80,128]{1,0:T(8,128)(2,1)S(1)}, bf16[80,128]{1,0:T(8,128)(2,1)S(1)}, u32[]{:S(2)}, u32[]{:S(2)}) collective-permute-start(bf16[80,128]{1,0:T(8,128)(2,1)S(1)} %gather_sum.8._.refs_0_), channel_id=1, source_target_pairs={{0,32},{16,48},{32,64},{48,80},{64,96},{80,112},{96,0},{112,16},{1... | collective-permute-start | bytes 61448 | tf_op jit(solution)/shard_map/ppermute | solution.py:370
  184.1 9.3 %collective-permute-start.21 = (bf16[4,80,128]{2,1,0:T(8,128)(2,1)S(1)}, bf16[4,80,128]{2,1,0:T(8,128)(2,1)S(1)}, u32[]{:S(2)}, u32[]{:S(2)}) collective-permute-start(bf16[4,80,128]{2,1,0:T(8,128)(2,1)S(1)} %stack.8.refs_9_.refs_2_), channel_id=1, source_target_pairs={{0,16},{16,0},{32,48},{48,32},{64,80},{80,64},{96,112},{112,96},{1... | collective-permute-start | bytes 245768 | tf_op jit(solution)/shard_map/ppermute | solution.py:381
  197.0 12.3 %all-to-all-start.4 = ((bf16[16,16,128]{2,1,0:T(8,128)(2,1)}), bf16[16,16,128]{2,1,0:T(8,128)(2,1)S(1)}, u32[]{:S(2)}, u32[]{:S(2)}) async-start(bf16[16,16,128]{2,1,0:T(8,128)(2,1)} %get-tuple-element.139), calls=%async_computation.4 | async-start | bytes 131072 | tf_op jit(solution)/shard_map/all_to_all | solution.py:879
  209.3 5.4 %collective-permute-start.26 = (bf16[16,128]{1,0:T(8,128)(2,1)S(1)}, bf16[16,128]{1,0:T(8,128)(2,1)S(1)}, u32[]{:S(2)}, u32[]{:S(2)}) collective-permute-start(bf16[16,128]{1,0:T(8,128)(2,1)S(1)} %gather_sum.9.refs_5_.refs_0_), channel_id=1, source_target_pairs={{0,96},{16,112},{32,0},{48,16},{64,32},{80,48},{96,64},{112,80},{1... | collective-permute-start | bytes 12296 | tf_op jit(solution)/shard_map/ppermute | solution.py:370
  209.7 5.0 %collective-permute-start.25 = (bf16[16,128]{1,0:T(8,128)(2,1)S(1)}, bf16[16,128]{1,0:T(8,128)(2,1)S(1)}, u32[]{:S(2)}, u32[]{:S(2)}) collective-permute-start(bf16[16,128]{1,0:T(8,128)(2,1)S(1)} %gather_sum.9.refs_5_.refs_0_), channel_id=1, source_target_pairs={{0,64},{16,80},{32,96},{48,112},{64,0},{80,16},{96,32},{112,48},{1... | collective-permute-start | bytes 12296 | tf_op jit(solution)/shard_map/ppermute | solution.py:370
  211.4 3.7 %collective-permute-start.24 = (bf16[16,128]{1,0:T(8,128)(2,1)S(1)}, bf16[16,128]{1,0:T(8,128)(2,1)S(1)}, u32[]{:S(2)}, u32[]{:S(2)}) collective-permute-start(bf16[16,128]{1,0:T(8,128)(2,1)S(1)} %gather_sum.9.refs_5_.refs_0_), channel_id=1, source_target_pairs={{0,32},{16,48},{32,64},{48,80},{64,96},{80,112},{96,0},{112,16},{1... | collective-permute-start | bytes 12296 | tf_op jit(solution)/shard_map/ppermute | solution.py:370
  215.0 3.7 %collective-permute-start.27 = (bf16[4,16,128]{2,1,0:T(8,128)(2,1)S(1)}, bf16[4,16,128]{2,1,0:T(8,128)(2,1)S(1)}, u32[]{:S(2)}, u32[]{:S(2)}) collective-permute-start(bf16[4,16,128]{2,1,0:T(8,128)(2,1)S(1)} %stack.9.refs_2_), channel_id=1, source_target_pairs={{0,16},{16,0},{32,48},{48,32},{64,80},{80,64},{96,112},{112,96},{1... | collective-permute-start | bytes 49160 | tf_op jit(solution)/shard_map/ppermute | solution.py:381

commit v4 on v3

--- a/solution.py
+++ b/solution.py
@@ -390,13 +390,32 @@
         ups[lax.rem(mate + count - 2 * j, count)] = other[j]
 
 
-def far_kernel(recv, packed_ref, _, far, packed, arrived):
-    sources, _, width = packed.shape
-    share = sources // CHUNKS
+def far_kernel(count_ref, list_ref, recv, packed_ref, blocks_ref, *refs):
+    held = (len(refs) - 7) // 2
+    sources, (_, far, blocks), targets = refs[:held], refs[held : held + 3], refs[held + 3 : -4]
+    packed, arrived, fetched, loaded = refs[-4:]
+    share = packed.shape[0] // CHUNKS
+    width = packed.shape[2]
+    entries = blocks_ref.shape[1]
+    count = count_ref[0]
 
     def fetch(i):
         some = slab(i, share)
         return [pltpu.make_async_copy(packed_ref.at[some], packed.at[some], arrived.at[i])]
+
+    def block(i):
+        entry = list_ref[i]
+        return pltpu.make_async_copy(
+            blocks_ref.at[entry // entries, entry % entries], blocks.at[i], fetched.at[i]
+        )
+
+    def ask(i, carry):
+        block(i).start()
+        return carry
+
+    def have(i, carry):
+        block(i).wait()
+        return carry
 
     def work(i):
         term = None
@@ -413,71 +432,52 @@
         def _():
             far[...] += term
 
+    loads = [
+        pltpu.make_async_copy(source, target, loaded.at[i])
+        for i, (source, target) in enumerate(zip(sources, targets))
+    ]
     begin, run = windowed(CHUNKS, CHUNKS, fetch, work)
     begin()
+    lax.fori_loop(0, count, ask, 0)
+    for copy in loads:
+        copy.start()
     run()
-
-
-def far_field(recv, packed, earlier):
+    lax.fori_loop(0, count, have, 0)
+    for copy in loads:
+        copy.wait()
+
+
+def far_field(listed, recv, packed, near_blocks, held, earlier):
     sources, rows, _ = packed.shape
-    return call(
+    leaves, entries, size, _ = near_blocks.shape
+    outs = [((rows, recv.shape[2]), F32, VMEM), ((leaves * entries, size, size), BF16, VMEM)]
+    far, blocks, *held = call(
         far_kernel,
-        (recv, packed, earlier),
-        (VMEM, HBM, AFTER_VMEM),
-        [((rows, recv.shape[2]), F32, VMEM)],
-        [pltpu.VMEM(packed.shape, BF16), semaphores(CHUNKS)],
+        (*listed, recv, packed, near_blocks, *held, earlier),
+        (SMEM, SMEM, VMEM, HBM, HBM) + (HBM,) * len(held) + (AFTER_VMEM,),
+        outs + [(a.shape, a.dtype, VMEM) for a in held],
+        [
+            pltpu.VMEM(packed.shape, BF16),
+            semaphores(CHUNKS),
+            semaphores(leaves * entries),
+            semaphores(len(held)),
+        ],
         "far_field",
         2 * packed.size * recv.shape[2],
         2 * packed.size,
-    )[0]
-
-
-def halo_kernel(count_ref, list_ref, index_ref, blocks_ref, before, after, near_ref, *refs):
-    refs = list(refs)
-    take = lambda count: [refs.pop(0) for _ in range(count)]
-    held = (len(refs) - 8) // 2
-    sources = take(held)
-    take(1)
-    near, *targets = take(1 + held)
-    blocks, halo, came, fetched, near_came, loaded = take(6)
-    leaves = near.shape[0]
-    reach = before.shape[0]
-    entries = blocks_ref.shape[1]
-    sides = [
-        pltpu.make_async_copy(before, halo.at[pl.ds(0, reach)], came.at[0]),
-        pltpu.make_async_copy(after, halo.at[pl.ds(reach, reach)], came.at[1]),
-    ]
-    get = [
-        pltpu.make_async_copy(near_ref.at[leaf], near.at[leaf], near_came.at[leaf])
-        for leaf in range(leaves)
-    ]
-    load = [
-        pltpu.make_async_copy(source, target, loaded.at[i])
-        for i, (source, target) in enumerate(zip(sources, targets))
-    ]
-
-    def block(i):
-        entry = list_ref[i]
-        return pltpu.make_async_copy(
-            blocks_ref.at[entry // entries, entry % entries], blocks.at[i], fetched.at[i]
-        )
-
-    def ask(i, carry):
-        block(i).start()
-        return carry
-
+    )
+    return far, blocks, held
+
+
+def halo_kernel(count_ref, list_ref, index_ref, blocks, before, after, near_in, _, near, halo):
+    leaves, reach, entries = near.shape[0], before.shape[0], index_ref.shape[1]
+    halo[:reach] = before[...]
+    halo[reach:] = after[...]
     count = count_ref[0]
-    at_once = 4
+    at_once = 8
 
     def add(group, carry):
         terms = []
-        for j in range(at_once):
-            i = group * at_once + j
-
-            @pl.when(i < count)
-            def _():
-                block(i).wait()
-
         for j in range(at_once):
             i = jnp.minimum(group * at_once + j, count - 1)
             weight = (group * at_once + j < count).astype(F32).astype(BF16)
@@ -490,38 +490,58 @@
             near[leaf] += term
         return carry
 
-    for side in sides:
-        side.start()
-    lax.fori_loop(0, count, ask, 0)
-    for copy in get + load:
-        copy.start()
-    for copy in sides + get:
-        copy.wait()
     lax.fori_loop(0, (count + at_once - 1) // at_once, add, 0)
-    for copy in load:
-        copy.wait()
-
-
-def halo_part(listed, near_index, near_blocks, before, after, near, held, earlier):
-    leaves, entries, size, _ = near_blocks.shape
-    halo = (2 * before.shape[0],) + before.shape[1:]
+
+
+def halo_part(listed, near_index, blocks, before, after, near, earlier):
     return call(
         halo_kernel,
-        (*listed, near_index, near_blocks, before, after, near, *held, earlier),
-        (SMEM, SMEM, SMEM, HBM, LOOSE, LOOSE) + (HBM,) * (1 + len(held)) + (AFTER_VMEM,),
-        [(a.shape, a.dtype, VMEM) for a in (near, *held)],
-        [
-            pltpu.VMEM((leaves * entries, size, size), BF16),
-            pltpu.VMEM(halo, BF16),
-            semaphores(2),
-            semaphores(leaves * entries),
-            semaphores(leaves),
-            semaphores(len(held)),
-        ],
+        (*listed, near_index, blocks, before, after, near, earlier),
+        (SMEM, SMEM, SMEM, VMEM, VMEM, VMEM, VMEM, AFTER_VMEM),
+        [(near.shape, F32, VMEM)],
+        [pltpu.VMEM((2 * before.shape[0],) + before.shape[1:], BF16)],
         "halo_part",
         1 << 28,
-        6 << 20,
-    )
+        2 << 20,
+        {6: 0},
+    )[0]
+
+
+def sum_kernel(place, *refs):
+    *parts, _, out, rows, split = refs
+    count = len(parts)
+    for j, part in enumerate(parts):
+        rows[lax.rem(place[0] + count - j, count)] = part[...].astype(F32)
+    total = rows[0]
+    for i in range(1, count):
+        total = total + rows[i]
+    store_split(split, jnp.concatenate(joined(total), axis=0), 5)
+    out[...] = split[...].astype(BF16)
+
+
+def sum_over(dots, axis, stride, count, earlier, after):
+    if count == 1:
+        return dots
+    place = lax.rem(lax.axis_index(axis).astype(jnp.int32) // stride, count).reshape(1)
+    size = lax.axis_size(axis)
+
+    def moved(i, j):
+        at = i // stride % count
+        return i + ((at + j) % count - at) * stride
+
+    parts = [dots]
+    for j in range(1, count):
+        parts.append(lax.ppermute(dots, axis, [(i, moved(i, j)) for i in range(size)]))
+    return call(
+        sum_kernel,
+        (place, *parts, earlier),
+        (SMEM,) + (VMEM,) * count + (after,),
+        [(dots.shape, BF16, VMEM)],
+        [pltpu.VMEM((count,) + dots.shape, F32), pltpu.VMEM((DOT_ROWS, dots.shape[1]), F32)],
+        "sum_over",
+        0,
+        1 << 18,
+    )[0]
 
 
 def load_kernel(*refs):
@@ -658,17 +678,15 @@
     products = jnp.concatenate(products + [jnp.zeros_like(products[0])] * (7 - k), axis=0)
     store_split(split, products, k + 1)
     dots = split[...].astype(BF16)
-    inner = send.shape[0]
     if sends:
-        slots = send_slot.shape[0]
+        slots, inner = send_slot.shape
         for r in range(inner):
             for s in range(slots):
                 send[r, s * rank : (s + 1) * rank] = skeletons[slab(send_slot[s, r], rank)]
             send[r, slots * rank : (slots + 1) * rank] = lifted
             send[r, (slots + 1) * rank :] = dots
     else:
-        for r in range(inner):
-            send[r] = dots
+        send[...] = dots
     for i in range(CHUNKS):
         for copy in stores(i):
             copy.wait()
@@ -698,8 +716,8 @@
         specs += [VMEM] * len(later)
         get("z", tall, F32, HBM)
     get("state", (STATE_ROWS, columns), F32, VMEM)
-    rows = ((slots + 1) * rank if sends else 0) + DOT_ROWS
-    get("send", (inner, rows, columns), BF16, VMEM)
+    rows = (slots + 1) * rank + DOT_ROWS
+    get("send", (inner, rows, columns) if sends else (DOT_ROWS, columns), BF16, VMEM)
     if sends:
         get("coarse", tall, BF16, HBM)
         get("low", (HW, size, columns), BF16, LOOSE)
@@ -745,33 +763,33 @@
     return dict(zip(names, results))
 
 
-def vectors_kernel(*refs, known, points):
+def vectors_kernel(*refs, wanted, held, final, points):
     refs = list(refs)
     take = lambda count: [refs.pop(0) for _ in range(count)]
     (state,) = take(1)
-    if not known:
+    if final:
         branch, column, other = take(3)
-    zs = take(known if known else STEPS + 1)
-    if known:
-        (krylov,) = take(1)
+    zs = take(wanted[-1] + 1)
+    _, krylov = take(2)
+    if final:
+        (hess_out,) = take(1)
+    result, left = take(2)
+    if final:
+        after, ups = take(2)
     else:
-        _, krylov, hess_out = take(3)
-    if known:
-        vectors, result, arrived, left = take(4)
         after = state
-    else:
-        result, left, after, ups = take(4)
-        vectors = zs
+    if not held:
+        vectors, arrived = take(2)
     parts = left.shape[1]
     group = zs[0].shape[0] // parts
-    size = zs[0].shape[1]
-    wanted = range(known) if known else [STEPS]
 
     def fetch(i):
+        if held:
+            return []
         some = slab(i, group)
         return [
             pltpu.make_async_copy(z.at[some], vectors.at[l, some], arrived.at[l, i])
-            for l, z in enumerate(zs if known else [])
+            for l, z in enumerate(zs)
         ]
 
     def store(n, i):
@@ -785,7 +803,7 @@
                 vector = None
                 for l in range(which + 1):
                     row = basis_row(which, l)
-                    values = vectors[l, leaf] if known else vectors[l][leaf]
+                    values = zs[l][leaf] if held else vectors[l, leaf]
                     term = after[row : row + 1, :] * values
                     vector = term if vector is None else vector + term
                 result[n, leaf] = vector
@@ -794,13 +812,13 @@
 
     begin, run = windowed(parts, parts, fetch, work)
     begin()
-    if not known:
+    if final:
         in_order(branch, column, other, ups)
         grams = [row / points for row in from_branches(ups, 0)]
         after[...] = state[...]
         coefficients(STEPS, grams, state, after)
     run()
-    if not known:
+    if final:
         for i in range(STEPS + 1):
             for j in range(STEPS):
                 row = i * STEPS + j
@@ -813,43 +831,42 @@
             store(n, i).wait()
 
 
-def basis_vectors(state, zs, parts):
-    known = len(zs)
+def vectors(state, zs, wanted, before, parts, products=None, points=0):
+    final = products is not None
+    held = wanted[0] > 0
     tall = zs[0].shape
+    count = wanted[-1] + 1
+    shape = (STEPS + 1,) + tall
+    scratch = [pltpu.VMEM((len(wanted),) + tall, F32), semaphores(len(wanted), parts)]
+    outs = [(shape, F32, HBM)]
+    args, specs = [state], [VMEM]
+    if final:
+        args += products
+        specs += [SMEM, VMEM, VMEM]
+        column = products[1].shape
+        outs.append(((STEPS + 1, STEPS, tall[2]), F32, FREE))
+        scratch += [
+            pltpu.VMEM(state.shape, F32),
+            pltpu.VMEM((2 * column[0],) + column[1:], BF16),
+        ]
+    args += zs[:count]
+    specs += [VMEM if held else HBM] * count
+    args.append(before)
+    specs.append(HBM if held else AFTER)
+    if not held:
+        scratch += [pltpu.VMEM((count,) + tall, F32), semaphores(count, parts)]
     return call(
-        functools.partial(vectors_kernel, known=known, points=0),
-        [state] + zs,
-        [VMEM] + [HBM] * known,
-        [((STEPS + 1,) + tall, F32, HBM)],
-        [
-            pltpu.VMEM((known,) + tall, F32),
-            pltpu.VMEM((known,) + tall, F32),
-            semaphores(known, parts),
-            semaphores(known, parts),
-        ],
-        "basis_vectors",
+        functools.partial(
+            vectors_kernel, wanted=wanted, held=held, final=final, points=points
+        ),
+        args,
+        specs,
+        outs,
+        scratch,
+        "last_vector" if final else "vectors",
         1 << 23,
-        8 << 20,
-    )[0]
-
-
-def last(points, branch, column, other, state, krylov, zs, parts):
-    tall = zs[0].shape
-    return call(
-        functools.partial(vectors_kernel, known=0, points=points),
-        [state, branch, column, other] + list(zs) + [krylov],
-        [VMEM, SMEM, VMEM, VMEM] + [VMEM] * len(zs) + [HBM],
-        [(krylov.shape, F32, HBM), ((STEPS + 1, STEPS, tall[2]), F32, FREE)],
-        [
-            pltpu.VMEM((1,) + tall, F32),
-            semaphores(1, parts),
-            pltpu.VMEM(state.shape, F32),
-            pltpu.VMEM((2 * column.shape[0],) + column.shape[1:], BF16),
-        ],
-        "last_vector",
-        1 << 22,
-        6 << 20,
-        {4 + len(zs): 0},
+        len(wanted) << 21,
+        {len(args) - 1: 0} if held else {},
     )
 
 
@@ -892,26 +909,30 @@
         after = lax.ppermute(out["low"], "inner", down_pairs)
         earlier = (packed,) if k == 1 else ()
         near = near_field(near_index, near_mask, near_blocks, out["coarse"], *earlier)
-        summed = gather_sum(recv, slots * rank, near)
-        local_far = far_field(recv, packed, summed)
+        done = near
+        if k == STEPS:
+            krylov = done = vectors(state, zs, list(range(STEPS - 1)), near, CHUNKS)[0]
+        summed = gather_sum(recv, slots * rank, done)
+        held = (near, basis, turned, transfer, lifting, top, *zs)
+        local_far, blocks, held = far_field(listed, recv, packed, near_blocks, held, summed)
+        near, *held = held
 
         def between(column):
-            held = (basis, turned, transfer, lifting, top, *zs)
-            return halo_part(
-                listed, near_index, near_blocks, before, after, near, held, column
-            )
-
-        column, other, (near, *held) = over_branches(summed, outer, local_far, between)
+            return halo_part(listed, near_index, blocks, before, after, near, column)
+
+        column, other, near = over_branches(summed, outer, local_far, between)
         later = [column, other, state, local_far, near, *held]
         out = stage(k, points, wanted, branch, zs[0], basis, transfer, later)
         state = out["state"]
         zs = zs + [out["z"]]
-    krylov = basis_vectors(state, zs[:STEPS], CHUNKS)
-    recv = exchange(out["send"], "inner")
-    summed = gather_sum(recv, 0, krylov)
-    loaded = load(zs, summed)
-    column, other, loaded = over_branches(summed, outer, loaded[0], lambda column: loaded)
-    krylov, hessenberg = last(points, branch, column, other, state, krylov, loaded, CHUNKS)
+    low = 4 if inner % 4 == 0 else inner
+    loaded = load(zs, out["send"])
+    summed = sum_over(out["send"], "inner", 1, low, loaded[0], AFTER_VMEM)
+    krylov = vectors(state, loaded, [STEPS - 1], krylov, CHUNKS)[0]
+    summed = sum_over(summed, "inner", low, inner // low, krylov, AFTER)
+    column, other, _ = over_branches(summed, outer, loaded[0], lambda column: None)
+    products = [branch, column, other]
+    krylov, hessenberg = vectors(state, loaded, [STEPS], krylov, CHUNKS, products, points)
     return krylov.reshape(STEPS + 1, *rhs.shape), hessenberg
 
 

time: 221 us -> 219 us (level)
  local copies, waits for them, and re-layouts: 0.71 us -> 6.68 us
  waiting for transfers between devices: 34.1 us -> 28.8 us
  Pallas kernels: 103 us -> 99.8 us
    all_to_all x5 -> x4, starting transfers between devices: 33.2 us -> 25.7 us  [exchange(): return lax.all_to_all(array, axis, split_axis=0, concat_axis=0, tiled=True)]
    ppermute x0 -> x6, starting transfers between devices: none -> 6.81 us  [sum_over(): lax.ppermute(dots, axis, [(i, moved(i, j)) for i in range(size)])]
    all_to_all x5 -> x4, waiting for transfers between devices: 32.6 us -> 26.6 us  [exchange(): return lax.all_to_all(array, axis, split_axis=0, concat_axis=0, tiled=True)]
    unnamed x12 -> x26, local copies, waits for them, and re-layouts: 0.71 us -> 6.68 us
    ppermute x15, starting transfers between devices: 13.6 us -> 19.6 us  [over_branches(): lax.ppermute(summed, 'outer', shift)]
    ppermute x5, starting transfers between devices: 16.1 us -> 11.1 us  [over_branches(): other = lax.ppermute(column, 'outer', [(o, o ^ 1) for o in range(outer)])]
    pallas_call x31 -> x33, Pallas kernels: 103 us -> 99.8 us  [call(): pl.pallas_call(kernel, in_specs=list(in_specs), out_specs=[spec for _, _,...]
  transfers between devices with their start and end apart: 33 -> 38, of which waited for: 8 -> 6; matrix products, arithmetic and copies ran while one was open for 0% -> 0% of each run, Pallas kernels for 36% -> 35%
where the time goes in v4:
time: 219 us; the launch traced here: 218 us
  Pallas kernels  99.8 us (46%)
  starting transfers between devices  81.5 us (37%)
  waiting for transfers between devices  28.8 us (13%)
  local copies, waits for them, and re-layouts  6.68 us (3%)
    pallas_call x33, Pallas kernels, call(): pl.pallas_call(kernel, in_specs=list(in_specs), out_specs=[spec for _, _,...  99.8 us
    all_to_all x4, waiting for transfers between devices, exchange(): return lax.all_to_all(array, axis, split_axis=0, concat_axis=0, tiled=True)  26.6 us
    all_to_all x4, starting transfers between devices, exchange(): return lax.all_to_all(array, axis, split_axis=0, concat_axis=0, tiled=True)  25.7 us
    ppermute x15, starting transfers between devices, over_branches(): lax.ppermute(summed, 'outer', shift)  19.6 us
    ppermute x4, starting transfers between devices, shards(): before = lax.ppermute(out['high'], 'inner', up_pairs)  13.1 us
    ppermute x5, starting transfers between devices, over_branches(): other = lax.ppermute(column, 'outer', [(o, o ^ 1) for o in range(outer)])  11.1 us
    ppermute x6, starting transfers between devices, sum_over(): lax.ppermute(dots, axis, [(i, moved(i, j)) for i in range(size)])  6.81 us
    unnamed x26, local copies, waits for them, and re-layouts  6.68 us
  transfers between devices with their start and end apart: 38, of which 6 were waited for; matrix products, arithmetic and copies ran while one was open for 0% of the time, Pallas kernels for 35%

profile of v4, /device:TPU:1, one launch (start us, length us, event | category | flops | bytes accessed | tf_op | source)
XLA Modules:
  0.0 218.0 jit_solution(13155760479329221648)
XLA Ops:
  1.3 4.2 %stage0.1 = (f32[64,128]{1,0:T(8,128)S(1)}, bf16[16,336,128]{2,1,0:T(8,128)(2,1)}, bf16[8,256,128]{2,1,0:T(8,128)(2,1)}, bf16[2,256,128]{2,1,0:T(8,128)(2,1)S(1)}, bf16[2,256,128]{2,1,0:T(8,128)(2,1)S(1)}) custom-call(s32[4,16]{1,0:T(4,128)S(1)} %bitcast.8, s32[1]{0:T(128)} %bitcast.2.refs_1_.branch, f32[8,256,128]{2,1,0:T(8,128)} %bitcast.14, ...), custom_call_target="tpu_custom_call" | custom-call | flops 134217728 | bytes 4194304 | tf_op jit(solution)/shard_map/stage0/pallas_call | solution.py:116
  5.5 8.6 %all-to-all-start = ((bf16[16,336,128]{2,1,0:T(8,128)(2,1)}), bf16[16,336,128]{2,1,0:T(8,128)(2,1)S(1)}, u32[]{:S(2)}, u32[]{:S(2)}) async-start(bf16[16,336,128]{2,1,0:T(8,128)(2,1)} %get-tuple-element.83), calls=%async_computation | async-start | bytes 2752512 | tf_op jit(solution)/shard_map/all_to_all | solution.py:896
  14.2 3.3 %collective-permute-start.4 = (bf16[2,256,128]{2,1,0:T(8,128)(2,1)S(1)}, bf16[2,256,128]{2,1,0:T(8,128)(2,1)S(1)}, u32[]{:S(2)}, u32[]{:S(2)}) collective-permute-start(bf16[2,256,128]{2,1,0:T(8,128)(2,1)S(1)} %get-tuple-element.94), channel_id=1, source_target_pairs={{0,1},{1,2},{2,3},{3,4},{4,5},{5,6},{6,7},{7,8},{8,9},{9,10},{10,1... | collective-permute-start | bytes 393224 | tf_op jit(solution)/shard_map/ppermute | solution.py:908
  17.4 1.3 collective-permute-start.5
  21.5 8.6 %pack.1 = (bf16[16,512,256]{2,1,0:T(8,128)(2,1)}, s32[1]{0:T(128)}, s32[64]{0:T(128)S(1)}, bf16[8,256,64]{2,1,0:T(8,128)(2,1)}, bf16[64,512]{1,0:T(8,128)(2,1)}, /*index=5*/bf16[64,512]{1,0:T(8,128)(2,1)}) custom-call(s32[1]{0:T(128)} %bitcast.2.refs_1_.branch, s32[8,48]{1,0:T(8,128)S(1)} %copy-done.11, s32[8,48]{1,0:T(8,128)S(1)} %copy-done.12, ...), custom_call_target="tpu_custom_call" | custom-call | bytes 10485760 | tf_op jit(solution)/shard_map/pack/pallas_call | solution.py:116
  30.1 6.8 %near_field.4.refs_0_ = f32[8,256,128]{2,1,0:T(8,128)} custom-call(s32[8,8]{1,0:T(8,128)S(1)} %copy-done.5, s32[8,8]{1,0:T(8,128)S(1)} %copy-done.7, bf16[8,8,256,256]{3,2,1,0:T(8,128)(2,1)} %blocks_ref.15, bf16[8,256,128]{2,1,0:T(8,128)(2,1)} %get-tuple-element.84.own_ref, bf16[16,512,256]{2,1,0:T(8,128)(2,1)} %get-tuple-element.85.refs_0_.packed_ref), custom_call_target="tpu_custom_call" | custom-call | flops 1073741824 | bytes 8388608 | tf_op jit(solution)/shard_map/near_field/pallas_call | solution.py:116
  38.2 2.4 %collective-permute-start.1 = (bf16[80,128]{1,0:T(8,128)(2,1)S(1)}, bf16[80,128]{1,0:T(8,128)(2,1)S(1)}, u32[]{:S(2)}, u32[]{:S(2)}) collective-permute-start(bf16[80,128]{1,0:T(8,128)(2,1)S(1)} %gather_sum.4.refs_7_.refs_0_), channel_id=1, source_target_pairs={{0,64},{16,80},{32,96},{48,112},{64,0},{80,16},{96,32},{112,48},{1... | collective-permute-start | bytes 61448 | tf_op jit(solution)/shard_map/ppermute | solution.py:370
  41.8 5.7 %far_field.4 = (f32[512,128]{1,0:T(8,128)S(1)}, bf16[64,256,256]{2,1,0:T(8,128)(2,1)S(1)}, f32[8,256,128]{2,1,0:T(8,128)S(1)}, bf16[8,64,256]{2,1,0:T(8,128)(2,1...) custom-call(s32[1]{0:T(128)} %get-tuple-element.86.count_ref, ...), custom_call_target="tpu_custom_call" | custom-call | flops 536870912 | bytes 4194304 | tf_op jit(solution)/shard_map/far_field/pallas_call | solution.py:116
  47.6 2.2 %collective-permute-start.3 = (bf16[4,80,128]{2,1,0:T(8,128)(2,1)S(1)}, bf16[4,80,128]{2,1,0:T(8,128)(2,1)S(1)}, u32[]{:S(2)}, u32[]{:S(2)}) collective-permute-start(bf16[4,80,128]{2,1,0:T(8,128)(2,1)S(1)} %stack.5._.refs_2_), channel_id=1, source_target_pairs={{0,16},{16,0},{32,48},{48,32},{64,80},{80,64},{96,112},{112,96},{1... | collective-permute-start | bytes 245768 | tf_op jit(solution)/shard_map/ppermute | solution.py:381
  49.8 2.2 %halo_part.4.refs_6_ = f32[8,256,128]{2,1,0:T(8,128)S(1)} custom-call(s32[1]{0:T(128)} %get-tuple-element.86.count_ref, s32[64]{0:T(128)S(1)} %get-tuple-element.87.list_ref, s32[8,8]{1,0:T(8,128)S(1)} %copy-done.6, bf16[64,256,256]{2,1,0:T(8,128)(2,1)S(1)} %get-tuple-element.93.blocks, ...), custom_call_target="tpu_custom_call", output_to_operand_aliasing={{}: (6, {})} | custom-call | flops 268435456 | bytes 2097152 | tf_op jit(solution)/shard_map/halo_part/pallas_call | solution.py:116
  52.1 4.6 %stage1.1 = (f32[8,256,128]{2,1,0:T(8,128)}, f32[64,128]{1,0:T(8,128)S(1)}, bf16[16,336,128]{2,1,0:T(8,128)(2,1)}, bf16[8,256,128]{2,1,0:T(8,128)(2,1)}, bf16[2,...) custom-call(s32[4,16]{1,0:T(4,128)S(1)} %bitcast.9, s32[1]{0:T(128)} %bitcast.2.refs_1_.branch, ...), custom_call_target="tpu_custom_call" | custom-call | flops 134217728 | bytes 5242880 | tf_op jit(solution)/shard_map/stage1/pallas_call | solution.py:116
  56.7 8.1 %all-to-all-start.1 = ((bf16[16,336,128]{2,1,0:T(8,128)(2,1)}), bf16[16,336,128]{2,1,0:T(8,128)(2,1)S(1)}, u32[]{:S(2)}, u32[]{:S(2)}) async-start(bf16[16,336,128]{2,1,0:T(8,128)(2,1)} %get-tuple-element.103), calls=%async_computation.1 | async-start | bytes 2752512 | tf_op jit(solution)/shard_map/all_to_all | solution.py:896
  64.8 3.3 %collective-permute-start.10 = (bf16[2,256,128]{2,1,0:T(8,128)(2,1)S(1)}, bf16[2,256,128]{2,1,0:T(8,128)(2,1)S(1)}, u32[]{:S(2)}, u32[]{:S(2)}) collective-permute-start(bf16[2,256,128]{2,1,0:T(8,128)(2,1)S(1)} %get-tuple-element.109), channel_id=1, source_target_pairs={{0,1},{1,2},{2,3},{3,4},{4,5},{5,6},{6,7},{7,8},{8,9},{9,10},{10,1... | collective-permute-start | bytes 393224 | tf_op jit(solution)/shard_map/ppermute | solution.py:908
  69.4 6.8 %near_field.5.refs_0_ = f32[8,256,128]{2,1,0:T(8,128)} custom-call(s32[8,8]{1,0:T(8,128)S(1)} %copy-done.6, s32[8,8]{1,0:T(8,128)S(1)} %copy-done.8, bf16[8,8,256,256]{3,2,1,0:T(8,128)(2,1)} %blocks_ref.15, bf16[8,256,128]{2,1,0:T(8,128)(2,1)} %get-tuple-element.104.own_ref), custom_call_target="tpu_custom_call" | custom-call | flops 1073741824 | bytes 8388608 | tf_op jit(solution)/shard_map/near_field/pallas_call | solution.py:116
  76.2 10.0 %all-to-all-done.1.recv = bf16[16,336,128]{2,1,0:T(8,128)(2,1)S(1)} async-done(((bf16[16,336,128]{2,1,0:T(8,128)(2,1)}), bf16[16,336,128]{2,1,0:T(8,128)(2,1)S(1)}, u32[]{:S(2)}, u32[]{:S(2)}) %all-to-all-start.1) | async-done | bytes 1376288 | tf_op jit(solution)/shard_map/all_to_all | solution.py:896
  87.3 1.7 collective-permute-start.8
  89.0 5.9 %far_field.5 = (f32[512,128]{1,0:T(8,128)S(1)}, bf16[64,256,256]{2,1,0:T(8,128)(2,1)S(1)}, f32[8,256,128]{2,1,0:T(8,128)S(1)}, bf16[8,64,256]{2,1,0:T(8,128)(2,1...) custom-call(s32[1]{0:T(128)} %get-tuple-element.86.count_ref, ...), custom_call_target="tpu_custom_call" | custom-call | flops 536870912 | bytes 4194304 | tf_op jit(solution)/shard_map/far_field/pallas_call | solution.py:116
  95.0 1.9 collective-permute-start.9
  96.9 2.2 halo_part.5.refs_6_
  99.1 4.8 %stage2.1 = (f32[8,256,128]{2,1,0:T(8,128)}, f32[64,128]{1,0:T(8,128)S(1)}, bf16[16,336,128]{2,1,0:T(8,128)(2,1)}, bf16[8,256,128]{2,1,0:T(8,128)(2,1)}, bf16[2,...) custom-call(s32[4,16]{1,0:T(4,128)S(1)} %bitcast.10, s32[1]{0:T(128)} %bitcast.2.refs_1_.branch, ...), custom_call_target="tpu_custom_call" | custom-call | flops 134217728 | bytes 6291456 | tf_op jit(solution)/shard_map/stage2/pallas_call | solution.py:116
  103.9 4.5 %all-to-all-start.2 = ((bf16[16,336,128]{2,1,0:T(8,128)(2,1)}), bf16[16,336,128]{2,1,0:T(8,128)(2,1)S(1)}, u32[]{:S(2)}, u32[]{:S(2)}) async-start(bf16[16,336,128]{2,1,0:T(8,128)(2,1)} %get-tuple-element.119), calls=%async_computation.2 | async-start | bytes 2752512 | tf_op jit(solution)/shard_map/all_to_all | solution.py:896
  108.4 3.3 %collective-permute-start.16 = (bf16[2,256,128]{2,1,0:T(8,128)(2,1)S(1)}, bf16[2,256,128]{2,1,0:T(8,128)(2,1)S(1)}, u32[]{:S(2)}, u32[]{:S(2)}) collective-permute-start(bf16[2,256,128]{2,1,0:T(8,128)(2,1)S(1)} %get-tuple-element.125), channel_id=1, source_target_pairs={{0,1},{1,2},{2,3},{3,4},{4,5},{5,6},{6,7},{7,8},{8,9},{9,10},{10,1... | collective-permute-start | bytes 393224 | tf_op jit(solution)/shard_map/ppermute | solution.py:908
  113.0 6.8 %near_field.6.refs_0_ = f32[8,256,128]{2,1,0:T(8,128)} custom-call(s32[8,8]{1,0:T(8,128)S(1)} %copy-done.6, s32[8,8]{1,0:T(8,128)S(1)} %copy-done.8, bf16[8,8,256,256]{3,2,1,0:T(8,128)(2,1)} %blocks_ref.15, bf16[8,256,128]{2,1,0:T(8,128)(2,1)} %get-tuple-element.120.own_ref), custom_call_target="tpu_custom_call" | custom-call | flops 1073741824 | bytes 8388608 | tf_op jit(solution)/shard_map/near_field/pallas_call | solution.py:116
  119.8 10.0 %all-to-all-done.2.recv = bf16[16,336,128]{2,1,0:T(8,128)(2,1)S(1)} async-done(((bf16[16,336,128]{2,1,0:T(8,128)(2,1)}), bf16[16,336,128]{2,1,0:T(8,128)(2,1)S(1)}, u32[]{:S(2)}, u32[]{:S(2)}) %all-to-all-start.2) | async-done | bytes 1376288 | tf_op jit(solution)/shard_map/all_to_all | solution.py:896
  131.1 1.7 collective-permute-start.13
  132.8 1.8 collective-permute-start.14
  134.5 6.3 %far_field.6 = (f32[512,128]{1,0:T(8,128)S(1)}, bf16[64,256,256]{2,1,0:T(8,128)(2,1)S(1)}, f32[8,256,128]{2,1,0:T(8,128)S(1)}, bf16[8,64,256]{2,1,0:T(8,128)(2,1...) custom-call(s32[1]{0:T(128)} %get-tuple-element.86.count_ref, ...), custom_call_target="tpu_custom_call" | custom-call | flops 536870912 | bytes 4194304 | tf_op jit(solution)/shard_map/far_field/pallas_call | solution.py:116
  140.8 2.2 %collective-permute-start.15 = (bf16[4,80,128]{2,1,0:T(8,128)(2,1)S(1)}, bf16[4,80,128]{2,1,0:T(8,128)(2,1)S(1)}, u32[]{:S(2)}, u32[]{:S(2)}) collective-permute-start(bf16[4,80,128]{2,1,0:T(8,128)(2,1)S(1)} %stack.7._.refs_2_), channel_id=1, source_target_pairs={{0,16},{16,0},{32,48},{48,32},{64,80},{80,64},{96,112},{112,96},{1... | collective-permute-start | bytes 245768 | tf_op jit(solution)/shard_map/ppermute | solution.py:381
  143.0 2.4 %halo_part.6.refs_6_ = f32[8,256,128]{2,1,0:T(8,128)S(1)} custom-call(s32[1]{0:T(128)} %get-tuple-element.86.count_ref, s32[64]{0:T(128)S(1)} %get-tuple-element.87.list_ref, s32[8,8]{1,0:T(8,128)S(1)} %copy-done.6, bf16[64,256,256]{2,1,0:T(8,128)(2,1)S(1)} %get-tuple-element.124.blocks, ...), custom_call_target="tpu_custom_call", output_to_operand_aliasing={{}: (6, {})} | custom-call | flops 268435456 | bytes 2097152 | tf_op jit(solution)/shard_map/halo_part/pallas_call | solution.py:116
  145.4 4.9 %stage3.1 = (f32[8,256,128]{2,1,0:T(8,128)}, f32[64,128]{1,0:T(8,128)S(1)}, bf16[16,336,128]{2,1,0:T(8,128)(2,1)}, bf16[8,256,128]{2,1,0:T(8,128)(2,1)}, bf16[2,...) custom-call(s32[4,16]{1,0:T(4,128)S(1)} %bitcast.11, s32[1]{0:T(128)} %bitcast.2.refs_1_.branch, ...), custom_call_target="tpu_custom_call" | custom-call | flops 134217728 | bytes 7340032 | tf_op jit(solution)/shard_map/stage3/pallas_call | solution.py:116
  150.3 4.5 %all-to-all-start.3 = ((bf16[16,336,128]{2,1,0:T(8,128)(2,1)}), bf16[16,336,128]{2,1,0:T(8,128)(2,1)S(1)}, u32[]{:S(2)}, u32[]{:S(2)}) async-start(bf16[16,336,128]{2,1,0:T(8,128)(2,1)} %get-tuple-element.136), calls=%async_computation.3 | async-start | bytes 2752512 | tf_op jit(solution)/shard_map/all_to_all | solution.py:896
  154.8 3.3 %collective-permute-start.22 = (bf16[2,256,128]{2,1,0:T(8,128)(2,1)S(1)}, bf16[2,256,128]{2,1,0:T(8,128)(2,1)S(1)}, u32[]{:S(2)}, u32[]{:S(2)}) collective-permute-start(bf16[2,256,128]{2,1,0:T(8,128)(2,1)S(1)} %get-tuple-element.142), channel_id=1, source_target_pairs={{0,1},{1,2},{2,3},{3,4},{4,5},{5,6},{6,7},{7,8},{8,9},{9,10},{10,1... | collective-permute-start | bytes 393224 | tf_op jit(solution)/shard_map/ppermute | solution.py:908
  159.4 6.8 %near_field.7.refs_4_.refs_0_ = f32[8,256,128]{2,1,0:T(8,128)} custom-call(s32[8,8]{1,0:T(8,128)S(1)} %copy-done.6, s32[8,8]{1,0:T(8,128)S(1)} %copy-done.8, bf16[8,8,256,256]{3,2,1,0:T(8,128)(2,1)} %blocks_ref.15, bf16[8,256,128]{2,1,0:T(8,128)(2,1)} %get-tuple-element.138.own_ref), custom_call_target="tpu_custom_call" | custom-call | flops 1073741824 | bytes 8388608 | tf_op jit(solution)/shard_map/near_field/pallas_call | solution.py:116
  166.2 3.5 %vectors.2.refs_0_.refs_5_ = f32[5,8,256,128]{3,2,1,0:T(8,128)} custom-call(f32[64,128]{1,0:T(8,128)S(1)} %get-tuple-element.137.refs_0_.refs_4_, f32[8,256,128]{2,1,0:T(8,128)} %bitcast.18, f32[8,256,128]{2,1,0:T(8,128)} %get-tuple-element.105.refs_7_.refs_2_.refs_1_, f32[8,256,128]{2,1,0:T(8,128)} %get-tuple-element.121.refs_8_.refs_3_.refs_2_, ...), custom_call_target="tpu_custom_call" | custom-call | flops 8388608 | bytes 6291456 | tf_op jit(solution)/shard_map/vectors/pallas_call | solution.py:116
  169.7 6.5 %all-to-all-done.3.recv = bf16[16,336,128]{2,1,0:T(8,128)(2,1)S(1)} async-done(((bf16[16,336,128]{2,1,0:T(8,128)(2,1)}), bf16[16,336,128]{2,1,0:T(8,128)(2,1)S(1)}, u32[]{:S(2)}, u32[]{:S(2)}) %all-to-all-start.3) | async-done | bytes 1376288 | tf_op jit(solution)/shard_map/all_to_all | solution.py:896
  176.7 1.4 collective-permute-start.19
  179.2 6.6 %far_field.7 = (f32[512,128]{1,0:T(8,128)S(1)}, bf16[64,256,256]{2,1,0:T(8,128)(2,1)S(1)}, f32[8,256,128]{2,1,0:T(8,128)S(1)}, bf16[8,64,256]{2,1,0:T(8,128)(2,1...) custom-call(s32[1]{0:T(128)} %get-tuple-element.86.count_ref, ...), custom_call_target="tpu_custom_call" | custom-call | flops 536870912 | bytes 4194304 | tf_op jit(solution)/shard_map/far_field/pallas_call | solution.py:116
  185.8 1.9 collective-permute-start.21
  187.8 2.2 halo_part.7.refs_6_
  190.0 3.0 %stage4.1 = (f32[8,256,128]{2,1,0:T(8,128)}, f32[64,128]{1,0:T(8,128)S(1)}, bf16[16,128]{1,0:T(8,128)(2,1)S(1)}) custom-call(s32[4,16]{1,0:T(4,128)S(1)} %bitcast.12, s32[1]{0:T(128)} %bitcast.2.refs_1_.branch, bf16[4,80,128]{2,1,0:T(8,128)(2,1)S(1)} %stack.8._.refs_2_, bf16[4,80,128]{2,1,0:T(8,128)(2,1)S(1)} %collective-permute-done.21.refs_3_, ...), custom_call_target="tpu_custom_call" | custom-call | flops 134217728 | bytes 8388608 | tf_op jit(solution)/shard_map/stage4/pallas_call | solution.py:116
  194.9 1.3 collective-permute-start.26
  196.2 2.5 %load.1 = (f32[8,256,128]{2,1,0:T(8,128)S(1)}, f32[8,256,128]{2,1,0:T(8,128)S(1)}, f32[8,256,128]{2,1,0:T(8,128)S(1)}, f32[8,256,128]{2,1,0:T(8,128)S(1)}, f32[8,256,128]{2,1,0:T(8,128)S(1)}) custom-call(f32[8,256,128]{2,1,0:T(8,128)} %bitcast.20, f32[8,256,128]{2,1,0:T(8,128)} %get-tuple-element.105.refs_7_.refs_2_.refs_1_, ...), custom_call_target="tpu_custom_call" | custom-call | bytes 5242880 | tf_op jit(solution)/shard_map/load/pallas_call | solution.py:116
  201.0 1.9 collective-permute-start.28
  202.9 1.4 collective-permute-start.29
  208.0 1.7 collective-permute-start.31
  209.7 1.5 collective-permute-start.32
  212.4 2.8 %collective-permute-start.33 = (bf16[4,16,128]{2,1,0:T(8,128)(2,1)S(1)}, bf16[4,16,128]{2,1,0:T(8,128)(2,1)S(1)}, u32[]{:S(2)}, u32[]{:S(2)}) collective-permute-start(bf16[4,16,128]{2,1,0:T(8,128)(2,1)S(1)} %stack.9.refs_2_), channel_id=1, source_target_pairs={{0,16},{16,0},{32,48},{48,32},{64,80},{80,64},{96,112},{112,96},{1... | collective-permute-start | bytes 49160 | tf_op jit(solution)/shard_map/ppermute | solution.py:381
  216.1 1.8 last_vector.1
  (87 shorter events, 23.8 us)
Async XLA Ops:
  5.5 31.4 %all-to-all-start = ((bf16[16,336,128]{2,1,0:T(8,128)(2,1)}), bf16[16,336,128]{2,1,0:T(8,128)(2,1)S(1)}, u32[]{:S(2)}, u32[]{:S(2)}) async-start(bf16[16,336,128]{2,1,0:T(8,128)(2,1)} %get-tuple-element.83), calls=%async_computation | async-start | bytes 2752512 | tf_op jit(solution)/shard_map/all_to_all | solution.py:896
  14.2 35.7 %collective-permute-start.4 = (bf16[2,256,128]{2,1,0:T(8,128)(2,1)S(1)}, bf16[2,256,128]{2,1,0:T(8,128)(2,1)S(1)}, u32[]{:S(2)}, u32[]{:S(2)}) collective-permute-start(bf16[2,256,128]{2,1,0:T(8,128)(2,1)S(1)} %get-tuple-element.94), channel_id=1, source_target_pairs={{0,1},{1,2},{2,3},{3,4},{4,5},{5,6},{6,7},{7,8},{8,9},{9,10},{10,1... | collective-permute-start | bytes 393224 | tf_op jit(solution)/shard_map/ppermute | solution.py:908
  17.4 32.4 %collective-permute-start.5 = (bf16[2,256,128]{2,1,0:T(8,128)(2,1)S(1)}, bf16[2,256,128]{2,1,0:T(8,128)(2,1)S(1)}, u32[]{:S(2)}, u32[]{:S(2)}) collective-permute-start(bf16[2,256,128]{2,1,0:T(8,128)(2,1)S(1)} %get-tuple-element.95), channel_id=1, source_target_pairs={{1,0},{2,1},{3,2},{4,3},{5,4},{6,5},{7,6},{8,7},{9,8},{10,9},{11,1... | collective-permute-start | bytes 393224 | tf_op jit(solution)/shard_map/ppermute | solution.py:909
  18.7 0.7 copy-start.5
  19.4 0.7 copy-start.7
  37.0 10.5 %collective-permute-start = (bf16[80,128]{1,0:T(8,128)(2,1)S(1)}, bf16[80,128]{1,0:T(8,128)(2,1)S(1)}, u32[]{:S(2)}, u32[]{:S(2)}) collective-permute-start(bf16[80,128]{1,0:T(8,128)(2,1)S(1)} %gather_sum.4.refs_7_.refs_0_), channel_id=1, source_target_pairs={{0,32},{16,48},{32,64},{48,80},{64,96},{80,112},{96,0},{112,16},{1... | collective-permute-start | bytes 61448 | tf_op jit(solution)/shard_map/ppermute | solution.py:370
  38.2 9.3 %collective-permute-start.1 = (bf16[80,128]{1,0:T(8,128)(2,1)S(1)}, bf16[80,128]{1,0:T(8,128)(2,1)S(1)}, u32[]{:S(2)}, u32[]{:S(2)}) collective-permute-start(bf16[80,128]{1,0:T(8,128)(2,1)S(1)} %gather_sum.4.refs_7_.refs_0_), channel_id=1, source_target_pairs={{0,64},{16,80},{32,96},{48,112},{64,0},{80,16},{96,32},{112,48},{1... | collective-permute-start | bytes 61448 | tf_op jit(solution)/shard_map/ppermute | solution.py:370
  40.7 6.8 %collective-permute-start.2 = (bf16[80,128]{1,0:T(8,128)(2,1)S(1)}, bf16[80,128]{1,0:T(8,128)(2,1)S(1)}, u32[]{:S(2)}, u32[]{:S(2)}) collective-permute-start(bf16[80,128]{1,0:T(8,128)(2,1)S(1)} %gather_sum.4.refs_7_.refs_0_), channel_id=1, source_target_pairs={{0,96},{16,112},{32,0},{48,16},{64,32},{80,48},{96,64},{112,80},{1... | collective-permute-start | bytes 61448 | tf_op jit(solution)/shard_map/ppermute | solution.py:370
  41.8 8.0 %copy-start.6 = (s32[8,8]{1,0:T(8,128)S(1)}, s32[8,8]{1,0:T(8,128)}, u32[]{:S(2)}) copy-start(s32[8,8]{1,0:T(8,128)} %index_ref.17) | copy-start | bytes 772
  47.6 4.5 %collective-permute-start.3 = (bf16[4,80,128]{2,1,0:T(8,128)(2,1)S(1)}, bf16[4,80,128]{2,1,0:T(8,128)(2,1)S(1)}, u32[]{:S(2)}, u32[]{:S(2)}) collective-permute-start(bf16[4,80,128]{2,1,0:T(8,128)(2,1)S(1)} %stack.5._.refs_2_), channel_id=1, source_target_pairs={{0,16},{16,0},{32,48},{48,32},{64,80},{80,64},{96,112},{112,96},{1... | collective-permute-start | bytes 245768 | tf_op jit(solution)/shard_map/ppermute | solution.py:381
  49.8 2.2 %copy-start.10 = (s32[1,16,4]{1,2,0:T(4,128)S(1)}, s32[1,16,4]{1,2,0:T(4,128)}, u32[]{:S(2)}) copy-start(s32[1,16,4]{1,2,0:T(4,128)} %param.19) | copy-start | bytes 772
  52.0 17.4 %copy-start.8 = (s32[8,8]{1,0:T(8,128)S(1)}, s32[8,8]{1,0:T(8,128)}, u32[]{:S(2)}) copy-start(s32[8,8]{1,0:T(8,128)} %mask_ref.9) | copy-start | bytes 772
  56.7 29.5 %all-to-all-start.1 = ((bf16[16,336,128]{2,1,0:T(8,128)(2,1)}), bf16[16,336,128]{2,1,0:T(8,128)(2,1)S(1)}, u32[]{:S(2)}, u32[]{:S(2)}) async-start(bf16[16,336,128]{2,1,0:T(8,128)(2,1)} %get-tuple-element.103), calls=%async_computation.1 | async-start | bytes 2752512 | tf_op jit(solution)/shard_map/all_to_all | solution.py:896
  64.8 32.1 %collective-permute-start.10 = (bf16[2,256,128]{2,1,0:T(8,128)(2,1)S(1)}, bf16[2,256,128]{2,1,0:T(8,128)(2,1)S(1)}, u32[]{:S(2)}, u32[]{:S(2)}) collective-permute-start(bf16[2,256,128]{2,1,0:T(8,128)(2,1)S(1)} %get-tuple-element.109), channel_id=1, source_target_pairs={{0,1},{1,2},{2,3},{3,4},{4,5},{5,6},{6,7},{7,8},{8,9},{9,10},{10,1... | collective-permute-start | bytes 393224 | tf_op jit(solution)/shard_map/ppermute | solution.py:908
  68.1 28.8 %collective-permute-start.11 = (bf16[2,256,128]{2,1,0:T(8,128)(2,1)S(1)}, bf16[2,256,128]{2,1,0:T(8,128)(2,1)S(1)}, u32[]{:S(2)}, u32[]{:S(2)}) collective-permute-start(bf16[2,256,128]{2,1,0:T(8,128)(2,1)S(1)} %get-tuple-element.110), channel_id=1, source_target_pairs={{1,0},{2,1},{3,2},{4,3},{5,4},{6,5},{7,6},{8,7},{9,8},{10,9},{11,1... | collective-permute-start | bytes 393224 | tf_op jit(solution)/shard_map/ppermute | solution.py:909
  86.3 8.7 %collective-permute-start.6 = (bf16[80,128]{1,0:T(8,128)(2,1)S(1)}, bf16[80,128]{1,0:T(8,128)(2,1)S(1)}, u32[]{:S(2)}, u32[]{:S(2)}) collective-permute-start(bf16[80,128]{1,0:T(8,128)(2,1)S(1)} %gather_sum.5.refs_8_.refs_0_), channel_id=1, source_target_pairs={{0,32},{16,48},{32,64},{48,80},{64,96},{80,112},{96,0},{112,16},{1... | collective-permute-start | bytes 61448 | tf_op jit(solution)/shard_map/ppermute | solution.py:370
  86.3 8.6 %collective-permute-start.7 = (bf16[80,128]{1,0:T(8,128)(2,1)S(1)}, bf16[80,128]{1,0:T(8,128)(2,1)S(1)}, u32[]{:S(2)}, u32[]{:S(2)}) collective-permute-start(bf16[80,128]{1,0:T(8,128)(2,1)S(1)} %gather_sum.5.refs_8_.refs_0_), channel_id=1, source_target_pairs={{0,64},{16,80},{32,96},{48,112},{64,0},{80,16},{96,32},{112,48},{1... | collective-permute-start | bytes 61448 | tf_op jit(solution)/shard_map/ppermute | solution.py:370
  87.3 7.7 %collective-permute-start.8 = (bf16[80,128]{1,0:T(8,128)(2,1)S(1)}, bf16[80,128]{1,0:T(8,128)(2,1)S(1)}, u32[]{:S(2)}, u32[]{:S(2)}) collective-permute-start(bf16[80,128]{1,0:T(8,128)(2,1)S(1)} %gather_sum.5.refs_8_.refs_0_), channel_id=1, source_target_pairs={{0,96},{16,112},{32,0},{48,16},{64,32},{80,48},{96,64},{112,80},{1... | collective-permute-start | bytes 61448 | tf_op jit(solution)/shard_map/ppermute | solution.py:370
  95.0 4.1 %collective-permute-start.9 = (bf16[4,80,128]{2,1,0:T(8,128)(2,1)S(1)}, bf16[4,80,128]{2,1,0:T(8,128)(2,1)S(1)}, u32[]{:S(2)}, u32[]{:S(2)}) collective-permute-start(bf16[4,80,128]{2,1,0:T(8,128)(2,1)S(1)} %stack.6._.refs_2_), channel_id=1, source_target_pairs={{0,16},{16,0},{32,48},{48,32},{64,80},{80,64},{96,112},{112,96},{1... | collective-permute-start | bytes 245768 | tf_op jit(solution)/shard_map/ppermute | solution.py:381
  103.9 25.9 %all-to-all-start.2 = ((bf16[16,336,128]{2,1,0:T(8,128)(2,1)}), bf16[16,336,128]{2,1,0:T(8,128)(2,1)S(1)}, u32[]{:S(2)}, u32[]{:S(2)}) async-start(bf16[16,336,128]{2,1,0:T(8,128)(2,1)} %get-tuple-element.119), calls=%async_computation.2 | async-start | bytes 2752512 | tf_op jit(solution)/shard_map/all_to_all | solution.py:896
  108.4 34.6 %collective-permute-start.16 = (bf16[2,256,128]{2,1,0:T(8,128)(2,1)S(1)}, bf16[2,256,128]{2,1,0:T(8,128)(2,1)S(1)}, u32[]{:S(2)}, u32[]{:S(2)}) collective-permute-start(bf16[2,256,128]{2,1,0:T(8,128)(2,1)S(1)} %get-tuple-element.125), channel_id=1, source_target_pairs={{0,1},{1,2},{2,3},{3,4},{4,5},{5,6},{6,7},{7,8},{8,9},{9,10},{10,1... | collective-permute-start | bytes 393224 | tf_op jit(solution)/shard_map/ppermute | solution.py:908
  111.7 31.3 %collective-permute-start.17 = (bf16[2,256,128]{2,1,0:T(8,128)(2,1)S(1)}, bf16[2,256,128]{2,1,0:T(8,128)(2,1)S(1)}, u32[]{:S(2)}, u32[]{:S(2)}) collective-permute-start(bf16[2,256,128]{2,1,0:T(8,128)(2,1)S(1)} %get-tuple-element.126), channel_id=1, source_target_pairs={{1,0},{2,1},{3,2},{4,3},{5,4},{6,5},{7,6},{8,7},{9,8},{10,9},{11,1... | collective-permute-start | bytes 393224 | tf_op jit(solution)/shard_map/ppermute | solution.py:909
  129.8 10.9 %collective-permute-start.12 = (bf16[80,128]{1,0:T(8,128)(2,1)S(1)}, bf16[80,128]{1,0:T(8,128)(2,1)S(1)}, u32[]{:S(2)}, u32[]{:S(2)}) collective-permute-start(bf16[80,128]{1,0:T(8,128)(2,1)S(1)} %gather_sum.6.refs_9_.refs_0_), channel_id=1, source_target_pairs={{0,32},{16,48},{32,64},{48,80},{64,96},{80,112},{96,0},{112,16},{1... | collective-permute-start | bytes 61448 | tf_op jit(solution)/shard_map/ppermute | solution.py:370
  131.1 9.7 %collective-permute-start.13 = (bf16[80,128]{1,0:T(8,128)(2,1)S(1)}, bf16[80,128]{1,0:T(8,128)(2,1)S(1)}, u32[]{:S(2)}, u32[]{:S(2)}) collective-permute-start(bf16[80,128]{1,0:T(8,128)(2,1)S(1)} %gather_sum.6.refs_9_.refs_0_), channel_id=1, source_target_pairs={{0,64},{16,80},{32,96},{48,112},{64,0},{80,16},{96,32},{112,48},{1... | collective-permute-start | bytes 61448 | tf_op jit(solution)/shard_map/ppermute | solution.py:370
  132.8 8.0 %collective-permute-start.14 = (bf16[80,128]{1,0:T(8,128)(2,1)S(1)}, bf16[80,128]{1,0:T(8,128)(2,1)S(1)}, u32[]{:S(2)}, u32[]{:S(2)}) collective-permute-start(bf16[80,128]{1,0:T(8,128)(2,1)S(1)} %gather_sum.6.refs_9_.refs_0_), channel_id=1, source_target_pairs={{0,96},{16,112},{32,0},{48,16},{64,32},{80,48},{96,64},{112,80},{1... | collective-permute-start | bytes 61448 | tf_op jit(solution)/shard_map/ppermute | solution.py:370
  140.8 4.6 %collective-permute-start.15 = (bf16[4,80,128]{2,1,0:T(8,128)(2,1)S(1)}, bf16[4,80,128]{2,1,0:T(8,128)(2,1)S(1)}, u32[]{:S(2)}, u32[]{:S(2)}) collective-permute-start(bf16[4,80,128]{2,1,0:T(8,128)(2,1)S(1)} %stack.7._.refs_2_), channel_id=1, source_target_pairs={{0,16},{16,0},{32,48},{48,32},{64,80},{80,64},{96,112},{112,96},{1... | collective-permute-start | bytes 245768 | tf_op jit(solution)/shard_map/ppermute | solution.py:381
  150.3 25.9 %all-to-all-start.3 = ((bf16[16,336,128]{2,1,0:T(8,128)(2,1)}), bf16[16,336,128]{2,1,0:T(8,128)(2,1)S(1)}, u32[]{:S(2)}, u32[]{:S(2)}) async-start(bf16[16,336,128]{2,1,0:T(8,128)(2,1)} %get-tuple-element.136), calls=%async_computation.3 | async-start | bytes 2752512 | tf_op jit(solution)/shard_map/all_to_all | solution.py:896
  154.8 32.9 %collective-permute-start.22 = (bf16[2,256,128]{2,1,0:T(8,128)(2,1)S(1)}, bf16[2,256,128]{2,1,0:T(8,128)(2,1)S(1)}, u32[]{:S(2)}, u32[]{:S(2)}) collective-permute-start(bf16[2,256,128]{2,1,0:T(8,128)(2,1)S(1)} %get-tuple-element.142), channel_id=1, source_target_pairs={{0,1},{1,2},{2,3},{3,4},{4,5},{5,6},{6,7},{7,8},{8,9},{9,10},{10,1... | collective-permute-start | bytes 393224 | tf_op jit(solution)/shard_map/ppermute | solution.py:908
  158.1 29.6 %collective-permute-start.23 = (bf16[2,256,128]{2,1,0:T(8,128)(2,1)S(1)}, bf16[2,256,128]{2,1,0:T(8,128)(2,1)S(1)}, u32[]{:S(2)}, u32[]{:S(2)}) collective-permute-start(bf16[2,256,128]{2,1,0:T(8,128)(2,1)S(1)} %get-tuple-element.143), channel_id=1, source_target_pairs={{1,0},{2,1},{3,2},{4,3},{5,4},{6,5},{7,6},{8,7},{9,8},{10,9},{11,1... | collective-permute-start | bytes 393224 | tf_op jit(solution)/shard_map/ppermute | solution.py:909
  176.3 9.5 %collective-permute-start.18 = (bf16[80,128]{1,0:T(8,128)(2,1)S(1)}, bf16[80,128]{1,0:T(8,128)(2,1)S(1)}, u32[]{:S(2)}, u32[]{:S(2)}) collective-permute-start(bf16[80,128]{1,0:T(8,128)(2,1)S(1)} %gather_sum.7.refs_10_.refs_0_), channel_id=1, source_target_pairs={{0,32},{16,48},{32,64},{48,80},{64,96},{80,112},{96,0},{112,16},{1... | collective-permute-start | bytes 61448 | tf_op jit(solution)/shard_map/ppermute | solution.py:370
  176.7 9.1 %collective-permute-start.19 = (bf16[80,128]{1,0:T(8,128)(2,1)S(1)}, bf16[80,128]{1,0:T(8,128)(2,1)S(1)}, u32[]{:S(2)}, u32[]{:S(2)}) collective-permute-start(bf16[80,128]{1,0:T(8,128)(2,1)S(1)} %gather_sum.7.refs_10_.refs_0_), channel_id=1, source_target_pairs={{0,64},{16,80},{32,96},{48,112},{64,0},{80,16},{96,32},{112,48},{1... | collective-permute-start | bytes 61448 | tf_op jit(solution)/shard_map/ppermute | solution.py:370
  178.1 7.7 %collective-permute-start.20 = (bf16[80,128]{1,0:T(8,128)(2,1)S(1)}, bf16[80,128]{1,0:T(8,128)(2,1)S(1)}, u32[]{:S(2)}, u32[]{:S(2)}) collective-permute-start(bf16[80,128]{1,0:T(8,128)(2,1)S(1)} %gather_sum.7.refs_10_.refs_0_), channel_id=1, source_target_pairs={{0,96},{16,112},{32,0},{48,16},{64,32},{80,48},{96,64},{112,80},{1... | collective-permute-start | bytes 61448 | tf_op jit(solution)/shard_map/ppermute | solution.py:370
  185.8 4.1 %collective-permute-start.21 = (bf16[4,80,128]{2,1,0:T(8,128)(2,1)S(1)}, bf16[4,80,128]{2,1,0:T(8,128)(2,1)S(1)}, u32[]{:S(2)}, u32[]{:S(2)}) collective-permute-start(bf16[4,80,128]{2,1,0:T(8,128)(2,1)S(1)} %stack.8._.refs_2_), channel_id=1, source_target_pairs={{0,16},{16,0},{32,48},{48,32},{64,80},{80,64},{96,112},{112,96},{1... | collective-permute-start | bytes 245768 | tf_op jit(solution)/shard_map/ppermute | solution.py:381
  192.9 7.8 %collective-permute-start.24 = (bf16[16,128]{1,0:T(8,128)(2,1)S(1)}, bf16[16,128]{1,0:T(8,128)(2,1)S(1)}, u32[]{:S(2)}, u32[]{:S(2)}) collective-permute-start(bf16[16,128]{1,0:T(8,128)(2,1)S(1)} %get-tuple-element.155.refs_5_.refs_0_), channel_id=1, source_target_pairs={{0,1},{1,2},{2,3},{3,0},{4,5},{5,6},{6,7},{7,4},{8,9},{9,10},{10,1... | collective-permute-start | bytes 12296 | tf_op jit(solution)/shard_map/ppermute | solution.py:534
  193.7 7.1 %collective-permute-start.25 = (bf16[16,128]{1,0:T(8,128)(2,1)S(1)}, bf16[16,128]{1,0:T(8,128)(2,1)S(1)}, u32[]{:S(2)}, u32[]{:S(2)}) collective-permute-start(bf16[16,128]{1,0:T(8,128)(2,1)S(1)} %get-tuple-element.155.refs_5_.refs_0_), channel_id=1, source_target_pairs={{0,2},{1,3},{2,0},{3,1},{4,6},{5,7},{6,4},{7,5},{8,10},{9,11},{10,... | collective-permute-start | bytes 12296 | tf_op jit(solution)/shard_map/ppermute | solution.py:534
  194.9 5.9 %collective-permute-start.26 = (bf16[16,128]{1,0:T(8,128)(2,1)S(1)}, bf16[16,128]{1,0:T(8,128)(2,1)S(1)}, u32[]{:S(2)}, u32[]{:S(2)}) collective-permute-start(bf16[16,128]{1,0:T(8,128)(2,1)S(1)} %get-tuple-element.155.refs_5_.refs_0_), channel_id=1, source_target_pairs={{0,3},{1,0},{2,1},{3,2},{4,7},{5,4},{6,5},{7,6},{8,11},{9,8},{10,9... | collective-permute-start | bytes 12296 | tf_op jit(solution)/shard_map/ppermute | solution.py:534
  198.7 1.0 copy-start
  199.7 1.0 copy-start.3
  200.8 5.9 %collective-permute-start.27 = (bf16[16,128]{1,0:T(8,128)(2,1)S(1)}, bf16[16,128]{1,0:T(8,128)(2,1)S(1)}, u32[]{:S(2)}, u32[]{:S(2)}) collective-permute-start(bf16[16,128]{1,0:T(8,128)(2,1)S(1)} %sum_over.2.refs_0_), channel_id=1, source_target_pairs={{0,4},{1,5},{2,6},{3,7},{4,8},{5,9},{6,10},{7,11},{8,12},{9,13},{1... | collective-permute-start | bytes 12296 | tf_op jit(solution)/shard_map/ppermute | solution.py:534
  201.0 5.7 %collective-permute-start.28 = (bf16[16,128]{1,0:T(8,128)(2,1)S(1)}, bf16[16,128]{1,0:T(8,128)(2,1)S(1)}, u32[]{:S(2)}, u32[]{:S(2)}) collective-permute-start(bf16[16,128]{1,0:T(8,128)(2,1)S(1)} %sum_over.2.refs_0_), channel_id=1, source_target_pairs={{0,8},{1,9},{2,10},{3,11},{4,12},{5,13},{6,14},{7,15},{8,0},{9,1},... | collective-permute-start | bytes 12296 | tf_op jit(solution)/shard_map/ppermute | solution.py:534
  202.9 3.8 %collective-permute-start.29 = (bf16[16,128]{1,0:T(8,128)(2,1)S(1)}, bf16[16,128]{1,0:T(8,128)(2,1)S(1)}, u32[]{:S(2)}, u32[]{:S(2)}) collective-permute-start(bf16[16,128]{1,0:T(8,128)(2,1)S(1)} %sum_over.2.refs_0_), channel_id=1, source_target_pairs={{0,12},{1,13},{2,14},{3,15},{4,0},{5,1},{6,2},{7,3},{8,4},{9,5},{1... | collective-permute-start | bytes 12296 | tf_op jit(solution)/shard_map/ppermute | solution.py:534
  204.4 1.2 copy-start.1
  206.7 9.5 %copy-start.2 = (f32[8,256,128]{2,1,0:T(8,128)S(1)}, f32[8,256,128]{2,1,0:T(8,128)}, u32[]{:S(2)}) copy-start(f32[8,256,128]{2,1,0:T(8,128)} %copy-done) | copy-start | bytes 3145732
  206.7 9.4 %copy-start.4 = (f32[8,256,128]{2,1,0:T(8,128)S(1)}, f32[8,256,128]{2,1,0:T(8,128)}, u32[]{:S(2)}) copy-start(f32[8,256,128]{2,1,0:T(8,128)} %copy-done.3) | copy-start | bytes 3145732
  206.8 4.4 %collective-permute-start.30 = (bf16[16,128]{1,0:T(8,128)(2,1)S(1)}, bf16[16,128]{1,0:T(8,128)(2,1)S(1)}, u32[]{:S(2)}, u32[]{:S(2)}) collective-permute-start(bf16[16,128]{1,0:T(8,128)(2,1)S(1)} %sum_over.3.refs_0_), channel_id=1, source_target_pairs={{0,32},{16,48},{32,64},{48,80},{64,96},{80,112},{96,0},{112,16},{1... | collective-permute-start | bytes 12296 | tf_op jit(solution)/shard_map/ppermute | solution.py:370
  208.0 4.0 %collective-permute-start.31 = (bf16[16,128]{1,0:T(8,128)(2,1)S(1)}, bf16[16,128]{1,0:T(8,128)(2,1)S(1)}, u32[]{:S(2)}, u32[]{:S(2)}) collective-permute-start(bf16[16,128]{1,0:T(8,128)(2,1)S(1)} %sum_over.3.refs_0_), channel_id=1, source_target_pairs={{0,64},{16,80},{32,96},{48,112},{64,0},{80,16},{96,32},{112,48},{1... | collective-permute-start | bytes 12296 | tf_op jit(solution)/shard_map/ppermute | solution.py:370
  209.7 2.8 %collective-permute-start.32 = (bf16[16,128]{1,0:T(8,128)(2,1)S(1)}, bf16[16,128]{1,0:T(8,128)(2,1)S(1)}, u32[]{:S(2)}, u32[]{:S(2)}) collective-permute-start(bf16[16,128]{1,0:T(8,128)(2,1)S(1)} %sum_over.3.refs_0_), channel_id=1, source_target_pairs={{0,96},{16,112},{32,0},{48,16},{64,32},{80,48},{96,64},{112,80},{1... | collective-permute-start | bytes 12296 | tf_op jit(solution)/shard_map/ppermute | solution.py:370
  212.4 3.7 %collective-permute-start.33 = (bf16[4,16,128]{2,1,0:T(8,128)(2,1)S(1)}, bf16[4,16,128]{2,1,0:T(8,128)(2,1)S(1)}, u32[]{:S(2)}, u32[]{:S(2)}) collective-permute-start(bf16[4,16,128]{2,1,0:T(8,128)(2,1)S(1)} %stack.9.refs_2_), channel_id=1, source_target_pairs={{0,16},{16,0},{32,48},{48,32},{64,80},{80,64},{96,112},{112,96},{1... | collective-permute-start | bytes 49160 | tf_op jit(solution)/shard_map/ppermute | solution.py:381
  (3 other events, 2.1 us)

commit v5 on v4

--- a/solution.py
+++ b/solution.py
@@ -103,7 +103,7 @@
 
 def call(kernel, args, in_specs, outs, scratch, name, flops, moved, aliases={}):
     def pinned(array, spec):
-        if not PIN or not any(spec is one for one in (VMEM, HBM, AFTER, AFTER_VMEM)):
+        if not PIN or not any(spec is one for one in (VMEM, HBM, SMEM, AFTER, AFTER_VMEM)):
             return array
         in_vmem = spec is VMEM or spec is AFTER_VMEM
         return pltpu.with_memory_space_constraint(array, pltpu.VMEM if in_vmem else pltpu.HBM)
@@ -469,7 +469,16 @@
     return far, blocks, held
 
 
-def halo_kernel(count_ref, list_ref, index_ref, blocks, before, after, near_in, _, near, halo):
+def halo_kernel(count_ref, list_ref, index_ref, blocks, before, after, near_in, *refs):
+    held = (len(refs) - 4) // 2
+    sources, near, targets = refs[:held], refs[held + 1], refs[held + 2 : -2]
+    halo, loaded = refs[-2:]
+    loads = [
+        pltpu.make_async_copy(source, target, loaded.at[i])
+        for i, (source, target) in enumerate(zip(sources, targets))
+    ]
+    for copy in loads:
+        copy.start()
     leaves, reach, entries = near.shape[0], before.shape[0], index_ref.shape[1]
     halo[:reach] = before[...]
     halo[reach:] = after[...]
@@ -491,27 +500,30 @@
         return carry
 
     lax.fori_loop(0, (count + at_once - 1) // at_once, add, 0)
-
-
-def halo_part(listed, near_index, blocks, before, after, near, earlier):
+    for copy in loads:
+        copy.wait()
+
+
+def halo_part(listed, near_index, blocks, before, after, near, held, earlier):
     return call(
         halo_kernel,
-        (*listed, near_index, blocks, before, after, near, earlier),
-        (SMEM, SMEM, SMEM, VMEM, VMEM, VMEM, VMEM, AFTER_VMEM),
-        [(near.shape, F32, VMEM)],
-        [pltpu.VMEM((2 * before.shape[0],) + before.shape[1:], BF16)],
+        (*listed, near_index, blocks, before, after, near, *held, earlier),
+        (SMEM, SMEM, SMEM, VMEM, VMEM, VMEM, VMEM) + (HBM,) * len(held) + (AFTER_VMEM,),
+        [(a.shape, a.dtype, VMEM) for a in (near, *held)],
+        [pltpu.VMEM((2 * before.shape[0],) + before.shape[1:], BF16), semaphores(len(held))],
         "halo_part",
         1 << 28,
         2 << 20,
         {6: 0},
-    )[0]
-
-
-def sum_kernel(place, *refs):
+    )
+
+
+def sum_kernel(*refs, axis, stride):
     *parts, _, out, rows, split = refs
     count = len(parts)
+    place = lax.rem(lax.axis_index(axis).astype(jnp.int32) // stride, count)
     for j, part in enumerate(parts):
-        rows[lax.rem(place[0] + count - j, count)] = part[...].astype(F32)
+        rows[lax.rem(place + count - j, count)] = part[...].astype(F32)
     total = rows[0]
     for i in range(1, count):
         total = total + rows[i]
@@ -522,7 +534,6 @@
 def sum_over(dots, axis, stride, count, earlier, after):
     if count == 1:
         return dots
-    place = lax.rem(lax.axis_index(axis).astype(jnp.int32) // stride, count).reshape(1)
     size = lax.axis_size(axis)
 
     def moved(i, j):
@@ -533,39 +544,15 @@
     for j in range(1, count):
         parts.append(lax.ppermute(dots, axis, [(i, moved(i, j)) for i in range(size)]))
     return call(
-        sum_kernel,
-        (place, *parts, earlier),
-        (SMEM,) + (VMEM,) * count + (after,),
+        functools.partial(sum_kernel, axis=axis, stride=stride),
+        (*parts, earlier),
+        (VMEM,) * count + (after,),
         [(dots.shape, BF16, VMEM)],
         [pltpu.VMEM((count,) + dots.shape, F32), pltpu.VMEM((DOT_ROWS, dots.shape[1]), F32)],
         "sum_over",
         0,
         1 << 18,
     )[0]
-
-
-def load_kernel(*refs):
-    count = (len(refs) - 2) // 2
-    copies = [
-        pltpu.make_async_copy(refs[i], refs[count + 1 + i], refs[-1].at[i]) for i in range(count)
-    ]
-    for copy in copies:
-        copy.start()
-    for copy in copies:
-        copy.wait()
-
-
-def load(arrays, earlier):
-    return call(
-        load_kernel,
-        (*arrays, earlier),
-        (HBM,) * len(arrays) + (AFTER_VMEM,),
-        [(a.shape, a.dtype, VMEM) for a in arrays],
-        [semaphores(len(arrays))],
-        "load",
-        0,
-        5 << 20,
-    )
 
 
 def stage_kernel(*refs, k, points):
@@ -714,7 +701,7 @@
     else:
         args += later
         specs += [VMEM] * len(later)
-        get("z", tall, F32, HBM)
+        get("z", tall, F32, HBM if sends else VMEM)
     get("state", (STATE_ROWS, columns), F32, VMEM)
     rows = (slots + 1) * rank + DOT_ROWS
     get("send", (inner, rows, columns) if sends else (DOT_ROWS, columns), BF16, VMEM)
@@ -913,26 +900,25 @@
         if k == STEPS:
             krylov = done = vectors(state, zs, list(range(STEPS - 1)), near, CHUNKS)[0]
         summed = gather_sum(recv, slots * rank, done)
-        held = (near, basis, turned, transfer, lifting, top, *zs)
-        local_far, blocks, held = far_field(listed, recv, packed, near_blocks, held, summed)
-        near, *held = held
+        local_far, blocks, (near,) = far_field(listed, recv, packed, near_blocks, (near,), summed)
 
         def between(column):
-            return halo_part(listed, near_index, blocks, before, after, near, column)
-
-        column, other, near = over_branches(summed, outer, local_far, between)
+            held = (basis, turned, transfer, lifting, top, *zs)
+            return halo_part(listed, near_index, blocks, before, after, near, held, column)
+
+        column, other, (near, *held) = over_branches(summed, outer, local_far, between)
         later = [column, other, state, local_far, near, *held]
         out = stage(k, points, wanted, branch, zs[0], basis, transfer, later)
         state = out["state"]
         zs = zs + [out["z"]]
     low = 4 if inner % 4 == 0 else inner
-    loaded = load(zs, out["send"])
-    summed = sum_over(out["send"], "inner", 1, low, loaded[0], AFTER_VMEM)
-    krylov = vectors(state, loaded, [STEPS - 1], krylov, CHUNKS)[0]
-    summed = sum_over(summed, "inner", low, inner // low, krylov, AFTER)
-    column, other, _ = over_branches(summed, outer, loaded[0], lambda column: None)
+    held = held[-STEPS:] + [out["z"]]
+    krylov = vectors(state, held, [STEPS - 1], krylov, CHUNKS)[0]
+    summed = sum_over(out["send"], "inner", 1, low, krylov, AFTER)
+    summed = sum_over(summed, "inner", low, inner // low, summed, AFTER_VMEM)
+    column, other, _ = over_branches(summed, outer, summed, lambda column: None)
     products = [branch, column, other]
-    krylov, hessenberg = vectors(state, loaded, [STEPS], krylov, CHUNKS, products, points)
+    krylov, hessenberg = vectors(state, held, [STEPS], krylov, CHUNKS, products, points)
     return krylov.reshape(STEPS + 1, *rhs.shape), hessenberg
 
 

time: 219 us -> 216 us (0.986)
  local copies, waits for them, and re-layouts: 6.68 us -> 0.56 us
  starting transfers between devices: 81.5 us -> 84.1 us
    unnamed x26 -> x2, local copies, waits for them, and re-layouts: 6.68 us -> 0.56 us
    ppermute x5, starting transfers between devices: 11.1 us -> 13.7 us  [over_branches(): other = lax.ppermute(column, 'outer', [(o, o ^ 1) for o in range(outer)])]
    pallas_call x33 -> x32, Pallas kernels: 99.8 us -> 98.5 us  [call(): pl.pallas_call(kernel, in_specs=list(in_specs), out_specs=[spec for _, _,...]
  transfers between devices with their start and end apart: 38 -> 38, of which waited for: 6 -> 8; matrix products, arithmetic and copies ran while one was open for 0% -> 0% of each run, Pallas kernels for 35% -> 35%
where the time goes in v5:
time: 216 us; the launch traced here: 214 us
  Pallas kernels  98.5 us (46%)
  starting transfers between devices  84.1 us (39%)
  waiting for transfers between devices  29.5 us (14%)
    pallas_call x32, Pallas kernels, call(): pl.pallas_call(kernel, in_specs=list(in_specs), out_specs=[spec for _, _,...  98.5 us
    all_to_all x4, waiting for transfers between devices, exchange(): return lax.all_to_all(array, axis, split_axis=0, concat_axis=0, tiled=True)  26.3 us
    all_to_all x4, starting transfers between devices, exchange(): return lax.all_to_all(array, axis, split_axis=0, concat_axis=0, tiled=True)  25.3 us
    ppermute x15, starting transfers between devices, over_branches(): lax.ppermute(summed, 'outer', shift)  19.5 us
    ppermute x5, starting transfers between devices, over_branches(): other = lax.ppermute(column, 'outer', [(o, o ^ 1) for o in range(outer)])  13.7 us
    ppermute x4, starting transfers between devices, shards(): before = lax.ppermute(out['high'], 'inner', up_pairs)  13.1 us
    ppermute x6, starting transfers between devices, sum_over(): lax.ppermute(dots, axis, [(i, moved(i, j)) for i in range(size)])  7.35 us
    ppermute x4, starting transfers between devices, shards(): after = lax.ppermute(out['low'], 'inner', down_pairs)  5.17 us
  transfers between devices with their start and end apart: 38, of which 8 were waited for; matrix products, arithmetic and copies ran while one was open for 0% of the time, Pallas kernels for 35%

profile of v5, /device:TPU:1, one launch (start us, length us, event | category | flops | bytes accessed | tf_op | source)
XLA Modules:
  0.0 214.0 jit_solution(17199918041578743390)
XLA Ops:
  0.6 4.3 %stage0.1 = (f32[64,128]{1,0:T(8,128)S(1)}, bf16[16,336,128]{2,1,0:T(8,128)(2,1)}, bf16[8,256,128]{2,1,0:T(8,128)(2,1)}, bf16[2,256,128]{2,1,0:T(8,128)(2,1)S(1)}, bf16[2,256,128]{2,1,0:T(8,128)(2,1)S(1)}) custom-call(s32[4,16]{1,0:T(4,128)} %bitcast.13, s32[1]{0:T(128)} %bitcast.2.refs_1_.branch, f32[8,256,128]{2,1,0:T(8,128)} %bitcast.7, ...), custom_call_target="tpu_custom_call" | custom-call | flops 134217728 | bytes 4194304 | tf_op jit(solution)/shard_map/stage0/pallas_call | solution.py:116
  5.0 8.6 %all-to-all-start = ((bf16[16,336,128]{2,1,0:T(8,128)(2,1)}), bf16[16,336,128]{2,1,0:T(8,128)(2,1)S(1)}, u32[]{:S(2)}, u32[]{:S(2)}) async-start(bf16[16,336,128]{2,1,0:T(8,128)(2,1)} %get-tuple-element.82), calls=%async_computation | async-start | bytes 2752512 | tf_op jit(solution)/shard_map/all_to_all | solution.py:883
  13.6 3.3 %collective-permute-start.4 = (bf16[2,256,128]{2,1,0:T(8,128)(2,1)S(1)}, bf16[2,256,128]{2,1,0:T(8,128)(2,1)S(1)}, u32[]{:S(2)}, u32[]{:S(2)}) collective-permute-start(bf16[2,256,128]{2,1,0:T(8,128)(2,1)S(1)} %get-tuple-element.90), channel_id=1, source_target_pairs={{0,1},{1,2},{2,3},{3,4},{4,5},{5,6},{6,7},{7,8},{8,9},{9,10},{10,1... | collective-permute-start | bytes 393224 | tf_op jit(solution)/shard_map/ppermute | solution.py:895
  16.9 1.3 collective-permute-start.5
  18.2 8.7 %pack.1 = (bf16[16,512,256]{2,1,0:T(8,128)(2,1)}, s32[1]{0:T(128)}, s32[64]{0:T(128)S(1)}, bf16[8,256,64]{2,1,0:T(8,128)(2,1)}, bf16[64,512]{1,0:T(8,128)(2,1)}, /*index=5*/bf16[64,512]{1,0:T(8,128)(2,1)}) custom-call(s32[1]{0:T(128)} %bitcast.2.refs_1_.branch, s32[8,48]{1,0:T(8,128)} %mask_ref.5, s32[8,48]{1,0:T(8,128)} %slot_ref.1, s32[8,8]{1,0:T(8,128)} %index_ref.17, ...), custom_call_target="tpu_custom_call" | custom-call | bytes 10485760 | tf_op jit(solution)/shard_map/pack/pallas_call | solution.py:116
  27.5 6.9 %near_field.4.refs_0_ = f32[8,256,128]{2,1,0:T(8,128)} custom-call(s32[8,8]{1,0:T(8,128)} %index_ref.17, s32[8,8]{1,0:T(8,128)} %mask_ref.9, bf16[8,8,256,256]{3,2,1,0:T(8,128)(2,1)} %blocks_ref.15, bf16[8,256,128]{2,1,0:T(8,128)(2,1)} %get-tuple-element.83.own_ref, bf16[16,512,256]{2,1,0:T(8,128)(2,1)} %get-tuple-element.84.refs_0_.packed_ref), custom_call_target="tpu_custom_call" | custom-call | flops 1073741824 | bytes 8388608 | tf_op jit(solution)/shard_map/near_field/pallas_call | solution.py:116
  35.7 2.5 %collective-permute-start.1 = (bf16[80,128]{1,0:T(8,128)(2,1)S(1)}, bf16[80,128]{1,0:T(8,128)(2,1)S(1)}, u32[]{:S(2)}, u32[]{:S(2)}) collective-permute-start(bf16[80,128]{1,0:T(8,128)(2,1)S(1)} %gather_sum.4.refs_1_.refs_0_), channel_id=1, source_target_pairs={{0,64},{16,80},{32,96},{48,112},{64,0},{80,16},{96,32},{112,48},{1... | collective-permute-start | bytes 61448 | tf_op jit(solution)/shard_map/ppermute | solution.py:370
  39.3 5.1 %far_field.4 = (f32[512,128]{1,0:T(8,128)S(1)}, bf16[64,256,256]{2,1,0:T(8,128)(2,1)S(1)}, f32[8,256,128]{2,1,0:T(8,128)S(1)}) custom-call(s32[1]{0:T(128)} %get-tuple-element.85.count_ref, s32[64]{0:T(128)} %copy-done, bf16[16,336,128]{2,1,0:T(8,128)(2,1)S(1)} %all-to-all-done.recv, bf16[16,512,256]{2,1,0:T(8,128)(2,1)} %get-tuple-element.84.refs_0_.packed_ref, ...), custom_call_target="tpu_custom_call" | custom-call | flops 536870912 | bytes 4194304 | tf_op jit(solution)/shard_map/far_field/pallas_call | solution.py:116
  44.5 2.6 %collective-permute-start.3 = (bf16[4,80,128]{2,1,0:T(8,128)(2,1)S(1)}, bf16[4,80,128]{2,1,0:T(8,128)(2,1)S(1)}, u32[]{:S(2)}, u32[]{:S(2)}) collective-permute-start(bf16[4,80,128]{2,1,0:T(8,128)(2,1)S(1)} %stack.5.refs_6_.refs_2_), channel_id=1, source_target_pairs={{0,16},{16,0},{32,48},{48,32},{64,80},{80,64},{96,112},{112,96},{1... | collective-permute-start | bytes 245768 | tf_op jit(solution)/shard_map/ppermute | solution.py:381
  47.1 3.0 %halo_part.4 = (f32[8,256,128]{2,1,0:T(8,128)S(1)}, bf16[8,64,256]{2,1,0:T(8,128)(2,1)S(1)}, bf16[8,256,64]{2,1,0:T(8,128)(2,1)S(1)}, bf16[8,64,64]{2,1,0:T(8,12...) custom-call(s32[1]{0:T(128)} %get-tuple-element.85.count_ref, ...), custom_call_target="tpu_custom_call", output_to_operand_aliasing={{0}: (6, {})} | custom-call | flops 268435456 | bytes 2097152 | tf_op jit(solution)/shard_map/halo_part/pallas_call | solution.py:116
  50.1 4.7 %stage1.1 = (f32[8,256,128]{2,1,0:T(8,128)}, f32[64,128]{1,0:T(8,128)S(1)}, bf16[16,336,128]{2,1,0:T(8,128)(2,1)}, bf16[8,256,128]{2,1,0:T(8,128)(2,1)}, bf16[2,...) custom-call(s32[4,16]{1,0:T(4,128)} %bitcast.14, s32[1]{0:T(128)} %bitcast.2.refs_1_.branch, ...), custom_call_target="tpu_custom_call" | custom-call | flops 134217728 | bytes 5242880 | tf_op jit(solution)/shard_map/stage1/pallas_call | solution.py:116
  54.8 7.7 %all-to-all-start.1 = ((bf16[16,336,128]{2,1,0:T(8,128)(2,1)}), bf16[16,336,128]{2,1,0:T(8,128)(2,1)S(1)}, u32[]{:S(2)}, u32[]{:S(2)}) async-start(bf16[16,336,128]{2,1,0:T(8,128)(2,1)} %get-tuple-element.103), calls=%async_computation.1 | async-start | bytes 2752512 | tf_op jit(solution)/shard_map/all_to_all | solution.py:883
  62.5 3.3 %collective-permute-start.10 = (bf16[2,256,128]{2,1,0:T(8,128)(2,1)S(1)}, bf16[2,256,128]{2,1,0:T(8,128)(2,1)S(1)}, u32[]{:S(2)}, u32[]{:S(2)}) collective-permute-start(bf16[2,256,128]{2,1,0:T(8,128)(2,1)S(1)} %get-tuple-element.108), channel_id=1, source_target_pairs={{0,1},{1,2},{2,3},{3,4},{4,5},{5,6},{6,7},{7,8},{8,9},{9,10},{10,1... | collective-permute-start | bytes 393224 | tf_op jit(solution)/shard_map/ppermute | solution.py:895
  65.8 1.3 collective-permute-start.11
  67.1 6.9 %near_field.5.refs_0_ = f32[8,256,128]{2,1,0:T(8,128)} custom-call(s32[8,8]{1,0:T(8,128)} %index_ref.17, s32[8,8]{1,0:T(8,128)} %mask_ref.9, bf16[8,8,256,256]{3,2,1,0:T(8,128)(2,1)} %blocks_ref.15, bf16[8,256,128]{2,1,0:T(8,128)(2,1)} %get-tuple-element.104.own_ref), custom_call_target="tpu_custom_call" | custom-call | flops 1073741824 | bytes 8388608 | tf_op jit(solution)/shard_map/near_field/pallas_call | solution.py:116
  74.0 9.9 %all-to-all-done.1.recv = bf16[16,336,128]{2,1,0:T(8,128)(2,1)S(1)} async-done(((bf16[16,336,128]{2,1,0:T(8,128)(2,1)}), bf16[16,336,128]{2,1,0:T(8,128)(2,1)S(1)}, u32[]{:S(2)}, u32[]{:S(2)}) %all-to-all-start.1) | async-done | bytes 1376288 | tf_op jit(solution)/shard_map/all_to_all | solution.py:883
  84.8 1.9 collective-permute-start.8
  86.7 5.1 %far_field.5 = (f32[512,128]{1,0:T(8,128)S(1)}, bf16[64,256,256]{2,1,0:T(8,128)(2,1)S(1)}, f32[8,256,128]{2,1,0:T(8,128)S(1)}) custom-call(s32[1]{0:T(128)} %get-tuple-element.85.count_ref, s32[64]{0:T(128)} %copy-done, bf16[16,336,128]{2,1,0:T(8,128)(2,1)S(1)} %all-to-all-done.1.recv, bf16[16,512,256]{2,1,0:T(8,128)(2,1)} %get-tuple-element.84.refs_0_.packed_ref, ...), custom_call_target="tpu_custom_call" | custom-call | flops 536870912 | bytes 4194304 | tf_op jit(solution)/shard_map/far_field/pallas_call | solution.py:116
  91.9 2.1 collective-permute-start.9
  93.9 3.3 %halo_part.5 = (f32[8,256,128]{2,1,0:T(8,128)S(1)}, bf16[8,64,256]{2,1,0:T(8,128)(2,1)S(1)}, bf16[8,256,64]{2,1,0:T(8,128)(2,1)S(1)}, bf16[8,64,64]{2,1,0:T(8,12...) custom-call(s32[1]{0:T(128)} %get-tuple-element.85.count_ref, ...), custom_call_target="tpu_custom_call", output_to_operand_aliasing={{0}: (6, {})} | custom-call | flops 268435456 | bytes 2097152 | tf_op jit(solution)/shard_map/halo_part/pallas_call | solution.py:116
  97.3 4.9 %stage2.1 = (f32[8,256,128]{2,1,0:T(8,128)}, f32[64,128]{1,0:T(8,128)S(1)}, bf16[16,336,128]{2,1,0:T(8,128)(2,1)}, bf16[8,256,128]{2,1,0:T(8,128)(2,1)}, bf16[2,...) custom-call(s32[4,16]{1,0:T(4,128)} %bitcast.15, s32[1]{0:T(128)} %bitcast.2.refs_1_.branch, ...), custom_call_target="tpu_custom_call" | custom-call | flops 134217728 | bytes 6291456 | tf_op jit(solution)/shard_map/stage2/pallas_call | solution.py:116
  102.1 4.5 %all-to-all-start.2 = ((bf16[16,336,128]{2,1,0:T(8,128)(2,1)}), bf16[16,336,128]{2,1,0:T(8,128)(2,1)S(1)}, u32[]{:S(2)}, u32[]{:S(2)}) async-start(bf16[16,336,128]{2,1,0:T(8,128)(2,1)} %get-tuple-element.120), calls=%async_computation.2 | async-start | bytes 2752512 | tf_op jit(solution)/shard_map/all_to_all | solution.py:883
  106.6 3.3 %collective-permute-start.16 = (bf16[2,256,128]{2,1,0:T(8,128)(2,1)S(1)}, bf16[2,256,128]{2,1,0:T(8,128)(2,1)S(1)}, u32[]{:S(2)}, u32[]{:S(2)}) collective-permute-start(bf16[2,256,128]{2,1,0:T(8,128)(2,1)S(1)} %get-tuple-element.125), channel_id=1, source_target_pairs={{0,1},{1,2},{2,3},{3,4},{4,5},{5,6},{6,7},{7,8},{8,9},{9,10},{10,1... | collective-permute-start | bytes 393224 | tf_op jit(solution)/shard_map/ppermute | solution.py:895
  111.2 6.9 %near_field.6.refs_0_ = f32[8,256,128]{2,1,0:T(8,128)} custom-call(s32[8,8]{1,0:T(8,128)} %index_ref.17, s32[8,8]{1,0:T(8,128)} %mask_ref.9, bf16[8,8,256,256]{3,2,1,0:T(8,128)(2,1)} %blocks_ref.15, bf16[8,256,128]{2,1,0:T(8,128)(2,1)} %get-tuple-element.121.own_ref), custom_call_target="tpu_custom_call" | custom-call | flops 1073741824 | bytes 8388608 | tf_op jit(solution)/shard_map/near_field/pallas_call | solution.py:116
  118.1 9.9 %all-to-all-done.2.recv = bf16[16,336,128]{2,1,0:T(8,128)(2,1)S(1)} async-done(((bf16[16,336,128]{2,1,0:T(8,128)(2,1)}), bf16[16,336,128]{2,1,0:T(8,128)(2,1)S(1)}, u32[]{:S(2)}, u32[]{:S(2)}) %all-to-all-start.2) | async-done | bytes 1376288 | tf_op jit(solution)/shard_map/all_to_all | solution.py:883
  128.8 2.0 collective-permute-start.13
  130.7 2.0 collective-permute-start.14
  132.7 5.1 %far_field.6 = (f32[512,128]{1,0:T(8,128)S(1)}, bf16[64,256,256]{2,1,0:T(8,128)(2,1)S(1)}, f32[8,256,128]{2,1,0:T(8,128)S(1)}) custom-call(s32[1]{0:T(128)} %get-tuple-element.85.count_ref, s32[64]{0:T(128)} %copy-done, bf16[16,336,128]{2,1,0:T(8,128)(2,1)S(1)} %all-to-all-done.2.recv, bf16[16,512,256]{2,1,0:T(8,128)(2,1)} %get-tuple-element.84.refs_0_.packed_ref, ...), custom_call_target="tpu_custom_call" | custom-call | flops 536870912 | bytes 4194304 | tf_op jit(solution)/shard_map/far_field/pallas_call | solution.py:116
  137.9 2.4 %collective-permute-start.15 = (bf16[4,80,128]{2,1,0:T(8,128)(2,1)S(1)}, bf16[4,80,128]{2,1,0:T(8,128)(2,1)S(1)}, u32[]{:S(2)}, u32[]{:S(2)}) collective-permute-start(bf16[4,80,128]{2,1,0:T(8,128)(2,1)S(1)} %stack.7.refs_8_.refs_2_), channel_id=1, source_target_pairs={{0,16},{16,0},{32,48},{48,32},{64,80},{80,64},{96,112},{112,96},{1... | collective-permute-start | bytes 245768 | tf_op jit(solution)/shard_map/ppermute | solution.py:381
  140.2 3.6 %halo_part.6 = (f32[8,256,128]{2,1,0:T(8,128)S(1)}, bf16[8,64,256]{2,1,0:T(8,128)(2,1)S(1)}, bf16[8,256,64]{2,1,0:T(8,128)(2,1)S(1)}, bf16[8,64,64]{2,1,0:T(8,12...) custom-call(s32[1]{0:T(128)} %get-tuple-element.85.count_ref, ...), custom_call_target="tpu_custom_call", output_to_operand_aliasing={{0}: (6, {})} | custom-call | flops 268435456 | bytes 2097152 | tf_op jit(solution)/shard_map/halo_part/pallas_call | solution.py:116
  143.9 5.0 %stage3.1 = (f32[8,256,128]{2,1,0:T(8,128)}, f32[64,128]{1,0:T(8,128)S(1)}, bf16[16,336,128]{2,1,0:T(8,128)(2,1)}, bf16[8,256,128]{2,1,0:T(8,128)(2,1)}, bf16[2,...) custom-call(s32[4,16]{1,0:T(4,128)} %bitcast.16, s32[1]{0:T(128)} %bitcast.2.refs_1_.branch, ...), custom_call_target="tpu_custom_call" | custom-call | flops 134217728 | bytes 7340032 | tf_op jit(solution)/shard_map/stage3/pallas_call | solution.py:116
  148.9 4.5 %all-to-all-start.3 = ((bf16[16,336,128]{2,1,0:T(8,128)(2,1)}), bf16[16,336,128]{2,1,0:T(8,128)(2,1)S(1)}, u32[]{:S(2)}, u32[]{:S(2)}) async-start(bf16[16,336,128]{2,1,0:T(8,128)(2,1)} %get-tuple-element.138), calls=%async_computation.3 | async-start | bytes 2752512 | tf_op jit(solution)/shard_map/all_to_all | solution.py:883
  153.4 3.3 %collective-permute-start.22 = (bf16[2,256,128]{2,1,0:T(8,128)(2,1)S(1)}, bf16[2,256,128]{2,1,0:T(8,128)(2,1)S(1)}, u32[]{:S(2)}, u32[]{:S(2)}) collective-permute-start(bf16[2,256,128]{2,1,0:T(8,128)(2,1)S(1)} %get-tuple-element.143), channel_id=1, source_target_pairs={{0,1},{1,2},{2,3},{3,4},{4,5},{5,6},{6,7},{7,8},{8,9},{9,10},{10,1... | collective-permute-start | bytes 393224 | tf_op jit(solution)/shard_map/ppermute | solution.py:895
  157.9 6.9 %near_field.7.refs_4_.refs_0_ = f32[8,256,128]{2,1,0:T(8,128)} custom-call(s32[8,8]{1,0:T(8,128)} %index_ref.17, s32[8,8]{1,0:T(8,128)} %mask_ref.9, bf16[8,8,256,256]{3,2,1,0:T(8,128)(2,1)} %blocks_ref.15, bf16[8,256,128]{2,1,0:T(8,128)(2,1)} %get-tuple-element.140.own_ref), custom_call_target="tpu_custom_call" | custom-call | flops 1073741824 | bytes 8388608 | tf_op jit(solution)/shard_map/near_field/pallas_call | solution.py:116
  164.8 3.5 %vectors.2.refs_0_.refs_5_ = f32[5,8,256,128]{3,2,1,0:T(8,128)} custom-call(f32[64,128]{1,0:T(8,128)S(1)} %get-tuple-element.139.refs_0_.refs_4_, f32[8,256,128]{2,1,0:T(8,128)} %bitcast.11, f32[8,256,128]{2,1,0:T(8,128)} %get-tuple-element.111.refs_6_.refs_2_, f32[8,256,128]{2,1,0:T(8,128)} %get-tuple-element.128.refs_7_.refs_3_, ...), custom_call_target="tpu_custom_call" | custom-call | flops 8388608 | bytes 6291456 | tf_op jit(solution)/shard_map/vectors/pallas_call | solution.py:116
  168.4 6.4 %all-to-all-done.3.recv = bf16[16,336,128]{2,1,0:T(8,128)(2,1)S(1)} async-done(((bf16[16,336,128]{2,1,0:T(8,128)(2,1)}), bf16[16,336,128]{2,1,0:T(8,128)(2,1)S(1)}, u32[]{:S(2)}, u32[]{:S(2)}) %all-to-all-start.3) | async-done | bytes 1376288 | tf_op jit(solution)/shard_map/all_to_all | solution.py:883
  175.7 1.9 collective-permute-start.20
  177.6 5.1 %far_field.7 = (f32[512,128]{1,0:T(8,128)S(1)}, bf16[64,256,256]{2,1,0:T(8,128)(2,1)S(1)}, f32[8,256,128]{2,1,0:T(8,128)S(1)}) custom-call(s32[1]{0:T(128)} %get-tuple-element.85.count_ref, s32[64]{0:T(128)} %copy-done, bf16[16,336,128]{2,1,0:T(8,128)(2,1)S(1)} %all-to-all-done.3.recv, bf16[16,512,256]{2,1,0:T(8,128)(2,1)} %get-tuple-element.84.refs_0_.packed_ref, ...), custom_call_target="tpu_custom_call" | custom-call | flops 536870912 | bytes 4194304 | tf_op jit(solution)/shard_map/far_field/pallas_call | solution.py:116
  182.7 2.1 collective-permute-start.21
  184.8 4.0 %halo_part.7 = (f32[8,256,128]{2,1,0:T(8,128)S(1)}, bf16[8,64,256]{2,1,0:T(8,128)(2,1)S(1)}, bf16[8,256,64]{2,1,0:T(8,128)(2,1)S(1)}, bf16[8,64,64]{2,1,0:T(8,12...) custom-call(s32[1]{0:T(128)} %get-tuple-element.85.count_ref, ...), custom_call_target="tpu_custom_call", output_to_operand_aliasing={{0}: (6, {})} | custom-call | flops 268435456 | bytes 2097152 | tf_op jit(solution)/shard_map/halo_part/pallas_call | solution.py:116
  188.8 2.4 %stage4.1 = (f32[8,256,128]{2,1,0:T(8,128)S(1)}, f32[64,128]{1,0:T(8,128)S(1)}, bf16[16,128]{1,0:T(8,128)(2,1)S(1)}) custom-call(s32[4,16]{1,0:T(4,128)} %bitcast.17, s32[1]{0:T(128)} %bitcast.2.refs_1_.branch, bf16[4,80,128]{2,1,0:T(8,128)(2,1)S(1)} %stack.8.refs_9_.refs_2_, bf16[4,80,128]{2,1,0:T(8,128)(2,1)S(1)} %collective-permute-done.21.refs_3_, ...), custom_call_target="tpu_custom_call" | custom-call | flops 134217728 | bytes 8388608 | tf_op jit(solution)/shard_map/stage4/pallas_call | solution.py:116
  191.6 1.5 collective-permute-start.25
  196.0 2.5 %collective-permute-start.28 = (bf16[16,128]{1,0:T(8,128)(2,1)S(1)}, bf16[16,128]{1,0:T(8,128)(2,1)S(1)}, u32[]{:S(2)}, u32[]{:S(2)}) collective-permute-start(bf16[16,128]{1,0:T(8,128)(2,1)S(1)} %sum_over.2.refs_0_.refs_4_), channel_id=1, source_target_pairs={{0,8},{1,9},{2,10},{3,11},{4,12},{5,13},{6,14},{7,15},{8,0},{9,1},... | collective-permute-start | bytes 12296 | tf_op jit(solution)/shard_map/ppermute | solution.py:545
  198.5 2.0 collective-permute-start.29
  202.0 2.0 collective-permute-start.31
  203.9 2.0 collective-permute-start.32
  206.7 4.6 %collective-permute-start.33 = (bf16[4,16,128]{2,1,0:T(8,128)(2,1)S(1)}, bf16[4,16,128]{2,1,0:T(8,128)(2,1)S(1)}, u32[]{:S(2)}, u32[]{:S(2)}) collective-permute-start(bf16[4,16,128]{2,1,0:T(8,128)(2,1)S(1)} %stack.9.refs_2_), channel_id=1, source_target_pairs={{0,16},{16,0},{32,48},{48,32},{64,80},{80,64},{96,112},{112,96},{1... | collective-permute-start | bytes 49160 | tf_op jit(solution)/shard_map/ppermute | solution.py:381
  212.1 1.7 last_vector.1
  (62 shorter events, 14.5 us)
Async XLA Ops:
  5.0 29.4 %all-to-all-start = ((bf16[16,336,128]{2,1,0:T(8,128)(2,1)}), bf16[16,336,128]{2,1,0:T(8,128)(2,1)S(1)}, u32[]{:S(2)}, u32[]{:S(2)}) async-start(bf16[16,336,128]{2,1,0:T(8,128)(2,1)} %get-tuple-element.82), calls=%async_computation | async-start | bytes 2752512 | tf_op jit(solution)/shard_map/all_to_all | solution.py:883
  13.6 33.5 %collective-permute-start.4 = (bf16[2,256,128]{2,1,0:T(8,128)(2,1)S(1)}, bf16[2,256,128]{2,1,0:T(8,128)(2,1)S(1)}, u32[]{:S(2)}, u32[]{:S(2)}) collective-permute-start(bf16[2,256,128]{2,1,0:T(8,128)(2,1)S(1)} %get-tuple-element.90), channel_id=1, source_target_pairs={{0,1},{1,2},{2,3},{3,4},{4,5},{5,6},{6,7},{7,8},{8,9},{9,10},{10,1... | collective-permute-start | bytes 393224 | tf_op jit(solution)/shard_map/ppermute | solution.py:895
  16.9 30.2 %collective-permute-start.5 = (bf16[2,256,128]{2,1,0:T(8,128)(2,1)S(1)}, bf16[2,256,128]{2,1,0:T(8,128)(2,1)S(1)}, u32[]{:S(2)}, u32[]{:S(2)}) collective-permute-start(bf16[2,256,128]{2,1,0:T(8,128)(2,1)S(1)} %get-tuple-element.91), channel_id=1, source_target_pairs={{1,0},{2,1},{3,2},{4,3},{5,4},{6,5},{7,6},{8,7},{9,8},{10,9},{11,1... | collective-permute-start | bytes 393224 | tf_op jit(solution)/shard_map/ppermute | solution.py:896
  26.9 0.6 copy-start
  34.5 9.9 %collective-permute-start = (bf16[80,128]{1,0:T(8,128)(2,1)S(1)}, bf16[80,128]{1,0:T(8,128)(2,1)S(1)}, u32[]{:S(2)}, u32[]{:S(2)}) collective-permute-start(bf16[80,128]{1,0:T(8,128)(2,1)S(1)} %gather_sum.4.refs_1_.refs_0_), channel_id=1, source_target_pairs={{0,32},{16,48},{32,64},{48,80},{64,96},{80,112},{96,0},{112,16},{1... | collective-permute-start | bytes 61448 | tf_op jit(solution)/shard_map/ppermute | solution.py:370
  35.7 8.7 %collective-permute-start.1 = (bf16[80,128]{1,0:T(8,128)(2,1)S(1)}, bf16[80,128]{1,0:T(8,128)(2,1)S(1)}, u32[]{:S(2)}, u32[]{:S(2)}) collective-permute-start(bf16[80,128]{1,0:T(8,128)(2,1)S(1)} %gather_sum.4.refs_1_.refs_0_), channel_id=1, source_target_pairs={{0,64},{16,80},{32,96},{48,112},{64,0},{80,16},{96,32},{112,48},{1... | collective-permute-start | bytes 61448 | tf_op jit(solution)/shard_map/ppermute | solution.py:370
  38.2 6.2 %collective-permute-start.2 = (bf16[80,128]{1,0:T(8,128)(2,1)S(1)}, bf16[80,128]{1,0:T(8,128)(2,1)S(1)}, u32[]{:S(2)}, u32[]{:S(2)}) collective-permute-start(bf16[80,128]{1,0:T(8,128)(2,1)S(1)} %gather_sum.4.refs_1_.refs_0_), channel_id=1, source_target_pairs={{0,96},{16,112},{32,0},{48,16},{64,32},{80,48},{96,64},{112,80},{1... | collective-permute-start | bytes 61448 | tf_op jit(solution)/shard_map/ppermute | solution.py:370
  44.5 5.6 %collective-permute-start.3 = (bf16[4,80,128]{2,1,0:T(8,128)(2,1)S(1)}, bf16[4,80,128]{2,1,0:T(8,128)(2,1)S(1)}, u32[]{:S(2)}, u32[]{:S(2)}) collective-permute-start(bf16[4,80,128]{2,1,0:T(8,128)(2,1)S(1)} %stack.5.refs_6_.refs_2_), channel_id=1, source_target_pairs={{0,16},{16,0},{32,48},{48,32},{64,80},{80,64},{96,112},{112,96},{1... | collective-permute-start | bytes 245768 | tf_op jit(solution)/shard_map/ppermute | solution.py:381
  54.8 29.1 %all-to-all-start.1 = ((bf16[16,336,128]{2,1,0:T(8,128)(2,1)}), bf16[16,336,128]{2,1,0:T(8,128)(2,1)S(1)}, u32[]{:S(2)}, u32[]{:S(2)}) async-start(bf16[16,336,128]{2,1,0:T(8,128)(2,1)} %get-tuple-element.103), calls=%async_computation.1 | async-start | bytes 2752512 | tf_op jit(solution)/shard_map/all_to_all | solution.py:883
  62.5 31.4 %collective-permute-start.10 = (bf16[2,256,128]{2,1,0:T(8,128)(2,1)S(1)}, bf16[2,256,128]{2,1,0:T(8,128)(2,1)S(1)}, u32[]{:S(2)}, u32[]{:S(2)}) collective-permute-start(bf16[2,256,128]{2,1,0:T(8,128)(2,1)S(1)} %get-tuple-element.108), channel_id=1, source_target_pairs={{0,1},{1,2},{2,3},{3,4},{4,5},{5,6},{6,7},{7,8},{8,9},{9,10},{10,1... | collective-permute-start | bytes 393224 | tf_op jit(solution)/shard_map/ppermute | solution.py:895
  65.8 28.2 %collective-permute-start.11 = (bf16[2,256,128]{2,1,0:T(8,128)(2,1)S(1)}, bf16[2,256,128]{2,1,0:T(8,128)(2,1)S(1)}, u32[]{:S(2)}, u32[]{:S(2)}) collective-permute-start(bf16[2,256,128]{2,1,0:T(8,128)(2,1)S(1)} %get-tuple-element.109), channel_id=1, source_target_pairs={{1,0},{2,1},{3,2},{4,3},{5,4},{6,5},{7,6},{8,7},{9,8},{10,9},{11,1... | collective-permute-start | bytes 393224 | tf_op jit(solution)/shard_map/ppermute | solution.py:896
  84.0 7.8 %collective-permute-start.6 = (bf16[80,128]{1,0:T(8,128)(2,1)S(1)}, bf16[80,128]{1,0:T(8,128)(2,1)S(1)}, u32[]{:S(2)}, u32[]{:S(2)}) collective-permute-start(bf16[80,128]{1,0:T(8,128)(2,1)S(1)} %gather_sum.5.refs_1_.refs_0_), channel_id=1, source_target_pairs={{0,32},{16,48},{32,64},{48,80},{64,96},{80,112},{96,0},{112,16},{1... | collective-permute-start | bytes 61448 | tf_op jit(solution)/shard_map/ppermute | solution.py:370
  84.2 7.6 %collective-permute-start.7 = (bf16[80,128]{1,0:T(8,128)(2,1)S(1)}, bf16[80,128]{1,0:T(8,128)(2,1)S(1)}, u32[]{:S(2)}, u32[]{:S(2)}) collective-permute-start(bf16[80,128]{1,0:T(8,128)(2,1)S(1)} %gather_sum.5.refs_1_.refs_0_), channel_id=1, source_target_pairs={{0,64},{16,80},{32,96},{48,112},{64,0},{80,16},{96,32},{112,48},{1... | collective-permute-start | bytes 61448 | tf_op jit(solution)/shard_map/ppermute | solution.py:370
  84.8 7.0 %collective-permute-start.8 = (bf16[80,128]{1,0:T(8,128)(2,1)S(1)}, bf16[80,128]{1,0:T(8,128)(2,1)S(1)}, u32[]{:S(2)}, u32[]{:S(2)}) collective-permute-start(bf16[80,128]{1,0:T(8,128)(2,1)S(1)} %gather_sum.5.refs_1_.refs_0_), channel_id=1, source_target_pairs={{0,96},{16,112},{32,0},{48,16},{64,32},{80,48},{96,64},{112,80},{1... | collective-permute-start | bytes 61448 | tf_op jit(solution)/shard_map/ppermute | solution.py:370
  91.9 5.4 %collective-permute-start.9 = (bf16[4,80,128]{2,1,0:T(8,128)(2,1)S(1)}, bf16[4,80,128]{2,1,0:T(8,128)(2,1)S(1)}, u32[]{:S(2)}, u32[]{:S(2)}) collective-permute-start(bf16[4,80,128]{2,1,0:T(8,128)(2,1)S(1)} %stack.6.refs_7_.refs_2_), channel_id=1, source_target_pairs={{0,16},{16,0},{32,48},{48,32},{64,80},{80,64},{96,112},{112,96},{1... | collective-permute-start | bytes 245768 | tf_op jit(solution)/shard_map/ppermute | solution.py:381
  102.1 25.9 %all-to-all-start.2 = ((bf16[16,336,128]{2,1,0:T(8,128)(2,1)}), bf16[16,336,128]{2,1,0:T(8,128)(2,1)S(1)}, u32[]{:S(2)}, u32[]{:S(2)}) async-start(bf16[16,336,128]{2,1,0:T(8,128)(2,1)} %get-tuple-element.120), calls=%async_computation.2 | async-start | bytes 2752512 | tf_op jit(solution)/shard_map/all_to_all | solution.py:883
  106.6 33.6 %collective-permute-start.16 = (bf16[2,256,128]{2,1,0:T(8,128)(2,1)S(1)}, bf16[2,256,128]{2,1,0:T(8,128)(2,1)S(1)}, u32[]{:S(2)}, u32[]{:S(2)}) collective-permute-start(bf16[2,256,128]{2,1,0:T(8,128)(2,1)S(1)} %get-tuple-element.125), channel_id=1, source_target_pairs={{0,1},{1,2},{2,3},{3,4},{4,5},{5,6},{6,7},{7,8},{8,9},{9,10},{10,1... | collective-permute-start | bytes 393224 | tf_op jit(solution)/shard_map/ppermute | solution.py:895
  109.9 30.3 %collective-permute-start.17 = (bf16[2,256,128]{2,1,0:T(8,128)(2,1)S(1)}, bf16[2,256,128]{2,1,0:T(8,128)(2,1)S(1)}, u32[]{:S(2)}, u32[]{:S(2)}) collective-permute-start(bf16[2,256,128]{2,1,0:T(8,128)(2,1)S(1)} %get-tuple-element.126), channel_id=1, source_target_pairs={{1,0},{2,1},{3,2},{4,3},{5,4},{6,5},{7,6},{8,7},{9,8},{10,9},{11,1... | collective-permute-start | bytes 393224 | tf_op jit(solution)/shard_map/ppermute | solution.py:896
  128.1 9.7 %collective-permute-start.12 = (bf16[80,128]{1,0:T(8,128)(2,1)S(1)}, bf16[80,128]{1,0:T(8,128)(2,1)S(1)}, u32[]{:S(2)}, u32[]{:S(2)}) collective-permute-start(bf16[80,128]{1,0:T(8,128)(2,1)S(1)} %gather_sum.6.refs_1_.refs_0_), channel_id=1, source_target_pairs={{0,32},{16,48},{32,64},{48,80},{64,96},{80,112},{96,0},{112,16},{1... | collective-permute-start | bytes 61448 | tf_op jit(solution)/shard_map/ppermute | solution.py:370
  128.8 9.1 %collective-permute-start.13 = (bf16[80,128]{1,0:T(8,128)(2,1)S(1)}, bf16[80,128]{1,0:T(8,128)(2,1)S(1)}, u32[]{:S(2)}, u32[]{:S(2)}) collective-permute-start(bf16[80,128]{1,0:T(8,128)(2,1)S(1)} %gather_sum.6.refs_1_.refs_0_), channel_id=1, source_target_pairs={{0,64},{16,80},{32,96},{48,112},{64,0},{80,16},{96,32},{112,48},{1... | collective-permute-start | bytes 61448 | tf_op jit(solution)/shard_map/ppermute | solution.py:370
  130.7 7.1 %collective-permute-start.14 = (bf16[80,128]{1,0:T(8,128)(2,1)S(1)}, bf16[80,128]{1,0:T(8,128)(2,1)S(1)}, u32[]{:S(2)}, u32[]{:S(2)}) collective-permute-start(bf16[80,128]{1,0:T(8,128)(2,1)S(1)} %gather_sum.6.refs_1_.refs_0_), channel_id=1, source_target_pairs={{0,96},{16,112},{32,0},{48,16},{64,32},{80,48},{96,64},{112,80},{1... | collective-permute-start | bytes 61448 | tf_op jit(solution)/shard_map/ppermute | solution.py:370
  137.9 6.0 %collective-permute-start.15 = (bf16[4,80,128]{2,1,0:T(8,128)(2,1)S(1)}, bf16[4,80,128]{2,1,0:T(8,128)(2,1)S(1)}, u32[]{:S(2)}, u32[]{:S(2)}) collective-permute-start(bf16[4,80,128]{2,1,0:T(8,128)(2,1)S(1)} %stack.7.refs_8_.refs_2_), channel_id=1, source_target_pairs={{0,16},{16,0},{32,48},{48,32},{64,80},{80,64},{96,112},{112,96},{1... | collective-permute-start | bytes 245768 | tf_op jit(solution)/shard_map/ppermute | solution.py:381
  148.9 25.9 %all-to-all-start.3 = ((bf16[16,336,128]{2,1,0:T(8,128)(2,1)}), bf16[16,336,128]{2,1,0:T(8,128)(2,1)S(1)}, u32[]{:S(2)}, u32[]{:S(2)}) async-start(bf16[16,336,128]{2,1,0:T(8,128)(2,1)} %get-tuple-element.138), calls=%async_computation.3 | async-start | bytes 2752512 | tf_op jit(solution)/shard_map/all_to_all | solution.py:883
  153.4 31.4 %collective-permute-start.22 = (bf16[2,256,128]{2,1,0:T(8,128)(2,1)S(1)}, bf16[2,256,128]{2,1,0:T(8,128)(2,1)S(1)}, u32[]{:S(2)}, u32[]{:S(2)}) collective-permute-start(bf16[2,256,128]{2,1,0:T(8,128)(2,1)S(1)} %get-tuple-element.143), channel_id=1, source_target_pairs={{0,1},{1,2},{2,3},{3,4},{4,5},{5,6},{6,7},{7,8},{8,9},{9,10},{10,1... | collective-permute-start | bytes 393224 | tf_op jit(solution)/shard_map/ppermute | solution.py:895
  156.6 28.2 %collective-permute-start.23 = (bf16[2,256,128]{2,1,0:T(8,128)(2,1)S(1)}, bf16[2,256,128]{2,1,0:T(8,128)(2,1)S(1)}, u32[]{:S(2)}, u32[]{:S(2)}) collective-permute-start(bf16[2,256,128]{2,1,0:T(8,128)(2,1)S(1)} %get-tuple-element.144), channel_id=1, source_target_pairs={{1,0},{2,1},{3,2},{4,3},{5,4},{6,5},{7,6},{8,7},{9,8},{10,9},{11,1... | collective-permute-start | bytes 393224 | tf_op jit(solution)/shard_map/ppermute | solution.py:896
  174.9 7.8 %collective-permute-start.18 = (bf16[80,128]{1,0:T(8,128)(2,1)S(1)}, bf16[80,128]{1,0:T(8,128)(2,1)S(1)}, u32[]{:S(2)}, u32[]{:S(2)}) collective-permute-start(bf16[80,128]{1,0:T(8,128)(2,1)S(1)} %gather_sum.7.refs_1_.refs_0_), channel_id=1, source_target_pairs={{0,32},{16,48},{32,64},{48,80},{64,96},{80,112},{96,0},{112,16},{1... | collective-permute-start | bytes 61448 | tf_op jit(solution)/shard_map/ppermute | solution.py:370
  174.9 7.8 %collective-permute-start.19 = (bf16[80,128]{1,0:T(8,128)(2,1)S(1)}, bf16[80,128]{1,0:T(8,128)(2,1)S(1)}, u32[]{:S(2)}, u32[]{:S(2)}) collective-permute-start(bf16[80,128]{1,0:T(8,128)(2,1)S(1)} %gather_sum.7.refs_1_.refs_0_), channel_id=1, source_target_pairs={{0,64},{16,80},{32,96},{48,112},{64,0},{80,16},{96,32},{112,48},{1... | collective-permute-start | bytes 61448 | tf_op jit(solution)/shard_map/ppermute | solution.py:370
  175.7 7.0 %collective-permute-start.20 = (bf16[80,128]{1,0:T(8,128)(2,1)S(1)}, bf16[80,128]{1,0:T(8,128)(2,1)S(1)}, u32[]{:S(2)}, u32[]{:S(2)}) collective-permute-start(bf16[80,128]{1,0:T(8,128)(2,1)S(1)} %gather_sum.7.refs_1_.refs_0_), channel_id=1, source_target_pairs={{0,96},{16,112},{32,0},{48,16},{64,32},{80,48},{96,64},{112,80},{1... | collective-permute-start | bytes 61448 | tf_op jit(solution)/shard_map/ppermute | solution.py:370
  182.7 6.1 %collective-permute-start.21 = (bf16[4,80,128]{2,1,0:T(8,128)(2,1)S(1)}, bf16[4,80,128]{2,1,0:T(8,128)(2,1)S(1)}, u32[]{:S(2)}, u32[]{:S(2)}) collective-permute-start(bf16[4,80,128]{2,1,0:T(8,128)(2,1)S(1)} %stack.8.refs_9_.refs_2_), channel_id=1, source_target_pairs={{0,16},{16,0},{32,48},{48,32},{64,80},{80,64},{96,112},{112,96},{1... | collective-permute-start | bytes 245768 | tf_op jit(solution)/shard_map/ppermute | solution.py:381
  191.2 3.9 %collective-permute-start.24 = (bf16[16,128]{1,0:T(8,128)(2,1)S(1)}, bf16[16,128]{1,0:T(8,128)(2,1)S(1)}, u32[]{:S(2)}, u32[]{:S(2)}) collective-permute-start(bf16[16,128]{1,0:T(8,128)(2,1)S(1)} %get-tuple-element.158.refs_0_), channel_id=1, source_target_pairs={{0,1},{1,2},{2,3},{3,0},{4,5},{5,6},{6,7},{7,4},{8,9},{9,10},{10,1... | collective-permute-start | bytes 12296 | tf_op jit(solution)/shard_map/ppermute | solution.py:545
  191.6 4.0 %collective-permute-start.25 = (bf16[16,128]{1,0:T(8,128)(2,1)S(1)}, bf16[16,128]{1,0:T(8,128)(2,1)S(1)}, u32[]{:S(2)}, u32[]{:S(2)}) collective-permute-start(bf16[16,128]{1,0:T(8,128)(2,1)S(1)} %get-tuple-element.158.refs_0_), channel_id=1, source_target_pairs={{0,2},{1,3},{2,0},{3,1},{4,6},{5,7},{6,4},{7,5},{8,10},{9,11},{10,... | collective-permute-start | bytes 12296 | tf_op jit(solution)/shard_map/ppermute | solution.py:545
  193.0 2.9 %collective-permute-start.26 = (bf16[16,128]{1,0:T(8,128)(2,1)S(1)}, bf16[16,128]{1,0:T(8,128)(2,1)S(1)}, u32[]{:S(2)}, u32[]{:S(2)}) collective-permute-start(bf16[16,128]{1,0:T(8,128)(2,1)S(1)} %get-tuple-element.158.refs_0_), channel_id=1, source_target_pairs={{0,3},{1,0},{2,1},{3,2},{4,7},{5,4},{6,5},{7,6},{8,11},{9,8},{10,9... | collective-permute-start | bytes 12296 | tf_op jit(solution)/shard_map/ppermute | solution.py:545
  195.9 4.6 %collective-permute-start.27 = (bf16[16,128]{1,0:T(8,128)(2,1)S(1)}, bf16[16,128]{1,0:T(8,128)(2,1)S(1)}, u32[]{:S(2)}, u32[]{:S(2)}) collective-permute-start(bf16[16,128]{1,0:T(8,128)(2,1)S(1)} %sum_over.2.refs_0_.refs_4_), channel_id=1, source_target_pairs={{0,4},{1,5},{2,6},{3,7},{4,8},{5,9},{6,10},{7,11},{8,12},{9,13},{1... | collective-permute-start | bytes 12296 | tf_op jit(solution)/shard_map/ppermute | solution.py:545
  196.0 4.5 %collective-permute-start.28 = (bf16[16,128]{1,0:T(8,128)(2,1)S(1)}, bf16[16,128]{1,0:T(8,128)(2,1)S(1)}, u32[]{:S(2)}, u32[]{:S(2)}) collective-permute-start(bf16[16,128]{1,0:T(8,128)(2,1)S(1)} %sum_over.2.refs_0_.refs_4_), channel_id=1, source_target_pairs={{0,8},{1,9},{2,10},{3,11},{4,12},{5,13},{6,14},{7,15},{8,0},{9,1},... | collective-permute-start | bytes 12296 | tf_op jit(solution)/shard_map/ppermute | solution.py:545
  198.5 2.8 %collective-permute-start.29 = (bf16[16,128]{1,0:T(8,128)(2,1)S(1)}, bf16[16,128]{1,0:T(8,128)(2,1)S(1)}, u32[]{:S(2)}, u32[]{:S(2)}) collective-permute-start(bf16[16,128]{1,0:T(8,128)(2,1)S(1)} %sum_over.2.refs_0_.refs_4_), channel_id=1, source_target_pairs={{0,12},{1,13},{2,14},{3,15},{4,0},{5,1},{6,2},{7,3},{8,4},{9,5},{1... | collective-permute-start | bytes 12296 | tf_op jit(solution)/shard_map/ppermute | solution.py:545
  201.3 4.6 %collective-permute-start.30 = (bf16[16,128]{1,0:T(8,128)(2,1)S(1)}, bf16[16,128]{1,0:T(8,128)(2,1)S(1)}, u32[]{:S(2)}, u32[]{:S(2)}) collective-permute-start(bf16[16,128]{1,0:T(8,128)(2,1)S(1)} %sum_over.3.refs_0_.refs_4_), channel_id=1, source_target_pairs={{0,32},{16,48},{32,64},{48,80},{64,96},{80,112},{96,0},{112,16},{1... | collective-permute-start | bytes 12296 | tf_op jit(solution)/shard_map/ppermute | solution.py:370
  202.0 4.0 %collective-permute-start.31 = (bf16[16,128]{1,0:T(8,128)(2,1)S(1)}, bf16[16,128]{1,0:T(8,128)(2,1)S(1)}, u32[]{:S(2)}, u32[]{:S(2)}) collective-permute-start(bf16[16,128]{1,0:T(8,128)(2,1)S(1)} %sum_over.3.refs_0_.refs_4_), channel_id=1, source_target_pairs={{0,64},{16,80},{32,96},{48,112},{64,0},{80,16},{96,32},{112,48},{1... | collective-permute-start | bytes 12296 | tf_op jit(solution)/shard_map/ppermute | solution.py:370
  203.9 2.7 %collective-permute-start.32 = (bf16[16,128]{1,0:T(8,128)(2,1)S(1)}, bf16[16,128]{1,0:T(8,128)(2,1)S(1)}, u32[]{:S(2)}, u32[]{:S(2)}) collective-permute-start(bf16[16,128]{1,0:T(8,128)(2,1)S(1)} %sum_over.3.refs_0_.refs_4_), channel_id=1, source_target_pairs={{0,96},{16,112},{32,0},{48,16},{64,32},{80,48},{96,64},{112,80},{1... | collective-permute-start | bytes 12296 | tf_op jit(solution)/shard_map/ppermute | solution.py:370
  206.7 5.4 %collective-permute-start.33 = (bf16[4,16,128]{2,1,0:T(8,128)(2,1)S(1)}, bf16[4,16,128]{2,1,0:T(8,128)(2,1)S(1)}, u32[]{:S(2)}, u32[]{:S(2)}) collective-permute-start(bf16[4,16,128]{2,1,0:T(8,128)(2,1)S(1)} %stack.9.refs_2_), channel_id=1, source_target_pairs={{0,16},{16,0},{32,48},{48,32},{64,80},{80,64},{96,112},{112,96},{1... | collective-permute-start | bytes 49160 | tf_op jit(solution)/shard_map/ppermute | solution.py:381

commit v6 on v5

--- a/solution.py
+++ b/solution.py
@@ -164,6 +164,7 @@
     sources, _, width = packed.shape
     slots = width // rank
     near_entries = index_ref.shape[1]
+    side = lax.broadcasted_iota(jnp.int32, (1, 2 * rank), 1) // rank
 
     def fetch(leaf):
         return [pltpu.make_async_copy(far_ref.at[leaf], blocks.at[leaf], arrived.at[leaf])]
@@ -175,11 +176,14 @@
     def work(leaf):
         total[...] = jnp.zeros(total.shape, F32)
         for f in range(entries):
-            weight = mask_ref[leaf, f].astype(F32)
-            total[slot_ref[leaf, f]] += blocks[leaf, f].astype(F32) * weight
+            slot = slot_ref[leaf, f]
+            block = blocks[leaf, f].astype(F32)
+            weight = jnp.where(side == slot % 2, mask_ref[leaf, f], 0).astype(F32)
+            total[slot // 2] += jnp.concatenate([block, block], axis=1) * weight
         rows = slab(leaf, rank)
+        pairs = slots // 2
         for source in range(sources):
-            sides = [total[source * slots + s] for s in range(slots)]
+            sides = [total[source * pairs + s] for s in range(pairs)]
             packed[source, rows] = jnp.concatenate(sides, axis=1).astype(BF16)
         store(leaf).start()
 
@@ -254,7 +258,7 @@
         ],
         [
             pltpu.VMEM(far_blocks.shape, BF16),
-            pltpu.VMEM((inner * slots, rank, rank), F32),
+            pltpu.VMEM((inner * slots // 2, rank, 2 * rank), F32),
             pltpu.VMEM(shape, BF16),
             pltpu.VMEM(basis.shape, BF16),
             pltpu.VMEM(transfer.shape, BF16),
@@ -417,7 +421,18 @@
         block(i).wait()
         return carry
 
+    loads = [
+        pltpu.make_async_copy(source, target, loaded.at[i])
+        for i, (source, target) in enumerate(zip(sources, targets))
+    ]
+
     def work(i):
+        @pl.when(i == 0)
+        def _():
+            lax.fori_loop(0, count, ask, 0)
+            for copy in loads:
+                copy.start()
+
         term = None
         for j in range(share):
             source = i * share + j
@@ -432,15 +447,8 @@
         def _():
             far[...] += term
 
-    loads = [
-        pltpu.make_async_copy(source, target, loaded.at[i])
-        for i, (source, target) in enumerate(zip(sources, targets))
-    ]
     begin, run = windowed(CHUNKS, CHUNKS, fetch, work)
     begin()
-    lax.fori_loop(0, count, ask, 0)
-    for copy in loads:
-        copy.start()
     run()
     lax.fori_loop(0, count, have, 0)
     for copy in loads:
@@ -577,25 +585,30 @@
         basis, transfer, vectors, came = take(4)
     else:
         ups, result, coef, combined = take(4)
+    streamed = zs if sends and not first else []
+    if streamed:
+        vectors = take(1)[0]
 
     leaves, rank, size = basis.shape
     group = leaves // CHUNKS
 
     def fetch(i):
-        if not first:
-            return []
         some = slab(i, group)
-        return [pltpu.make_async_copy(z_any.at[some], vectors.at[some], arrived.at[i])]
-
-    def stores(i):
-        some = slab(i, group)
+        if first:
+            return [pltpu.make_async_copy(z_any.at[some], vectors.at[some], arrived.at[0, i])]
+        return [
+            pltpu.make_async_copy(z.at[some], vectors.at[l, some], arrived.at[l, i])
+            for l, z in enumerate(streamed)
+        ]
+
+    def stores(leaf):
         pairs = []
         if not first:
-            pairs.append((result.at[some], z_any.at[some]))
+            pairs.append((result.at[leaf], z_any.at[leaf]))
         if sends:
-            pairs.append((coarse.at[some], coarse_any.at[some]))
+            pairs.append((coarse.at[leaf], coarse_any.at[leaf]))
         return [
-            pltpu.make_async_copy(source, target, left.at[n, i])
+            pltpu.make_async_copy(source, target, left.at[n, leaf])
             for n, (source, target) in enumerate(pairs)
         ]
 
@@ -606,7 +619,7 @@
                 others = []
                 z = vectors[leaf]
             else:
-                others = [ref[leaf] for ref in zs]
+                others = [vectors[l, leaf] if streamed else zs[l][leaf] for l in range(k)]
                 z = near[leaf] + dot(turned[leaf], combined[slab(leaf, rank)])
                 for l in range(m):
                     z = z - coef[l : l + 1, :] * others[l + 1]
@@ -618,8 +631,9 @@
                 skeletons[slab(leaf, rank)] = dot(basis[leaf], rounded).astype(BF16)
             for l, vector in enumerate(others + [z]):
                 sums[l] += jnp.sum((z * vector).reshape(size // 8, 8, z.shape[1]), axis=0)
-        for copy in stores(i):
-            copy.start()
+        for j in range(group):
+            for copy in stores(i * group + j):
+                copy.start()
 
     begin, run = windowed(CHUNKS, CHUNKS, fetch, work)
     if first:
@@ -674,8 +688,8 @@
             send[r, (slots + 1) * rank :] = dots
     else:
         send[...] = dots
-    for i in range(CHUNKS):
-        for copy in stores(i):
+    for leaf in range(leaves):
+        for copy in stores(leaf):
             copy.wait()
     if sends:
         for copy in halos:
@@ -700,7 +714,7 @@
         specs += [HBM] * 3
     else:
         args += later
-        specs += [VMEM] * len(later)
+        specs += [VMEM] * (len(later) - k) + [HBM if sends else VMEM] * k
         get("z", tall, F32, HBM if sends else VMEM)
     get("state", (STATE_ROWS, columns), F32, VMEM)
     rows = (slots + 1) * rank + DOT_ROWS
@@ -713,8 +727,8 @@
     scratch = [
         pltpu.VMEM((STEPS + 1, 8, columns), F32),
         pltpu.VMEM((DOT_ROWS, columns), F32),
-        semaphores(CHUNKS),
-        semaphores(2, CHUNKS),
+        semaphores(max(k, 1), CHUNKS),
+        semaphores(2, leaves),
     ]
     if sends:
         scratch += [
@@ -737,6 +751,8 @@
             pltpu.VMEM((8, columns), F32),
             pltpu.VMEM((leaves * rank, columns), BF16),
         ]
+        if sends:
+            scratch.append(pltpu.VMEM((k,) + tall, F32))
     results = call(
         functools.partial(stage_kernel, k=k, points=points),
         args,
@@ -903,10 +919,12 @@
         local_far, blocks, (near,) = far_field(listed, recv, packed, near_blocks, (near,), summed)
 
         def between(column):
-            held = (basis, turned, transfer, lifting, top, *zs)
+            held = (basis, turned, transfer, lifting, top) + (tuple(zs) if k == STEPS else ())
             return halo_part(listed, near_index, blocks, before, after, near, held, column)
 
         column, other, (near, *held) = over_branches(summed, outer, local_far, between)
+        if k < STEPS:
+            held = held + zs
         later = [column, other, state, local_far, near, *held]
         out = stage(k, points, wanted, branch, zs[0], basis, transfer, later)
         state = out["state"]

time: 216 us -> 219 us (1.014)
  Pallas kernels: 98.5 us -> 103 us
  starting transfers between devices: 84.1 us -> 81.9 us
    pallas_call x32, Pallas kernels: 98.5 us -> 103 us  [call(): pl.pallas_call(kernel, in_specs=list(in_specs), out_specs=[spec for _, _,...]
where the time goes in v6:
time: 219 us; the launch traced here: 216 us
  Pallas kernels  103 us (47%)
  starting transfers between devices  81.9 us (37%)
  waiting for transfers between devices  29.7 us (14%)
    pallas_call x32, Pallas kernels, call(): pl.pallas_call(kernel, in_specs=list(in_specs), out_specs=[spec for _, _,...  103 us
    all_to_all x4, waiting for transfers between devices, exchange(): return lax.all_to_all(array, axis, split_axis=0, concat_axis=0, tiled=True)  26.5 us
    all_to_all x4, starting transfers between devices, exchange(): return lax.all_to_all(array, axis, split_axis=0, concat_axis=0, tiled=True)  23.6 us
    ppermute x15, starting transfers between devices, over_branches(): lax.ppermute(summed, 'outer', shift)  18.1 us
    ppermute x5, starting transfers between devices, over_branches(): other = lax.ppermute(column, 'outer', [(o, o ^ 1) for o in range(outer)])  14.7 us
    ppermute x4, starting transfers between devices, shards(): before = lax.ppermute(out['high'], 'inner', up_pairs)  12.9 us
    ppermute x6, starting transfers between devices, sum_over(): lax.ppermute(dots, axis, [(i, moved(i, j)) for i in range(size)])  7.35 us
    ppermute x4, starting transfers between devices, shards(): after = lax.ppermute(out['low'], 'inner', down_pairs)  5.17 us
  transfers between devices with their start and end apart: 38, of which 8 were waited for; matrix products, arithmetic and copies ran while one was open for 0% of the time, Pallas kernels for 35%

profile of v6, /device:TPU:1, one launch (start us, length us, event | category | flops | bytes accessed | tf_op | source)
XLA Modules:
  0.0 216.4 jit_solution(12489092520775465721)
XLA Ops:
  0.6 4.4 %stage0.1 = (f32[64,128]{1,0:T(8,128)S(1)}, bf16[16,336,128]{2,1,0:T(8,128)(2,1)}, bf16[8,256,128]{2,1,0:T(8,128)(2,1)}, bf16[2,256,128]{2,1,0:T(8,128)(2,1)S(1)}, bf16[2,256,128]{2,1,0:T(8,128)(2,1)S(1)}) custom-call(s32[4,16]{1,0:T(4,128)} %bitcast.13, s32[1]{0:T(128)} %bitcast.2.refs_1_.branch, f32[8,256,128]{2,1,0:T(8,128)} %bitcast.7, ...), custom_call_target="tpu_custom_call" | custom-call | flops 134217728 | bytes 4194304 | tf_op jit(solution)/shard_map/stage0/pallas_call | solution.py:116
  5.1 8.6 %all-to-all-start = ((bf16[16,336,128]{2,1,0:T(8,128)(2,1)}), bf16[16,336,128]{2,1,0:T(8,128)(2,1)S(1)}, u32[]{:S(2)}, u32[]{:S(2)}) async-start(bf16[16,336,128]{2,1,0:T(8,128)(2,1)} %get-tuple-element.76), calls=%async_computation | async-start | bytes 2752512 | tf_op jit(solution)/shard_map/all_to_all | solution.py:899
  13.7 3.3 %collective-permute-start.4 = (bf16[2,256,128]{2,1,0:T(8,128)(2,1)S(1)}, bf16[2,256,128]{2,1,0:T(8,128)(2,1)S(1)}, u32[]{:S(2)}, u32[]{:S(2)}) collective-permute-start(bf16[2,256,128]{2,1,0:T(8,128)(2,1)S(1)} %get-tuple-element.84), channel_id=1, source_target_pairs={{0,1},{1,2},{2,3},{3,4},{4,5},{5,6},{6,7},{7,8},{8,9},{9,10},{10,1... | collective-permute-start | bytes 393224 | tf_op jit(solution)/shard_map/ppermute | solution.py:911
  16.9 1.3 collective-permute-start.5
  18.2 8.5 %pack.1 = (bf16[16,512,256]{2,1,0:T(8,128)(2,1)}, s32[1]{0:T(128)}, s32[64]{0:T(128)S(1)}, bf16[8,256,64]{2,1,0:T(8,128)(2,1)}, bf16[64,512]{1,0:T(8,128)(2,1)}, /*index=5*/bf16[64,512]{1,0:T(8,128)(2,1)}) custom-call(s32[1]{0:T(128)} %bitcast.2.refs_1_.branch, s32[8,48]{1,0:T(8,128)} %mask_ref.5, s32[8,48]{1,0:T(8,128)} %slot_ref.1, s32[8,8]{1,0:T(8,128)} %index_ref.17, ...), custom_call_target="tpu_custom_call" | custom-call | bytes 10485760 | tf_op jit(solution)/shard_map/pack/pallas_call | solution.py:116
  27.3 6.9 %near_field.4.refs_0_ = f32[8,256,128]{2,1,0:T(8,128)} custom-call(s32[8,8]{1,0:T(8,128)} %index_ref.17, s32[8,8]{1,0:T(8,128)} %mask_ref.9, bf16[8,8,256,256]{3,2,1,0:T(8,128)(2,1)} %blocks_ref.15, bf16[8,256,128]{2,1,0:T(8,128)(2,1)} %get-tuple-element.77.own_ref, bf16[16,512,256]{2,1,0:T(8,128)(2,1)} %get-tuple-element.78.refs_0_.packed_ref), custom_call_target="tpu_custom_call" | custom-call | flops 1073741824 | bytes 8388608 | tf_op jit(solution)/shard_map/near_field/pallas_call | solution.py:116
  35.5 2.5 %collective-permute-start.1 = (bf16[80,128]{1,0:T(8,128)(2,1)S(1)}, bf16[80,128]{1,0:T(8,128)(2,1)S(1)}, u32[]{:S(2)}, u32[]{:S(2)}) collective-permute-start(bf16[80,128]{1,0:T(8,128)(2,1)S(1)} %gather_sum.4.refs_1_.refs_0_), channel_id=1, source_target_pairs={{0,64},{16,80},{32,96},{48,112},{64,0},{80,16},{96,32},{112,48},{1... | collective-permute-start | bytes 61448 | tf_op jit(solution)/shard_map/ppermute | solution.py:374
  39.1 5.4 %far_field.4 = (f32[512,128]{1,0:T(8,128)S(1)}, bf16[64,256,256]{2,1,0:T(8,128)(2,1)S(1)}, f32[8,256,128]{2,1,0:T(8,128)S(1)}) custom-call(s32[1]{0:T(128)} %get-tuple-element.79.count_ref, s32[64]{0:T(128)} %copy-done, bf16[16,336,128]{2,1,0:T(8,128)(2,1)S(1)} %all-to-all-done.recv, bf16[16,512,256]{2,1,0:T(8,128)(2,1)} %get-tuple-element.78.refs_0_.packed_ref, ...), custom_call_target="tpu_custom_call" | custom-call | flops 536870912 | bytes 4194304 | tf_op jit(solution)/shard_map/far_field/pallas_call | solution.py:116
  44.6 2.7 %collective-permute-start.3 = (bf16[4,80,128]{2,1,0:T(8,128)(2,1)S(1)}, bf16[4,80,128]{2,1,0:T(8,128)(2,1)S(1)}, u32[]{:S(2)}, u32[]{:S(2)}) collective-permute-start(bf16[4,80,128]{2,1,0:T(8,128)(2,1)S(1)} %stack.5.refs_5_.refs_2_), channel_id=1, source_target_pairs={{0,16},{16,0},{32,48},{48,32},{64,80},{80,64},{96,112},{112,96},{1... | collective-permute-start | bytes 245768 | tf_op jit(solution)/shard_map/ppermute | solution.py:385
  47.2 2.8 %halo_part.4 = (f32[8,256,128]{2,1,0:T(8,128)S(1)}, bf16[8,64,256]{2,1,0:T(8,128)(2,1)S(1)}, bf16[8,256,64]{2,1,0:T(8,128)(2,1)S(1)}, bf16[8,64,64]{2,1,0:T(8,12...) custom-call(s32[1]{0:T(128)} %get-tuple-element.79.count_ref, ...), custom_call_target="tpu_custom_call", output_to_operand_aliasing={{0}: (6, {})} | custom-call | flops 268435456 | bytes 2097152 | tf_op jit(solution)/shard_map/halo_part/pallas_call | solution.py:116
  50.1 5.6 %stage1.1 = (f32[8,256,128]{2,1,0:T(8,128)}, f32[64,128]{1,0:T(8,128)S(1)}, bf16[16,336,128]{2,1,0:T(8,128)(2,1)}, bf16[8,256,128]{2,1,0:T(8,128)(2,1)}, bf16[2,...) custom-call(s32[4,16]{1,0:T(4,128)} %bitcast.14, s32[1]{0:T(128)} %bitcast.2.refs_1_.branch, ...), custom_call_target="tpu_custom_call" | custom-call | flops 134217728 | bytes 5242880 | tf_op jit(solution)/shard_map/stage1/pallas_call | solution.py:116
  55.7 7.1 %all-to-all-start.1 = ((bf16[16,336,128]{2,1,0:T(8,128)(2,1)}), bf16[16,336,128]{2,1,0:T(8,128)(2,1)S(1)}, u32[]{:S(2)}, u32[]{:S(2)}) async-start(bf16[16,336,128]{2,1,0:T(8,128)(2,1)} %get-tuple-element.96), calls=%async_computation.1 | async-start | bytes 2752512 | tf_op jit(solution)/shard_map/all_to_all | solution.py:899
  62.8 3.3 %collective-permute-start.10 = (bf16[2,256,128]{2,1,0:T(8,128)(2,1)S(1)}, bf16[2,256,128]{2,1,0:T(8,128)(2,1)S(1)}, u32[]{:S(2)}, u32[]{:S(2)}) collective-permute-start(bf16[2,256,128]{2,1,0:T(8,128)(2,1)S(1)} %get-tuple-element.101), channel_id=1, source_target_pairs={{0,1},{1,2},{2,3},{3,4},{4,5},{5,6},{6,7},{7,8},{8,9},{9,10},{10,1... | collective-permute-start | bytes 393224 | tf_op jit(solution)/shard_map/ppermute | solution.py:911
  66.0 1.3 collective-permute-start.11
  67.3 6.9 %near_field.5.refs_0_ = f32[8,256,128]{2,1,0:T(8,128)} custom-call(s32[8,8]{1,0:T(8,128)} %index_ref.17, s32[8,8]{1,0:T(8,128)} %mask_ref.9, bf16[8,8,256,256]{3,2,1,0:T(8,128)(2,1)} %blocks_ref.15, bf16[8,256,128]{2,1,0:T(8,128)(2,1)} %get-tuple-element.97.own_ref), custom_call_target="tpu_custom_call" | custom-call | flops 1073741824 | bytes 8388608 | tf_op jit(solution)/shard_map/near_field/pallas_call | solution.py:116
  74.2 9.8 %all-to-all-done.1.recv = bf16[16,336,128]{2,1,0:T(8,128)(2,1)S(1)} async-done(((bf16[16,336,128]{2,1,0:T(8,128)(2,1)}), bf16[16,336,128]{2,1,0:T(8,128)(2,1)S(1)}, u32[]{:S(2)}, u32[]{:S(2)}) %all-to-all-start.1) | async-done | bytes 1376288 | tf_op jit(solution)/shard_map/all_to_all | solution.py:899
  85.2 1.8 collective-permute-start.8
  86.9 5.4 %far_field.5 = (f32[512,128]{1,0:T(8,128)S(1)}, bf16[64,256,256]{2,1,0:T(8,128)(2,1)S(1)}, f32[8,256,128]{2,1,0:T(8,128)S(1)}) custom-call(s32[1]{0:T(128)} %get-tuple-element.79.count_ref, s32[64]{0:T(128)} %copy-done, bf16[16,336,128]{2,1,0:T(8,128)(2,1)S(1)} %all-to-all-done.1.recv, bf16[16,512,256]{2,1,0:T(8,128)(2,1)} %get-tuple-element.78.refs_0_.packed_ref, ...), custom_call_target="tpu_custom_call" | custom-call | flops 536870912 | bytes 4194304 | tf_op jit(solution)/shard_map/far_field/pallas_call | solution.py:116
  92.4 2.1 collective-permute-start.9
  94.5 2.8 %halo_part.5 = (f32[8,256,128]{2,1,0:T(8,128)S(1)}, bf16[8,64,256]{2,1,0:T(8,128)(2,1)S(1)}, bf16[8,256,64]{2,1,0:T(8,128)(2,1)S(1)}, bf16[8,64,64]{2,1,0:T(8,12...) custom-call(s32[1]{0:T(128)} %get-tuple-element.79.count_ref, ...), custom_call_target="tpu_custom_call", output_to_operand_aliasing={{0}: (6, {})} | custom-call | flops 268435456 | bytes 2097152 | tf_op jit(solution)/shard_map/halo_part/pallas_call | solution.py:116
  97.3 5.9 %stage2.1 = (f32[8,256,128]{2,1,0:T(8,128)}, f32[64,128]{1,0:T(8,128)S(1)}, bf16[16,336,128]{2,1,0:T(8,128)(2,1)}, bf16[8,256,128]{2,1,0:T(8,128)(2,1)}, bf16[2,...) custom-call(s32[4,16]{1,0:T(4,128)} %bitcast.15, s32[1]{0:T(128)} %bitcast.2.refs_1_.branch, ...), custom_call_target="tpu_custom_call" | custom-call | flops 134217728 | bytes 6291456 | tf_op jit(solution)/shard_map/stage2/pallas_call | solution.py:116
  103.3 4.2 %all-to-all-start.2 = ((bf16[16,336,128]{2,1,0:T(8,128)(2,1)}), bf16[16,336,128]{2,1,0:T(8,128)(2,1)S(1)}, u32[]{:S(2)}, u32[]{:S(2)}) async-start(bf16[16,336,128]{2,1,0:T(8,128)(2,1)} %get-tuple-element.111), calls=%async_computation.2 | async-start | bytes 2752512 | tf_op jit(solution)/shard_map/all_to_all | solution.py:899
  107.5 3.3 %collective-permute-start.16 = (bf16[2,256,128]{2,1,0:T(8,128)(2,1)S(1)}, bf16[2,256,128]{2,1,0:T(8,128)(2,1)S(1)}, u32[]{:S(2)}, u32[]{:S(2)}) collective-permute-start(bf16[2,256,128]{2,1,0:T(8,128)(2,1)S(1)} %get-tuple-element.116), channel_id=1, source_target_pairs={{0,1},{1,2},{2,3},{3,4},{4,5},{5,6},{6,7},{7,8},{8,9},{9,10},{10,1... | collective-permute-start | bytes 393224 | tf_op jit(solution)/shard_map/ppermute | solution.py:911
  110.7 1.3 collective-permute-start.17
  112.0 6.9 %near_field.6.refs_0_ = f32[8,256,128]{2,1,0:T(8,128)} custom-call(s32[8,8]{1,0:T(8,128)} %index_ref.17, s32[8,8]{1,0:T(8,128)} %mask_ref.9, bf16[8,8,256,256]{3,2,1,0:T(8,128)(2,1)} %blocks_ref.15, bf16[8,256,128]{2,1,0:T(8,128)(2,1)} %get-tuple-element.112.own_ref), custom_call_target="tpu_custom_call" | custom-call | flops 1073741824 | bytes 8388608 | tf_op jit(solution)/shard_map/near_field/pallas_call | solution.py:116
  118.9 9.9 %all-to-all-done.2.recv = bf16[16,336,128]{2,1,0:T(8,128)(2,1)S(1)} async-done(((bf16[16,336,128]{2,1,0:T(8,128)(2,1)}), bf16[16,336,128]{2,1,0:T(8,128)(2,1)S(1)}, u32[]{:S(2)}, u32[]{:S(2)}) %all-to-all-start.2) | async-done | bytes 1376288 | tf_op jit(solution)/shard_map/all_to_all | solution.py:899
  129.7 1.5 collective-permute-start.13
  132.2 5.4 %far_field.6 = (f32[512,128]{1,0:T(8,128)S(1)}, bf16[64,256,256]{2,1,0:T(8,128)(2,1)S(1)}, f32[8,256,128]{2,1,0:T(8,128)S(1)}) custom-call(s32[1]{0:T(128)} %get-tuple-element.79.count_ref, s32[64]{0:T(128)} %copy-done, bf16[16,336,128]{2,1,0:T(8,128)(2,1)S(1)} %all-to-all-done.2.recv, bf16[16,512,256]{2,1,0:T(8,128)(2,1)} %get-tuple-element.78.refs_0_.packed_ref, ...), custom_call_target="tpu_custom_call" | custom-call | flops 536870912 | bytes 4194304 | tf_op jit(solution)/shard_map/far_field/pallas_call | solution.py:116
  137.6 3.3 %collective-permute-start.15 = (bf16[4,80,128]{2,1,0:T(8,128)(2,1)S(1)}, bf16[4,80,128]{2,1,0:T(8,128)(2,1)S(1)}, u32[]{:S(2)}, u32[]{:S(2)}) collective-permute-start(bf16[4,80,128]{2,1,0:T(8,128)(2,1)S(1)} %stack.7.refs_5_.refs_2_), channel_id=1, source_target_pairs={{0,16},{16,0},{32,48},{48,32},{64,80},{80,64},{96,112},{112,96},{1... | collective-permute-start | bytes 245768 | tf_op jit(solution)/shard_map/ppermute | solution.py:385
  140.9 3.0 %halo_part.6 = (f32[8,256,128]{2,1,0:T(8,128)S(1)}, bf16[8,64,256]{2,1,0:T(8,128)(2,1)S(1)}, bf16[8,256,64]{2,1,0:T(8,128)(2,1)S(1)}, bf16[8,64,64]{2,1,0:T(8,12...) custom-call(s32[1]{0:T(128)} %get-tuple-element.79.count_ref, ...), custom_call_target="tpu_custom_call", output_to_operand_aliasing={{0}: (6, {})} | custom-call | flops 268435456 | bytes 2097152 | tf_op jit(solution)/shard_map/halo_part/pallas_call | solution.py:116
  144.0 6.4 %stage3.1 = (f32[8,256,128]{2,1,0:T(8,128)}, f32[64,128]{1,0:T(8,128)S(1)}, bf16[16,336,128]{2,1,0:T(8,128)(2,1)}, bf16[8,256,128]{2,1,0:T(8,128)(2,1)}, bf16[2,...) custom-call(s32[4,16]{1,0:T(4,128)} %bitcast.16, s32[1]{0:T(128)} %bitcast.2.refs_1_.branch, ...), custom_call_target="tpu_custom_call" | custom-call | flops 134217728 | bytes 7340032 | tf_op jit(solution)/shard_map/stage3/pallas_call | solution.py:116
  150.4 3.7 %all-to-all-start.3 = ((bf16[16,336,128]{2,1,0:T(8,128)(2,1)}), bf16[16,336,128]{2,1,0:T(8,128)(2,1)S(1)}, u32[]{:S(2)}, u32[]{:S(2)}) async-start(bf16[16,336,128]{2,1,0:T(8,128)(2,1)} %get-tuple-element.126), calls=%async_computation.3 | async-start | bytes 2752512 | tf_op jit(solution)/shard_map/all_to_all | solution.py:899
  154.1 3.1 %collective-permute-start.22 = (bf16[2,256,128]{2,1,0:T(8,128)(2,1)S(1)}, bf16[2,256,128]{2,1,0:T(8,128)(2,1)S(1)}, u32[]{:S(2)}, u32[]{:S(2)}) collective-permute-start(bf16[2,256,128]{2,1,0:T(8,128)(2,1)S(1)} %get-tuple-element.131), channel_id=1, source_target_pairs={{0,1},{1,2},{2,3},{3,4},{4,5},{5,6},{6,7},{7,8},{8,9},{9,10},{10,1... | collective-permute-start | bytes 393224 | tf_op jit(solution)/shard_map/ppermute | solution.py:911
  158.5 6.9 %near_field.7.refs_4_.refs_0_ = f32[8,256,128]{2,1,0:T(8,128)} custom-call(s32[8,8]{1,0:T(8,128)} %index_ref.17, s32[8,8]{1,0:T(8,128)} %mask_ref.9, bf16[8,8,256,256]{3,2,1,0:T(8,128)(2,1)} %blocks_ref.15, bf16[8,256,128]{2,1,0:T(8,128)(2,1)} %get-tuple-element.128.own_ref), custom_call_target="tpu_custom_call" | custom-call | flops 1073741824 | bytes 8388608 | tf_op jit(solution)/shard_map/near_field/pallas_call | solution.py:116
  165.4 3.5 %vectors.2.refs_0_.refs_5_ = f32[5,8,256,128]{3,2,1,0:T(8,128)} custom-call(f32[64,128]{1,0:T(8,128)S(1)} %get-tuple-element.127.refs_0_.refs_4_, f32[8,256,128]{2,1,0:T(8,128)} %bitcast.11, f32[8,256,128]{2,1,0:T(8,128)} %get-tuple-element.110.refs_13_.refs_2_.refs_6_, f32[8,256,128]{2,1,0:T(8,128)} %get-tuple-element.125.refs_14_.refs_3_.refs_7_, ...), custom_call_target="tpu_custom_call" | custom-call | flops 8388608 | bytes 6291456 | tf_op jit(solution)/shard_map/vectors/pallas_call | solution.py:116
  169.0 6.8 %all-to-all-done.3.recv = bf16[16,336,128]{2,1,0:T(8,128)(2,1)S(1)} async-done(((bf16[16,336,128]{2,1,0:T(8,128)(2,1)}), bf16[16,336,128]{2,1,0:T(8,128)(2,1)S(1)}, u32[]{:S(2)}, u32[]{:S(2)}) %all-to-all-start.3) | async-done | bytes 1376288 | tf_op jit(solution)/shard_map/all_to_all | solution.py:899
  176.7 1.9 collective-permute-start.20
  178.5 5.4 %far_field.7 = (f32[512,128]{1,0:T(8,128)S(1)}, bf16[64,256,256]{2,1,0:T(8,128)(2,1)S(1)}, f32[8,256,128]{2,1,0:T(8,128)S(1)}) custom-call(s32[1]{0:T(128)} %get-tuple-element.79.count_ref, s32[64]{0:T(128)} %copy-done, bf16[16,336,128]{2,1,0:T(8,128)(2,1)S(1)} %all-to-all-done.3.recv, bf16[16,512,256]{2,1,0:T(8,128)(2,1)} %get-tuple-element.78.refs_0_.packed_ref, ...), custom_call_target="tpu_custom_call" | custom-call | flops 536870912 | bytes 4194304 | tf_op jit(solution)/shard_map/far_field/pallas_call | solution.py:116
  184.0 2.0 collective-permute-start.21
  186.0 4.0 %halo_part.7 = (f32[8,256,128]{2,1,0:T(8,128)S(1)}, bf16[8,64,256]{2,1,0:T(8,128)(2,1)S(1)}, bf16[8,256,64]{2,1,0:T(8,128)(2,1)S(1)}, bf16[8,64,64]{2,1,0:T(8,12...) custom-call(s32[1]{0:T(128)} %get-tuple-element.79.count_ref, ...), custom_call_target="tpu_custom_call", output_to_operand_aliasing={{0}: (6, {})} | custom-call | flops 268435456 | bytes 2097152 | tf_op jit(solution)/shard_map/halo_part/pallas_call | solution.py:116
  190.0 3.9 %stage4.1 = (f32[8,256,128]{2,1,0:T(8,128)S(1)}, f32[64,128]{1,0:T(8,128)S(1)}, bf16[16,128]{1,0:T(8,128)(2,1)S(1)}) custom-call(s32[4,16]{1,0:T(4,128)} %bitcast.17, s32[1]{0:T(128)} %bitcast.2.refs_1_.branch, bf16[4,80,128]{2,1,0:T(8,128)(2,1)S(1)} %stack.8.refs_9_.refs_2_, bf16[4,80,128]{2,1,0:T(8,128)(2,1)S(1)} %collective-permute-done.21.refs_3_, ...), custom_call_target="tpu_custom_call" | custom-call | flops 134217728 | bytes 8388608 | tf_op jit(solution)/shard_map/stage4/pallas_call | solution.py:116
  194.3 1.6 collective-permute-start.25
  198.8 2.3 %collective-permute-start.28 = (bf16[16,128]{1,0:T(8,128)(2,1)S(1)}, bf16[16,128]{1,0:T(8,128)(2,1)S(1)}, u32[]{:S(2)}, u32[]{:S(2)}) collective-permute-start(bf16[16,128]{1,0:T(8,128)(2,1)S(1)} %sum_over.2.refs_0_.refs_4_), channel_id=1, source_target_pairs={{0,8},{1,9},{2,10},{3,11},{4,12},{5,13},{6,14},{7,15},{8,0},{9,1},... | collective-permute-start | bytes 12296 | tf_op jit(solution)/shard_map/ppermute | solution.py:553
  201.1 2.0 collective-permute-start.29
  204.2 2.2 %collective-permute-start.31 = (bf16[16,128]{1,0:T(8,128)(2,1)S(1)}, bf16[16,128]{1,0:T(8,128)(2,1)S(1)}, u32[]{:S(2)}, u32[]{:S(2)}) collective-permute-start(bf16[16,128]{1,0:T(8,128)(2,1)S(1)} %sum_over.3.refs_0_.refs_4_), channel_id=1, source_target_pairs={{0,64},{16,80},{32,96},{48,112},{64,0},{80,16},{96,32},{112,48},{1... | collective-permute-start | bytes 12296 | tf_op jit(solution)/shard_map/ppermute | solution.py:374
  206.4 2.0 collective-permute-start.32
  209.1 4.6 %collective-permute-start.33 = (bf16[4,16,128]{2,1,0:T(8,128)(2,1)S(1)}, bf16[4,16,128]{2,1,0:T(8,128)(2,1)S(1)}, u32[]{:S(2)}, u32[]{:S(2)}) collective-permute-start(bf16[4,16,128]{2,1,0:T(8,128)(2,1)S(1)} %stack.9.refs_2_), channel_id=1, source_target_pairs={{0,16},{16,0},{32,48},{48,32},{64,80},{80,64},{96,112},{112,96},{1... | collective-permute-start | bytes 49160 | tf_op jit(solution)/shard_map/ppermute | solution.py:385
  214.5 1.7 last_vector.1
  (62 shorter events, 14.4 us)
Async XLA Ops:
  5.1 29.1 %all-to-all-start = ((bf16[16,336,128]{2,1,0:T(8,128)(2,1)}), bf16[16,336,128]{2,1,0:T(8,128)(2,1)S(1)}, u32[]{:S(2)}, u32[]{:S(2)}) async-start(bf16[16,336,128]{2,1,0:T(8,128)(2,1)} %get-tuple-element.76), calls=%async_computation | async-start | bytes 2752512 | tf_op jit(solution)/shard_map/all_to_all | solution.py:899
  13.7 33.6 %collective-permute-start.4 = (bf16[2,256,128]{2,1,0:T(8,128)(2,1)S(1)}, bf16[2,256,128]{2,1,0:T(8,128)(2,1)S(1)}, u32[]{:S(2)}, u32[]{:S(2)}) collective-permute-start(bf16[2,256,128]{2,1,0:T(8,128)(2,1)S(1)} %get-tuple-element.84), channel_id=1, source_target_pairs={{0,1},{1,2},{2,3},{3,4},{4,5},{5,6},{6,7},{7,8},{8,9},{9,10},{10,1... | collective-permute-start | bytes 393224 | tf_op jit(solution)/shard_map/ppermute | solution.py:911
  16.9 30.3 %collective-permute-start.5 = (bf16[2,256,128]{2,1,0:T(8,128)(2,1)S(1)}, bf16[2,256,128]{2,1,0:T(8,128)(2,1)S(1)}, u32[]{:S(2)}, u32[]{:S(2)}) collective-permute-start(bf16[2,256,128]{2,1,0:T(8,128)(2,1)S(1)} %get-tuple-element.85), channel_id=1, source_target_pairs={{1,0},{2,1},{3,2},{4,3},{5,4},{6,5},{7,6},{8,7},{9,8},{10,9},{11,1... | collective-permute-start | bytes 393224 | tf_op jit(solution)/shard_map/ppermute | solution.py:912
  26.7 0.6 copy-start
  34.3 10.3 %collective-permute-start = (bf16[80,128]{1,0:T(8,128)(2,1)S(1)}, bf16[80,128]{1,0:T(8,128)(2,1)S(1)}, u32[]{:S(2)}, u32[]{:S(2)}) collective-permute-start(bf16[80,128]{1,0:T(8,128)(2,1)S(1)} %gather_sum.4.refs_1_.refs_0_), channel_id=1, source_target_pairs={{0,32},{16,48},{32,64},{48,80},{64,96},{80,112},{96,0},{112,16},{1... | collective-permute-start | bytes 61448 | tf_op jit(solution)/shard_map/ppermute | solution.py:374
  35.5 9.0 %collective-permute-start.1 = (bf16[80,128]{1,0:T(8,128)(2,1)S(1)}, bf16[80,128]{1,0:T(8,128)(2,1)S(1)}, u32[]{:S(2)}, u32[]{:S(2)}) collective-permute-start(bf16[80,128]{1,0:T(8,128)(2,1)S(1)} %gather_sum.4.refs_1_.refs_0_), channel_id=1, source_target_pairs={{0,64},{16,80},{32,96},{48,112},{64,0},{80,16},{96,32},{112,48},{1... | collective-permute-start | bytes 61448 | tf_op jit(solution)/shard_map/ppermute | solution.py:374
  38.0 6.6 %collective-permute-start.2 = (bf16[80,128]{1,0:T(8,128)(2,1)S(1)}, bf16[80,128]{1,0:T(8,128)(2,1)S(1)}, u32[]{:S(2)}, u32[]{:S(2)}) collective-permute-start(bf16[80,128]{1,0:T(8,128)(2,1)S(1)} %gather_sum.4.refs_1_.refs_0_), channel_id=1, source_target_pairs={{0,96},{16,112},{32,0},{48,16},{64,32},{80,48},{96,64},{112,80},{1... | collective-permute-start | bytes 61448 | tf_op jit(solution)/shard_map/ppermute | solution.py:374
  44.6 5.5 %collective-permute-start.3 = (bf16[4,80,128]{2,1,0:T(8,128)(2,1)S(1)}, bf16[4,80,128]{2,1,0:T(8,128)(2,1)S(1)}, u32[]{:S(2)}, u32[]{:S(2)}) collective-permute-start(bf16[4,80,128]{2,1,0:T(8,128)(2,1)S(1)} %stack.5.refs_5_.refs_2_), channel_id=1, source_target_pairs={{0,16},{16,0},{32,48},{48,32},{64,80},{80,64},{96,112},{112,96},{1... | collective-permute-start | bytes 245768 | tf_op jit(solution)/shard_map/ppermute | solution.py:385
  55.7 28.4 %all-to-all-start.1 = ((bf16[16,336,128]{2,1,0:T(8,128)(2,1)}), bf16[16,336,128]{2,1,0:T(8,128)(2,1)S(1)}, u32[]{:S(2)}, u32[]{:S(2)}) async-start(bf16[16,336,128]{2,1,0:T(8,128)(2,1)} %get-tuple-element.96), calls=%async_computation.1 | async-start | bytes 2752512 | tf_op jit(solution)/shard_map/all_to_all | solution.py:899
  62.8 31.7 %collective-permute-start.10 = (bf16[2,256,128]{2,1,0:T(8,128)(2,1)S(1)}, bf16[2,256,128]{2,1,0:T(8,128)(2,1)S(1)}, u32[]{:S(2)}, u32[]{:S(2)}) collective-permute-start(bf16[2,256,128]{2,1,0:T(8,128)(2,1)S(1)} %get-tuple-element.101), channel_id=1, source_target_pairs={{0,1},{1,2},{2,3},{3,4},{4,5},{5,6},{6,7},{7,8},{8,9},{9,10},{10,1... | collective-permute-start | bytes 393224 | tf_op jit(solution)/shard_map/ppermute | solution.py:911
  66.0 28.5 %collective-permute-start.11 = (bf16[2,256,128]{2,1,0:T(8,128)(2,1)S(1)}, bf16[2,256,128]{2,1,0:T(8,128)(2,1)S(1)}, u32[]{:S(2)}, u32[]{:S(2)}) collective-permute-start(bf16[2,256,128]{2,1,0:T(8,128)(2,1)S(1)} %get-tuple-element.102), channel_id=1, source_target_pairs={{1,0},{2,1},{3,2},{4,3},{5,4},{6,5},{7,6},{8,7},{9,8},{10,9},{11,1... | collective-permute-start | bytes 393224 | tf_op jit(solution)/shard_map/ppermute | solution.py:912
  84.1 8.2 %collective-permute-start.6 = (bf16[80,128]{1,0:T(8,128)(2,1)S(1)}, bf16[80,128]{1,0:T(8,128)(2,1)S(1)}, u32[]{:S(2)}, u32[]{:S(2)}) collective-permute-start(bf16[80,128]{1,0:T(8,128)(2,1)S(1)} %gather_sum.5.refs_1_.refs_0_), channel_id=1, source_target_pairs={{0,32},{16,48},{32,64},{48,80},{64,96},{80,112},{96,0},{112,16},{1... | collective-permute-start | bytes 61448 | tf_op jit(solution)/shard_map/ppermute | solution.py:374
  84.5 7.9 %collective-permute-start.7 = (bf16[80,128]{1,0:T(8,128)(2,1)S(1)}, bf16[80,128]{1,0:T(8,128)(2,1)S(1)}, u32[]{:S(2)}, u32[]{:S(2)}) collective-permute-start(bf16[80,128]{1,0:T(8,128)(2,1)S(1)} %gather_sum.5.refs_1_.refs_0_), channel_id=1, source_target_pairs={{0,64},{16,80},{32,96},{48,112},{64,0},{80,16},{96,32},{112,48},{1... | collective-permute-start | bytes 61448 | tf_op jit(solution)/shard_map/ppermute | solution.py:374
  85.2 7.2 %collective-permute-start.8 = (bf16[80,128]{1,0:T(8,128)(2,1)S(1)}, bf16[80,128]{1,0:T(8,128)(2,1)S(1)}, u32[]{:S(2)}, u32[]{:S(2)}) collective-permute-start(bf16[80,128]{1,0:T(8,128)(2,1)S(1)} %gather_sum.5.refs_1_.refs_0_), channel_id=1, source_target_pairs={{0,96},{16,112},{32,0},{48,16},{64,32},{80,48},{96,64},{112,80},{1... | collective-permute-start | bytes 61448 | tf_op jit(solution)/shard_map/ppermute | solution.py:374
  92.4 5.0 %collective-permute-start.9 = (bf16[4,80,128]{2,1,0:T(8,128)(2,1)S(1)}, bf16[4,80,128]{2,1,0:T(8,128)(2,1)S(1)}, u32[]{:S(2)}, u32[]{:S(2)}) collective-permute-start(bf16[4,80,128]{2,1,0:T(8,128)(2,1)S(1)} %stack.6.refs_5_.refs_2_), channel_id=1, source_target_pairs={{0,16},{16,0},{32,48},{48,32},{64,80},{80,64},{96,112},{112,96},{1... | collective-permute-start | bytes 245768 | tf_op jit(solution)/shard_map/ppermute | solution.py:385
  103.3 25.6 %all-to-all-start.2 = ((bf16[16,336,128]{2,1,0:T(8,128)(2,1)}), bf16[16,336,128]{2,1,0:T(8,128)(2,1)S(1)}, u32[]{:S(2)}, u32[]{:S(2)}) async-start(bf16[16,336,128]{2,1,0:T(8,128)(2,1)} %get-tuple-element.111), calls=%async_computation.2 | async-start | bytes 2752512 | tf_op jit(solution)/shard_map/all_to_all | solution.py:899
  107.5 33.5 %collective-permute-start.16 = (bf16[2,256,128]{2,1,0:T(8,128)(2,1)S(1)}, bf16[2,256,128]{2,1,0:T(8,128)(2,1)S(1)}, u32[]{:S(2)}, u32[]{:S(2)}) collective-permute-start(bf16[2,256,128]{2,1,0:T(8,128)(2,1)S(1)} %get-tuple-element.116), channel_id=1, source_target_pairs={{0,1},{1,2},{2,3},{3,4},{4,5},{5,6},{6,7},{7,8},{8,9},{9,10},{10,1... | collective-permute-start | bytes 393224 | tf_op jit(solution)/shard_map/ppermute | solution.py:911
  110.7 30.2 %collective-permute-start.17 = (bf16[2,256,128]{2,1,0:T(8,128)(2,1)S(1)}, bf16[2,256,128]{2,1,0:T(8,128)(2,1)S(1)}, u32[]{:S(2)}, u32[]{:S(2)}) collective-permute-start(bf16[2,256,128]{2,1,0:T(8,128)(2,1)S(1)} %get-tuple-element.117), channel_id=1, source_target_pairs={{1,0},{2,1},{3,2},{4,3},{5,4},{6,5},{7,6},{8,7},{9,8},{10,9},{11,1... | collective-permute-start | bytes 393224 | tf_op jit(solution)/shard_map/ppermute | solution.py:912
  128.9 8.7 %collective-permute-start.12 = (bf16[80,128]{1,0:T(8,128)(2,1)S(1)}, bf16[80,128]{1,0:T(8,128)(2,1)S(1)}, u32[]{:S(2)}, u32[]{:S(2)}) collective-permute-start(bf16[80,128]{1,0:T(8,128)(2,1)S(1)} %gather_sum.6.refs_1_.refs_0_), channel_id=1, source_target_pairs={{0,32},{16,48},{32,64},{48,80},{64,96},{80,112},{96,0},{112,16},{1... | collective-permute-start | bytes 61448 | tf_op jit(solution)/shard_map/ppermute | solution.py:374
  129.7 7.9 %collective-permute-start.13 = (bf16[80,128]{1,0:T(8,128)(2,1)S(1)}, bf16[80,128]{1,0:T(8,128)(2,1)S(1)}, u32[]{:S(2)}, u32[]{:S(2)}) collective-permute-start(bf16[80,128]{1,0:T(8,128)(2,1)S(1)} %gather_sum.6.refs_1_.refs_0_), channel_id=1, source_target_pairs={{0,64},{16,80},{32,96},{48,112},{64,0},{80,16},{96,32},{112,48},{1... | collective-permute-start | bytes 61448 | tf_op jit(solution)/shard_map/ppermute | solution.py:374
  131.2 6.4 %collective-permute-start.14 = (bf16[80,128]{1,0:T(8,128)(2,1)S(1)}, bf16[80,128]{1,0:T(8,128)(2,1)S(1)}, u32[]{:S(2)}, u32[]{:S(2)}) collective-permute-start(bf16[80,128]{1,0:T(8,128)(2,1)S(1)} %gather_sum.6.refs_1_.refs_0_), channel_id=1, source_target_pairs={{0,96},{16,112},{32,0},{48,16},{64,32},{80,48},{96,64},{112,80},{1... | collective-permute-start | bytes 61448 | tf_op jit(solution)/shard_map/ppermute | solution.py:374
  137.6 6.3 %collective-permute-start.15 = (bf16[4,80,128]{2,1,0:T(8,128)(2,1)S(1)}, bf16[4,80,128]{2,1,0:T(8,128)(2,1)S(1)}, u32[]{:S(2)}, u32[]{:S(2)}) collective-permute-start(bf16[4,80,128]{2,1,0:T(8,128)(2,1)S(1)} %stack.7.refs_5_.refs_2_), channel_id=1, source_target_pairs={{0,16},{16,0},{32,48},{48,32},{64,80},{80,64},{96,112},{112,96},{1... | collective-permute-start | bytes 245768 | tf_op jit(solution)/shard_map/ppermute | solution.py:385
  150.4 25.4 %all-to-all-start.3 = ((bf16[16,336,128]{2,1,0:T(8,128)(2,1)}), bf16[16,336,128]{2,1,0:T(8,128)(2,1)S(1)}, u32[]{:S(2)}, u32[]{:S(2)}) async-start(bf16[16,336,128]{2,1,0:T(8,128)(2,1)} %get-tuple-element.126), calls=%async_computation.3 | async-start | bytes 2752512 | tf_op jit(solution)/shard_map/all_to_all | solution.py:899
  154.1 31.9 %collective-permute-start.22 = (bf16[2,256,128]{2,1,0:T(8,128)(2,1)S(1)}, bf16[2,256,128]{2,1,0:T(8,128)(2,1)S(1)}, u32[]{:S(2)}, u32[]{:S(2)}) collective-permute-start(bf16[2,256,128]{2,1,0:T(8,128)(2,1)S(1)} %get-tuple-element.131), channel_id=1, source_target_pairs={{0,1},{1,2},{2,3},{3,4},{4,5},{5,6},{6,7},{7,8},{8,9},{9,10},{10,1... | collective-permute-start | bytes 393224 | tf_op jit(solution)/shard_map/ppermute | solution.py:911
  157.2 28.8 %collective-permute-start.23 = (bf16[2,256,128]{2,1,0:T(8,128)(2,1)S(1)}, bf16[2,256,128]{2,1,0:T(8,128)(2,1)S(1)}, u32[]{:S(2)}, u32[]{:S(2)}) collective-permute-start(bf16[2,256,128]{2,1,0:T(8,128)(2,1)S(1)} %get-tuple-element.132), channel_id=1, source_target_pairs={{1,0},{2,1},{3,2},{4,3},{5,4},{6,5},{7,6},{8,7},{9,8},{10,9},{11,1... | collective-permute-start | bytes 393224 | tf_op jit(solution)/shard_map/ppermute | solution.py:912
  175.8 8.1 %collective-permute-start.18 = (bf16[80,128]{1,0:T(8,128)(2,1)S(1)}, bf16[80,128]{1,0:T(8,128)(2,1)S(1)}, u32[]{:S(2)}, u32[]{:S(2)}) collective-permute-start(bf16[80,128]{1,0:T(8,128)(2,1)S(1)} %gather_sum.7.refs_1_.refs_0_), channel_id=1, source_target_pairs={{0,32},{16,48},{32,64},{48,80},{64,96},{80,112},{96,0},{112,16},{1... | collective-permute-start | bytes 61448 | tf_op jit(solution)/shard_map/ppermute | solution.py:374
  175.9 8.1 %collective-permute-start.19 = (bf16[80,128]{1,0:T(8,128)(2,1)S(1)}, bf16[80,128]{1,0:T(8,128)(2,1)S(1)}, u32[]{:S(2)}, u32[]{:S(2)}) collective-permute-start(bf16[80,128]{1,0:T(8,128)(2,1)S(1)} %gather_sum.7.refs_1_.refs_0_), channel_id=1, source_target_pairs={{0,64},{16,80},{32,96},{48,112},{64,0},{80,16},{96,32},{112,48},{1... | collective-permute-start | bytes 61448 | tf_op jit(solution)/shard_map/ppermute | solution.py:374
  176.7 7.3 %collective-permute-start.20 = (bf16[80,128]{1,0:T(8,128)(2,1)S(1)}, bf16[80,128]{1,0:T(8,128)(2,1)S(1)}, u32[]{:S(2)}, u32[]{:S(2)}) collective-permute-start(bf16[80,128]{1,0:T(8,128)(2,1)S(1)} %gather_sum.7.refs_1_.refs_0_), channel_id=1, source_target_pairs={{0,96},{16,112},{32,0},{48,16},{64,32},{80,48},{96,64},{112,80},{1... | collective-permute-start | bytes 61448 | tf_op jit(solution)/shard_map/ppermute | solution.py:374
  184.0 6.0 %collective-permute-start.21 = (bf16[4,80,128]{2,1,0:T(8,128)(2,1)S(1)}, bf16[4,80,128]{2,1,0:T(8,128)(2,1)S(1)}, u32[]{:S(2)}, u32[]{:S(2)}) collective-permute-start(bf16[4,80,128]{2,1,0:T(8,128)(2,1)S(1)} %stack.8.refs_9_.refs_2_), channel_id=1, source_target_pairs={{0,16},{16,0},{32,48},{48,32},{64,80},{80,64},{96,112},{112,96},{1... | collective-permute-start | bytes 245768 | tf_op jit(solution)/shard_map/ppermute | solution.py:385
  193.9 4.0 %collective-permute-start.24 = (bf16[16,128]{1,0:T(8,128)(2,1)S(1)}, bf16[16,128]{1,0:T(8,128)(2,1)S(1)}, u32[]{:S(2)}, u32[]{:S(2)}) collective-permute-start(bf16[16,128]{1,0:T(8,128)(2,1)S(1)} %get-tuple-element.146.refs_0_), channel_id=1, source_target_pairs={{0,1},{1,2},{2,3},{3,0},{4,5},{5,6},{6,7},{7,4},{8,9},{9,10},{10,1... | collective-permute-start | bytes 12296 | tf_op jit(solution)/shard_map/ppermute | solution.py:553
  194.3 4.0 %collective-permute-start.25 = (bf16[16,128]{1,0:T(8,128)(2,1)S(1)}, bf16[16,128]{1,0:T(8,128)(2,1)S(1)}, u32[]{:S(2)}, u32[]{:S(2)}) collective-permute-start(bf16[16,128]{1,0:T(8,128)(2,1)S(1)} %get-tuple-element.146.refs_0_), channel_id=1, source_target_pairs={{0,2},{1,3},{2,0},{3,1},{4,6},{5,7},{6,4},{7,5},{8,10},{9,11},{10,... | collective-permute-start | bytes 12296 | tf_op jit(solution)/shard_map/ppermute | solution.py:553
  195.9 2.8 %collective-permute-start.26 = (bf16[16,128]{1,0:T(8,128)(2,1)S(1)}, bf16[16,128]{1,0:T(8,128)(2,1)S(1)}, u32[]{:S(2)}, u32[]{:S(2)}) collective-permute-start(bf16[16,128]{1,0:T(8,128)(2,1)S(1)} %get-tuple-element.146.refs_0_), channel_id=1, source_target_pairs={{0,3},{1,0},{2,1},{3,2},{4,7},{5,4},{6,5},{7,6},{8,11},{9,8},{10,9... | collective-permute-start | bytes 12296 | tf_op jit(solution)/shard_map/ppermute | solution.py:553
  198.7 4.4 %collective-permute-start.27 = (bf16[16,128]{1,0:T(8,128)(2,1)S(1)}, bf16[16,128]{1,0:T(8,128)(2,1)S(1)}, u32[]{:S(2)}, u32[]{:S(2)}) collective-permute-start(bf16[16,128]{1,0:T(8,128)(2,1)S(1)} %sum_over.2.refs_0_.refs_4_), channel_id=1, source_target_pairs={{0,4},{1,5},{2,6},{3,7},{4,8},{5,9},{6,10},{7,11},{8,12},{9,13},{1... | collective-permute-start | bytes 12296 | tf_op jit(solution)/shard_map/ppermute | solution.py:553
  198.8 4.3 %collective-permute-start.28 = (bf16[16,128]{1,0:T(8,128)(2,1)S(1)}, bf16[16,128]{1,0:T(8,128)(2,1)S(1)}, u32[]{:S(2)}, u32[]{:S(2)}) collective-permute-start(bf16[16,128]{1,0:T(8,128)(2,1)S(1)} %sum_over.2.refs_0_.refs_4_), channel_id=1, source_target_pairs={{0,8},{1,9},{2,10},{3,11},{4,12},{5,13},{6,14},{7,15},{8,0},{9,1},... | collective-permute-start | bytes 12296 | tf_op jit(solution)/shard_map/ppermute | solution.py:553
  201.1 2.7 %collective-permute-start.29 = (bf16[16,128]{1,0:T(8,128)(2,1)S(1)}, bf16[16,128]{1,0:T(8,128)(2,1)S(1)}, u32[]{:S(2)}, u32[]{:S(2)}) collective-permute-start(bf16[16,128]{1,0:T(8,128)(2,1)S(1)} %sum_over.2.refs_0_.refs_4_), channel_id=1, source_target_pairs={{0,12},{1,13},{2,14},{3,15},{4,0},{5,1},{6,2},{7,3},{8,4},{9,5},{1... | collective-permute-start | bytes 12296 | tf_op jit(solution)/shard_map/ppermute | solution.py:553
  203.9 4.4 %collective-permute-start.30 = (bf16[16,128]{1,0:T(8,128)(2,1)S(1)}, bf16[16,128]{1,0:T(8,128)(2,1)S(1)}, u32[]{:S(2)}, u32[]{:S(2)}) collective-permute-start(bf16[16,128]{1,0:T(8,128)(2,1)S(1)} %sum_over.3.refs_0_.refs_4_), channel_id=1, source_target_pairs={{0,32},{16,48},{32,64},{48,80},{64,96},{80,112},{96,0},{112,16},{1... | collective-permute-start | bytes 12296 | tf_op jit(solution)/shard_map/ppermute | solution.py:374
  204.2 4.2 %collective-permute-start.31 = (bf16[16,128]{1,0:T(8,128)(2,1)S(1)}, bf16[16,128]{1,0:T(8,128)(2,1)S(1)}, u32[]{:S(2)}, u32[]{:S(2)}) collective-permute-start(bf16[16,128]{1,0:T(8,128)(2,1)S(1)} %sum_over.3.refs_0_.refs_4_), channel_id=1, source_target_pairs={{0,64},{16,80},{32,96},{48,112},{64,0},{80,16},{96,32},{112,48},{1... | collective-permute-start | bytes 12296 | tf_op jit(solution)/shard_map/ppermute | solution.py:374
  206.4 2.7 %collective-permute-start.32 = (bf16[16,128]{1,0:T(8,128)(2,1)S(1)}, bf16[16,128]{1,0:T(8,128)(2,1)S(1)}, u32[]{:S(2)}, u32[]{:S(2)}) collective-permute-start(bf16[16,128]{1,0:T(8,128)(2,1)S(1)} %sum_over.3.refs_0_.refs_4_), channel_id=1, source_target_pairs={{0,96},{16,112},{32,0},{48,16},{64,32},{80,48},{96,64},{112,80},{1... | collective-permute-start | bytes 12296 | tf_op jit(solution)/shard_map/ppermute | solution.py:374
  209.1 5.4 %collective-permute-start.33 = (bf16[4,16,128]{2,1,0:T(8,128)(2,1)S(1)}, bf16[4,16,128]{2,1,0:T(8,128)(2,1)S(1)}, u32[]{:S(2)}, u32[]{:S(2)}) collective-permute-start(bf16[4,16,128]{2,1,0:T(8,128)(2,1)S(1)} %stack.9.refs_2_), channel_id=1, source_target_pairs={{0,16},{16,0},{32,48},{48,32},{64,80},{80,64},{96,112},{112,96},{1... | collective-permute-start | bytes 49160 | tf_op jit(solution)/shard_map/ppermute | solution.py:385

commit v7 on v5

--- a/solution.py
+++ b/solution.py
@@ -157,9 +157,10 @@
 
 
 def pack_kernel(branch, mask_ref, slot_ref, index_ref, near_mask_ref, far_ref, *refs):
-    basis_ref, transfer_ref, top_ref = refs[:3]
-    out_ref, count_ref, list_ref, basis_out, transfer_out, top_out = refs[3:9]
-    blocks, total, packed, basis, transfer, top, turned, lifting, row, arrived, left, came = refs[9:]
+    basis_ref, transfer_ref, top_ref, near_ref = refs[:4]
+    out_ref, count_ref, list_ref, basis_out, transfer_out, top_out, listed_ref = refs[4:11]
+    blocks, total, packed, basis, transfer, top, turned, lifting, row, chosen = refs[11:21]
+    arrived, left, came, moved, given = refs[21:]
     leaves, entries, rank, _ = blocks.shape
     sources, _, width = packed.shape
     slots = width // rank
@@ -183,6 +184,28 @@
             packed[source, rows] = jnp.concatenate(sides, axis=1).astype(BF16)
         store(leaf).start()
 
+    piece = chosen.shape[0] // given.shape[0]
+
+    def move(leaf, n, i):
+        return pltpu.make_async_copy(near_ref.at[leaf, n], chosen.at[i], moved.at[i])
+
+    def moved_one(i, carry):
+        entry = list_ref[i]
+        move(entry // near_entries, entry % near_entries, i).wait()
+        return carry
+
+    def give(i):
+        some = slab(i, piece)
+        return pltpu.make_async_copy(chosen.at[some], listed_ref.at[some], given.at[i])
+
+    def start_give(i, carry):
+        give(i).start()
+        return carry
+
+    def end_give(i, carry):
+        give(i).wait()
+        return carry
+
     def list_one(i, count):
         leaf, n = i // near_entries, i % near_entries
         place = index_ref[leaf, n]
@@ -192,6 +215,7 @@
         @pl.when(hit)
         def _():
             list_ref[count] = i
+            move(leaf, n, count).start()
 
         return count + hit.astype(jnp.int32)
 
@@ -202,9 +226,10 @@
     ]
     for copy in small:
         copy.start()
-    begin, run = windowed(leaves, AHEAD, fetch, work)
+    begin, run = windowed(leaves, leaves, fetch, work)
     begin()
-    count_ref[0] = lax.fori_loop(0, list_ref.shape[0], list_one, 0)
+    count = lax.fori_loop(0, list_ref.shape[0], list_one, 0)
+    count_ref[0] = count
     for copy in small:
         copy.wait()
     turn = lambda a: a.astype(F32).T.astype(BF16)
@@ -227,23 +252,29 @@
     ]
     for copy in results:
         copy.start()
+    lax.fori_loop(0, count, moved_one, 0)
+    pieces = (count + piece - 1) // piece
+    lax.fori_loop(0, pieces, start_give, 0)
     run()
     for leaf in range(leaves):
         store(leaf).wait()
     for copy in results:
         copy.wait()
-
-
-def pack(branch, basis, transfer, top_blocks, far_blocks, far_mask, far_slot, near_index, near_mask, inner, slots):
+    lax.fori_loop(0, pieces, end_give, 0)
+
+
+def pack(branch, basis, transfer, top_blocks, near_blocks, far_blocks, far_mask, far_slot, near_index, near_mask, inner, slots):
     leaves, entries, rank, _ = far_blocks.shape
     shape = (inner, leaves * rank, slots * rank)
     turned = (leaves, basis.shape[2], rank)
     lifting = (rank, leaves * rank)
     row = (rank, top_blocks.shape[1] * rank)
+    listed = (near_index.size,) + near_blocks.shape[2:]
     return call(
         pack_kernel,
-        (branch, far_mask, far_slot, near_index, near_mask, far_blocks, basis, transfer, top_blocks),
-        (SMEM,) * 5 + (HBM,) * 4,
+        (branch, far_mask, far_slot, near_index, near_mask, far_blocks, basis, transfer, top_blocks,
+         near_blocks),
+        (SMEM,) * 5 + (HBM,) * 5,
         [
             (shape, BF16, HBM),
             ((1,), jnp.int32, SMEM),
@@ -251,6 +282,7 @@
             (turned, BF16, HBM),
             (lifting, BF16, HBM),
             (row, BF16, HBM),
+            (listed, BF16, HBM),
         ],
         [
             pltpu.VMEM(far_blocks.shape, BF16),
@@ -262,9 +294,12 @@
             pltpu.VMEM(turned, BF16),
             pltpu.VMEM(lifting, BF16),
             pltpu.VMEM(row, BF16),
+            pltpu.VMEM(listed, BF16),
             semaphores(leaves),
             semaphores(leaves),
             semaphores(3),
+            semaphores(near_index.size),
+            semaphores(near_index.size // 8),
         ],
         "pack",
         0,
@@ -275,20 +310,14 @@
 def near_kernel(index_ref, mask_ref, blocks_ref, own_ref, *refs):
     out_ref, blocks, own, result, arrived, came, left = refs[-7:]
     leaves, entries, size, _ = blocks.shape
+    pair = leaves // CHUNKS
 
     def fetch(leaf):
-        halves = [pl.ds(j * (entries // 2), entries // 2) for j in range(2)]
-        return [
-            pltpu.make_async_copy(
-                blocks_ref.at[leaf, half], blocks.at[leaf, half], arrived.at[leaf, j]
-            )
-            for j, half in enumerate(halves)
-        ]
-
-    def store(leaf):
-        return pltpu.make_async_copy(
-            result.at[leaf], out_ref.at[leaf], left.at[leaf]
-        )
+        return [pltpu.make_async_copy(blocks_ref.at[leaf], blocks.at[leaf], arrived.at[leaf])]
+
+    def store(i):
+        some = slab(i, pair)
+        return pltpu.make_async_copy(result.at[some], out_ref.at[some], left.at[i])
 
     def work(leaf):
         total = None
@@ -300,7 +329,10 @@
             term = dot(blocks[leaf, n], values)
             total = term if total is None else total + term
         result[leaf] = total
-        store(leaf).start()
+
+        @pl.when(leaf % pair == pair - 1)
+        def _():
+            store(leaf // pair).start()
 
     begin, run = windowed(leaves, AHEAD, fetch, work)
     copy = pltpu.make_async_copy(own_ref, own, came)
@@ -308,8 +340,8 @@
     begin()
     copy.wait()
     run()
-    for leaf in range(leaves):
-        store(leaf).wait()
+    for i in range(CHUNKS):
+        store(i).wait()
 
 
 def near_field(near_index, near_mask, near_blocks, own, *earlier):
@@ -324,7 +356,7 @@
             pltpu.VMEM(near_blocks.shape, BF16),
             pltpu.VMEM(own.shape, BF16),
             pltpu.VMEM((leaves, size, columns), F32),
-            semaphores(leaves, 2),
+            semaphores(leaves),
             semaphores(),
             semaphores(leaves),
         ],
@@ -390,24 +422,22 @@
         ups[lax.rem(mate + count - 2 * j, count)] = other[j]
 
 
-def far_kernel(count_ref, list_ref, recv, packed_ref, blocks_ref, *refs):
+def far_kernel(count_ref, recv, packed_ref, blocks_ref, *refs):
     held = (len(refs) - 7) // 2
     sources, (_, far, blocks), targets = refs[:held], refs[held : held + 3], refs[held + 3 : -4]
     packed, arrived, fetched, loaded = refs[-4:]
     share = packed.shape[0] // CHUNKS
     width = packed.shape[2]
-    entries = blocks_ref.shape[1]
-    count = count_ref[0]
+    piece = blocks.shape[0] // fetched.shape[0]
+    count = (count_ref[0] + piece - 1) // piece
 
     def fetch(i):
         some = slab(i, share)
         return [pltpu.make_async_copy(packed_ref.at[some], packed.at[some], arrived.at[i])]
 
     def block(i):
-        entry = list_ref[i]
-        return pltpu.make_async_copy(
-            blocks_ref.at[entry // entries, entry % entries], blocks.at[i], fetched.at[i]
-        )
+        some = slab(i, piece)
+        return pltpu.make_async_copy(blocks_ref.at[some], blocks.at[some], fetched.at[i])
 
     def ask(i, carry):
         block(i).start()
@@ -447,19 +477,18 @@
         copy.wait()
 
 
-def far_field(listed, recv, packed, near_blocks, held, earlier):
+def far_field(count, recv, packed, blocks, held, earlier):
     sources, rows, _ = packed.shape
-    leaves, entries, size, _ = near_blocks.shape
-    outs = [((rows, recv.shape[2]), F32, VMEM), ((leaves * entries, size, size), BF16, VMEM)]
+    outs = [((rows, recv.shape[2]), F32, VMEM), (blocks.shape, BF16, VMEM)]
     far, blocks, *held = call(
         far_kernel,
-        (*listed, recv, packed, near_blocks, *held, earlier),
-        (SMEM, SMEM, VMEM, HBM, HBM) + (HBM,) * len(held) + (AFTER_VMEM,),
+        (count, recv, packed, blocks, *held, earlier),
+        (SMEM, VMEM, HBM, HBM) + (HBM,) * len(held) + (AFTER_VMEM,),
         outs + [(a.shape, a.dtype, VMEM) for a in held],
         [
             pltpu.VMEM(packed.shape, BF16),
             semaphores(CHUNKS),
-            semaphores(leaves * entries),
+            semaphores(blocks.shape[0] // 8),
             semaphores(len(held)),
         ],
         "far_field",
@@ -569,10 +598,10 @@
         (z_any,) = take(1)
     state_out, send = take(2)
     if sends:
-        coarse_any, low_any, high_any = take(3)
+        coarse_any, low, high = take(3)
     sums, split, arrived, left = take(4)
     if sends:
-        coarse, skeletons, out = take(3)
+        coarse, skeletons = take(2)
     if first:
         basis, transfer, vectors, came = take(4)
     else:
@@ -587,10 +616,12 @@
         some = slab(i, group)
         return [pltpu.make_async_copy(z_any.at[some], vectors.at[some], arrived.at[i])]
 
+    pieces = 2
+
     def stores(i):
-        some = slab(i, group)
+        some = slab(i, leaves // pieces)
         pairs = []
-        if not first:
+        if not first and sends:
             pairs.append((result.at[some], z_any.at[some]))
         if sends:
             pairs.append((coarse.at[some], coarse_any.at[some]))
@@ -611,15 +642,22 @@
                 for l in range(m):
                     z = z - coef[l : l + 1, :] * others[l + 1]
                 z = z * coef[STEPS : STEPS + 1, :]
-                result[leaf] = z
+                if sends:
+                    result[leaf] = z
+                else:
+                    z_any[leaf] = z
             if sends:
                 rounded = z.astype(BF16)
                 coarse[leaf] = rounded
                 skeletons[slab(leaf, rank)] = dot(basis[leaf], rounded).astype(BF16)
             for l, vector in enumerate(others + [z]):
                 sums[l] += jnp.sum((z * vector).reshape(size // 8, 8, z.shape[1]), axis=0)
-        for copy in stores(i):
-            copy.start()
+        share = CHUNKS // pieces
+
+        @pl.when(i % share == share - 1)
+        def _():
+            for copy in stores(i // share):
+                copy.start()
 
     begin, run = windowed(CHUNKS, CHUNKS, fetch, work)
     if first:
@@ -650,12 +688,8 @@
     run()
 
     if sends:
-        halos = [
-            pltpu.make_async_copy(coarse.at[pl.ds(0, HW)], low_any, out.at[0]),
-            pltpu.make_async_copy(coarse.at[pl.ds(leaves - HW, HW)], high_any, out.at[1]),
-        ]
-        for copy in halos:
-            copy.start()
+        low[...] = coarse[:HW]
+        high[...] = coarse[leaves - HW :]
         if first:
             lifted = dot_first(transfer[...].reshape(leaves * rank, rank), skeletons[...])
         else:
@@ -674,11 +708,8 @@
             send[r, (slots + 1) * rank :] = dots
     else:
         send[...] = dots
-    for i in range(CHUNKS):
+    for i in range(pieces):
         for copy in stores(i):
-            copy.wait()
-    if sends:
-        for copy in halos:
             copy.wait()
 
 
@@ -707,8 +738,8 @@
     get("send", (inner, rows, columns) if sends else (DOT_ROWS, columns), BF16, VMEM)
     if sends:
         get("coarse", tall, BF16, HBM)
-        get("low", (HW, size, columns), BF16, LOOSE)
-        get("high", (HW, size, columns), BF16, LOOSE)
+        get("low", (HW, size, columns), BF16, VMEM)
+        get("high", (HW, size, columns), BF16, VMEM)
 
     scratch = [
         pltpu.VMEM((STEPS + 1, 8, columns), F32),
@@ -720,7 +751,6 @@
         scratch += [
             pltpu.VMEM(tall, BF16),
             pltpu.VMEM((leaves * rank, columns), BF16),
-            semaphores(2),
         ]
     if first:
         scratch += [
@@ -884,8 +914,8 @@
 
     zs = [rhs.reshape(leaves, -1, rhs.shape[1])]
     out = stage(0, points, wanted, branch, zs[0], basis, transfer, None)
-    packed, count, entries, turned, lifting, top = pack(
-        branch, basis, transfer, top_blocks, far_blocks, far_mask, far_slot, near_index, near_mask,
+    packed, count, entries, turned, lifting, top, listed_blocks = pack(
+        branch, basis, transfer, top_blocks, near_blocks, far_blocks, far_mask, far_slot, near_index, near_mask,
         inner, slots,
     )
     listed = (count, entries)
@@ -900,7 +930,9 @@
         if k == STEPS:
             krylov = done = vectors(state, zs, list(range(STEPS - 1)), near, CHUNKS)[0]
         summed = gather_sum(recv, slots * rank, done)
-        local_far, blocks, (near,) = far_field(listed, recv, packed, near_blocks, (near,), summed)
+        local_far, blocks, (near,) = far_field(
+            count, recv, packed, listed_blocks, (near,), summed
+        )
 
         def between(column):
             held = (basis, turned, transfer, lifting, top, *zs)
@@ -913,12 +945,12 @@
         zs = zs + [out["z"]]
     low = 4 if inner % 4 == 0 else inner
     held = held[-STEPS:] + [out["z"]]
-    krylov = vectors(state, held, [STEPS - 1], krylov, CHUNKS)[0]
+    krylov = vectors(state, held, [STEPS - 1], krylov, 2)[0]
     summed = sum_over(out["send"], "inner", 1, low, krylov, AFTER)
     summed = sum_over(summed, "inner", low, inner // low, summed, AFTER_VMEM)
     column, other, _ = over_branches(summed, outer, summed, lambda column: None)
     products = [branch, column, other]
-    krylov, hessenberg = vectors(state, held, [STEPS], krylov, CHUNKS, products, points)
+    krylov, hessenberg = vectors(state, held, [STEPS], krylov, 2, products, points)
     return krylov.reshape(STEPS + 1, *rhs.shape), hessenberg
 
 

time: 216 us -> 216 us (level)
  waiting for transfers between devices: 29.5 us -> 34.2 us
  starting transfers between devices: 84.1 us -> 81.9 us
    ppermute x6, waiting for transfers between devices: 1.56 us -> 5.44 us  [sum_over(): lax.ppermute(dots, axis, [(i, moved(i, j)) for i in range(size)])]
    ppermute x6, starting transfers between devices: 7.35 us -> 4.51 us  [sum_over(): lax.ppermute(dots, axis, [(i, moved(i, j)) for i in range(size)])]
    ppermute x15, waiting for transfers between devices: 0.79 us -> 3.48 us  [over_branches(): lax.ppermute(summed, 'outer', shift)]
    ppermute x5, starting transfers between devices: 13.7 us -> 16.3 us  [over_branches(): other = lax.ppermute(column, 'outer', [(o, o ^ 1) for o in range(outer)])]
  transfers between devices with their start and end apart: 38 -> 38, of which waited for: 8 -> 12; matrix products, arithmetic and copies ran while one was open for 0% -> 0% of each run, Pallas kernels for 35% -> 35%
where the time goes in v7:
time: 216 us; the launch traced here: 215 us
  Pallas kernels  97.7 us (45%)
  starting transfers between devices  81.9 us (38%)
  waiting for transfers between devices  34.2 us (16%)
    pallas_call x32, Pallas kernels, call(): pl.pallas_call(kernel, in_specs=list(in_specs), out_specs=[spec for _, _,...  97.7 us
    all_to_all x4, starting transfers between devices, exchange(): return lax.all_to_all(array, axis, split_axis=0, concat_axis=0, tiled=True)  25 us
    all_to_all x4, waiting for transfers between devices, exchange(): return lax.all_to_all(array, axis, split_axis=0, concat_axis=0, tiled=True)  24.4 us
    ppermute x15, starting transfers between devices, over_branches(): lax.ppermute(summed, 'outer', shift)  17.8 us
    ppermute x5, starting transfers between devices, over_branches(): other = lax.ppermute(column, 'outer', [(o, o ^ 1) for o in range(outer)])  16.3 us
    ppermute x4, starting transfers between devices, shards(): before = lax.ppermute(out['high'], 'inner', up_pairs)  13.1 us
    ppermute x6, waiting for transfers between devices, sum_over(): lax.ppermute(dots, axis, [(i, moved(i, j)) for i in range(size)])  5.44 us
    ppermute x4, starting transfers between devices, shards(): after = lax.ppermute(out['low'], 'inner', down_pairs)  5.17 us
  transfers between devices with their start and end apart: 38, of which 12 were waited for; matrix products, arithmetic and copies ran while one was open for 0% of the time, Pallas kernels for 35%

profile of v7, /device:TPU:1, one launch (start us, length us, event | category | flops | bytes accessed | tf_op | source)
XLA Modules:
  0.0 215.0 jit_solution(16156609698177619988)
XLA Ops:
  0.6 4.3 %stage0.1 = (f32[64,128]{1,0:T(8,128)S(1)}, bf16[16,336,128]{2,1,0:T(8,128)(2,1)}, bf16[8,256,128]{2,1,0:T(8,128)(2,1)}, bf16[2,256,128]{2,1,0:T(8,128)(2,1)S(1)}, bf16[2,256,128]{2,1,0:T(8,128)(2,1)S(1)}) custom-call(s32[4,16]{1,0:T(4,128)} %bitcast.13, s32[1]{0:T(128)} %bitcast.2.refs_1_.branch, f32[8,256,128]{2,1,0:T(8,128)} %bitcast.7, ...), custom_call_target="tpu_custom_call" | custom-call | flops 134217728 | bytes 4194304 | tf_op jit(solution)/shard_map/stage0/pallas_call | solution.py:116
  5.0 8.6 %all-to-all-start = ((bf16[16,336,128]{2,1,0:T(8,128)(2,1)}), bf16[16,336,128]{2,1,0:T(8,128)(2,1)S(1)}, u32[]{:S(2)}, u32[]{:S(2)}) async-start(bf16[16,336,128]{2,1,0:T(8,128)(2,1)} %get-tuple-element.83), calls=%async_computation | async-start | bytes 2752512 | tf_op jit(solution)/shard_map/all_to_all | solution.py:913
  13.6 3.3 %collective-permute-start.4 = (bf16[2,256,128]{2,1,0:T(8,128)(2,1)S(1)}, bf16[2,256,128]{2,1,0:T(8,128)(2,1)S(1)}, u32[]{:S(2)}, u32[]{:S(2)}) collective-permute-start(bf16[2,256,128]{2,1,0:T(8,128)(2,1)S(1)} %get-tuple-element.92), channel_id=1, source_target_pairs={{0,1},{1,2},{2,3},{3,4},{4,5},{5,6},{6,7},{7,8},{8,9},{9,10},{10,1... | collective-permute-start | bytes 393224 | tf_op jit(solution)/shard_map/ppermute | solution.py:925
  16.9 1.3 collective-permute-start.5
  18.2 12.0 %pack.1 = (bf16[16,512,256]{2,1,0:T(8,128)(2,1)}, s32[1]{0:T(128)}, s32[64]{0:T(128)S(1)}, bf16[8,256,64]{2,1,0:T(8,128)(2,1)}, bf16[64,512]{1,0:T(8,128)(2,1)},...) custom-call(s32[1]{0:T(128)} %bitcast.2.refs_1_.branch, s32[8,48]{1,0:T(8,128)} %mask_ref.5, s32[8,48]{1,0:T(8,128)} %slot_ref.1, ...), custom_call_target="tpu_custom_call" | custom-call | bytes 10485760 | tf_op jit(solution)/shard_map/pack/pallas_call | solution.py:116
  30.2 7.0 %near_field.4.refs_0_ = f32[8,256,128]{2,1,0:T(8,128)} custom-call(s32[8,8]{1,0:T(8,128)} %index_ref.17, s32[8,8]{1,0:T(8,128)} %mask_ref.9, bf16[8,8,256,256]{3,2,1,0:T(8,128)(2,1)} %blocks_ref.7, bf16[8,256,128]{2,1,0:T(8,128)(2,1)} %get-tuple-element.84.own_ref, bf16[16,512,256]{2,1,0:T(8,128)(2,1)} %get-tuple-element.85.refs_0_.packed_ref), custom_call_target="tpu_custom_call" | custom-call | flops 1073741824 | bytes 8388608 | tf_op jit(solution)/shard_map/near_field/pallas_call | solution.py:116
  37.3 2.7 %collective-permute-start.2 = (bf16[80,128]{1,0:T(8,128)(2,1)S(1)}, bf16[80,128]{1,0:T(8,128)(2,1)S(1)}, u32[]{:S(2)}, u32[]{:S(2)}) collective-permute-start(bf16[80,128]{1,0:T(8,128)(2,1)S(1)} %gather_sum.4.refs_1_.refs_0_), channel_id=1, source_target_pairs={{0,96},{16,112},{32,0},{48,16},{64,32},{80,48},{96,64},{112,80},{1... | collective-permute-start | bytes 61448 | tf_op jit(solution)/shard_map/ppermute | solution.py:402
  41.1 3.9 %far_field.4 = (f32[512,128]{1,0:T(8,128)S(1)}, bf16[64,256,256]{2,1,0:T(8,128)(2,1)S(1)}, f32[8,256,128]{2,1,0:T(8,128)S(1)}) custom-call(s32[1]{0:T(128)} %get-tuple-element.86.count_ref, bf16[16,336,128]{2,1,0:T(8,128)(2,1)S(1)} %all-to-all-done.recv, bf16[16,512,256]{2,1,0:T(8,128)(2,1)} %get-tuple-element.85.refs_0_.packed_ref, ...), custom_call_target="tpu_custom_call" | custom-call | flops 536870912 | bytes 4194304 | tf_op jit(solution)/shard_map/far_field/pallas_call | solution.py:116
  45.1 2.7 %collective-permute-start.3 = (bf16[4,80,128]{2,1,0:T(8,128)(2,1)S(1)}, bf16[4,80,128]{2,1,0:T(8,128)(2,1)S(1)}, u32[]{:S(2)}, u32[]{:S(2)}) collective-permute-start(bf16[4,80,128]{2,1,0:T(8,128)(2,1)S(1)} %stack.5.refs_6_.refs_2_), channel_id=1, source_target_pairs={{0,16},{16,0},{32,48},{48,32},{64,80},{80,64},{96,112},{112,96},{1... | collective-permute-start | bytes 245768 | tf_op jit(solution)/shard_map/ppermute | solution.py:413
  47.7 3.0 %halo_part.4 = (f32[8,256,128]{2,1,0:T(8,128)S(1)}, bf16[8,64,256]{2,1,0:T(8,128)(2,1)S(1)}, bf16[8,256,64]{2,1,0:T(8,128)(2,1)S(1)}, bf16[8,64,64]{2,1,0:T(8,12...) custom-call(s32[1]{0:T(128)} %get-tuple-element.86.count_ref, ...), custom_call_target="tpu_custom_call", output_to_operand_aliasing={{0}: (6, {})} | custom-call | flops 268435456 | bytes 2097152 | tf_op jit(solution)/shard_map/halo_part/pallas_call | solution.py:116
  50.8 4.9 %stage1.1 = (f32[8,256,128]{2,1,0:T(8,128)}, f32[64,128]{1,0:T(8,128)S(1)}, bf16[16,336,128]{2,1,0:T(8,128)(2,1)}, bf16[8,256,128]{2,1,0:T(8,128)(2,1)}, bf16[2,...) custom-call(s32[4,16]{1,0:T(4,128)} %bitcast.14, s32[1]{0:T(128)} %bitcast.2.refs_1_.branch, ...), custom_call_target="tpu_custom_call" | custom-call | flops 134217728 | bytes 5242880 | tf_op jit(solution)/shard_map/stage1/pallas_call | solution.py:116
  55.6 7.7 %all-to-all-start.1 = ((bf16[16,336,128]{2,1,0:T(8,128)(2,1)}), bf16[16,336,128]{2,1,0:T(8,128)(2,1)S(1)}, u32[]{:S(2)}, u32[]{:S(2)}) async-start(bf16[16,336,128]{2,1,0:T(8,128)(2,1)} %get-tuple-element.105), calls=%async_computation.1 | async-start | bytes 2752512 | tf_op jit(solution)/shard_map/all_to_all | solution.py:913
  63.4 3.3 %collective-permute-start.10 = (bf16[2,256,128]{2,1,0:T(8,128)(2,1)S(1)}, bf16[2,256,128]{2,1,0:T(8,128)(2,1)S(1)}, u32[]{:S(2)}, u32[]{:S(2)}) collective-permute-start(bf16[2,256,128]{2,1,0:T(8,128)(2,1)S(1)} %get-tuple-element.110), channel_id=1, source_target_pairs={{0,1},{1,2},{2,3},{3,4},{4,5},{5,6},{6,7},{7,8},{8,9},{9,10},{10,1... | collective-permute-start | bytes 393224 | tf_op jit(solution)/shard_map/ppermute | solution.py:925
  66.7 1.3 collective-permute-start.11
  68.0 7.0 %near_field.5.refs_0_ = f32[8,256,128]{2,1,0:T(8,128)} custom-call(s32[8,8]{1,0:T(8,128)} %index_ref.17, s32[8,8]{1,0:T(8,128)} %mask_ref.9, bf16[8,8,256,256]{3,2,1,0:T(8,128)(2,1)} %blocks_ref.7, bf16[8,256,128]{2,1,0:T(8,128)(2,1)} %get-tuple-element.106.own_ref), custom_call_target="tpu_custom_call" | custom-call | flops 1073741824 | bytes 8388608 | tf_op jit(solution)/shard_map/near_field/pallas_call | solution.py:116
  74.9 8.3 %all-to-all-done.1.recv = bf16[16,336,128]{2,1,0:T(8,128)(2,1)S(1)} async-done(((bf16[16,336,128]{2,1,0:T(8,128)(2,1)}), bf16[16,336,128]{2,1,0:T(8,128)(2,1)S(1)}, u32[]{:S(2)}, u32[]{:S(2)}) %all-to-all-start.1) | async-done | bytes 1376288 | tf_op jit(solution)/shard_map/all_to_all | solution.py:913
  83.3 3.3 %collective-permute-start.8 = (bf16[80,128]{1,0:T(8,128)(2,1)S(1)}, bf16[80,128]{1,0:T(8,128)(2,1)S(1)}, u32[]{:S(2)}, u32[]{:S(2)}) collective-permute-start(bf16[80,128]{1,0:T(8,128)(2,1)S(1)} %gather_sum.5.refs_1_.refs_0_), channel_id=1, source_target_pairs={{0,96},{16,112},{32,0},{48,16},{64,32},{80,48},{96,64},{112,80},{1... | collective-permute-start | bytes 61448 | tf_op jit(solution)/shard_map/ppermute | solution.py:402
  87.7 3.9 %far_field.5 = (f32[512,128]{1,0:T(8,128)S(1)}, bf16[64,256,256]{2,1,0:T(8,128)(2,1)S(1)}, f32[8,256,128]{2,1,0:T(8,128)S(1)}) custom-call(s32[1]{0:T(128)} %get-tuple-element.86.count_ref, bf16[16,336,128]{2,1,0:T(8,128)(2,1)S(1)} %all-to-all-done.1.recv, bf16[16,512,256]{2,1,0:T(8,128)(2,1)} %get-tuple-element.85.refs_0_.packed_ref, ...), custom_call_target="tpu_custom_call" | custom-call | flops 536870912 | bytes 4194304 | tf_op jit(solution)/shard_map/far_field/pallas_call | solution.py:116
  91.7 3.1 %collective-permute-start.9 = (bf16[4,80,128]{2,1,0:T(8,128)(2,1)S(1)}, bf16[4,80,128]{2,1,0:T(8,128)(2,1)S(1)}, u32[]{:S(2)}, u32[]{:S(2)}) collective-permute-start(bf16[4,80,128]{2,1,0:T(8,128)(2,1)S(1)} %stack.6.refs_7_.refs_2_), channel_id=1, source_target_pairs={{0,16},{16,0},{32,48},{48,32},{64,80},{80,64},{96,112},{112,96},{1... | collective-permute-start | bytes 245768 | tf_op jit(solution)/shard_map/ppermute | solution.py:413
  94.7 3.3 %halo_part.5 = (f32[8,256,128]{2,1,0:T(8,128)S(1)}, bf16[8,64,256]{2,1,0:T(8,128)(2,1)S(1)}, bf16[8,256,64]{2,1,0:T(8,128)(2,1)S(1)}, bf16[8,64,64]{2,1,0:T(8,12...) custom-call(s32[1]{0:T(128)} %get-tuple-element.86.count_ref, ...), custom_call_target="tpu_custom_call", output_to_operand_aliasing={{0}: (6, {})} | custom-call | flops 268435456 | bytes 2097152 | tf_op jit(solution)/shard_map/halo_part/pallas_call | solution.py:116
  98.1 4.9 %stage2.1 = (f32[8,256,128]{2,1,0:T(8,128)}, f32[64,128]{1,0:T(8,128)S(1)}, bf16[16,336,128]{2,1,0:T(8,128)(2,1)}, bf16[8,256,128]{2,1,0:T(8,128)(2,1)}, bf16[2,...) custom-call(s32[4,16]{1,0:T(4,128)} %bitcast.15, s32[1]{0:T(128)} %bitcast.2.refs_1_.branch, ...), custom_call_target="tpu_custom_call" | custom-call | flops 134217728 | bytes 6291456 | tf_op jit(solution)/shard_map/stage2/pallas_call | solution.py:116
  103.0 4.3 %all-to-all-start.2 = ((bf16[16,336,128]{2,1,0:T(8,128)(2,1)}), bf16[16,336,128]{2,1,0:T(8,128)(2,1)S(1)}, u32[]{:S(2)}, u32[]{:S(2)}) async-start(bf16[16,336,128]{2,1,0:T(8,128)(2,1)} %get-tuple-element.122), calls=%async_computation.2 | async-start | bytes 2752512 | tf_op jit(solution)/shard_map/all_to_all | solution.py:913
  107.3 3.3 %collective-permute-start.16 = (bf16[2,256,128]{2,1,0:T(8,128)(2,1)S(1)}, bf16[2,256,128]{2,1,0:T(8,128)(2,1)S(1)}, u32[]{:S(2)}, u32[]{:S(2)}) collective-permute-start(bf16[2,256,128]{2,1,0:T(8,128)(2,1)S(1)} %get-tuple-element.127), channel_id=1, source_target_pairs={{0,1},{1,2},{2,3},{3,4},{4,5},{5,6},{6,7},{7,8},{8,9},{9,10},{10,1... | collective-permute-start | bytes 393224 | tf_op jit(solution)/shard_map/ppermute | solution.py:925
  110.6 1.3 collective-permute-start.17
  111.9 7.0 %near_field.6.refs_0_ = f32[8,256,128]{2,1,0:T(8,128)} custom-call(s32[8,8]{1,0:T(8,128)} %index_ref.17, s32[8,8]{1,0:T(8,128)} %mask_ref.9, bf16[8,8,256,256]{3,2,1,0:T(8,128)(2,1)} %blocks_ref.7, bf16[8,256,128]{2,1,0:T(8,128)(2,1)} %get-tuple-element.123.own_ref), custom_call_target="tpu_custom_call" | custom-call | flops 1073741824 | bytes 8388608 | tf_op jit(solution)/shard_map/near_field/pallas_call | solution.py:116
  118.9 9.9 %all-to-all-done.2.recv = bf16[16,336,128]{2,1,0:T(8,128)(2,1)S(1)} async-done(((bf16[16,336,128]{2,1,0:T(8,128)(2,1)}), bf16[16,336,128]{2,1,0:T(8,128)(2,1)S(1)}, u32[]{:S(2)}, u32[]{:S(2)}) %all-to-all-start.2) | async-done | bytes 1376288 | tf_op jit(solution)/shard_map/all_to_all | solution.py:913
  128.8 2.3 %collective-permute-start.14 = (bf16[80,128]{1,0:T(8,128)(2,1)S(1)}, bf16[80,128]{1,0:T(8,128)(2,1)S(1)}, u32[]{:S(2)}, u32[]{:S(2)}) collective-permute-start(bf16[80,128]{1,0:T(8,128)(2,1)S(1)} %gather_sum.6.refs_1_.refs_0_), channel_id=1, source_target_pairs={{0,96},{16,112},{32,0},{48,16},{64,32},{80,48},{96,64},{112,80},{1... | collective-permute-start | bytes 61448 | tf_op jit(solution)/shard_map/ppermute | solution.py:402
  131.8 3.9 %far_field.6 = (f32[512,128]{1,0:T(8,128)S(1)}, bf16[64,256,256]{2,1,0:T(8,128)(2,1)S(1)}, f32[8,256,128]{2,1,0:T(8,128)S(1)}) custom-call(s32[1]{0:T(128)} %get-tuple-element.86.count_ref, bf16[16,336,128]{2,1,0:T(8,128)(2,1)S(1)} %all-to-all-done.2.recv, bf16[16,512,256]{2,1,0:T(8,128)(2,1)} %get-tuple-element.85.refs_0_.packed_ref, ...), custom_call_target="tpu_custom_call" | custom-call | flops 536870912 | bytes 4194304 | tf_op jit(solution)/shard_map/far_field/pallas_call | solution.py:116
  135.8 2.7 %collective-permute-start.15 = (bf16[4,80,128]{2,1,0:T(8,128)(2,1)S(1)}, bf16[4,80,128]{2,1,0:T(8,128)(2,1)S(1)}, u32[]{:S(2)}, u32[]{:S(2)}) collective-permute-start(bf16[4,80,128]{2,1,0:T(8,128)(2,1)S(1)} %stack.7.refs_8_.refs_2_), channel_id=1, source_target_pairs={{0,16},{16,0},{32,48},{48,32},{64,80},{80,64},{96,112},{112,96},{1... | collective-permute-start | bytes 245768 | tf_op jit(solution)/shard_map/ppermute | solution.py:413
  138.4 3.6 %halo_part.6 = (f32[8,256,128]{2,1,0:T(8,128)S(1)}, bf16[8,64,256]{2,1,0:T(8,128)(2,1)S(1)}, bf16[8,256,64]{2,1,0:T(8,128)(2,1)S(1)}, bf16[8,64,64]{2,1,0:T(8,12...) custom-call(s32[1]{0:T(128)} %get-tuple-element.86.count_ref, ...), custom_call_target="tpu_custom_call", output_to_operand_aliasing={{0}: (6, {})} | custom-call | flops 268435456 | bytes 2097152 | tf_op jit(solution)/shard_map/halo_part/pallas_call | solution.py:116
  142.1 5.1 %stage3.1 = (f32[8,256,128]{2,1,0:T(8,128)}, f32[64,128]{1,0:T(8,128)S(1)}, bf16[16,336,128]{2,1,0:T(8,128)(2,1)}, bf16[8,256,128]{2,1,0:T(8,128)(2,1)}, bf16[2,...) custom-call(s32[4,16]{1,0:T(4,128)} %bitcast.16, s32[1]{0:T(128)} %bitcast.2.refs_1_.branch, ...), custom_call_target="tpu_custom_call" | custom-call | flops 134217728 | bytes 7340032 | tf_op jit(solution)/shard_map/stage3/pallas_call | solution.py:116
  147.1 4.3 %all-to-all-start.3 = ((bf16[16,336,128]{2,1,0:T(8,128)(2,1)}), bf16[16,336,128]{2,1,0:T(8,128)(2,1)S(1)}, u32[]{:S(2)}, u32[]{:S(2)}) async-start(bf16[16,336,128]{2,1,0:T(8,128)(2,1)} %get-tuple-element.140), calls=%async_computation.3 | async-start | bytes 2752512 | tf_op jit(solution)/shard_map/all_to_all | solution.py:913
  151.5 3.3 %collective-permute-start.22 = (bf16[2,256,128]{2,1,0:T(8,128)(2,1)S(1)}, bf16[2,256,128]{2,1,0:T(8,128)(2,1)S(1)}, u32[]{:S(2)}, u32[]{:S(2)}) collective-permute-start(bf16[2,256,128]{2,1,0:T(8,128)(2,1)S(1)} %get-tuple-element.145), channel_id=1, source_target_pairs={{0,1},{1,2},{2,3},{3,4},{4,5},{5,6},{6,7},{7,8},{8,9},{9,10},{10,1... | collective-permute-start | bytes 393224 | tf_op jit(solution)/shard_map/ppermute | solution.py:925
  156.1 7.0 %near_field.7.refs_4_.refs_0_ = f32[8,256,128]{2,1,0:T(8,128)} custom-call(s32[8,8]{1,0:T(8,128)} %index_ref.17, s32[8,8]{1,0:T(8,128)} %mask_ref.9, bf16[8,8,256,256]{3,2,1,0:T(8,128)(2,1)} %blocks_ref.7, bf16[8,256,128]{2,1,0:T(8,128)(2,1)} %get-tuple-element.142.own_ref), custom_call_target="tpu_custom_call" | custom-call | flops 1073741824 | bytes 8388608 | tf_op jit(solution)/shard_map/near_field/pallas_call | solution.py:116
  163.1 3.5 %vectors.2.refs_0_.refs_5_ = f32[5,8,256,128]{3,2,1,0:T(8,128)} custom-call(f32[64,128]{1,0:T(8,128)S(1)} %get-tuple-element.141.refs_0_.refs_4_, f32[8,256,128]{2,1,0:T(8,128)} %bitcast.11, f32[8,256,128]{2,1,0:T(8,128)} %get-tuple-element.113.refs_6_.refs_2_, f32[8,256,128]{2,1,0:T(8,128)} %get-tuple-element.130.refs_7_.refs_3_, ...), custom_call_target="tpu_custom_call" | custom-call | flops 8388608 | bytes 6291456 | tf_op jit(solution)/shard_map/vectors/pallas_call | solution.py:116
  166.6 6.3 %all-to-all-done.3.recv = bf16[16,336,128]{2,1,0:T(8,128)(2,1)S(1)} async-done(((bf16[16,336,128]{2,1,0:T(8,128)(2,1)}), bf16[16,336,128]{2,1,0:T(8,128)(2,1)S(1)}, u32[]{:S(2)}, u32[]{:S(2)}) %all-to-all-start.3) | async-done | bytes 1376288 | tf_op jit(solution)/shard_map/all_to_all | solution.py:913
  173.0 2.3 %collective-permute-start.20 = (bf16[80,128]{1,0:T(8,128)(2,1)S(1)}, bf16[80,128]{1,0:T(8,128)(2,1)S(1)}, u32[]{:S(2)}, u32[]{:S(2)}) collective-permute-start(bf16[80,128]{1,0:T(8,128)(2,1)S(1)} %gather_sum.7.refs_1_.refs_0_), channel_id=1, source_target_pairs={{0,96},{16,112},{32,0},{48,16},{64,32},{80,48},{96,64},{112,80},{1... | collective-permute-start | bytes 61448 | tf_op jit(solution)/shard_map/ppermute | solution.py:402
  176.4 3.9 %far_field.7 = (f32[512,128]{1,0:T(8,128)S(1)}, bf16[64,256,256]{2,1,0:T(8,128)(2,1)S(1)}, f32[8,256,128]{2,1,0:T(8,128)S(1)}) custom-call(s32[1]{0:T(128)} %get-tuple-element.86.count_ref, bf16[16,336,128]{2,1,0:T(8,128)(2,1)S(1)} %all-to-all-done.3.recv, bf16[16,512,256]{2,1,0:T(8,128)(2,1)} %get-tuple-element.85.refs_0_.packed_ref, ...), custom_call_target="tpu_custom_call" | custom-call | flops 536870912 | bytes 4194304 | tf_op jit(solution)/shard_map/far_field/pallas_call | solution.py:116
  180.4 3.1 %collective-permute-start.21 = (bf16[4,80,128]{2,1,0:T(8,128)(2,1)S(1)}, bf16[4,80,128]{2,1,0:T(8,128)(2,1)S(1)}, u32[]{:S(2)}, u32[]{:S(2)}) collective-permute-start(bf16[4,80,128]{2,1,0:T(8,128)(2,1)S(1)} %stack.8.refs_9_.refs_2_), channel_id=1, source_target_pairs={{0,16},{16,0},{32,48},{48,32},{64,80},{80,64},{96,112},{112,96},{1... | collective-permute-start | bytes 245768 | tf_op jit(solution)/shard_map/ppermute | solution.py:413
  183.4 4.0 %halo_part.7 = (f32[8,256,128]{2,1,0:T(8,128)S(1)}, bf16[8,64,256]{2,1,0:T(8,128)(2,1)S(1)}, bf16[8,256,64]{2,1,0:T(8,128)(2,1)S(1)}, bf16[8,64,64]{2,1,0:T(8,12...) custom-call(s32[1]{0:T(128)} %get-tuple-element.86.count_ref, ...), custom_call_target="tpu_custom_call", output_to_operand_aliasing={{0}: (6, {})} | custom-call | flops 268435456 | bytes 2097152 | tf_op jit(solution)/shard_map/halo_part/pallas_call | solution.py:116
  187.4 2.3 %stage4.1 = (f32[8,256,128]{2,1,0:T(8,128)S(1)}, f32[64,128]{1,0:T(8,128)S(1)}, bf16[16,128]{1,0:T(8,128)(2,1)S(1)}) custom-call(s32[4,16]{1,0:T(4,128)} %bitcast.17, s32[1]{0:T(128)} %bitcast.2.refs_1_.branch, bf16[4,80,128]{2,1,0:T(8,128)(2,1)S(1)} %stack.8.refs_9_.refs_2_, bf16[4,80,128]{2,1,0:T(8,128)(2,1)S(1)} %collective-permute-done.21.refs_3_, ...), custom_call_target="tpu_custom_call" | custom-call | flops 134217728 | bytes 8388608 | tf_op jit(solution)/shard_map/stage4/pallas_call | solution.py:116
  190.4 1.5 collective-permute-start.25
  193.0 1.3 collective-permute-done.25.refs_2_
  198.1 2.0 collective-permute-done.28.refs_2_
  200.9 2.3 %collective-permute-start.32 = (bf16[16,128]{1,0:T(8,128)(2,1)S(1)}, bf16[16,128]{1,0:T(8,128)(2,1)S(1)}, u32[]{:S(2)}, u32[]{:S(2)}) collective-permute-start(bf16[16,128]{1,0:T(8,128)(2,1)S(1)} %sum_over.3.refs_0_.refs_4_), channel_id=1, source_target_pairs={{0,96},{16,112},{32,0},{48,16},{64,32},{80,48},{96,64},{112,80},{1... | collective-permute-start | bytes 12296 | tf_op jit(solution)/shard_map/ppermute | solution.py:402
  204.0 3.2 %collective-permute-done.31.refs_2_ = bf16[16,128]{1,0:T(8,128)(2,1)S(1)} collective-permute-done((bf16[16,128]{1,0:T(8,128)(2,1)S(1)}, bf16[16,128]{1,0:T(8,128)(2,1)S(1)}, u32[]{:S(2)}, u32[]{:S(2)}) %collective-permute-start.31) | collective-permute-done | bytes 4128 | tf_op jit(solution)/shard_map/ppermute | solution.py:402
  207.4 4.9 %collective-permute-start.33 = (bf16[4,16,128]{2,1,0:T(8,128)(2,1)S(1)}, bf16[4,16,128]{2,1,0:T(8,128)(2,1)S(1)}, u32[]{:S(2)}, u32[]{:S(2)}) collective-permute-start(bf16[4,16,128]{2,1,0:T(8,128)(2,1)S(1)} %stack.9.refs_2_), channel_id=1, source_target_pairs={{0,16},{16,0},{32,48},{48,32},{64,80},{80,64},{96,112},{112,96},{1... | collective-permute-start | bytes 49160 | tf_op jit(solution)/shard_map/ppermute | solution.py:413
  213.1 1.8 last_vector.1
  (62 shorter events, 13.9 us)
Async XLA Ops:
  5.0 32.2 %all-to-all-start = ((bf16[16,336,128]{2,1,0:T(8,128)(2,1)}), bf16[16,336,128]{2,1,0:T(8,128)(2,1)S(1)}, u32[]{:S(2)}, u32[]{:S(2)}) async-start(bf16[16,336,128]{2,1,0:T(8,128)(2,1)} %get-tuple-element.83), calls=%async_computation | async-start | bytes 2752512 | tf_op jit(solution)/shard_map/all_to_all | solution.py:913
  13.6 34.2 %collective-permute-start.4 = (bf16[2,256,128]{2,1,0:T(8,128)(2,1)S(1)}, bf16[2,256,128]{2,1,0:T(8,128)(2,1)S(1)}, u32[]{:S(2)}, u32[]{:S(2)}) collective-permute-start(bf16[2,256,128]{2,1,0:T(8,128)(2,1)S(1)} %get-tuple-element.92), channel_id=1, source_target_pairs={{0,1},{1,2},{2,3},{3,4},{4,5},{5,6},{6,7},{7,8},{8,9},{9,10},{10,1... | collective-permute-start | bytes 393224 | tf_op jit(solution)/shard_map/ppermute | solution.py:925
  16.9 30.9 %collective-permute-start.5 = (bf16[2,256,128]{2,1,0:T(8,128)(2,1)S(1)}, bf16[2,256,128]{2,1,0:T(8,128)(2,1)S(1)}, u32[]{:S(2)}, u32[]{:S(2)}) collective-permute-start(bf16[2,256,128]{2,1,0:T(8,128)(2,1)S(1)} %get-tuple-element.93), channel_id=1, source_target_pairs={{1,0},{2,1},{3,2},{4,3},{5,4},{6,5},{7,6},{8,7},{9,8},{10,9},{11,1... | collective-permute-start | bytes 393224 | tf_op jit(solution)/shard_map/ppermute | solution.py:926
  30.2 7.0 %copy-start = (s32[64]{0:T(128)}, s32[64]{0:T(128)S(1)}, u32[]{:S(2)}) copy-start(s32[64]{0:T(128)S(1)} %get-tuple-element.90.list_ref) | copy-start | bytes 772
  37.3 7.8 %collective-permute-start.2 = (bf16[80,128]{1,0:T(8,128)(2,1)S(1)}, bf16[80,128]{1,0:T(8,128)(2,1)S(1)}, u32[]{:S(2)}, u32[]{:S(2)}) collective-permute-start(bf16[80,128]{1,0:T(8,128)(2,1)S(1)} %gather_sum.4.refs_1_.refs_0_), channel_id=1, source_target_pairs={{0,96},{16,112},{32,0},{48,16},{64,32},{80,48},{96,64},{112,80},{1... | collective-permute-start | bytes 61448 | tf_op jit(solution)/shard_map/ppermute | solution.py:402
  39.9 5.1 %collective-permute-start.1 = (bf16[80,128]{1,0:T(8,128)(2,1)S(1)}, bf16[80,128]{1,0:T(8,128)(2,1)S(1)}, u32[]{:S(2)}, u32[]{:S(2)}) collective-permute-start(bf16[80,128]{1,0:T(8,128)(2,1)S(1)} %gather_sum.4.refs_1_.refs_0_), channel_id=1, source_target_pairs={{0,64},{16,80},{32,96},{48,112},{64,0},{80,16},{96,32},{112,48},{1... | collective-permute-start | bytes 61448 | tf_op jit(solution)/shard_map/ppermute | solution.py:402
  40.4 4.7 %collective-permute-start = (bf16[80,128]{1,0:T(8,128)(2,1)S(1)}, bf16[80,128]{1,0:T(8,128)(2,1)S(1)}, u32[]{:S(2)}, u32[]{:S(2)}) collective-permute-start(bf16[80,128]{1,0:T(8,128)(2,1)S(1)} %gather_sum.4.refs_1_.refs_0_), channel_id=1, source_target_pairs={{0,32},{16,48},{32,64},{48,80},{64,96},{80,112},{96,0},{112,16},{1... | collective-permute-start | bytes 61448 | tf_op jit(solution)/shard_map/ppermute | solution.py:402
  45.1 5.7 %collective-permute-start.3 = (bf16[4,80,128]{2,1,0:T(8,128)(2,1)S(1)}, bf16[4,80,128]{2,1,0:T(8,128)(2,1)S(1)}, u32[]{:S(2)}, u32[]{:S(2)}) collective-permute-start(bf16[4,80,128]{2,1,0:T(8,128)(2,1)S(1)} %stack.5.refs_6_.refs_2_), channel_id=1, source_target_pairs={{0,16},{16,0},{32,48},{48,32},{64,80},{80,64},{96,112},{112,96},{1... | collective-permute-start | bytes 245768 | tf_op jit(solution)/shard_map/ppermute | solution.py:413
  55.6 27.6 %all-to-all-start.1 = ((bf16[16,336,128]{2,1,0:T(8,128)(2,1)}), bf16[16,336,128]{2,1,0:T(8,128)(2,1)S(1)}, u32[]{:S(2)}, u32[]{:S(2)}) async-start(bf16[16,336,128]{2,1,0:T(8,128)(2,1)} %get-tuple-element.105), calls=%async_computation.1 | async-start | bytes 2752512 | tf_op jit(solution)/shard_map/all_to_all | solution.py:913
  63.4 31.3 %collective-permute-start.10 = (bf16[2,256,128]{2,1,0:T(8,128)(2,1)S(1)}, bf16[2,256,128]{2,1,0:T(8,128)(2,1)S(1)}, u32[]{:S(2)}, u32[]{:S(2)}) collective-permute-start(bf16[2,256,128]{2,1,0:T(8,128)(2,1)S(1)} %get-tuple-element.110), channel_id=1, source_target_pairs={{0,1},{1,2},{2,3},{3,4},{4,5},{5,6},{6,7},{7,8},{8,9},{9,10},{10,1... | collective-permute-start | bytes 393224 | tf_op jit(solution)/shard_map/ppermute | solution.py:925
  66.7 28.1 %collective-permute-start.11 = (bf16[2,256,128]{2,1,0:T(8,128)(2,1)S(1)}, bf16[2,256,128]{2,1,0:T(8,128)(2,1)S(1)}, u32[]{:S(2)}, u32[]{:S(2)}) collective-permute-start(bf16[2,256,128]{2,1,0:T(8,128)(2,1)S(1)} %get-tuple-element.111), channel_id=1, source_target_pairs={{1,0},{2,1},{3,2},{4,3},{5,4},{6,5},{7,6},{8,7},{9,8},{10,9},{11,1... | collective-permute-start | bytes 393224 | tf_op jit(solution)/shard_map/ppermute | solution.py:926
  83.3 8.3 %collective-permute-start.8 = (bf16[80,128]{1,0:T(8,128)(2,1)S(1)}, bf16[80,128]{1,0:T(8,128)(2,1)S(1)}, u32[]{:S(2)}, u32[]{:S(2)}) collective-permute-start(bf16[80,128]{1,0:T(8,128)(2,1)S(1)} %gather_sum.5.refs_1_.refs_0_), channel_id=1, source_target_pairs={{0,96},{16,112},{32,0},{48,16},{64,32},{80,48},{96,64},{112,80},{1... | collective-permute-start | bytes 61448 | tf_op jit(solution)/shard_map/ppermute | solution.py:402
  86.6 5.1 %collective-permute-start.7 = (bf16[80,128]{1,0:T(8,128)(2,1)S(1)}, bf16[80,128]{1,0:T(8,128)(2,1)S(1)}, u32[]{:S(2)}, u32[]{:S(2)}) collective-permute-start(bf16[80,128]{1,0:T(8,128)(2,1)S(1)} %gather_sum.5.refs_1_.refs_0_), channel_id=1, source_target_pairs={{0,64},{16,80},{32,96},{48,112},{64,0},{80,16},{96,32},{112,48},{1... | collective-permute-start | bytes 61448 | tf_op jit(solution)/shard_map/ppermute | solution.py:402
  87.7 3.9 %collective-permute-start.6 = (bf16[80,128]{1,0:T(8,128)(2,1)S(1)}, bf16[80,128]{1,0:T(8,128)(2,1)S(1)}, u32[]{:S(2)}, u32[]{:S(2)}) collective-permute-start(bf16[80,128]{1,0:T(8,128)(2,1)S(1)} %gather_sum.5.refs_1_.refs_0_), channel_id=1, source_target_pairs={{0,32},{16,48},{32,64},{48,80},{64,96},{80,112},{96,0},{112,16},{1... | collective-permute-start | bytes 61448 | tf_op jit(solution)/shard_map/ppermute | solution.py:402
  91.7 6.4 %collective-permute-start.9 = (bf16[4,80,128]{2,1,0:T(8,128)(2,1)S(1)}, bf16[4,80,128]{2,1,0:T(8,128)(2,1)S(1)}, u32[]{:S(2)}, u32[]{:S(2)}) collective-permute-start(bf16[4,80,128]{2,1,0:T(8,128)(2,1)S(1)} %stack.6.refs_7_.refs_2_), channel_id=1, source_target_pairs={{0,16},{16,0},{32,48},{48,32},{64,80},{80,64},{96,112},{112,96},{1... | collective-permute-start | bytes 245768 | tf_op jit(solution)/shard_map/ppermute | solution.py:413
  103.0 25.8 %all-to-all-start.2 = ((bf16[16,336,128]{2,1,0:T(8,128)(2,1)}), bf16[16,336,128]{2,1,0:T(8,128)(2,1)S(1)}, u32[]{:S(2)}, u32[]{:S(2)}) async-start(bf16[16,336,128]{2,1,0:T(8,128)(2,1)} %get-tuple-element.122), calls=%async_computation.2 | async-start | bytes 2752512 | tf_op jit(solution)/shard_map/all_to_all | solution.py:913
  107.3 31.1 %collective-permute-start.16 = (bf16[2,256,128]{2,1,0:T(8,128)(2,1)S(1)}, bf16[2,256,128]{2,1,0:T(8,128)(2,1)S(1)}, u32[]{:S(2)}, u32[]{:S(2)}) collective-permute-start(bf16[2,256,128]{2,1,0:T(8,128)(2,1)S(1)} %get-tuple-element.127), channel_id=1, source_target_pairs={{0,1},{1,2},{2,3},{3,4},{4,5},{5,6},{6,7},{7,8},{8,9},{9,10},{10,1... | collective-permute-start | bytes 393224 | tf_op jit(solution)/shard_map/ppermute | solution.py:925
  110.6 27.8 %collective-permute-start.17 = (bf16[2,256,128]{2,1,0:T(8,128)(2,1)S(1)}, bf16[2,256,128]{2,1,0:T(8,128)(2,1)S(1)}, u32[]{:S(2)}, u32[]{:S(2)}) collective-permute-start(bf16[2,256,128]{2,1,0:T(8,128)(2,1)S(1)} %get-tuple-element.128), channel_id=1, source_target_pairs={{1,0},{2,1},{3,2},{4,3},{5,4},{6,5},{7,6},{8,7},{9,8},{10,9},{11,1... | collective-permute-start | bytes 393224 | tf_op jit(solution)/shard_map/ppermute | solution.py:926
  128.8 6.9 %collective-permute-start.14 = (bf16[80,128]{1,0:T(8,128)(2,1)S(1)}, bf16[80,128]{1,0:T(8,128)(2,1)S(1)}, u32[]{:S(2)}, u32[]{:S(2)}) collective-permute-start(bf16[80,128]{1,0:T(8,128)(2,1)S(1)} %gather_sum.6.refs_1_.refs_0_), channel_id=1, source_target_pairs={{0,96},{16,112},{32,0},{48,16},{64,32},{80,48},{96,64},{112,80},{1... | collective-permute-start | bytes 61448 | tf_op jit(solution)/shard_map/ppermute | solution.py:402
  131.2 4.6 %collective-permute-start.13 = (bf16[80,128]{1,0:T(8,128)(2,1)S(1)}, bf16[80,128]{1,0:T(8,128)(2,1)S(1)}, u32[]{:S(2)}, u32[]{:S(2)}) collective-permute-start(bf16[80,128]{1,0:T(8,128)(2,1)S(1)} %gather_sum.6.refs_1_.refs_0_), channel_id=1, source_target_pairs={{0,64},{16,80},{32,96},{48,112},{64,0},{80,16},{96,32},{112,48},{1... | collective-permute-start | bytes 61448 | tf_op jit(solution)/shard_map/ppermute | solution.py:402
  131.3 4.4 %collective-permute-start.12 = (bf16[80,128]{1,0:T(8,128)(2,1)S(1)}, bf16[80,128]{1,0:T(8,128)(2,1)S(1)}, u32[]{:S(2)}, u32[]{:S(2)}) collective-permute-start(bf16[80,128]{1,0:T(8,128)(2,1)S(1)} %gather_sum.6.refs_1_.refs_0_), channel_id=1, source_target_pairs={{0,32},{16,48},{32,64},{48,80},{64,96},{80,112},{96,0},{112,16},{1... | collective-permute-start | bytes 61448 | tf_op jit(solution)/shard_map/ppermute | solution.py:402
  135.8 6.3 %collective-permute-start.15 = (bf16[4,80,128]{2,1,0:T(8,128)(2,1)S(1)}, bf16[4,80,128]{2,1,0:T(8,128)(2,1)S(1)}, u32[]{:S(2)}, u32[]{:S(2)}) collective-permute-start(bf16[4,80,128]{2,1,0:T(8,128)(2,1)S(1)} %stack.7.refs_8_.refs_2_), channel_id=1, source_target_pairs={{0,16},{16,0},{32,48},{48,32},{64,80},{80,64},{96,112},{112,96},{1... | collective-permute-start | bytes 245768 | tf_op jit(solution)/shard_map/ppermute | solution.py:413
  147.1 25.8 %all-to-all-start.3 = ((bf16[16,336,128]{2,1,0:T(8,128)(2,1)}), bf16[16,336,128]{2,1,0:T(8,128)(2,1)S(1)}, u32[]{:S(2)}, u32[]{:S(2)}) async-start(bf16[16,336,128]{2,1,0:T(8,128)(2,1)} %get-tuple-element.140), calls=%async_computation.3 | async-start | bytes 2752512 | tf_op jit(solution)/shard_map/all_to_all | solution.py:913
  151.5 32.0 %collective-permute-start.22 = (bf16[2,256,128]{2,1,0:T(8,128)(2,1)S(1)}, bf16[2,256,128]{2,1,0:T(8,128)(2,1)S(1)}, u32[]{:S(2)}, u32[]{:S(2)}) collective-permute-start(bf16[2,256,128]{2,1,0:T(8,128)(2,1)S(1)} %get-tuple-element.145), channel_id=1, source_target_pairs={{0,1},{1,2},{2,3},{3,4},{4,5},{5,6},{6,7},{7,8},{8,9},{9,10},{10,1... | collective-permute-start | bytes 393224 | tf_op jit(solution)/shard_map/ppermute | solution.py:925
  154.8 28.7 %collective-permute-start.23 = (bf16[2,256,128]{2,1,0:T(8,128)(2,1)S(1)}, bf16[2,256,128]{2,1,0:T(8,128)(2,1)S(1)}, u32[]{:S(2)}, u32[]{:S(2)}) collective-permute-start(bf16[2,256,128]{2,1,0:T(8,128)(2,1)S(1)} %get-tuple-element.146), channel_id=1, source_target_pairs={{1,0},{2,1},{3,2},{4,3},{5,4},{6,5},{7,6},{8,7},{9,8},{10,9},{11,1... | collective-permute-start | bytes 393224 | tf_op jit(solution)/shard_map/ppermute | solution.py:926
  173.0 7.4 %collective-permute-start.20 = (bf16[80,128]{1,0:T(8,128)(2,1)S(1)}, bf16[80,128]{1,0:T(8,128)(2,1)S(1)}, u32[]{:S(2)}, u32[]{:S(2)}) collective-permute-start(bf16[80,128]{1,0:T(8,128)(2,1)S(1)} %gather_sum.7.refs_1_.refs_0_), channel_id=1, source_target_pairs={{0,96},{16,112},{32,0},{48,16},{64,32},{80,48},{96,64},{112,80},{1... | collective-permute-start | bytes 61448 | tf_op jit(solution)/shard_map/ppermute | solution.py:402
  175.3 5.1 %collective-permute-start.19 = (bf16[80,128]{1,0:T(8,128)(2,1)S(1)}, bf16[80,128]{1,0:T(8,128)(2,1)S(1)}, u32[]{:S(2)}, u32[]{:S(2)}) collective-permute-start(bf16[80,128]{1,0:T(8,128)(2,1)S(1)} %gather_sum.7.refs_1_.refs_0_), channel_id=1, source_target_pairs={{0,64},{16,80},{32,96},{48,112},{64,0},{80,16},{96,32},{112,48},{1... | collective-permute-start | bytes 61448 | tf_op jit(solution)/shard_map/ppermute | solution.py:402
  176.4 3.9 %collective-permute-start.18 = (bf16[80,128]{1,0:T(8,128)(2,1)S(1)}, bf16[80,128]{1,0:T(8,128)(2,1)S(1)}, u32[]{:S(2)}, u32[]{:S(2)}) collective-permute-start(bf16[80,128]{1,0:T(8,128)(2,1)S(1)} %gather_sum.7.refs_1_.refs_0_), channel_id=1, source_target_pairs={{0,32},{16,48},{32,64},{48,80},{64,96},{80,112},{96,0},{112,16},{1... | collective-permute-start | bytes 61448 | tf_op jit(solution)/shard_map/ppermute | solution.py:402
  180.4 7.0 %collective-permute-start.21 = (bf16[4,80,128]{2,1,0:T(8,128)(2,1)S(1)}, bf16[4,80,128]{2,1,0:T(8,128)(2,1)S(1)}, u32[]{:S(2)}, u32[]{:S(2)}) collective-permute-start(bf16[4,80,128]{2,1,0:T(8,128)(2,1)S(1)} %stack.8.refs_9_.refs_2_), channel_id=1, source_target_pairs={{0,16},{16,0},{32,48},{48,32},{64,80},{80,64},{96,112},{112,96},{1... | collective-permute-start | bytes 245768 | tf_op jit(solution)/shard_map/ppermute | solution.py:413
  189.8 3.2 %collective-permute-start.26 = (bf16[16,128]{1,0:T(8,128)(2,1)S(1)}, bf16[16,128]{1,0:T(8,128)(2,1)S(1)}, u32[]{:S(2)}, u32[]{:S(2)}) collective-permute-start(bf16[16,128]{1,0:T(8,128)(2,1)S(1)} %get-tuple-element.160.refs_0_), channel_id=1, source_target_pairs={{0,3},{1,0},{2,1},{3,2},{4,7},{5,4},{6,5},{7,6},{8,11},{9,8},{10,9... | collective-permute-start | bytes 12296 | tf_op jit(solution)/shard_map/ppermute | solution.py:574
  190.4 4.0 %collective-permute-start.25 = (bf16[16,128]{1,0:T(8,128)(2,1)S(1)}, bf16[16,128]{1,0:T(8,128)(2,1)S(1)}, u32[]{:S(2)}, u32[]{:S(2)}) collective-permute-start(bf16[16,128]{1,0:T(8,128)(2,1)S(1)} %get-tuple-element.160.refs_0_), channel_id=1, source_target_pairs={{0,2},{1,3},{2,0},{3,1},{4,6},{5,7},{6,4},{7,5},{8,10},{9,11},{10,... | collective-permute-start | bytes 12296 | tf_op jit(solution)/shard_map/ppermute | solution.py:574
  191.9 3.7 %collective-permute-start.24 = (bf16[16,128]{1,0:T(8,128)(2,1)S(1)}, bf16[16,128]{1,0:T(8,128)(2,1)S(1)}, u32[]{:S(2)}, u32[]{:S(2)}) collective-permute-start(bf16[16,128]{1,0:T(8,128)(2,1)S(1)} %get-tuple-element.160.refs_0_), channel_id=1, source_target_pairs={{0,1},{1,2},{2,3},{3,0},{4,5},{5,6},{6,7},{7,4},{8,9},{9,10},{10,1... | collective-permute-start | bytes 12296 | tf_op jit(solution)/shard_map/ppermute | solution.py:574
  195.6 2.5 %collective-permute-start.29 = (bf16[16,128]{1,0:T(8,128)(2,1)S(1)}, bf16[16,128]{1,0:T(8,128)(2,1)S(1)}, u32[]{:S(2)}, u32[]{:S(2)}) collective-permute-start(bf16[16,128]{1,0:T(8,128)(2,1)S(1)} %sum_over.2.refs_0_.refs_4_), channel_id=1, source_target_pairs={{0,12},{1,13},{2,14},{3,15},{4,0},{5,1},{6,2},{7,3},{8,4},{9,5},{1... | collective-permute-start | bytes 12296 | tf_op jit(solution)/shard_map/ppermute | solution.py:574
  196.1 4.0 %collective-permute-start.28 = (bf16[16,128]{1,0:T(8,128)(2,1)S(1)}, bf16[16,128]{1,0:T(8,128)(2,1)S(1)}, u32[]{:S(2)}, u32[]{:S(2)}) collective-permute-start(bf16[16,128]{1,0:T(8,128)(2,1)S(1)} %sum_over.2.refs_0_.refs_4_), channel_id=1, source_target_pairs={{0,8},{1,9},{2,10},{3,11},{4,12},{5,13},{6,14},{7,15},{8,0},{9,1},... | collective-permute-start | bytes 12296 | tf_op jit(solution)/shard_map/ppermute | solution.py:574
  197.2 3.7 %collective-permute-start.27 = (bf16[16,128]{1,0:T(8,128)(2,1)S(1)}, bf16[16,128]{1,0:T(8,128)(2,1)S(1)}, u32[]{:S(2)}, u32[]{:S(2)}) collective-permute-start(bf16[16,128]{1,0:T(8,128)(2,1)S(1)} %sum_over.2.refs_0_.refs_4_), channel_id=1, source_target_pairs={{0,4},{1,5},{2,6},{3,7},{4,8},{5,9},{6,10},{7,11},{8,12},{9,13},{1... | collective-permute-start | bytes 12296 | tf_op jit(solution)/shard_map/ppermute | solution.py:574
  200.9 3.1 %collective-permute-start.32 = (bf16[16,128]{1,0:T(8,128)(2,1)S(1)}, bf16[16,128]{1,0:T(8,128)(2,1)S(1)}, u32[]{:S(2)}, u32[]{:S(2)}) collective-permute-start(bf16[16,128]{1,0:T(8,128)(2,1)S(1)} %sum_over.3.refs_0_.refs_4_), channel_id=1, source_target_pairs={{0,96},{16,112},{32,0},{48,16},{64,32},{80,48},{96,64},{112,80},{1... | collective-permute-start | bytes 12296 | tf_op jit(solution)/shard_map/ppermute | solution.py:402
  203.3 4.0 %collective-permute-start.31 = (bf16[16,128]{1,0:T(8,128)(2,1)S(1)}, bf16[16,128]{1,0:T(8,128)(2,1)S(1)}, u32[]{:S(2)}, u32[]{:S(2)}) collective-permute-start(bf16[16,128]{1,0:T(8,128)(2,1)S(1)} %sum_over.3.refs_0_.refs_4_), channel_id=1, source_target_pairs={{0,64},{16,80},{32,96},{48,112},{64,0},{80,16},{96,32},{112,48},{1... | collective-permute-start | bytes 12296 | tf_op jit(solution)/shard_map/ppermute | solution.py:402
  203.7 3.7 %collective-permute-start.30 = (bf16[16,128]{1,0:T(8,128)(2,1)S(1)}, bf16[16,128]{1,0:T(8,128)(2,1)S(1)}, u32[]{:S(2)}, u32[]{:S(2)}) collective-permute-start(bf16[16,128]{1,0:T(8,128)(2,1)S(1)} %sum_over.3.refs_0_.refs_4_), channel_id=1, source_target_pairs={{0,32},{16,48},{32,64},{48,80},{64,96},{80,112},{96,0},{112,16},{1... | collective-permute-start | bytes 12296 | tf_op jit(solution)/shard_map/ppermute | solution.py:402
  207.4 5.7 %collective-permute-start.33 = (bf16[4,16,128]{2,1,0:T(8,128)(2,1)S(1)}, bf16[4,16,128]{2,1,0:T(8,128)(2,1)S(1)}, u32[]{:S(2)}, u32[]{:S(2)}) collective-permute-start(bf16[4,16,128]{2,1,0:T(8,128)(2,1)S(1)} %stack.9.refs_2_), channel_id=1, source_target_pairs={{0,16},{16,0},{32,48},{48,32},{64,80},{80,64},{96,112},{112,96},{1... | collective-permute-start | bytes 49160 | tf_op jit(solution)/shard_map/ppermute | solution.py:413

commit v8 on v7

--- a/solution.py
+++ b/solution.py
@@ -157,10 +157,10 @@
 
 
 def pack_kernel(branch, mask_ref, slot_ref, index_ref, near_mask_ref, far_ref, *refs):
-    basis_ref, transfer_ref, top_ref, near_ref = refs[:4]
-    out_ref, count_ref, list_ref, basis_out, transfer_out, top_out, listed_ref = refs[4:11]
-    blocks, total, packed, basis, transfer, top, turned, lifting, row, chosen = refs[11:21]
-    arrived, left, came, moved, given = refs[21:]
+    basis_ref, transfer_ref, top_ref = refs[:3]
+    out_ref, count_ref, list_ref, basis_out, transfer_out, top_out = refs[3:9]
+    blocks, total, packed, basis, transfer, top, turned, lifting, row = refs[9:18]
+    arrived, left, came = refs[18:]
     leaves, entries, rank, _ = blocks.shape
     sources, _, width = packed.shape
     slots = width // rank
@@ -184,28 +184,6 @@
             packed[source, rows] = jnp.concatenate(sides, axis=1).astype(BF16)
         store(leaf).start()
 
-    piece = chosen.shape[0] // given.shape[0]
-
-    def move(leaf, n, i):
-        return pltpu.make_async_copy(near_ref.at[leaf, n], chosen.at[i], moved.at[i])
-
-    def moved_one(i, carry):
-        entry = list_ref[i]
-        move(entry // near_entries, entry % near_entries, i).wait()
-        return carry
-
-    def give(i):
-        some = slab(i, piece)
-        return pltpu.make_async_copy(chosen.at[some], listed_ref.at[some], given.at[i])
-
-    def start_give(i, carry):
-        give(i).start()
-        return carry
-
-    def end_give(i, carry):
-        give(i).wait()
-        return carry
-
     def list_one(i, count):
         leaf, n = i // near_entries, i % near_entries
         place = index_ref[leaf, n]
@@ -215,7 +193,6 @@
         @pl.when(hit)
         def _():
             list_ref[count] = i
-            move(leaf, n, count).start()
 
         return count + hit.astype(jnp.int32)
 
@@ -252,29 +229,23 @@
     ]
     for copy in results:
         copy.start()
-    lax.fori_loop(0, count, moved_one, 0)
-    pieces = (count + piece - 1) // piece
-    lax.fori_loop(0, pieces, start_give, 0)
     run()
     for leaf in range(leaves):
         store(leaf).wait()
     for copy in results:
         copy.wait()
-    lax.fori_loop(0, pieces, end_give, 0)
-
-
-def pack(branch, basis, transfer, top_blocks, near_blocks, far_blocks, far_mask, far_slot, near_index, near_mask, inner, slots):
+
+
+def pack(branch, basis, transfer, top_blocks, far_blocks, far_mask, far_slot, near_index, near_mask, inner, slots):
     leaves, entries, rank, _ = far_blocks.shape
     shape = (inner, leaves * rank, slots * rank)
     turned = (leaves, basis.shape[2], rank)
     lifting = (rank, leaves * rank)
     row = (rank, top_blocks.shape[1] * rank)
-    listed = (near_index.size,) + near_blocks.shape[2:]
     return call(
         pack_kernel,
-        (branch, far_mask, far_slot, near_index, near_mask, far_blocks, basis, transfer, top_blocks,
-         near_blocks),
-        (SMEM,) * 5 + (HBM,) * 5,
+        (branch, far_mask, far_slot, near_index, near_mask, far_blocks, basis, transfer, top_blocks),
+        (SMEM,) * 5 + (HBM,) * 4,
         [
             (shape, BF16, HBM),
             ((1,), jnp.int32, SMEM),
@@ -282,7 +253,6 @@
             (turned, BF16, HBM),
             (lifting, BF16, HBM),
             (row, BF16, HBM),
-            (listed, BF16, HBM),
         ],
         [
             pltpu.VMEM(far_blocks.shape, BF16),
@@ -294,17 +264,57 @@
             pltpu.VMEM(turned, BF16),
             pltpu.VMEM(lifting, BF16),
             pltpu.VMEM(row, BF16),
-            pltpu.VMEM(listed, BF16),
             semaphores(leaves),
             semaphores(leaves),
             semaphores(3),
-            semaphores(near_index.size),
-            semaphores(near_index.size // 8),
         ],
         "pack",
         0,
         10 << 20,
     )
+
+
+def choose_kernel(count_ref, list_ref, near_ref, _, out_ref, chosen, moved, given):
+    piece = chosen.shape[0] // given.shape[0]
+    entries = near_ref.shape[1]
+    count = count_ref[0]
+
+    def move(i):
+        entry = list_ref[i]
+        source = near_ref.at[entry // entries, entry % entries]
+        return pltpu.make_async_copy(source, chosen.at[i], moved.at[i])
+
+    def give(i):
+        some = slab(i, piece)
+        return pltpu.make_async_copy(chosen.at[some], out_ref.at[some], given.at[i])
+
+    def each(number, do):
+        def body(i, carry):
+            do(i)
+            return carry
+
+        lax.fori_loop(0, number, body, 0)
+
+    pieces = (count + piece - 1) // piece
+    each(count, lambda i: move(i).start())
+    each(count, lambda i: move(i).wait())
+    each(pieces, lambda i: give(i).start())
+    each(pieces, lambda i: give(i).wait())
+
+
+def choose(listed, near_blocks, earlier):
+    leaves, entries, size, _ = near_blocks.shape
+    shape = (leaves * entries, size, size)
+    return call(
+        choose_kernel,
+        (*listed, near_blocks, earlier),
+        (SMEM, SMEM, HBM, AFTER),
+        [(shape, BF16, HBM)],
+        [pltpu.VMEM(shape, BF16), semaphores(shape[0]), semaphores(shape[0] // 8)],
+        "choose",
+        0,
+        5 << 20,
+    )[0]
 
 
 def near_kernel(index_ref, mask_ref, blocks_ref, own_ref, *refs):
@@ -422,12 +432,13 @@
         ups[lax.rem(mate + count - 2 * j, count)] = other[j]
 
 
-def far_kernel(count_ref, recv, packed_ref, blocks_ref, *refs):
+def far_kernel(count_ref, list_ref, recv, packed_ref, blocks_ref, *refs):
     held = (len(refs) - 7) // 2
     sources, (_, far, blocks), targets = refs[:held], refs[held : held + 3], refs[held + 3 : -4]
     packed, arrived, fetched, loaded = refs[-4:]
     share = packed.shape[0] // CHUNKS
     width = packed.shape[2]
+    chosen = len(blocks_ref.shape) == 3
     piece = blocks.shape[0] // fetched.shape[0]
     count = (count_ref[0] + piece - 1) // piece
 
@@ -436,8 +447,12 @@
         return [pltpu.make_async_copy(packed_ref.at[some], packed.at[some], arrived.at[i])]
 
     def block(i):
-        some = slab(i, piece)
-        return pltpu.make_async_copy(blocks_ref.at[some], blocks.at[some], fetched.at[i])
+        if chosen:
+            some = slab(i, piece)
+            return pltpu.make_async_copy(blocks_ref.at[some], blocks.at[some], fetched.at[i])
+        entry, entries = list_ref[i], blocks_ref.shape[1]
+        source = blocks_ref.at[entry // entries, entry % entries]
+        return pltpu.make_async_copy(source, blocks.at[i], fetched.at[i])
 
     def ask(i, carry):
         block(i).start()
@@ -477,18 +492,21 @@
         copy.wait()
 
 
-def far_field(count, recv, packed, blocks, held, earlier):
+def far_field(listed, recv, packed, near_blocks, held, earlier):
     sources, rows, _ = packed.shape
-    outs = [((rows, recv.shape[2]), F32, VMEM), (blocks.shape, BF16, VMEM)]
+    size = near_blocks.shape[-1]
+    number = near_blocks.size // size**2
+    pieces = number // 8 if near_blocks.ndim == 3 else number
+    outs = [((rows, recv.shape[2]), F32, VMEM), ((number, size, size), BF16, VMEM)]
     far, blocks, *held = call(
         far_kernel,
-        (count, recv, packed, blocks, *held, earlier),
-        (SMEM, VMEM, HBM, HBM) + (HBM,) * len(held) + (AFTER_VMEM,),
+        (*listed, recv, packed, near_blocks, *held, earlier),
+        (SMEM, SMEM, VMEM, HBM, HBM) + (HBM,) * len(held) + (AFTER_VMEM,),
         outs + [(a.shape, a.dtype, VMEM) for a in held],
         [
             pltpu.VMEM(packed.shape, BF16),
             semaphores(CHUNKS),
-            semaphores(blocks.shape[0] // 8),
+            semaphores(pieces),
             semaphores(len(held)),
         ],
         "far_field",
@@ -616,7 +634,7 @@
         some = slab(i, group)
         return [pltpu.make_async_copy(z_any.at[some], vectors.at[some], arrived.at[i])]
 
-    pieces = 2
+    pieces = CHUNKS
 
     def stores(i):
         some = slab(i, leaves // pieces)
@@ -652,12 +670,8 @@
                 skeletons[slab(leaf, rank)] = dot(basis[leaf], rounded).astype(BF16)
             for l, vector in enumerate(others + [z]):
                 sums[l] += jnp.sum((z * vector).reshape(size // 8, 8, z.shape[1]), axis=0)
-        share = CHUNKS // pieces
-
-        @pl.when(i % share == share - 1)
-        def _():
-            for copy in stores(i // share):
-                copy.start()
+        for copy in stores(i):
+            copy.start()
 
     begin, run = windowed(CHUNKS, CHUNKS, fetch, work)
     if first:
@@ -685,7 +699,11 @@
         for i, weight in enumerate(weights):
             coef[i : i + 1, :] = weight
         coef[STEPS : STEPS + 1, :] = inverse
-    run()
+    if first:
+        run()
+    else:
+        for i in range(CHUNKS):
+            work(i)
 
     if sends:
         low[...] = coarse[:HW]
@@ -914,8 +932,8 @@
 
     zs = [rhs.reshape(leaves, -1, rhs.shape[1])]
     out = stage(0, points, wanted, branch, zs[0], basis, transfer, None)
-    packed, count, entries, turned, lifting, top, listed_blocks = pack(
-        branch, basis, transfer, top_blocks, near_blocks, far_blocks, far_mask, far_slot, near_index, near_mask,
+    packed, count, entries, turned, lifting, top = pack(
+        branch, basis, transfer, top_blocks, far_blocks, far_mask, far_slot, near_index, near_mask,
         inner, slots,
     )
     listed = (count, entries)
@@ -927,11 +945,15 @@
         earlier = (packed,) if k == 1 else ()
         near = near_field(near_index, near_mask, near_blocks, out["coarse"], *earlier)
         done = near
+        if k == 1:
+            chosen = near_blocks
+        elif k == 2:
+            chosen = done = choose(listed, near_blocks, near)
         if k == STEPS:
             krylov = done = vectors(state, zs, list(range(STEPS - 1)), near, CHUNKS)[0]
         summed = gather_sum(recv, slots * rank, done)
         local_far, blocks, (near,) = far_field(
-            count, recv, packed, listed_blocks, (near,), summed
+            listed, recv, packed, chosen, (near,), summed
         )
 
         def between(column):

time: 216 us -> 217 us (level)
  Pallas kernels: 97.7 us -> 102 us
  waiting for transfers between devices: 34.2 us -> 30.9 us
    pallas_call x32 -> x33, Pallas kernels: 97.7 us -> 102 us  [call(): pl.pallas_call(kernel, in_specs=list(in_specs), out_specs=[spec for _, _,...]
    all_to_all x4, waiting for transfers between devices: 24.4 us -> 21.2 us  [exchange(): return lax.all_to_all(array, axis, split_axis=0, concat_axis=0, tiled=True)]
  transfers between devices with their start and end apart: 38 -> 38, of which waited for: 12 -> 11; matrix products, arithmetic and copies ran while one was open for 0% -> 0% of each run, Pallas kernels for 35% -> 37%
where the time goes in v8:
time: 217 us; the launch traced here: 215 us
  Pallas kernels  102 us (47%)
  starting transfers between devices  80.2 us (37%)
  waiting for transfers between devices  30.9 us (14%)
    pallas_call x33, Pallas kernels, call(): pl.pallas_call(kernel, in_specs=list(in_specs), out_specs=[spec for _, _,...  102 us
    all_to_all x4, starting transfers between devices, exchange(): return lax.all_to_all(array, axis, split_axis=0, concat_axis=0, tiled=True)  24.6 us
    all_to_all x4, waiting for transfers between devices, exchange(): return lax.all_to_all(array, axis, split_axis=0, concat_axis=0, tiled=True)  21.2 us
    ppermute x15, starting transfers between devices, over_branches(): lax.ppermute(summed, 'outer', shift)  18.3 us
    ppermute x5, starting transfers between devices, over_branches(): other = lax.ppermute(column, 'outer', [(o, o ^ 1) for o in range(outer)])  14.7 us
    ppermute x4, starting transfers between devices, shards(): before = lax.ppermute(out['high'], 'inner', up_pairs)  13.1 us
    ppermute x6, waiting for transfers between devices, sum_over(): lax.ppermute(dots, axis, [(i, moved(i, j)) for i in range(size)])  5.51 us
    ppermute x4, starting transfers between devices, shards(): after = lax.ppermute(out['low'], 'inner', down_pairs)  5.17 us
  transfers between devices with their start and end apart: 38, of which 11 were waited for; matrix products, arithmetic and copies ran while one was open for 0% of the time, Pallas kernels for 37%

profile of v8, /device:TPU:1, one launch (start us, length us, event | category | flops | bytes accessed | tf_op | source)
XLA Modules:
  0.0 215.2 jit_solution(3942176580219230470)
XLA Ops:
  0.6 4.3 %stage0.1 = (f32[64,128]{1,0:T(8,128)S(1)}, bf16[16,336,128]{2,1,0:T(8,128)(2,1)}, bf16[8,256,128]{2,1,0:T(8,128)(2,1)}, bf16[2,256,128]{2,1,0:T(8,128)(2,1)S(1)}, bf16[2,256,128]{2,1,0:T(8,128)(2,1)S(1)}) custom-call(s32[4,16]{1,0:T(4,128)} %bitcast.13, s32[1]{0:T(128)} %bitcast.2.refs_1_.branch, f32[8,256,128]{2,1,0:T(8,128)} %bitcast.7, ...), custom_call_target="tpu_custom_call" | custom-call | flops 134217728 | bytes 4194304 | tf_op jit(solution)/shard_map/stage0/pallas_call | solution.py:116
  4.9 8.6 %all-to-all-start = ((bf16[16,336,128]{2,1,0:T(8,128)(2,1)}), bf16[16,336,128]{2,1,0:T(8,128)(2,1)S(1)}, u32[]{:S(2)}, u32[]{:S(2)}) async-start(bf16[16,336,128]{2,1,0:T(8,128)(2,1)} %get-tuple-element.82), calls=%async_computation | async-start | bytes 2752512 | tf_op jit(solution)/shard_map/all_to_all | solution.py:931
  13.5 3.3 %collective-permute-start.4 = (bf16[2,256,128]{2,1,0:T(8,128)(2,1)S(1)}, bf16[2,256,128]{2,1,0:T(8,128)(2,1)S(1)}, u32[]{:S(2)}, u32[]{:S(2)}) collective-permute-start(bf16[2,256,128]{2,1,0:T(8,128)(2,1)S(1)} %get-tuple-element.90), channel_id=1, source_target_pairs={{0,1},{1,2},{2,3},{3,4},{4,5},{5,6},{6,7},{7,8},{8,9},{9,10},{10,1... | collective-permute-start | bytes 393224 | tf_op jit(solution)/shard_map/ppermute | solution.py:943
  16.8 1.3 collective-permute-start.5
  18.1 9.9 %pack.1 = (bf16[16,512,256]{2,1,0:T(8,128)(2,1)}, s32[1]{0:T(128)}, s32[64]{0:T(128)S(1)}, bf16[8,256,64]{2,1,0:T(8,128)(2,1)}, bf16[64,512]{1,0:T(8,128)(2,1)}, /*index=5*/bf16[64,512]{1,0:T(8,128)(2,1)}) custom-call(s32[1]{0:T(128)} %bitcast.2.refs_1_.branch, s32[8,48]{1,0:T(8,128)} %mask_ref.5, s32[8,48]{1,0:T(8,128)} %slot_ref.1, s32[8,8]{1,0:T(8,128)} %index_ref.17, ...), custom_call_target="tpu_custom_call" | custom-call | bytes 10485760 | tf_op jit(solution)/shard_map/pack/pallas_call | solution.py:116
  28.6 7.0 %near_field.4.refs_0_ = f32[8,256,128]{2,1,0:T(8,128)} custom-call(s32[8,8]{1,0:T(8,128)} %index_ref.17, s32[8,8]{1,0:T(8,128)} %mask_ref.9, bf16[8,8,256,256]{3,2,1,0:T(8,128)(2,1)} %blocks_ref.9, bf16[8,256,128]{2,1,0:T(8,128)(2,1)} %get-tuple-element.83.own_ref, bf16[16,512,256]{2,1,0:T(8,128)(2,1)} %get-tuple-element.84.refs_0_.packed_ref), custom_call_target="tpu_custom_call" | custom-call | flops 1073741824 | bytes 8388608 | tf_op jit(solution)/shard_map/near_field/pallas_call | solution.py:116
  35.7 2.6 %collective-permute-start.2 = (bf16[80,128]{1,0:T(8,128)(2,1)S(1)}, bf16[80,128]{1,0:T(8,128)(2,1)S(1)}, u32[]{:S(2)}, u32[]{:S(2)}) collective-permute-start(bf16[80,128]{1,0:T(8,128)(2,1)S(1)} %gather_sum.4.refs_1_.refs_0_), channel_id=1, source_target_pairs={{0,96},{16,112},{32,0},{48,16},{64,32},{80,48},{96,64},{112,80},{1... | collective-permute-start | bytes 61448 | tf_op jit(solution)/shard_map/ppermute | solution.py:412
  39.3 5.1 %far_field.4 = (f32[512,128]{1,0:T(8,128)S(1)}, bf16[64,256,256]{2,1,0:T(8,128)(2,1)S(1)}, f32[8,256,128]{2,1,0:T(8,128)S(1)}) custom-call(s32[1]{0:T(128)} %get-tuple-element.85.count_ref, s32[64]{0:T(128)} %copy-done, bf16[16,336,128]{2,1,0:T(8,128)(2,1)S(1)} %all-to-all-done.recv, bf16[16,512,256]{2,1,0:T(8,128)(2,1)} %get-tuple-element.84.refs_0_.packed_ref, ...), custom_call_target="tpu_custom_call" | custom-call | flops 536870912 | bytes 4194304 | tf_op jit(solution)/shard_map/far_field/pallas_call | solution.py:116
  44.4 2.5 %collective-permute-start.3 = (bf16[4,80,128]{2,1,0:T(8,128)(2,1)S(1)}, bf16[4,80,128]{2,1,0:T(8,128)(2,1)S(1)}, u32[]{:S(2)}, u32[]{:S(2)}) collective-permute-start(bf16[4,80,128]{2,1,0:T(8,128)(2,1)S(1)} %stack.5.refs_6_.refs_2_), channel_id=1, source_target_pairs={{0,16},{16,0},{32,48},{48,32},{64,80},{80,64},{96,112},{112,96},{1... | collective-permute-start | bytes 245768 | tf_op jit(solution)/shard_map/ppermute | solution.py:423
  47.0 3.0 %halo_part.4 = (f32[8,256,128]{2,1,0:T(8,128)S(1)}, bf16[8,64,256]{2,1,0:T(8,128)(2,1)S(1)}, bf16[8,256,64]{2,1,0:T(8,128)(2,1)S(1)}, bf16[8,64,64]{2,1,0:T(8,12...) custom-call(s32[1]{0:T(128)} %get-tuple-element.85.count_ref, ...), custom_call_target="tpu_custom_call", output_to_operand_aliasing={{0}: (6, {})} | custom-call | flops 268435456 | bytes 2097152 | tf_op jit(solution)/shard_map/halo_part/pallas_call | solution.py:116
  50.0 4.6 %stage1.1 = (f32[8,256,128]{2,1,0:T(8,128)}, f32[64,128]{1,0:T(8,128)S(1)}, bf16[16,336,128]{2,1,0:T(8,128)(2,1)}, bf16[8,256,128]{2,1,0:T(8,128)(2,1)}, bf16[2,...) custom-call(s32[4,16]{1,0:T(4,128)} %bitcast.14, s32[1]{0:T(128)} %bitcast.2.refs_1_.branch, ...), custom_call_target="tpu_custom_call" | custom-call | flops 134217728 | bytes 5242880 | tf_op jit(solution)/shard_map/stage1/pallas_call | solution.py:116
  54.6 7.7 %all-to-all-start.1 = ((bf16[16,336,128]{2,1,0:T(8,128)(2,1)}), bf16[16,336,128]{2,1,0:T(8,128)(2,1)S(1)}, u32[]{:S(2)}, u32[]{:S(2)}) async-start(bf16[16,336,128]{2,1,0:T(8,128)(2,1)} %get-tuple-element.103), calls=%async_computation.1 | async-start | bytes 2752512 | tf_op jit(solution)/shard_map/all_to_all | solution.py:931
  62.3 3.3 %collective-permute-start.10 = (bf16[2,256,128]{2,1,0:T(8,128)(2,1)S(1)}, bf16[2,256,128]{2,1,0:T(8,128)(2,1)S(1)}, u32[]{:S(2)}, u32[]{:S(2)}) collective-permute-start(bf16[2,256,128]{2,1,0:T(8,128)(2,1)S(1)} %get-tuple-element.108), channel_id=1, source_target_pairs={{0,1},{1,2},{2,3},{3,4},{4,5},{5,6},{6,7},{7,8},{8,9},{9,10},{10,1... | collective-permute-start | bytes 393224 | tf_op jit(solution)/shard_map/ppermute | solution.py:943
  65.6 1.3 collective-permute-start.11
  66.9 7.0 %near_field.5._.refs_0_ = f32[8,256,128]{2,1,0:T(8,128)} custom-call(s32[8,8]{1,0:T(8,128)} %index_ref.17, s32[8,8]{1,0:T(8,128)} %mask_ref.9, bf16[8,8,256,256]{3,2,1,0:T(8,128)(2,1)} %blocks_ref.9, bf16[8,256,128]{2,1,0:T(8,128)(2,1)} %get-tuple-element.104.own_ref), custom_call_target="tpu_custom_call" | custom-call | flops 1073741824 | bytes 8388608 | tf_op jit(solution)/shard_map/near_field/pallas_call | solution.py:116
  73.9 4.9 %choose.1.refs_0_.blocks_ref = bf16[64,256,256]{2,1,0:T(8,128)(2,1)} custom-call(s32[1]{0:T(128)} %get-tuple-element.85.count_ref, s32[64]{0:T(128)} %copy-done, bf16[8,8,256,256]{3,2,1,0:T(8,128)(2,1)} %blocks_ref.9, f32[8,256,128]{2,1,0:T(8,128)} %near_field.5._.refs_0_), custom_call_target="tpu_custom_call" | custom-call | bytes 5242880 | tf_op jit(solution)/shard_map/choose/pallas_call | solution.py:116
  78.7 5.0 %all-to-all-done.1.recv = bf16[16,336,128]{2,1,0:T(8,128)(2,1)S(1)} async-done(((bf16[16,336,128]{2,1,0:T(8,128)(2,1)}), bf16[16,336,128]{2,1,0:T(8,128)(2,1)S(1)}, u32[]{:S(2)}, u32[]{:S(2)}) %all-to-all-start.1) | async-done | bytes 1376288 | tf_op jit(solution)/shard_map/all_to_all | solution.py:931
  83.8 2.0 collective-permute-start.8
  87.0 4.5 %far_field.5 = (f32[512,128]{1,0:T(8,128)S(1)}, bf16[64,256,256]{2,1,0:T(8,128)(2,1)S(1)}, f32[8,256,128]{2,1,0:T(8,128)S(1)}) custom-call(s32[1]{0:T(128)} %get-tuple-element.85.count_ref, s32[64]{0:T(128)} %copy-done, bf16[16,336,128]{2,1,0:T(8,128)(2,1)S(1)} %all-to-all-done.1.recv, bf16[16,512,256]{2,1,0:T(8,128)(2,1)} %get-tuple-element.84.refs_0_.packed_ref, ...), custom_call_target="tpu_custom_call" | custom-call | flops 536870912 | bytes 4194304 | tf_op jit(solution)/shard_map/far_field/pallas_call | solution.py:116
  91.6 2.5 %collective-permute-start.9 = (bf16[4,80,128]{2,1,0:T(8,128)(2,1)S(1)}, bf16[4,80,128]{2,1,0:T(8,128)(2,1)S(1)}, u32[]{:S(2)}, u32[]{:S(2)}) collective-permute-start(bf16[4,80,128]{2,1,0:T(8,128)(2,1)S(1)} %stack.6.refs_7_.refs_2_), channel_id=1, source_target_pairs={{0,16},{16,0},{32,48},{48,32},{64,80},{80,64},{96,112},{112,96},{1... | collective-permute-start | bytes 245768 | tf_op jit(solution)/shard_map/ppermute | solution.py:423
  94.1 3.3 %halo_part.5 = (f32[8,256,128]{2,1,0:T(8,128)S(1)}, bf16[8,64,256]{2,1,0:T(8,128)(2,1)S(1)}, bf16[8,256,64]{2,1,0:T(8,128)(2,1)S(1)}, bf16[8,64,64]{2,1,0:T(8,12...) custom-call(s32[1]{0:T(128)} %get-tuple-element.85.count_ref, ...), custom_call_target="tpu_custom_call", output_to_operand_aliasing={{0}: (6, {})} | custom-call | flops 268435456 | bytes 2097152 | tf_op jit(solution)/shard_map/halo_part/pallas_call | solution.py:116
  97.4 4.7 %stage2.1 = (f32[8,256,128]{2,1,0:T(8,128)}, f32[64,128]{1,0:T(8,128)S(1)}, bf16[16,336,128]{2,1,0:T(8,128)(2,1)}, bf16[8,256,128]{2,1,0:T(8,128)(2,1)}, bf16[2,...) custom-call(s32[4,16]{1,0:T(4,128)} %bitcast.15, s32[1]{0:T(128)} %bitcast.2.refs_1_.branch, ...), custom_call_target="tpu_custom_call" | custom-call | flops 134217728 | bytes 6291456 | tf_op jit(solution)/shard_map/stage2/pallas_call | solution.py:116
  102.1 4.3 %all-to-all-start.2 = ((bf16[16,336,128]{2,1,0:T(8,128)(2,1)}), bf16[16,336,128]{2,1,0:T(8,128)(2,1)S(1)}, u32[]{:S(2)}, u32[]{:S(2)}) async-start(bf16[16,336,128]{2,1,0:T(8,128)(2,1)} %get-tuple-element.120), calls=%async_computation.2 | async-start | bytes 2752512 | tf_op jit(solution)/shard_map/all_to_all | solution.py:931
  106.4 3.3 %collective-permute-start.16 = (bf16[2,256,128]{2,1,0:T(8,128)(2,1)S(1)}, bf16[2,256,128]{2,1,0:T(8,128)(2,1)S(1)}, u32[]{:S(2)}, u32[]{:S(2)}) collective-permute-start(bf16[2,256,128]{2,1,0:T(8,128)(2,1)S(1)} %get-tuple-element.125), channel_id=1, source_target_pairs={{0,1},{1,2},{2,3},{3,4},{4,5},{5,6},{6,7},{7,8},{8,9},{9,10},{10,1... | collective-permute-start | bytes 393224 | tf_op jit(solution)/shard_map/ppermute | solution.py:943
  109.6 1.3 collective-permute-start.17
  110.9 7.0 %near_field.6.refs_0_ = f32[8,256,128]{2,1,0:T(8,128)} custom-call(s32[8,8]{1,0:T(8,128)} %index_ref.17, s32[8,8]{1,0:T(8,128)} %mask_ref.9, bf16[8,8,256,256]{3,2,1,0:T(8,128)(2,1)} %blocks_ref.9, bf16[8,256,128]{2,1,0:T(8,128)(2,1)} %get-tuple-element.121.own_ref), custom_call_target="tpu_custom_call" | custom-call | flops 1073741824 | bytes 8388608 | tf_op jit(solution)/shard_map/near_field/pallas_call | solution.py:116
  117.9 9.9 %all-to-all-done.2.recv = bf16[16,336,128]{2,1,0:T(8,128)(2,1)S(1)} async-done(((bf16[16,336,128]{2,1,0:T(8,128)(2,1)}), bf16[16,336,128]{2,1,0:T(8,128)(2,1)S(1)}, u32[]{:S(2)}, u32[]{:S(2)}) %all-to-all-start.2) | async-done | bytes 1376288 | tf_op jit(solution)/shard_map/all_to_all | solution.py:931
  127.8 3.0 %collective-permute-start.14 = (bf16[80,128]{1,0:T(8,128)(2,1)S(1)}, bf16[80,128]{1,0:T(8,128)(2,1)S(1)}, u32[]{:S(2)}, u32[]{:S(2)}) collective-permute-start(bf16[80,128]{1,0:T(8,128)(2,1)S(1)} %gather_sum.6.refs_1_.refs_0_), channel_id=1, source_target_pairs={{0,96},{16,112},{32,0},{48,16},{64,32},{80,48},{96,64},{112,80},{1... | collective-permute-start | bytes 61448 | tf_op jit(solution)/shard_map/ppermute | solution.py:412
  131.5 4.5 %far_field.6 = (f32[512,128]{1,0:T(8,128)S(1)}, bf16[64,256,256]{2,1,0:T(8,128)(2,1)S(1)}, f32[8,256,128]{2,1,0:T(8,128)S(1)}) custom-call(s32[1]{0:T(128)} %get-tuple-element.85.count_ref, s32[64]{0:T(128)} %copy-done, bf16[16,336,128]{2,1,0:T(8,128)(2,1)S(1)} %all-to-all-done.2.recv, bf16[16,512,256]{2,1,0:T(8,128)(2,1)} %get-tuple-element.84.refs_0_.packed_ref, ...), custom_call_target="tpu_custom_call" | custom-call | flops 536870912 | bytes 4194304 | tf_op jit(solution)/shard_map/far_field/pallas_call | solution.py:116
  136.1 2.6 %collective-permute-start.15 = (bf16[4,80,128]{2,1,0:T(8,128)(2,1)S(1)}, bf16[4,80,128]{2,1,0:T(8,128)(2,1)S(1)}, u32[]{:S(2)}, u32[]{:S(2)}) collective-permute-start(bf16[4,80,128]{2,1,0:T(8,128)(2,1)S(1)} %stack.7.refs_8_.refs_2_), channel_id=1, source_target_pairs={{0,16},{16,0},{32,48},{48,32},{64,80},{80,64},{96,112},{112,96},{1... | collective-permute-start | bytes 245768 | tf_op jit(solution)/shard_map/ppermute | solution.py:423
  138.6 3.6 %halo_part.6 = (f32[8,256,128]{2,1,0:T(8,128)S(1)}, bf16[8,64,256]{2,1,0:T(8,128)(2,1)S(1)}, bf16[8,256,64]{2,1,0:T(8,128)(2,1)S(1)}, bf16[8,64,64]{2,1,0:T(8,12...) custom-call(s32[1]{0:T(128)} %get-tuple-element.85.count_ref, ...), custom_call_target="tpu_custom_call", output_to_operand_aliasing={{0}: (6, {})} | custom-call | flops 268435456 | bytes 2097152 | tf_op jit(solution)/shard_map/halo_part/pallas_call | solution.py:116
  142.3 4.8 %stage3.1 = (f32[8,256,128]{2,1,0:T(8,128)}, f32[64,128]{1,0:T(8,128)S(1)}, bf16[16,336,128]{2,1,0:T(8,128)(2,1)}, bf16[8,256,128]{2,1,0:T(8,128)(2,1)}, bf16[2,...) custom-call(s32[4,16]{1,0:T(4,128)} %bitcast.16, s32[1]{0:T(128)} %bitcast.2.refs_1_.branch, ...), custom_call_target="tpu_custom_call" | custom-call | flops 134217728 | bytes 7340032 | tf_op jit(solution)/shard_map/stage3/pallas_call | solution.py:116
  147.1 4.0 %all-to-all-start.3 = ((bf16[16,336,128]{2,1,0:T(8,128)(2,1)}), bf16[16,336,128]{2,1,0:T(8,128)(2,1)S(1)}, u32[]{:S(2)}, u32[]{:S(2)}) async-start(bf16[16,336,128]{2,1,0:T(8,128)(2,1)} %get-tuple-element.138), calls=%async_computation.3 | async-start | bytes 2752512 | tf_op jit(solution)/shard_map/all_to_all | solution.py:931
  151.1 3.3 %collective-permute-start.22 = (bf16[2,256,128]{2,1,0:T(8,128)(2,1)S(1)}, bf16[2,256,128]{2,1,0:T(8,128)(2,1)S(1)}, u32[]{:S(2)}, u32[]{:S(2)}) collective-permute-start(bf16[2,256,128]{2,1,0:T(8,128)(2,1)S(1)} %get-tuple-element.143), channel_id=1, source_target_pairs={{0,1},{1,2},{2,3},{3,4},{4,5},{5,6},{6,7},{7,8},{8,9},{9,10},{10,1... | collective-permute-start | bytes 393224 | tf_op jit(solution)/shard_map/ppermute | solution.py:943
  155.7 7.0 %near_field.7.refs_4_.refs_0_ = f32[8,256,128]{2,1,0:T(8,128)} custom-call(s32[8,8]{1,0:T(8,128)} %index_ref.17, s32[8,8]{1,0:T(8,128)} %mask_ref.9, bf16[8,8,256,256]{3,2,1,0:T(8,128)(2,1)} %blocks_ref.9, bf16[8,256,128]{2,1,0:T(8,128)(2,1)} %get-tuple-element.140.own_ref), custom_call_target="tpu_custom_call" | custom-call | flops 1073741824 | bytes 8388608 | tf_op jit(solution)/shard_map/near_field/pallas_call | solution.py:116
  162.7 3.5 %vectors.2.refs_0_.refs_5_ = f32[5,8,256,128]{3,2,1,0:T(8,128)} custom-call(f32[64,128]{1,0:T(8,128)S(1)} %get-tuple-element.139.refs_0_.refs_4_, f32[8,256,128]{2,1,0:T(8,128)} %bitcast.11, f32[8,256,128]{2,1,0:T(8,128)} %get-tuple-element.111.refs_6_.refs_2_, f32[8,256,128]{2,1,0:T(8,128)} %get-tuple-element.128.refs_7_.refs_3_, ...), custom_call_target="tpu_custom_call" | custom-call | flops 8388608 | bytes 6291456 | tf_op jit(solution)/shard_map/vectors/pallas_call | solution.py:116
  166.2 6.3 %all-to-all-done.3.recv = bf16[16,336,128]{2,1,0:T(8,128)(2,1)S(1)} async-done(((bf16[16,336,128]{2,1,0:T(8,128)(2,1)}), bf16[16,336,128]{2,1,0:T(8,128)(2,1)S(1)}, u32[]{:S(2)}, u32[]{:S(2)}) %all-to-all-start.3) | async-done | bytes 1376288 | tf_op jit(solution)/shard_map/all_to_all | solution.py:931
  172.6 2.8 %collective-permute-start.20 = (bf16[80,128]{1,0:T(8,128)(2,1)S(1)}, bf16[80,128]{1,0:T(8,128)(2,1)S(1)}, u32[]{:S(2)}, u32[]{:S(2)}) collective-permute-start(bf16[80,128]{1,0:T(8,128)(2,1)S(1)} %gather_sum.7.refs_1_.refs_0_), channel_id=1, source_target_pairs={{0,96},{16,112},{32,0},{48,16},{64,32},{80,48},{96,64},{112,80},{1... | collective-permute-start | bytes 61448 | tf_op jit(solution)/shard_map/ppermute | solution.py:412
  176.7 4.5 %far_field.7 = (f32[512,128]{1,0:T(8,128)S(1)}, bf16[64,256,256]{2,1,0:T(8,128)(2,1)S(1)}, f32[8,256,128]{2,1,0:T(8,128)S(1)}) custom-call(s32[1]{0:T(128)} %get-tuple-element.85.count_ref, s32[64]{0:T(128)} %copy-done, bf16[16,336,128]{2,1,0:T(8,128)(2,1)S(1)} %all-to-all-done.3.recv, bf16[16,512,256]{2,1,0:T(8,128)(2,1)} %get-tuple-element.84.refs_0_.packed_ref, ...), custom_call_target="tpu_custom_call" | custom-call | flops 536870912 | bytes 4194304 | tf_op jit(solution)/shard_map/far_field/pallas_call | solution.py:116
  181.3 2.5 %collective-permute-start.21 = (bf16[4,80,128]{2,1,0:T(8,128)(2,1)S(1)}, bf16[4,80,128]{2,1,0:T(8,128)(2,1)S(1)}, u32[]{:S(2)}, u32[]{:S(2)}) collective-permute-start(bf16[4,80,128]{2,1,0:T(8,128)(2,1)S(1)} %stack.8.refs_9_.refs_2_), channel_id=1, source_target_pairs={{0,16},{16,0},{32,48},{48,32},{64,80},{80,64},{96,112},{112,96},{1... | collective-permute-start | bytes 245768 | tf_op jit(solution)/shard_map/ppermute | solution.py:423
  183.8 4.0 %halo_part.7 = (f32[8,256,128]{2,1,0:T(8,128)S(1)}, bf16[8,64,256]{2,1,0:T(8,128)(2,1)S(1)}, bf16[8,256,64]{2,1,0:T(8,128)(2,1)S(1)}, bf16[8,64,64]{2,1,0:T(8,12...) custom-call(s32[1]{0:T(128)} %get-tuple-element.85.count_ref, ...), custom_call_target="tpu_custom_call", output_to_operand_aliasing={{0}: (6, {})} | custom-call | flops 268435456 | bytes 2097152 | tf_op jit(solution)/shard_map/halo_part/pallas_call | solution.py:116
  187.7 1.9 stage4.1
  192.9 1.5 collective-permute-done.25.refs_2_
  198.1 1.9 collective-permute-done.28.refs_2_
  200.8 3.0 %collective-permute-start.32 = (bf16[16,128]{1,0:T(8,128)(2,1)S(1)}, bf16[16,128]{1,0:T(8,128)(2,1)S(1)}, u32[]{:S(2)}, u32[]{:S(2)}) collective-permute-start(bf16[16,128]{1,0:T(8,128)(2,1)S(1)} %sum_over.3.refs_0_.refs_4_), channel_id=1, source_target_pairs={{0,96},{16,112},{32,0},{48,16},{64,32},{80,48},{96,64},{112,80},{1... | collective-permute-start | bytes 12296 | tf_op jit(solution)/shard_map/ppermute | solution.py:412
  204.5 3.2 %collective-permute-done.31.refs_2_ = bf16[16,128]{1,0:T(8,128)(2,1)S(1)} collective-permute-done((bf16[16,128]{1,0:T(8,128)(2,1)S(1)}, bf16[16,128]{1,0:T(8,128)(2,1)S(1)}, u32[]{:S(2)}, u32[]{:S(2)}) %collective-permute-start.31) | collective-permute-done | bytes 4128 | tf_op jit(solution)/shard_map/ppermute | solution.py:412
  207.8 4.6 %collective-permute-start.33 = (bf16[4,16,128]{2,1,0:T(8,128)(2,1)S(1)}, bf16[4,16,128]{2,1,0:T(8,128)(2,1)S(1)}, u32[]{:S(2)}, u32[]{:S(2)}) collective-permute-start(bf16[4,16,128]{2,1,0:T(8,128)(2,1)S(1)} %stack.9.refs_2_), channel_id=1, source_target_pairs={{0,16},{16,0},{32,48},{48,32},{64,80},{80,64},{96,112},{112,96},{1... | collective-permute-start | bytes 49160 | tf_op jit(solution)/shard_map/ppermute | solution.py:423
  213.2 1.8 last_vector.1
  (63 shorter events, 15.8 us)
Async XLA Ops:
  4.9 30.7 %all-to-all-start = ((bf16[16,336,128]{2,1,0:T(8,128)(2,1)}), bf16[16,336,128]{2,1,0:T(8,128)(2,1)S(1)}, u32[]{:S(2)}, u32[]{:S(2)}) async-start(bf16[16,336,128]{2,1,0:T(8,128)(2,1)} %get-tuple-element.82), calls=%async_computation | async-start | bytes 2752512 | tf_op jit(solution)/shard_map/all_to_all | solution.py:931
  13.5 33.5 %collective-permute-start.4 = (bf16[2,256,128]{2,1,0:T(8,128)(2,1)S(1)}, bf16[2,256,128]{2,1,0:T(8,128)(2,1)S(1)}, u32[]{:S(2)}, u32[]{:S(2)}) collective-permute-start(bf16[2,256,128]{2,1,0:T(8,128)(2,1)S(1)} %get-tuple-element.90), channel_id=1, source_target_pairs={{0,1},{1,2},{2,3},{3,4},{4,5},{5,6},{6,7},{7,8},{8,9},{9,10},{10,1... | collective-permute-start | bytes 393224 | tf_op jit(solution)/shard_map/ppermute | solution.py:943
  16.8 30.2 %collective-permute-start.5 = (bf16[2,256,128]{2,1,0:T(8,128)(2,1)S(1)}, bf16[2,256,128]{2,1,0:T(8,128)(2,1)S(1)}, u32[]{:S(2)}, u32[]{:S(2)}) collective-permute-start(bf16[2,256,128]{2,1,0:T(8,128)(2,1)S(1)} %get-tuple-element.91), channel_id=1, source_target_pairs={{1,0},{2,1},{3,2},{4,3},{5,4},{6,5},{7,6},{8,7},{9,8},{10,9},{11,1... | collective-permute-start | bytes 393224 | tf_op jit(solution)/shard_map/ppermute | solution.py:944
  28.0 0.6 copy-start
  35.7 8.7 %collective-permute-start.2 = (bf16[80,128]{1,0:T(8,128)(2,1)S(1)}, bf16[80,128]{1,0:T(8,128)(2,1)S(1)}, u32[]{:S(2)}, u32[]{:S(2)}) collective-permute-start(bf16[80,128]{1,0:T(8,128)(2,1)S(1)} %gather_sum.4.refs_1_.refs_0_), channel_id=1, source_target_pairs={{0,96},{16,112},{32,0},{48,16},{64,32},{80,48},{96,64},{112,80},{1... | collective-permute-start | bytes 61448 | tf_op jit(solution)/shard_map/ppermute | solution.py:412
  38.2 6.2 %collective-permute-start.1 = (bf16[80,128]{1,0:T(8,128)(2,1)S(1)}, bf16[80,128]{1,0:T(8,128)(2,1)S(1)}, u32[]{:S(2)}, u32[]{:S(2)}) collective-permute-start(bf16[80,128]{1,0:T(8,128)(2,1)S(1)} %gather_sum.4.refs_1_.refs_0_), channel_id=1, source_target_pairs={{0,64},{16,80},{32,96},{48,112},{64,0},{80,16},{96,32},{112,48},{1... | collective-permute-start | bytes 61448 | tf_op jit(solution)/shard_map/ppermute | solution.py:412
  38.7 5.7 %collective-permute-start = (bf16[80,128]{1,0:T(8,128)(2,1)S(1)}, bf16[80,128]{1,0:T(8,128)(2,1)S(1)}, u32[]{:S(2)}, u32[]{:S(2)}) collective-permute-start(bf16[80,128]{1,0:T(8,128)(2,1)S(1)} %gather_sum.4.refs_1_.refs_0_), channel_id=1, source_target_pairs={{0,32},{16,48},{32,64},{48,80},{64,96},{80,112},{96,0},{112,16},{1... | collective-permute-start | bytes 61448 | tf_op jit(solution)/shard_map/ppermute | solution.py:412
  44.4 5.5 %collective-permute-start.3 = (bf16[4,80,128]{2,1,0:T(8,128)(2,1)S(1)}, bf16[4,80,128]{2,1,0:T(8,128)(2,1)S(1)}, u32[]{:S(2)}, u32[]{:S(2)}) collective-permute-start(bf16[4,80,128]{2,1,0:T(8,128)(2,1)S(1)} %stack.5.refs_6_.refs_2_), channel_id=1, source_target_pairs={{0,16},{16,0},{32,48},{48,32},{64,80},{80,64},{96,112},{112,96},{1... | collective-permute-start | bytes 245768 | tf_op jit(solution)/shard_map/ppermute | solution.py:423
  54.6 29.1 %all-to-all-start.1 = ((bf16[16,336,128]{2,1,0:T(8,128)(2,1)}), bf16[16,336,128]{2,1,0:T(8,128)(2,1)S(1)}, u32[]{:S(2)}, u32[]{:S(2)}) async-start(bf16[16,336,128]{2,1,0:T(8,128)(2,1)} %get-tuple-element.103), calls=%async_computation.1 | async-start | bytes 2752512 | tf_op jit(solution)/shard_map/all_to_all | solution.py:931
  62.3 31.8 %collective-permute-start.10 = (bf16[2,256,128]{2,1,0:T(8,128)(2,1)S(1)}, bf16[2,256,128]{2,1,0:T(8,128)(2,1)S(1)}, u32[]{:S(2)}, u32[]{:S(2)}) collective-permute-start(bf16[2,256,128]{2,1,0:T(8,128)(2,1)S(1)} %get-tuple-element.108), channel_id=1, source_target_pairs={{0,1},{1,2},{2,3},{3,4},{4,5},{5,6},{6,7},{7,8},{8,9},{9,10},{10,1... | collective-permute-start | bytes 393224 | tf_op jit(solution)/shard_map/ppermute | solution.py:943
  65.6 28.5 %collective-permute-start.11 = (bf16[2,256,128]{2,1,0:T(8,128)(2,1)S(1)}, bf16[2,256,128]{2,1,0:T(8,128)(2,1)S(1)}, u32[]{:S(2)}, u32[]{:S(2)}) collective-permute-start(bf16[2,256,128]{2,1,0:T(8,128)(2,1)S(1)} %get-tuple-element.109), channel_id=1, source_target_pairs={{1,0},{2,1},{3,2},{4,3},{5,4},{6,5},{7,6},{8,7},{9,8},{10,9},{11,1... | collective-permute-start | bytes 393224 | tf_op jit(solution)/shard_map/ppermute | solution.py:944
  83.8 7.8 %collective-permute-start.8 = (bf16[80,128]{1,0:T(8,128)(2,1)S(1)}, bf16[80,128]{1,0:T(8,128)(2,1)S(1)}, u32[]{:S(2)}, u32[]{:S(2)}) collective-permute-start(bf16[80,128]{1,0:T(8,128)(2,1)S(1)} %gather_sum.5.refs_1_.refs_0_), channel_id=1, source_target_pairs={{0,96},{16,112},{32,0},{48,16},{64,32},{80,48},{96,64},{112,80},{1... | collective-permute-start | bytes 61448 | tf_op jit(solution)/shard_map/ppermute | solution.py:412
  85.8 5.8 %collective-permute-start.7 = (bf16[80,128]{1,0:T(8,128)(2,1)S(1)}, bf16[80,128]{1,0:T(8,128)(2,1)S(1)}, u32[]{:S(2)}, u32[]{:S(2)}) collective-permute-start(bf16[80,128]{1,0:T(8,128)(2,1)S(1)} %gather_sum.5.refs_1_.refs_0_), channel_id=1, source_target_pairs={{0,64},{16,80},{32,96},{48,112},{64,0},{80,16},{96,32},{112,48},{1... | collective-permute-start | bytes 61448 | tf_op jit(solution)/shard_map/ppermute | solution.py:412
  87.0 4.6 %collective-permute-start.6 = (bf16[80,128]{1,0:T(8,128)(2,1)S(1)}, bf16[80,128]{1,0:T(8,128)(2,1)S(1)}, u32[]{:S(2)}, u32[]{:S(2)}) collective-permute-start(bf16[80,128]{1,0:T(8,128)(2,1)S(1)} %gather_sum.5.refs_1_.refs_0_), channel_id=1, source_target_pairs={{0,32},{16,48},{32,64},{48,80},{64,96},{80,112},{96,0},{112,16},{1... | collective-permute-start | bytes 61448 | tf_op jit(solution)/shard_map/ppermute | solution.py:412
  91.6 5.8 %collective-permute-start.9 = (bf16[4,80,128]{2,1,0:T(8,128)(2,1)S(1)}, bf16[4,80,128]{2,1,0:T(8,128)(2,1)S(1)}, u32[]{:S(2)}, u32[]{:S(2)}) collective-permute-start(bf16[4,80,128]{2,1,0:T(8,128)(2,1)S(1)} %stack.6.refs_7_.refs_2_), channel_id=1, source_target_pairs={{0,16},{16,0},{32,48},{48,32},{64,80},{80,64},{96,112},{112,96},{1... | collective-permute-start | bytes 245768 | tf_op jit(solution)/shard_map/ppermute | solution.py:423
  102.1 25.7 %all-to-all-start.2 = ((bf16[16,336,128]{2,1,0:T(8,128)(2,1)}), bf16[16,336,128]{2,1,0:T(8,128)(2,1)S(1)}, u32[]{:S(2)}, u32[]{:S(2)}) async-start(bf16[16,336,128]{2,1,0:T(8,128)(2,1)} %get-tuple-element.120), calls=%async_computation.2 | async-start | bytes 2752512 | tf_op jit(solution)/shard_map/all_to_all | solution.py:931
  106.4 32.3 %collective-permute-start.16 = (bf16[2,256,128]{2,1,0:T(8,128)(2,1)S(1)}, bf16[2,256,128]{2,1,0:T(8,128)(2,1)S(1)}, u32[]{:S(2)}, u32[]{:S(2)}) collective-permute-start(bf16[2,256,128]{2,1,0:T(8,128)(2,1)S(1)} %get-tuple-element.125), channel_id=1, source_target_pairs={{0,1},{1,2},{2,3},{3,4},{4,5},{5,6},{6,7},{7,8},{8,9},{9,10},{10,1... | collective-permute-start | bytes 393224 | tf_op jit(solution)/shard_map/ppermute | solution.py:943
  109.6 29.0 %collective-permute-start.17 = (bf16[2,256,128]{2,1,0:T(8,128)(2,1)S(1)}, bf16[2,256,128]{2,1,0:T(8,128)(2,1)S(1)}, u32[]{:S(2)}, u32[]{:S(2)}) collective-permute-start(bf16[2,256,128]{2,1,0:T(8,128)(2,1)S(1)} %get-tuple-element.126), channel_id=1, source_target_pairs={{1,0},{2,1},{3,2},{4,3},{5,4},{6,5},{7,6},{8,7},{9,8},{10,9},{11,1... | collective-permute-start | bytes 393224 | tf_op jit(solution)/shard_map/ppermute | solution.py:944
  127.8 8.2 %collective-permute-start.14 = (bf16[80,128]{1,0:T(8,128)(2,1)S(1)}, bf16[80,128]{1,0:T(8,128)(2,1)S(1)}, u32[]{:S(2)}, u32[]{:S(2)}) collective-permute-start(bf16[80,128]{1,0:T(8,128)(2,1)S(1)} %gather_sum.6.refs_1_.refs_0_), channel_id=1, source_target_pairs={{0,96},{16,112},{32,0},{48,16},{64,32},{80,48},{96,64},{112,80},{1... | collective-permute-start | bytes 61448 | tf_op jit(solution)/shard_map/ppermute | solution.py:412
  130.8 5.2 %collective-permute-start.13 = (bf16[80,128]{1,0:T(8,128)(2,1)S(1)}, bf16[80,128]{1,0:T(8,128)(2,1)S(1)}, u32[]{:S(2)}, u32[]{:S(2)}) collective-permute-start(bf16[80,128]{1,0:T(8,128)(2,1)S(1)} %gather_sum.6.refs_1_.refs_0_), channel_id=1, source_target_pairs={{0,64},{16,80},{32,96},{48,112},{64,0},{80,16},{96,32},{112,48},{1... | collective-permute-start | bytes 61448 | tf_op jit(solution)/shard_map/ppermute | solution.py:412
  131.0 5.1 %collective-permute-start.12 = (bf16[80,128]{1,0:T(8,128)(2,1)S(1)}, bf16[80,128]{1,0:T(8,128)(2,1)S(1)}, u32[]{:S(2)}, u32[]{:S(2)}) collective-permute-start(bf16[80,128]{1,0:T(8,128)(2,1)S(1)} %gather_sum.6.refs_1_.refs_0_), channel_id=1, source_target_pairs={{0,32},{16,48},{32,64},{48,80},{64,96},{80,112},{96,0},{112,16},{1... | collective-permute-start | bytes 61448 | tf_op jit(solution)/shard_map/ppermute | solution.py:412
  136.1 6.2 %collective-permute-start.15 = (bf16[4,80,128]{2,1,0:T(8,128)(2,1)S(1)}, bf16[4,80,128]{2,1,0:T(8,128)(2,1)S(1)}, u32[]{:S(2)}, u32[]{:S(2)}) collective-permute-start(bf16[4,80,128]{2,1,0:T(8,128)(2,1)S(1)} %stack.7.refs_8_.refs_2_), channel_id=1, source_target_pairs={{0,16},{16,0},{32,48},{48,32},{64,80},{80,64},{96,112},{112,96},{1... | collective-permute-start | bytes 245768 | tf_op jit(solution)/shard_map/ppermute | solution.py:423
  147.1 25.5 %all-to-all-start.3 = ((bf16[16,336,128]{2,1,0:T(8,128)(2,1)}), bf16[16,336,128]{2,1,0:T(8,128)(2,1)S(1)}, u32[]{:S(2)}, u32[]{:S(2)}) async-start(bf16[16,336,128]{2,1,0:T(8,128)(2,1)} %get-tuple-element.138), calls=%async_computation.3 | async-start | bytes 2752512 | tf_op jit(solution)/shard_map/all_to_all | solution.py:931
  151.1 32.6 %collective-permute-start.22 = (bf16[2,256,128]{2,1,0:T(8,128)(2,1)S(1)}, bf16[2,256,128]{2,1,0:T(8,128)(2,1)S(1)}, u32[]{:S(2)}, u32[]{:S(2)}) collective-permute-start(bf16[2,256,128]{2,1,0:T(8,128)(2,1)S(1)} %get-tuple-element.143), channel_id=1, source_target_pairs={{0,1},{1,2},{2,3},{3,4},{4,5},{5,6},{6,7},{7,8},{8,9},{9,10},{10,1... | collective-permute-start | bytes 393224 | tf_op jit(solution)/shard_map/ppermute | solution.py:943
  154.4 29.4 %collective-permute-start.23 = (bf16[2,256,128]{2,1,0:T(8,128)(2,1)S(1)}, bf16[2,256,128]{2,1,0:T(8,128)(2,1)S(1)}, u32[]{:S(2)}, u32[]{:S(2)}) collective-permute-start(bf16[2,256,128]{2,1,0:T(8,128)(2,1)S(1)} %get-tuple-element.144), channel_id=1, source_target_pairs={{1,0},{2,1},{3,2},{4,3},{5,4},{6,5},{7,6},{8,7},{9,8},{10,9},{11,1... | collective-permute-start | bytes 393224 | tf_op jit(solution)/shard_map/ppermute | solution.py:944
  172.6 8.6 %collective-permute-start.20 = (bf16[80,128]{1,0:T(8,128)(2,1)S(1)}, bf16[80,128]{1,0:T(8,128)(2,1)S(1)}, u32[]{:S(2)}, u32[]{:S(2)}) collective-permute-start(bf16[80,128]{1,0:T(8,128)(2,1)S(1)} %gather_sum.7.refs_1_.refs_0_), channel_id=1, source_target_pairs={{0,96},{16,112},{32,0},{48,16},{64,32},{80,48},{96,64},{112,80},{1... | collective-permute-start | bytes 61448 | tf_op jit(solution)/shard_map/ppermute | solution.py:412
  175.4 5.8 %collective-permute-start.19 = (bf16[80,128]{1,0:T(8,128)(2,1)S(1)}, bf16[80,128]{1,0:T(8,128)(2,1)S(1)}, u32[]{:S(2)}, u32[]{:S(2)}) collective-permute-start(bf16[80,128]{1,0:T(8,128)(2,1)S(1)} %gather_sum.7.refs_1_.refs_0_), channel_id=1, source_target_pairs={{0,64},{16,80},{32,96},{48,112},{64,0},{80,16},{96,32},{112,48},{1... | collective-permute-start | bytes 61448 | tf_op jit(solution)/shard_map/ppermute | solution.py:412
  176.7 4.6 %collective-permute-start.18 = (bf16[80,128]{1,0:T(8,128)(2,1)S(1)}, bf16[80,128]{1,0:T(8,128)(2,1)S(1)}, u32[]{:S(2)}, u32[]{:S(2)}) collective-permute-start(bf16[80,128]{1,0:T(8,128)(2,1)S(1)} %gather_sum.7.refs_1_.refs_0_), channel_id=1, source_target_pairs={{0,32},{16,48},{32,64},{48,80},{64,96},{80,112},{96,0},{112,16},{1... | collective-permute-start | bytes 61448 | tf_op jit(solution)/shard_map/ppermute | solution.py:412
  181.3 6.4 %collective-permute-start.21 = (bf16[4,80,128]{2,1,0:T(8,128)(2,1)S(1)}, bf16[4,80,128]{2,1,0:T(8,128)(2,1)S(1)}, u32[]{:S(2)}, u32[]{:S(2)}) collective-permute-start(bf16[4,80,128]{2,1,0:T(8,128)(2,1)S(1)} %stack.8.refs_9_.refs_2_), channel_id=1, source_target_pairs={{0,16},{16,0},{32,48},{48,32},{64,80},{80,64},{96,112},{112,96},{1... | collective-permute-start | bytes 245768 | tf_op jit(solution)/shard_map/ppermute | solution.py:423
  189.7 3.2 %collective-permute-start.26 = (bf16[16,128]{1,0:T(8,128)(2,1)S(1)}, bf16[16,128]{1,0:T(8,128)(2,1)S(1)}, u32[]{:S(2)}, u32[]{:S(2)}) collective-permute-start(bf16[16,128]{1,0:T(8,128)(2,1)S(1)} %get-tuple-element.158.refs_0_), channel_id=1, source_target_pairs={{0,3},{1,0},{2,1},{3,2},{4,7},{5,4},{6,5},{7,6},{8,11},{9,8},{10,9... | collective-permute-start | bytes 12296 | tf_op jit(solution)/shard_map/ppermute | solution.py:592
  190.5 4.0 %collective-permute-start.25 = (bf16[16,128]{1,0:T(8,128)(2,1)S(1)}, bf16[16,128]{1,0:T(8,128)(2,1)S(1)}, u32[]{:S(2)}, u32[]{:S(2)}) collective-permute-start(bf16[16,128]{1,0:T(8,128)(2,1)S(1)} %get-tuple-element.158.refs_0_), channel_id=1, source_target_pairs={{0,2},{1,3},{2,0},{3,1},{4,6},{5,7},{6,4},{7,5},{8,10},{9,11},{10,... | collective-permute-start | bytes 12296 | tf_op jit(solution)/shard_map/ppermute | solution.py:592
  191.8 3.7 %collective-permute-start.24 = (bf16[16,128]{1,0:T(8,128)(2,1)S(1)}, bf16[16,128]{1,0:T(8,128)(2,1)S(1)}, u32[]{:S(2)}, u32[]{:S(2)}) collective-permute-start(bf16[16,128]{1,0:T(8,128)(2,1)S(1)} %get-tuple-element.158.refs_0_), channel_id=1, source_target_pairs={{0,1},{1,2},{2,3},{3,0},{4,5},{5,6},{6,7},{7,4},{8,9},{9,10},{10,1... | collective-permute-start | bytes 12296 | tf_op jit(solution)/shard_map/ppermute | solution.py:592
  195.6 2.5 %collective-permute-start.29 = (bf16[16,128]{1,0:T(8,128)(2,1)S(1)}, bf16[16,128]{1,0:T(8,128)(2,1)S(1)}, u32[]{:S(2)}, u32[]{:S(2)}) collective-permute-start(bf16[16,128]{1,0:T(8,128)(2,1)S(1)} %sum_over.2.refs_0_.refs_4_), channel_id=1, source_target_pairs={{0,12},{1,13},{2,14},{3,15},{4,0},{5,1},{6,2},{7,3},{8,4},{9,5},{1... | collective-permute-start | bytes 12296 | tf_op jit(solution)/shard_map/ppermute | solution.py:592
  196.0 4.0 %collective-permute-start.28 = (bf16[16,128]{1,0:T(8,128)(2,1)S(1)}, bf16[16,128]{1,0:T(8,128)(2,1)S(1)}, u32[]{:S(2)}, u32[]{:S(2)}) collective-permute-start(bf16[16,128]{1,0:T(8,128)(2,1)S(1)} %sum_over.2.refs_0_.refs_4_), channel_id=1, source_target_pairs={{0,8},{1,9},{2,10},{3,11},{4,12},{5,13},{6,14},{7,15},{8,0},{9,1},... | collective-permute-start | bytes 12296 | tf_op jit(solution)/shard_map/ppermute | solution.py:592
  197.1 3.7 %collective-permute-start.27 = (bf16[16,128]{1,0:T(8,128)(2,1)S(1)}, bf16[16,128]{1,0:T(8,128)(2,1)S(1)}, u32[]{:S(2)}, u32[]{:S(2)}) collective-permute-start(bf16[16,128]{1,0:T(8,128)(2,1)S(1)} %sum_over.2.refs_0_.refs_4_), channel_id=1, source_target_pairs={{0,4},{1,5},{2,6},{3,7},{4,8},{5,9},{6,10},{7,11},{8,12},{9,13},{1... | collective-permute-start | bytes 12296 | tf_op jit(solution)/shard_map/ppermute | solution.py:592
  200.8 3.7 %collective-permute-start.32 = (bf16[16,128]{1,0:T(8,128)(2,1)S(1)}, bf16[16,128]{1,0:T(8,128)(2,1)S(1)}, u32[]{:S(2)}, u32[]{:S(2)}) collective-permute-start(bf16[16,128]{1,0:T(8,128)(2,1)S(1)} %sum_over.3.refs_0_.refs_4_), channel_id=1, source_target_pairs={{0,96},{16,112},{32,0},{48,16},{64,32},{80,48},{96,64},{112,80},{1... | collective-permute-start | bytes 12296 | tf_op jit(solution)/shard_map/ppermute | solution.py:412
  203.8 4.0 %collective-permute-start.31 = (bf16[16,128]{1,0:T(8,128)(2,1)S(1)}, bf16[16,128]{1,0:T(8,128)(2,1)S(1)}, u32[]{:S(2)}, u32[]{:S(2)}) collective-permute-start(bf16[16,128]{1,0:T(8,128)(2,1)S(1)} %sum_over.3.refs_0_.refs_4_), channel_id=1, source_target_pairs={{0,64},{16,80},{32,96},{48,112},{64,0},{80,16},{96,32},{112,48},{1... | collective-permute-start | bytes 12296 | tf_op jit(solution)/shard_map/ppermute | solution.py:412
  204.0 3.8 %collective-permute-start.30 = (bf16[16,128]{1,0:T(8,128)(2,1)S(1)}, bf16[16,128]{1,0:T(8,128)(2,1)S(1)}, u32[]{:S(2)}, u32[]{:S(2)}) collective-permute-start(bf16[16,128]{1,0:T(8,128)(2,1)S(1)} %sum_over.3.refs_0_.refs_4_), channel_id=1, source_target_pairs={{0,32},{16,48},{32,64},{48,80},{64,96},{80,112},{96,0},{112,16},{1... | collective-permute-start | bytes 12296 | tf_op jit(solution)/shard_map/ppermute | solution.py:412
  207.8 5.5 %collective-permute-start.33 = (bf16[4,16,128]{2,1,0:T(8,128)(2,1)S(1)}, bf16[4,16,128]{2,1,0:T(8,128)(2,1)S(1)}, u32[]{:S(2)}, u32[]{:S(2)}) collective-permute-start(bf16[4,16,128]{2,1,0:T(8,128)(2,1)S(1)} %stack.9.refs_2_), channel_id=1, source_target_pairs={{0,16},{16,0},{32,48},{48,32},{64,80},{80,64},{96,112},{112,96},{1... | collective-permute-start | bytes 49160 | tf_op jit(solution)/shard_map/ppermute | solution.py:423

commit v9 on v8

--- a/solution.py
+++ b/solution.py
@@ -90,6 +90,7 @@
 
 
 SMEM = pl.BlockSpec(memory_space=pltpu.SMEM)
+INDEX = pl.BlockSpec(memory_space=pltpu.SMEM)
 VMEM = pl.BlockSpec(memory_space=pltpu.VMEM)
 HBM = pl.BlockSpec(memory_space=pl.ANY)
 AFTER = pl.BlockSpec(memory_space=pl.ANY)
@@ -97,6 +98,7 @@
 LOOSE = pl.BlockSpec(memory_space=pl.ANY)
 FREE = pl.BlockSpec(memory_space=pltpu.VMEM)
 AHEAD = 3
+LISTED, PLACE, OWN, INDICES = 64, 128, 192, 256
 CHUNKS = 4
 PIN = True
 
@@ -158,9 +160,9 @@
 
 def pack_kernel(branch, mask_ref, slot_ref, index_ref, near_mask_ref, far_ref, *refs):
     basis_ref, transfer_ref, top_ref = refs[:3]
-    out_ref, count_ref, list_ref, basis_out, transfer_out, top_out = refs[3:9]
-    blocks, total, packed, basis, transfer, top, turned, lifting, row = refs[9:18]
-    arrived, left, came = refs[18:]
+    out_ref, index_out, basis_out, transfer_out, top_out = refs[3:8]
+    blocks, total, packed, basis, transfer, top, turned, lifting, row = refs[8:17]
+    arrived, left, came = refs[17:]
     leaves, entries, rank, _ = blocks.shape
     sources, _, width = packed.shape
     slots = width // rank
@@ -188,11 +190,15 @@
         leaf, n = i // near_entries, i % near_entries
         place = index_ref[leaf, n]
         hit = (near_mask_ref[leaf, n] != 0) & ((place < HW) | (place >= HW + leaves))
-        list_ref[i] = 0
+        own = (place >= HW) & (place < HW + leaves) & (near_mask_ref[leaf, n] != 0)
+        index_out[OWN + i] = jnp.where(own, place - HW + 1, 0)
+        index_out[LISTED + i] = 0
+        index_out[PLACE + i] = 0
 
         @pl.when(hit)
         def _():
-            list_ref[count] = i
+            index_out[LISTED + count] = i
+            index_out[PLACE + count] = jnp.where(place < HW, place, place - leaves)
 
         return count + hit.astype(jnp.int32)
 
@@ -203,10 +209,9 @@
     ]
     for copy in small:
         copy.start()
-    begin, run = windowed(leaves, leaves, fetch, work)
+    begin, run = windowed(leaves, AHEAD, fetch, work)
     begin()
-    count = lax.fori_loop(0, list_ref.shape[0], list_one, 0)
-    count_ref[0] = count
+    index_out[0] = lax.fori_loop(0, leaves * near_entries, list_one, 0)
     for copy in small:
         copy.wait()
     turn = lambda a: a.astype(F32).T.astype(BF16)
@@ -248,8 +253,7 @@
         (SMEM,) * 5 + (HBM,) * 4,
         [
             (shape, BF16, HBM),
-            ((1,), jnp.int32, SMEM),
-            ((near_index.size,), jnp.int32, SMEM),
+            ((INDICES,), jnp.int32, INDEX),
             (turned, BF16, HBM),
             (lifting, BF16, HBM),
             (row, BF16, HBM),
@@ -274,13 +278,13 @@
     )
 
 
-def choose_kernel(count_ref, list_ref, near_ref, _, out_ref, chosen, moved, given):
+def choose_kernel(index_ref, near_ref, _, out_ref, chosen, moved, given):
     piece = chosen.shape[0] // given.shape[0]
     entries = near_ref.shape[1]
-    count = count_ref[0]
+    count = index_ref[0]
 
     def move(i):
-        entry = list_ref[i]
+        entry = index_ref[LISTED + i]
         source = near_ref.at[entry // entries, entry % entries]
         return pltpu.make_async_copy(source, chosen.at[i], moved.at[i])
 
@@ -302,13 +306,13 @@
     each(pieces, lambda i: give(i).wait())
 
 
-def choose(listed, near_blocks, earlier):
+def choose(index, near_blocks, earlier):
     leaves, entries, size, _ = near_blocks.shape
     shape = (leaves * entries, size, size)
     return call(
         choose_kernel,
-        (*listed, near_blocks, earlier),
-        (SMEM, SMEM, HBM, AFTER),
+        (index, near_blocks, earlier),
+        (INDEX, HBM, AFTER),
         [(shape, BF16, HBM)],
         [pltpu.VMEM(shape, BF16), semaphores(shape[0]), semaphores(shape[0] // 8)],
         "choose",
@@ -317,7 +321,7 @@
     )[0]
 
 
-def near_kernel(index_ref, mask_ref, blocks_ref, own_ref, *refs):
+def near_kernel(index_ref, blocks_ref, own_ref, *refs):
     out_ref, blocks, own, result, arrived, came, left = refs[-7:]
     leaves, entries, size, _ = blocks.shape
     pair = leaves // CHUNKS
@@ -332,10 +336,9 @@
     def work(leaf):
         total = None
         for n in range(entries):
-            place = index_ref[leaf, n] - HW
-            inside = (place >= 0) & (place < leaves)
-            weight = jnp.where(inside, mask_ref[leaf, n], 0).astype(F32).astype(BF16)
-            values = own[jnp.clip(place, 0, leaves - 1)] * weight
+            place = index_ref[OWN + leaf * entries + n]
+            weight = (place > 0).astype(F32).astype(BF16)
+            values = own[jnp.maximum(place - 1, 0)] * weight
             term = dot(blocks[leaf, n], values)
             total = term if total is None else total + term
         result[leaf] = total
@@ -354,13 +357,13 @@
         store(i).wait()
 
 
-def near_field(near_index, near_mask, near_blocks, own, *earlier):
+def near_field(index, near_blocks, own, *earlier):
     leaves, _, size, _ = near_blocks.shape
     columns = own.shape[2]
     return call(
         near_kernel,
-        (near_index, near_mask, near_blocks, own) + earlier,
-        (SMEM, SMEM, HBM, HBM) + (AFTER,) * len(earlier),
+        (index, near_blocks, own) + earlier,
+        (INDEX, HBM, HBM) + (AFTER,) * len(earlier),
         [((leaves, size, columns), F32, HBM)],
         [
             pltpu.VMEM(near_blocks.shape, BF16),
@@ -432,7 +435,7 @@
         ups[lax.rem(mate + count - 2 * j, count)] = other[j]
 
 
-def far_kernel(count_ref, list_ref, recv, packed_ref, blocks_ref, *refs):
+def far_kernel(index_ref, recv, packed_ref, blocks_ref, *refs):
     held = (len(refs) - 7) // 2
     sources, (_, far, blocks), targets = refs[:held], refs[held : held + 3], refs[held + 3 : -4]
     packed, arrived, fetched, loaded = refs[-4:]
@@ -440,7 +443,7 @@
     width = packed.shape[2]
     chosen = len(blocks_ref.shape) == 3
     piece = blocks.shape[0] // fetched.shape[0]
-    count = (count_ref[0] + piece - 1) // piece
+    count = (index_ref[0] + piece - 1) // piece
 
     def fetch(i):
         some = slab(i, share)
@@ -450,7 +453,7 @@
         if chosen:
             some = slab(i, piece)
             return pltpu.make_async_copy(blocks_ref.at[some], blocks.at[some], fetched.at[i])
-        entry, entries = list_ref[i], blocks_ref.shape[1]
+        entry, entries = index_ref[LISTED + i], blocks_ref.shape[1]
         source = blocks_ref.at[entry // entries, entry % entries]
         return pltpu.make_async_copy(source, blocks.at[i], fetched.at[i])
 
@@ -492,7 +495,7 @@
         copy.wait()
 
 
-def far_field(listed, recv, packed, near_blocks, held, earlier):
+def far_field(index, recv, packed, near_blocks, held, earlier):
     sources, rows, _ = packed.shape
     size = near_blocks.shape[-1]
     number = near_blocks.size // size**2
@@ -500,8 +503,8 @@
     outs = [((rows, recv.shape[2]), F32, VMEM), ((number, size, size), BF16, VMEM)]
     far, blocks, *held = call(
         far_kernel,
-        (*listed, recv, packed, near_blocks, *held, earlier),
-        (SMEM, SMEM, VMEM, HBM, HBM) + (HBM,) * len(held) + (AFTER_VMEM,),
+        (index, recv, packed, near_blocks, *held, earlier),
+        (INDEX, VMEM, HBM, HBM) + (HBM,) * len(held) + (AFTER_VMEM,),
         outs + [(a.shape, a.dtype, VMEM) for a in held],
         [
             pltpu.VMEM(packed.shape, BF16),
@@ -516,7 +519,7 @@
     return far, blocks, held
 
 
-def halo_kernel(count_ref, list_ref, index_ref, blocks, before, after, near_in, *refs):
+def halo_kernel(index_ref, blocks, before, after, near_in, *refs):
     held = (len(refs) - 4) // 2
     sources, near, targets = refs[:held], refs[held + 1], refs[held + 2 : -2]
     halo, loaded = refs[-2:]
@@ -526,10 +529,11 @@
     ]
     for copy in loads:
         copy.start()
-    leaves, reach, entries = near.shape[0], before.shape[0], index_ref.shape[1]
+    reach = before.shape[0]
+    entries = blocks.shape[0] // near.shape[0]
     halo[:reach] = before[...]
     halo[reach:] = after[...]
-    count = count_ref[0]
+    count = index_ref[0]
     at_once = 8
 
     def add(group, carry):
@@ -537,10 +541,8 @@
         for j in range(at_once):
             i = jnp.minimum(group * at_once + j, count - 1)
             weight = (group * at_once + j < count).astype(F32).astype(BF16)
-            entry = list_ref[i]
-            leaf = entry // entries
-            place = index_ref[leaf, entry % entries]
-            values = halo[jnp.where(place < reach, place, place - leaves)] * weight
+            leaf = index_ref[LISTED + i] // entries
+            values = halo[index_ref[PLACE + i]] * weight
             terms.append((leaf, dot(blocks[i], values)))
         for leaf, term in terms:
             near[leaf] += term
@@ -551,17 +553,17 @@
         copy.wait()
 
 
-def halo_part(listed, near_index, blocks, before, after, near, held, earlier):
+def halo_part(index, blocks, before, after, near, held, earlier):
     return call(
         halo_kernel,
-        (*listed, near_index, blocks, before, after, near, *held, earlier),
-        (SMEM, SMEM, SMEM, VMEM, VMEM, VMEM, VMEM) + (HBM,) * len(held) + (AFTER_VMEM,),
+        (index, blocks, before, after, near, *held, earlier),
+        (INDEX, VMEM, VMEM, VMEM, VMEM) + (HBM,) * len(held) + (AFTER_VMEM,),
         [(a.shape, a.dtype, VMEM) for a in (near, *held)],
         [pltpu.VMEM((2 * before.shape[0],) + before.shape[1:], BF16), semaphores(len(held))],
         "halo_part",
         1 << 28,
         2 << 20,
-        {6: 0},
+        {4: 0},
     )
 
 
@@ -932,33 +934,32 @@
 
     zs = [rhs.reshape(leaves, -1, rhs.shape[1])]
     out = stage(0, points, wanted, branch, zs[0], basis, transfer, None)
-    packed, count, entries, turned, lifting, top = pack(
+    packed, index, turned, lifting, top = pack(
         branch, basis, transfer, top_blocks, far_blocks, far_mask, far_slot, near_index, near_mask,
         inner, slots,
     )
-    listed = (count, entries)
     state = out["state"]
     for k in range(1, STEPS + 1):
         recv = exchange(out["send"], "inner")
         before = lax.ppermute(out["high"], "inner", up_pairs)
         after = lax.ppermute(out["low"], "inner", down_pairs)
         earlier = (packed,) if k == 1 else ()
-        near = near_field(near_index, near_mask, near_blocks, out["coarse"], *earlier)
+        near = near_field(index, near_blocks, out["coarse"], *earlier)
         done = near
         if k == 1:
             chosen = near_blocks
         elif k == 2:
-            chosen = done = choose(listed, near_blocks, near)
+            chosen = done = choose(index, near_blocks, near)
         if k == STEPS:
             krylov = done = vectors(state, zs, list(range(STEPS - 1)), near, CHUNKS)[0]
         summed = gather_sum(recv, slots * rank, done)
         local_far, blocks, (near,) = far_field(
-            listed, recv, packed, chosen, (near,), summed
+            index, recv, packed, chosen, (near,), summed
         )
 
         def between(column):
             held = (basis, turned, transfer, lifting, top, *zs)
-            return halo_part(listed, near_index, blocks, before, after, near, held, column)
+            return halo_part(index, blocks, before, after, near, held, column)
 
         column, other, (near, *held) = over_branches(summed, outer, local_far, between)
         later = [column, other, state, local_far, near, *held]

time: 217 us -> 209 us (0.963)
  Pallas kernels: 102 us -> 94.1 us
    pallas_call x33, Pallas kernels: 102 us -> 94.1 us  [call(): pl.pallas_call(kernel, in_specs=list(in_specs), out_specs=[spec for _, _,...]
    ppermute x15, starting transfers between devices: 18.3 us -> 15.8 us  [over_branches(): lax.ppermute(summed, 'outer', shift)]
  transfers between devices with their start and end apart: 38 -> 38, of which waited for: 11 -> 12; matrix products, arithmetic and copies ran while one was open for 0% -> 0% of each run, Pallas kernels for 37% -> 35%
where the time goes in v9:
time: 209 us; the launch traced here: 208 us
  Pallas kernels  94.1 us (45%)
  starting transfers between devices  80.5 us (39%)
  waiting for transfers between devices  32.3 us (15%)
    pallas_call x33, Pallas kernels, call(): pl.pallas_call(kernel, in_specs=list(in_specs), out_specs=[spec for _, _,...  94.1 us
    all_to_all x4, starting transfers between devices, exchange(): return lax.all_to_all(array, axis, split_axis=0, concat_axis=0, tiled=True)  25.1 us
    all_to_all x4, waiting for transfers between devices, exchange(): return lax.all_to_all(array, axis, split_axis=0, concat_axis=0, tiled=True)  22.4 us
    ppermute x5, starting transfers between devices, over_branches(): other = lax.ppermute(column, 'outer', [(o, o ^ 1) for o in range(outer)])  16.8 us
    ppermute x15, starting transfers between devices, over_branches(): lax.ppermute(summed, 'outer', shift)  15.8 us
    ppermute x4, starting transfers between devices, shards(): before = lax.ppermute(out['high'], 'inner', up_pairs)  13.1 us
    ppermute x6, waiting for transfers between devices, sum_over(): lax.ppermute(dots, axis, [(i, moved(i, j)) for i in range(size)])  5.44 us
    ppermute x4, starting transfers between devices, shards(): after = lax.ppermute(out['low'], 'inner', down_pairs)  5.17 us
  transfers between devices with their start and end apart: 38, of which 12 were waited for; matrix products, arithmetic and copies ran while one was open for 0% of the time, Pallas kernels for 35%

profile of v9, /device:TPU:1, one launch (start us, length us, event | category | flops | bytes accessed | tf_op | source)
XLA Modules:
  0.0 208.1 jit_solution(12029395772832572296)
XLA Ops:
  0.6 4.3 %stage0.1 = (f32[64,128]{1,0:T(8,128)S(1)}, bf16[16,336,128]{2,1,0:T(8,128)(2,1)}, bf16[8,256,128]{2,1,0:T(8,128)(2,1)}, bf16[2,256,128]{2,1,0:T(8,128)(2,1)S(1)}, bf16[2,256,128]{2,1,0:T(8,128)(2,1)S(1)}) custom-call(s32[4,16]{1,0:T(4,128)} %bitcast.13, s32[1]{0:T(128)} %bitcast.2.refs_1_.branch, f32[8,256,128]{2,1,0:T(8,128)} %bitcast.7, ...), custom_call_target="tpu_custom_call" | custom-call | flops 134217728 | bytes 4194304 | tf_op jit(solution)/shard_map/stage0/pallas_call | solution.py:118
  4.9 8.6 %all-to-all-start = ((bf16[16,336,128]{2,1,0:T(8,128)(2,1)}), bf16[16,336,128]{2,1,0:T(8,128)(2,1)S(1)}, u32[]{:S(2)}, u32[]{:S(2)}) async-start(bf16[16,336,128]{2,1,0:T(8,128)(2,1)} %get-tuple-element.81), calls=%async_computation | async-start | bytes 2752512 | tf_op jit(solution)/shard_map/all_to_all | solution.py:933
  13.5 3.3 %collective-permute-start.4 = (bf16[2,256,128]{2,1,0:T(8,128)(2,1)S(1)}, bf16[2,256,128]{2,1,0:T(8,128)(2,1)S(1)}, u32[]{:S(2)}, u32[]{:S(2)}) collective-permute-start(bf16[2,256,128]{2,1,0:T(8,128)(2,1)S(1)} %get-tuple-element.88), channel_id=1, source_target_pairs={{0,1},{1,2},{2,3},{3,4},{4,5},{5,6},{6,7},{7,8},{8,9},{9,10},{10,1... | collective-permute-start | bytes 393224 | tf_op jit(solution)/shard_map/ppermute | solution.py:944
  16.8 1.3 collective-permute-start.5
  18.1 9.6 %pack.1 = (bf16[16,512,256]{2,1,0:T(8,128)(2,1)}, s32[256]{0:T(256)S(1)}, bf16[8,256,64]{2,1,0:T(8,128)(2,1)}, bf16[64,512]{1,0:T(8,128)(2,1)}, bf16[64,512]{1,0:T(8,128)(2,1)}) custom-call(s32[1]{0:T(128)} %bitcast.2.refs_1_.branch, s32[8,48]{1,0:T(8,128)} %mask_ref.1, s32[8,48]{1,0:T(8,128)} %slot_ref.1, s32[8,8]{1,0:T(8,128)} %index_ref.1, ...), custom_call_target="tpu_custom_call" | custom-call | bytes 10485760 | tf_op jit(solution)/shard_map/pack/pallas_call | solution.py:118
  27.7 6.7 %near_field.4.refs_0_ = f32[8,256,128]{2,1,0:T(8,128)} custom-call(s32[256]{0:T(256)S(1)} %get-tuple-element.82.index_ref, bf16[8,8,256,256]{3,2,1,0:T(8,128)(2,1)} %blocks_ref.9, bf16[8,256,128]{2,1,0:T(8,128)(2,1)} %get-tuple-element.83.own_ref, bf16[16,512,256]{2,1,0:T(8,128)(2,1)} %get-tuple-element.84.refs_0_.packed_ref), custom_call_target="tpu_custom_call" | custom-call | flops 1073741824 | bytes 8388608 | tf_op jit(solution)/shard_map/near_field/pallas_call | solution.py:118
  34.5 2.5 %collective-permute-start.2 = (bf16[80,128]{1,0:T(8,128)(2,1)S(1)}, bf16[80,128]{1,0:T(8,128)(2,1)S(1)}, u32[]{:S(2)}, u32[]{:S(2)}) collective-permute-start(bf16[80,128]{1,0:T(8,128)(2,1)S(1)} %gather_sum.4.refs_1_.refs_0_), channel_id=1, source_target_pairs={{0,96},{16,112},{32,0},{48,16},{64,32},{80,48},{96,64},{112,80},{1... | collective-permute-start | bytes 61448 | tf_op jit(solution)/shard_map/ppermute | solution.py:415
  38.2 4.3 %far_field.4 = (f32[512,128]{1,0:T(8,128)S(1)}, bf16[64,256,256]{2,1,0:T(8,128)(2,1)S(1)}, f32[8,256,128]{2,1,0:T(8,128)S(1)}) custom-call(s32[256]{0:T(256)S(1)} %get-tuple-element.82.index_ref, bf16[16,336,128]{2,1,0:T(8,128)(2,1)S(1)} %all-to-all-done.recv, bf16[16,512,256]{2,1,0:T(8,128)(2,1)} %get-tuple-element.84.refs_0_.packed_ref, ...), custom_call_target="tpu_custom_call" | custom-call | flops 536870912 | bytes 4194304 | tf_op jit(solution)/shard_map/far_field/pallas_call | solution.py:118
  42.6 2.5 %collective-permute-start.3 = (bf16[4,80,128]{2,1,0:T(8,128)(2,1)S(1)}, bf16[4,80,128]{2,1,0:T(8,128)(2,1)S(1)}, u32[]{:S(2)}, u32[]{:S(2)}) collective-permute-start(bf16[4,80,128]{2,1,0:T(8,128)(2,1)S(1)} %stack.5.refs_6_.refs_2_), channel_id=1, source_target_pairs={{0,16},{16,0},{32,48},{48,32},{64,80},{80,64},{96,112},{112,96},{1... | collective-permute-start | bytes 245768 | tf_op jit(solution)/shard_map/ppermute | solution.py:426
  45.1 2.2 %halo_part.4 = (f32[8,256,128]{2,1,0:T(8,128)S(1)}, bf16[8,64,256]{2,1,0:T(8,128)(2,1)S(1)}, bf16[8,256,64]{2,1,0:T(8,128)(2,1)S(1)}, bf16[8,64,64]{2,1,0:T(8,12...) custom-call(s32[256]{0:T(256)S(1)} %get-tuple-element.82.index_ref, ...), custom_call_target="tpu_custom_call", output_to_operand_aliasing={{0}: (4, {})} | custom-call | flops 268435456 | bytes 2097152 | tf_op jit(solution)/shard_map/halo_part/pallas_call | solution.py:118
  47.2 4.6 %stage1.1 = (f32[8,256,128]{2,1,0:T(8,128)}, f32[64,128]{1,0:T(8,128)S(1)}, bf16[16,336,128]{2,1,0:T(8,128)(2,1)}, bf16[8,256,128]{2,1,0:T(8,128)(2,1)}, bf16[2,...) custom-call(s32[4,16]{1,0:T(4,128)} %bitcast.14, s32[1]{0:T(128)} %bitcast.2.refs_1_.branch, ...), custom_call_target="tpu_custom_call" | custom-call | flops 134217728 | bytes 5242880 | tf_op jit(solution)/shard_map/stage1/pallas_call | solution.py:118
  51.8 7.8 %all-to-all-start.1 = ((bf16[16,336,128]{2,1,0:T(8,128)(2,1)}), bf16[16,336,128]{2,1,0:T(8,128)(2,1)S(1)}, u32[]{:S(2)}, u32[]{:S(2)}) async-start(bf16[16,336,128]{2,1,0:T(8,128)(2,1)} %get-tuple-element.101), calls=%async_computation.1 | async-start | bytes 2752512 | tf_op jit(solution)/shard_map/all_to_all | solution.py:933
  59.6 3.3 %collective-permute-start.10 = (bf16[2,256,128]{2,1,0:T(8,128)(2,1)S(1)}, bf16[2,256,128]{2,1,0:T(8,128)(2,1)S(1)}, u32[]{:S(2)}, u32[]{:S(2)}) collective-permute-start(bf16[2,256,128]{2,1,0:T(8,128)(2,1)S(1)} %get-tuple-element.106), channel_id=1, source_target_pairs={{0,1},{1,2},{2,3},{3,4},{4,5},{5,6},{6,7},{7,8},{8,9},{9,10},{10,1... | collective-permute-start | bytes 393224 | tf_op jit(solution)/shard_map/ppermute | solution.py:944
  64.2 6.7 %near_field.5._.refs_0_ = f32[8,256,128]{2,1,0:T(8,128)} custom-call(s32[256]{0:T(256)S(1)} %get-tuple-element.82.index_ref, bf16[8,8,256,256]{3,2,1,0:T(8,128)(2,1)} %blocks_ref.9, bf16[8,256,128]{2,1,0:T(8,128)(2,1)} %get-tuple-element.102.own_ref), custom_call_target="tpu_custom_call" | custom-call | flops 1073741824 | bytes 8388608 | tf_op jit(solution)/shard_map/near_field/pallas_call | solution.py:118
  71.0 4.2 %choose.1.refs_0_.blocks_ref = bf16[64,256,256]{2,1,0:T(8,128)(2,1)} custom-call(s32[256]{0:T(256)S(1)} %get-tuple-element.82.index_ref, bf16[8,8,256,256]{3,2,1,0:T(8,128)(2,1)} %blocks_ref.9, f32[8,256,128]{2,1,0:T(8,128)} %near_field.5._.refs_0_), custom_call_target="tpu_custom_call" | custom-call | bytes 5242880 | tf_op jit(solution)/shard_map/choose/pallas_call | solution.py:118
  75.2 5.9 %all-to-all-done.1.recv = bf16[16,336,128]{2,1,0:T(8,128)(2,1)S(1)} async-done(((bf16[16,336,128]{2,1,0:T(8,128)(2,1)}), bf16[16,336,128]{2,1,0:T(8,128)(2,1)S(1)}, u32[]{:S(2)}, u32[]{:S(2)}) %all-to-all-start.1) | async-done | bytes 1376288 | tf_op jit(solution)/shard_map/all_to_all | solution.py:933
  81.1 2.2 %collective-permute-start.8 = (bf16[80,128]{1,0:T(8,128)(2,1)S(1)}, bf16[80,128]{1,0:T(8,128)(2,1)S(1)}, u32[]{:S(2)}, u32[]{:S(2)}) collective-permute-start(bf16[80,128]{1,0:T(8,128)(2,1)S(1)} %gather_sum.5.refs_1_.refs_0_), channel_id=1, source_target_pairs={{0,96},{16,112},{32,0},{48,16},{64,32},{80,48},{96,64},{112,80},{1... | collective-permute-start | bytes 61448 | tf_op jit(solution)/shard_map/ppermute | solution.py:415
  84.2 3.8 %far_field.5 = (f32[512,128]{1,0:T(8,128)S(1)}, bf16[64,256,256]{2,1,0:T(8,128)(2,1)S(1)}, f32[8,256,128]{2,1,0:T(8,128)S(1)}) custom-call(s32[256]{0:T(256)S(1)} %get-tuple-element.82.index_ref, bf16[16,336,128]{2,1,0:T(8,128)(2,1)S(1)} %all-to-all-done.1.recv, bf16[16,512,256]{2,1,0:T(8,128)(2,1)} %get-tuple-element.84.refs_0_.packed_ref, ...), custom_call_target="tpu_custom_call" | custom-call | flops 536870912 | bytes 4194304 | tf_op jit(solution)/shard_map/far_field/pallas_call | solution.py:118
  88.1 3.2 %collective-permute-start.9 = (bf16[4,80,128]{2,1,0:T(8,128)(2,1)S(1)}, bf16[4,80,128]{2,1,0:T(8,128)(2,1)S(1)}, u32[]{:S(2)}, u32[]{:S(2)}) collective-permute-start(bf16[4,80,128]{2,1,0:T(8,128)(2,1)S(1)} %stack.6.refs_7_.refs_2_), channel_id=1, source_target_pairs={{0,16},{16,0},{32,48},{48,32},{64,80},{80,64},{96,112},{112,96},{1... | collective-permute-start | bytes 245768 | tf_op jit(solution)/shard_map/ppermute | solution.py:426
  91.3 2.5 %halo_part.5 = (f32[8,256,128]{2,1,0:T(8,128)S(1)}, bf16[8,64,256]{2,1,0:T(8,128)(2,1)S(1)}, bf16[8,256,64]{2,1,0:T(8,128)(2,1)S(1)}, bf16[8,64,64]{2,1,0:T(8,12...) custom-call(s32[256]{0:T(256)S(1)} %get-tuple-element.82.index_ref, ...), custom_call_target="tpu_custom_call", output_to_operand_aliasing={{0}: (4, {})} | custom-call | flops 268435456 | bytes 2097152 | tf_op jit(solution)/shard_map/halo_part/pallas_call | solution.py:118
  93.8 4.7 %stage2.1 = (f32[8,256,128]{2,1,0:T(8,128)}, f32[64,128]{1,0:T(8,128)S(1)}, bf16[16,336,128]{2,1,0:T(8,128)(2,1)}, bf16[8,256,128]{2,1,0:T(8,128)(2,1)}, bf16[2,...) custom-call(s32[4,16]{1,0:T(4,128)} %bitcast.15, s32[1]{0:T(128)} %bitcast.2.refs_1_.branch, ...), custom_call_target="tpu_custom_call" | custom-call | flops 134217728 | bytes 6291456 | tf_op jit(solution)/shard_map/stage2/pallas_call | solution.py:118
  98.5 4.4 %all-to-all-start.2 = ((bf16[16,336,128]{2,1,0:T(8,128)(2,1)}), bf16[16,336,128]{2,1,0:T(8,128)(2,1)S(1)}, u32[]{:S(2)}, u32[]{:S(2)}) async-start(bf16[16,336,128]{2,1,0:T(8,128)(2,1)} %get-tuple-element.118), calls=%async_computation.2 | async-start | bytes 2752512 | tf_op jit(solution)/shard_map/all_to_all | solution.py:933
  102.8 3.3 %collective-permute-start.16 = (bf16[2,256,128]{2,1,0:T(8,128)(2,1)S(1)}, bf16[2,256,128]{2,1,0:T(8,128)(2,1)S(1)}, u32[]{:S(2)}, u32[]{:S(2)}) collective-permute-start(bf16[2,256,128]{2,1,0:T(8,128)(2,1)S(1)} %get-tuple-element.123), channel_id=1, source_target_pairs={{0,1},{1,2},{2,3},{3,4},{4,5},{5,6},{6,7},{7,8},{8,9},{9,10},{10,1... | collective-permute-start | bytes 393224 | tf_op jit(solution)/shard_map/ppermute | solution.py:944
  106.1 1.3 collective-permute-start.17
  107.4 6.7 %near_field.6.refs_0_ = f32[8,256,128]{2,1,0:T(8,128)} custom-call(s32[256]{0:T(256)S(1)} %get-tuple-element.82.index_ref, bf16[8,8,256,256]{3,2,1,0:T(8,128)(2,1)} %blocks_ref.9, bf16[8,256,128]{2,1,0:T(8,128)(2,1)} %get-tuple-element.119.own_ref), custom_call_target="tpu_custom_call" | custom-call | flops 1073741824 | bytes 8388608 | tf_op jit(solution)/shard_map/near_field/pallas_call | solution.py:118
  114.1 10.0 %all-to-all-done.2.recv = bf16[16,336,128]{2,1,0:T(8,128)(2,1)S(1)} async-done(((bf16[16,336,128]{2,1,0:T(8,128)(2,1)}), bf16[16,336,128]{2,1,0:T(8,128)(2,1)S(1)}, u32[]{:S(2)}, u32[]{:S(2)}) %all-to-all-start.2) | async-done | bytes 1376288 | tf_op jit(solution)/shard_map/all_to_all | solution.py:933
  124.2 2.2 %collective-permute-start.14 = (bf16[80,128]{1,0:T(8,128)(2,1)S(1)}, bf16[80,128]{1,0:T(8,128)(2,1)S(1)}, u32[]{:S(2)}, u32[]{:S(2)}) collective-permute-start(bf16[80,128]{1,0:T(8,128)(2,1)S(1)} %gather_sum.6.refs_1_.refs_0_), channel_id=1, source_target_pairs={{0,96},{16,112},{32,0},{48,16},{64,32},{80,48},{96,64},{112,80},{1... | collective-permute-start | bytes 61448 | tf_op jit(solution)/shard_map/ppermute | solution.py:415
  127.1 3.8 %far_field.6 = (f32[512,128]{1,0:T(8,128)S(1)}, bf16[64,256,256]{2,1,0:T(8,128)(2,1)S(1)}, f32[8,256,128]{2,1,0:T(8,128)S(1)}) custom-call(s32[256]{0:T(256)S(1)} %get-tuple-element.82.index_ref, bf16[16,336,128]{2,1,0:T(8,128)(2,1)S(1)} %all-to-all-done.2.recv, bf16[16,512,256]{2,1,0:T(8,128)(2,1)} %get-tuple-element.84.refs_0_.packed_ref, ...), custom_call_target="tpu_custom_call" | custom-call | flops 536870912 | bytes 4194304 | tf_op jit(solution)/shard_map/far_field/pallas_call | solution.py:118
  130.9 3.2 %collective-permute-start.15 = (bf16[4,80,128]{2,1,0:T(8,128)(2,1)S(1)}, bf16[4,80,128]{2,1,0:T(8,128)(2,1)S(1)}, u32[]{:S(2)}, u32[]{:S(2)}) collective-permute-start(bf16[4,80,128]{2,1,0:T(8,128)(2,1)S(1)} %stack.7.refs_8_.refs_2_), channel_id=1, source_target_pairs={{0,16},{16,0},{32,48},{48,32},{64,80},{80,64},{96,112},{112,96},{1... | collective-permute-start | bytes 245768 | tf_op jit(solution)/shard_map/ppermute | solution.py:426
  134.1 2.8 %halo_part.6 = (f32[8,256,128]{2,1,0:T(8,128)S(1)}, bf16[8,64,256]{2,1,0:T(8,128)(2,1)S(1)}, bf16[8,256,64]{2,1,0:T(8,128)(2,1)S(1)}, bf16[8,64,64]{2,1,0:T(8,12...) custom-call(s32[256]{0:T(256)S(1)} %get-tuple-element.82.index_ref, ...), custom_call_target="tpu_custom_call", output_to_operand_aliasing={{0}: (4, {})} | custom-call | flops 268435456 | bytes 2097152 | tf_op jit(solution)/shard_map/halo_part/pallas_call | solution.py:118
  136.9 4.8 %stage3.1 = (f32[8,256,128]{2,1,0:T(8,128)}, f32[64,128]{1,0:T(8,128)S(1)}, bf16[16,336,128]{2,1,0:T(8,128)(2,1)}, bf16[8,256,128]{2,1,0:T(8,128)(2,1)}, bf16[2,...) custom-call(s32[4,16]{1,0:T(4,128)} %bitcast.16, s32[1]{0:T(128)} %bitcast.2.refs_1_.branch, ...), custom_call_target="tpu_custom_call" | custom-call | flops 134217728 | bytes 7340032 | tf_op jit(solution)/shard_map/stage3/pallas_call | solution.py:118
  141.7 4.3 %all-to-all-start.3 = ((bf16[16,336,128]{2,1,0:T(8,128)(2,1)}), bf16[16,336,128]{2,1,0:T(8,128)(2,1)S(1)}, u32[]{:S(2)}, u32[]{:S(2)}) async-start(bf16[16,336,128]{2,1,0:T(8,128)(2,1)} %get-tuple-element.136), calls=%async_computation.3 | async-start | bytes 2752512 | tf_op jit(solution)/shard_map/all_to_all | solution.py:933
  146.0 3.3 %collective-permute-start.22 = (bf16[2,256,128]{2,1,0:T(8,128)(2,1)S(1)}, bf16[2,256,128]{2,1,0:T(8,128)(2,1)S(1)}, u32[]{:S(2)}, u32[]{:S(2)}) collective-permute-start(bf16[2,256,128]{2,1,0:T(8,128)(2,1)S(1)} %get-tuple-element.141), channel_id=1, source_target_pairs={{0,1},{1,2},{2,3},{3,4},{4,5},{5,6},{6,7},{7,8},{8,9},{9,10},{10,1... | collective-permute-start | bytes 393224 | tf_op jit(solution)/shard_map/ppermute | solution.py:944
  150.6 6.8 %near_field.7.refs_4_.refs_0_ = f32[8,256,128]{2,1,0:T(8,128)} custom-call(s32[256]{0:T(256)S(1)} %get-tuple-element.82.index_ref, bf16[8,8,256,256]{3,2,1,0:T(8,128)(2,1)} %blocks_ref.9, bf16[8,256,128]{2,1,0:T(8,128)(2,1)} %get-tuple-element.138.own_ref), custom_call_target="tpu_custom_call" | custom-call | flops 1073741824 | bytes 8388608 | tf_op jit(solution)/shard_map/near_field/pallas_call | solution.py:118
  157.4 3.5 %vectors.2.refs_0_.refs_5_ = f32[5,8,256,128]{3,2,1,0:T(8,128)} custom-call(f32[64,128]{1,0:T(8,128)S(1)} %get-tuple-element.137.refs_0_.refs_4_, f32[8,256,128]{2,1,0:T(8,128)} %bitcast.11, f32[8,256,128]{2,1,0:T(8,128)} %get-tuple-element.109.refs_6_.refs_2_, f32[8,256,128]{2,1,0:T(8,128)} %get-tuple-element.126.refs_7_.refs_3_, ...), custom_call_target="tpu_custom_call" | custom-call | flops 8388608 | bytes 6291456 | tf_op jit(solution)/shard_map/vectors/pallas_call | solution.py:118
  160.9 6.5 %all-to-all-done.3.recv = bf16[16,336,128]{2,1,0:T(8,128)(2,1)S(1)} async-done(((bf16[16,336,128]{2,1,0:T(8,128)(2,1)}), bf16[16,336,128]{2,1,0:T(8,128)(2,1)S(1)}, u32[]{:S(2)}, u32[]{:S(2)}) %all-to-all-start.3) | async-done | bytes 1376288 | tf_op jit(solution)/shard_map/all_to_all | solution.py:933
  167.5 2.2 %collective-permute-start.20 = (bf16[80,128]{1,0:T(8,128)(2,1)S(1)}, bf16[80,128]{1,0:T(8,128)(2,1)S(1)}, u32[]{:S(2)}, u32[]{:S(2)}) collective-permute-start(bf16[80,128]{1,0:T(8,128)(2,1)S(1)} %gather_sum.7.refs_1_.refs_0_), channel_id=1, source_target_pairs={{0,96},{16,112},{32,0},{48,16},{64,32},{80,48},{96,64},{112,80},{1... | collective-permute-start | bytes 61448 | tf_op jit(solution)/shard_map/ppermute | solution.py:415
  170.7 3.8 %far_field.7 = (f32[512,128]{1,0:T(8,128)S(1)}, bf16[64,256,256]{2,1,0:T(8,128)(2,1)S(1)}, f32[8,256,128]{2,1,0:T(8,128)S(1)}) custom-call(s32[256]{0:T(256)S(1)} %get-tuple-element.82.index_ref, bf16[16,336,128]{2,1,0:T(8,128)(2,1)S(1)} %all-to-all-done.3.recv, bf16[16,512,256]{2,1,0:T(8,128)(2,1)} %get-tuple-element.84.refs_0_.packed_ref, ...), custom_call_target="tpu_custom_call" | custom-call | flops 536870912 | bytes 4194304 | tf_op jit(solution)/shard_map/far_field/pallas_call | solution.py:118
  174.5 3.2 %collective-permute-start.21 = (bf16[4,80,128]{2,1,0:T(8,128)(2,1)S(1)}, bf16[4,80,128]{2,1,0:T(8,128)(2,1)S(1)}, u32[]{:S(2)}, u32[]{:S(2)}) collective-permute-start(bf16[4,80,128]{2,1,0:T(8,128)(2,1)S(1)} %stack.8.refs_9_.refs_2_), channel_id=1, source_target_pairs={{0,16},{16,0},{32,48},{48,32},{64,80},{80,64},{96,112},{112,96},{1... | collective-permute-start | bytes 245768 | tf_op jit(solution)/shard_map/ppermute | solution.py:426
  177.8 3.1 %halo_part.7 = (f32[8,256,128]{2,1,0:T(8,128)S(1)}, bf16[8,64,256]{2,1,0:T(8,128)(2,1)S(1)}, bf16[8,256,64]{2,1,0:T(8,128)(2,1)S(1)}, bf16[8,64,64]{2,1,0:T(8,12...) custom-call(s32[256]{0:T(256)S(1)} %get-tuple-element.82.index_ref, ...), custom_call_target="tpu_custom_call", output_to_operand_aliasing={{0}: (4, {})} | custom-call | flops 268435456 | bytes 2097152 | tf_op jit(solution)/shard_map/halo_part/pallas_call | solution.py:118
  180.9 2.0 stage4.1
  183.5 1.5 collective-permute-start.25
  186.2 1.3 collective-permute-done.25.refs_2_
  191.3 2.0 collective-permute-done.28.refs_2_
  194.1 2.2 %collective-permute-start.32 = (bf16[16,128]{1,0:T(8,128)(2,1)S(1)}, bf16[16,128]{1,0:T(8,128)(2,1)S(1)}, u32[]{:S(2)}, u32[]{:S(2)}) collective-permute-start(bf16[16,128]{1,0:T(8,128)(2,1)S(1)} %sum_over.3.refs_0_.refs_4_), channel_id=1, source_target_pairs={{0,96},{16,112},{32,0},{48,16},{64,32},{80,48},{96,64},{112,80},{1... | collective-permute-start | bytes 12296 | tf_op jit(solution)/shard_map/ppermute | solution.py:415
  197.1 3.2 %collective-permute-done.31.refs_2_ = bf16[16,128]{1,0:T(8,128)(2,1)S(1)} collective-permute-done((bf16[16,128]{1,0:T(8,128)(2,1)S(1)}, bf16[16,128]{1,0:T(8,128)(2,1)S(1)}, u32[]{:S(2)}, u32[]{:S(2)}) %collective-permute-start.31) | collective-permute-done | bytes 4128 | tf_op jit(solution)/shard_map/ppermute | solution.py:415
  200.4 4.8 %collective-permute-start.33 = (bf16[4,16,128]{2,1,0:T(8,128)(2,1)S(1)}, bf16[4,16,128]{2,1,0:T(8,128)(2,1)S(1)}, u32[]{:S(2)}, u32[]{:S(2)}) collective-permute-start(bf16[4,16,128]{2,1,0:T(8,128)(2,1)S(1)} %stack.9.refs_2_), channel_id=1, source_target_pairs={{0,16},{16,0},{32,48},{48,32},{64,80},{80,64},{96,112},{112,96},{1... | collective-permute-start | bytes 49160 | tf_op jit(solution)/shard_map/ppermute | solution.py:426
  206.1 1.8 last_vector.1
  (61 shorter events, 14.9 us)
Async XLA Ops:
  4.9 29.6 %all-to-all-start = ((bf16[16,336,128]{2,1,0:T(8,128)(2,1)}), bf16[16,336,128]{2,1,0:T(8,128)(2,1)S(1)}, u32[]{:S(2)}, u32[]{:S(2)}) async-start(bf16[16,336,128]{2,1,0:T(8,128)(2,1)} %get-tuple-element.81), calls=%async_computation | async-start | bytes 2752512 | tf_op jit(solution)/shard_map/all_to_all | solution.py:933
  13.5 31.5 %collective-permute-start.4 = (bf16[2,256,128]{2,1,0:T(8,128)(2,1)S(1)}, bf16[2,256,128]{2,1,0:T(8,128)(2,1)S(1)}, u32[]{:S(2)}, u32[]{:S(2)}) collective-permute-start(bf16[2,256,128]{2,1,0:T(8,128)(2,1)S(1)} %get-tuple-element.88), channel_id=1, source_target_pairs={{0,1},{1,2},{2,3},{3,4},{4,5},{5,6},{6,7},{7,8},{8,9},{9,10},{10,1... | collective-permute-start | bytes 393224 | tf_op jit(solution)/shard_map/ppermute | solution.py:944
  16.8 28.3 %collective-permute-start.5 = (bf16[2,256,128]{2,1,0:T(8,128)(2,1)S(1)}, bf16[2,256,128]{2,1,0:T(8,128)(2,1)S(1)}, u32[]{:S(2)}, u32[]{:S(2)}) collective-permute-start(bf16[2,256,128]{2,1,0:T(8,128)(2,1)S(1)} %get-tuple-element.89), channel_id=1, source_target_pairs={{1,0},{2,1},{3,2},{4,3},{5,4},{6,5},{7,6},{8,7},{9,8},{10,9},{11,1... | collective-permute-start | bytes 393224 | tf_op jit(solution)/shard_map/ppermute | solution.py:945
  34.5 8.0 %collective-permute-start.2 = (bf16[80,128]{1,0:T(8,128)(2,1)S(1)}, bf16[80,128]{1,0:T(8,128)(2,1)S(1)}, u32[]{:S(2)}, u32[]{:S(2)}) collective-permute-start(bf16[80,128]{1,0:T(8,128)(2,1)S(1)} %gather_sum.4.refs_1_.refs_0_), channel_id=1, source_target_pairs={{0,96},{16,112},{32,0},{48,16},{64,32},{80,48},{96,64},{112,80},{1... | collective-permute-start | bytes 61448 | tf_op jit(solution)/shard_map/ppermute | solution.py:415
  37.1 5.5 %collective-permute-start.1 = (bf16[80,128]{1,0:T(8,128)(2,1)S(1)}, bf16[80,128]{1,0:T(8,128)(2,1)S(1)}, u32[]{:S(2)}, u32[]{:S(2)}) collective-permute-start(bf16[80,128]{1,0:T(8,128)(2,1)S(1)} %gather_sum.4.refs_1_.refs_0_), channel_id=1, source_target_pairs={{0,64},{16,80},{32,96},{48,112},{64,0},{80,16},{96,32},{112,48},{1... | collective-permute-start | bytes 61448 | tf_op jit(solution)/shard_map/ppermute | solution.py:415
  37.6 5.0 %collective-permute-start = (bf16[80,128]{1,0:T(8,128)(2,1)S(1)}, bf16[80,128]{1,0:T(8,128)(2,1)S(1)}, u32[]{:S(2)}, u32[]{:S(2)}) collective-permute-start(bf16[80,128]{1,0:T(8,128)(2,1)S(1)} %gather_sum.4.refs_1_.refs_0_), channel_id=1, source_target_pairs={{0,32},{16,48},{32,64},{48,80},{64,96},{80,112},{96,0},{112,16},{1... | collective-permute-start | bytes 61448 | tf_op jit(solution)/shard_map/ppermute | solution.py:415
  42.6 4.6 %collective-permute-start.3 = (bf16[4,80,128]{2,1,0:T(8,128)(2,1)S(1)}, bf16[4,80,128]{2,1,0:T(8,128)(2,1)S(1)}, u32[]{:S(2)}, u32[]{:S(2)}) collective-permute-start(bf16[4,80,128]{2,1,0:T(8,128)(2,1)S(1)} %stack.5.refs_6_.refs_2_), channel_id=1, source_target_pairs={{0,16},{16,0},{32,48},{48,32},{64,80},{80,64},{96,112},{112,96},{1... | collective-permute-start | bytes 245768 | tf_op jit(solution)/shard_map/ppermute | solution.py:426
  51.8 29.2 %all-to-all-start.1 = ((bf16[16,336,128]{2,1,0:T(8,128)(2,1)}), bf16[16,336,128]{2,1,0:T(8,128)(2,1)S(1)}, u32[]{:S(2)}, u32[]{:S(2)}) async-start(bf16[16,336,128]{2,1,0:T(8,128)(2,1)} %get-tuple-element.101), calls=%async_computation.1 | async-start | bytes 2752512 | tf_op jit(solution)/shard_map/all_to_all | solution.py:933
  59.6 31.6 %collective-permute-start.10 = (bf16[2,256,128]{2,1,0:T(8,128)(2,1)S(1)}, bf16[2,256,128]{2,1,0:T(8,128)(2,1)S(1)}, u32[]{:S(2)}, u32[]{:S(2)}) collective-permute-start(bf16[2,256,128]{2,1,0:T(8,128)(2,1)S(1)} %get-tuple-element.106), channel_id=1, source_target_pairs={{0,1},{1,2},{2,3},{3,4},{4,5},{5,6},{6,7},{7,8},{8,9},{9,10},{10,1... | collective-permute-start | bytes 393224 | tf_op jit(solution)/shard_map/ppermute | solution.py:944
  62.9 28.4 %collective-permute-start.11 = (bf16[2,256,128]{2,1,0:T(8,128)(2,1)S(1)}, bf16[2,256,128]{2,1,0:T(8,128)(2,1)S(1)}, u32[]{:S(2)}, u32[]{:S(2)}) collective-permute-start(bf16[2,256,128]{2,1,0:T(8,128)(2,1)S(1)} %get-tuple-element.107), channel_id=1, source_target_pairs={{1,0},{2,1},{3,2},{4,3},{5,4},{6,5},{7,6},{8,7},{9,8},{10,9},{11,1... | collective-permute-start | bytes 393224 | tf_op jit(solution)/shard_map/ppermute | solution.py:945
  81.1 6.9 %collective-permute-start.8 = (bf16[80,128]{1,0:T(8,128)(2,1)S(1)}, bf16[80,128]{1,0:T(8,128)(2,1)S(1)}, u32[]{:S(2)}, u32[]{:S(2)}) collective-permute-start(bf16[80,128]{1,0:T(8,128)(2,1)S(1)} %gather_sum.5.refs_1_.refs_0_), channel_id=1, source_target_pairs={{0,96},{16,112},{32,0},{48,16},{64,32},{80,48},{96,64},{112,80},{1... | collective-permute-start | bytes 61448 | tf_op jit(solution)/shard_map/ppermute | solution.py:415
  83.3 4.8 %collective-permute-start.7 = (bf16[80,128]{1,0:T(8,128)(2,1)S(1)}, bf16[80,128]{1,0:T(8,128)(2,1)S(1)}, u32[]{:S(2)}, u32[]{:S(2)}) collective-permute-start(bf16[80,128]{1,0:T(8,128)(2,1)S(1)} %gather_sum.5.refs_1_.refs_0_), channel_id=1, source_target_pairs={{0,64},{16,80},{32,96},{48,112},{64,0},{80,16},{96,32},{112,48},{1... | collective-permute-start | bytes 61448 | tf_op jit(solution)/shard_map/ppermute | solution.py:415
  84.2 3.8 %collective-permute-start.6 = (bf16[80,128]{1,0:T(8,128)(2,1)S(1)}, bf16[80,128]{1,0:T(8,128)(2,1)S(1)}, u32[]{:S(2)}, u32[]{:S(2)}) collective-permute-start(bf16[80,128]{1,0:T(8,128)(2,1)S(1)} %gather_sum.5.refs_1_.refs_0_), channel_id=1, source_target_pairs={{0,32},{16,48},{32,64},{48,80},{64,96},{80,112},{96,0},{112,16},{1... | collective-permute-start | bytes 61448 | tf_op jit(solution)/shard_map/ppermute | solution.py:415
  88.1 5.7 %collective-permute-start.9 = (bf16[4,80,128]{2,1,0:T(8,128)(2,1)S(1)}, bf16[4,80,128]{2,1,0:T(8,128)(2,1)S(1)}, u32[]{:S(2)}, u32[]{:S(2)}) collective-permute-start(bf16[4,80,128]{2,1,0:T(8,128)(2,1)S(1)} %stack.6.refs_7_.refs_2_), channel_id=1, source_target_pairs={{0,16},{16,0},{32,48},{48,32},{64,80},{80,64},{96,112},{112,96},{1... | collective-permute-start | bytes 245768 | tf_op jit(solution)/shard_map/ppermute | solution.py:426
  98.5 25.7 %all-to-all-start.2 = ((bf16[16,336,128]{2,1,0:T(8,128)(2,1)}), bf16[16,336,128]{2,1,0:T(8,128)(2,1)S(1)}, u32[]{:S(2)}, u32[]{:S(2)}) async-start(bf16[16,336,128]{2,1,0:T(8,128)(2,1)} %get-tuple-element.118), calls=%async_computation.2 | async-start | bytes 2752512 | tf_op jit(solution)/shard_map/all_to_all | solution.py:933
  102.8 31.3 %collective-permute-start.16 = (bf16[2,256,128]{2,1,0:T(8,128)(2,1)S(1)}, bf16[2,256,128]{2,1,0:T(8,128)(2,1)S(1)}, u32[]{:S(2)}, u32[]{:S(2)}) collective-permute-start(bf16[2,256,128]{2,1,0:T(8,128)(2,1)S(1)} %get-tuple-element.123), channel_id=1, source_target_pairs={{0,1},{1,2},{2,3},{3,4},{4,5},{5,6},{6,7},{7,8},{8,9},{9,10},{10,1... | collective-permute-start | bytes 393224 | tf_op jit(solution)/shard_map/ppermute | solution.py:944
  106.1 28.0 %collective-permute-start.17 = (bf16[2,256,128]{2,1,0:T(8,128)(2,1)S(1)}, bf16[2,256,128]{2,1,0:T(8,128)(2,1)S(1)}, u32[]{:S(2)}, u32[]{:S(2)}) collective-permute-start(bf16[2,256,128]{2,1,0:T(8,128)(2,1)S(1)} %get-tuple-element.124), channel_id=1, source_target_pairs={{1,0},{2,1},{3,2},{4,3},{5,4},{6,5},{7,6},{8,7},{9,8},{10,9},{11,1... | collective-permute-start | bytes 393224 | tf_op jit(solution)/shard_map/ppermute | solution.py:945
  124.2 6.6 %collective-permute-start.14 = (bf16[80,128]{1,0:T(8,128)(2,1)S(1)}, bf16[80,128]{1,0:T(8,128)(2,1)S(1)}, u32[]{:S(2)}, u32[]{:S(2)}) collective-permute-start(bf16[80,128]{1,0:T(8,128)(2,1)S(1)} %gather_sum.6.refs_1_.refs_0_), channel_id=1, source_target_pairs={{0,96},{16,112},{32,0},{48,16},{64,32},{80,48},{96,64},{112,80},{1... | collective-permute-start | bytes 61448 | tf_op jit(solution)/shard_map/ppermute | solution.py:415
  126.4 4.5 %collective-permute-start.13 = (bf16[80,128]{1,0:T(8,128)(2,1)S(1)}, bf16[80,128]{1,0:T(8,128)(2,1)S(1)}, u32[]{:S(2)}, u32[]{:S(2)}) collective-permute-start(bf16[80,128]{1,0:T(8,128)(2,1)S(1)} %gather_sum.6.refs_1_.refs_0_), channel_id=1, source_target_pairs={{0,64},{16,80},{32,96},{48,112},{64,0},{80,16},{96,32},{112,48},{1... | collective-permute-start | bytes 61448 | tf_op jit(solution)/shard_map/ppermute | solution.py:415
  126.9 4.0 %collective-permute-start.12 = (bf16[80,128]{1,0:T(8,128)(2,1)S(1)}, bf16[80,128]{1,0:T(8,128)(2,1)S(1)}, u32[]{:S(2)}, u32[]{:S(2)}) collective-permute-start(bf16[80,128]{1,0:T(8,128)(2,1)S(1)} %gather_sum.6.refs_1_.refs_0_), channel_id=1, source_target_pairs={{0,32},{16,48},{32,64},{48,80},{64,96},{80,112},{96,0},{112,16},{1... | collective-permute-start | bytes 61448 | tf_op jit(solution)/shard_map/ppermute | solution.py:415
  130.9 6.0 %collective-permute-start.15 = (bf16[4,80,128]{2,1,0:T(8,128)(2,1)S(1)}, bf16[4,80,128]{2,1,0:T(8,128)(2,1)S(1)}, u32[]{:S(2)}, u32[]{:S(2)}) collective-permute-start(bf16[4,80,128]{2,1,0:T(8,128)(2,1)S(1)} %stack.7.refs_8_.refs_2_), channel_id=1, source_target_pairs={{0,16},{16,0},{32,48},{48,32},{64,80},{80,64},{96,112},{112,96},{1... | collective-permute-start | bytes 245768 | tf_op jit(solution)/shard_map/ppermute | solution.py:426
  141.7 25.7 %all-to-all-start.3 = ((bf16[16,336,128]{2,1,0:T(8,128)(2,1)}), bf16[16,336,128]{2,1,0:T(8,128)(2,1)S(1)}, u32[]{:S(2)}, u32[]{:S(2)}) async-start(bf16[16,336,128]{2,1,0:T(8,128)(2,1)} %get-tuple-element.136), calls=%async_computation.3 | async-start | bytes 2752512 | tf_op jit(solution)/shard_map/all_to_all | solution.py:933
  146.0 31.7 %collective-permute-start.22 = (bf16[2,256,128]{2,1,0:T(8,128)(2,1)S(1)}, bf16[2,256,128]{2,1,0:T(8,128)(2,1)S(1)}, u32[]{:S(2)}, u32[]{:S(2)}) collective-permute-start(bf16[2,256,128]{2,1,0:T(8,128)(2,1)S(1)} %get-tuple-element.141), channel_id=1, source_target_pairs={{0,1},{1,2},{2,3},{3,4},{4,5},{5,6},{6,7},{7,8},{8,9},{9,10},{10,1... | collective-permute-start | bytes 393224 | tf_op jit(solution)/shard_map/ppermute | solution.py:944
  149.3 28.4 %collective-permute-start.23 = (bf16[2,256,128]{2,1,0:T(8,128)(2,1)S(1)}, bf16[2,256,128]{2,1,0:T(8,128)(2,1)S(1)}, u32[]{:S(2)}, u32[]{:S(2)}) collective-permute-start(bf16[2,256,128]{2,1,0:T(8,128)(2,1)S(1)} %get-tuple-element.142), channel_id=1, source_target_pairs={{1,0},{2,1},{3,2},{4,3},{5,4},{6,5},{7,6},{8,7},{9,8},{10,9},{11,1... | collective-permute-start | bytes 393224 | tf_op jit(solution)/shard_map/ppermute | solution.py:945
  167.5 7.0 %collective-permute-start.20 = (bf16[80,128]{1,0:T(8,128)(2,1)S(1)}, bf16[80,128]{1,0:T(8,128)(2,1)S(1)}, u32[]{:S(2)}, u32[]{:S(2)}) collective-permute-start(bf16[80,128]{1,0:T(8,128)(2,1)S(1)} %gather_sum.7.refs_1_.refs_0_), channel_id=1, source_target_pairs={{0,96},{16,112},{32,0},{48,16},{64,32},{80,48},{96,64},{112,80},{1... | collective-permute-start | bytes 61448 | tf_op jit(solution)/shard_map/ppermute | solution.py:415
  169.7 4.8 %collective-permute-start.19 = (bf16[80,128]{1,0:T(8,128)(2,1)S(1)}, bf16[80,128]{1,0:T(8,128)(2,1)S(1)}, u32[]{:S(2)}, u32[]{:S(2)}) collective-permute-start(bf16[80,128]{1,0:T(8,128)(2,1)S(1)} %gather_sum.7.refs_1_.refs_0_), channel_id=1, source_target_pairs={{0,64},{16,80},{32,96},{48,112},{64,0},{80,16},{96,32},{112,48},{1... | collective-permute-start | bytes 61448 | tf_op jit(solution)/shard_map/ppermute | solution.py:415
  170.7 3.8 %collective-permute-start.18 = (bf16[80,128]{1,0:T(8,128)(2,1)S(1)}, bf16[80,128]{1,0:T(8,128)(2,1)S(1)}, u32[]{:S(2)}, u32[]{:S(2)}) collective-permute-start(bf16[80,128]{1,0:T(8,128)(2,1)S(1)} %gather_sum.7.refs_1_.refs_0_), channel_id=1, source_target_pairs={{0,32},{16,48},{32,64},{48,80},{64,96},{80,112},{96,0},{112,16},{1... | collective-permute-start | bytes 61448 | tf_op jit(solution)/shard_map/ppermute | solution.py:415
  174.5 6.4 %collective-permute-start.21 = (bf16[4,80,128]{2,1,0:T(8,128)(2,1)S(1)}, bf16[4,80,128]{2,1,0:T(8,128)(2,1)S(1)}, u32[]{:S(2)}, u32[]{:S(2)}) collective-permute-start(bf16[4,80,128]{2,1,0:T(8,128)(2,1)S(1)} %stack.8.refs_9_.refs_2_), channel_id=1, source_target_pairs={{0,16},{16,0},{32,48},{48,32},{64,80},{80,64},{96,112},{112,96},{1... | collective-permute-start | bytes 245768 | tf_op jit(solution)/shard_map/ppermute | solution.py:426
  182.9 3.3 %collective-permute-start.26 = (bf16[16,128]{1,0:T(8,128)(2,1)S(1)}, bf16[16,128]{1,0:T(8,128)(2,1)S(1)}, u32[]{:S(2)}, u32[]{:S(2)}) collective-permute-start(bf16[16,128]{1,0:T(8,128)(2,1)S(1)} %get-tuple-element.156.refs_0_), channel_id=1, source_target_pairs={{0,3},{1,0},{2,1},{3,2},{4,7},{5,4},{6,5},{7,6},{8,11},{9,8},{10,9... | collective-permute-start | bytes 12296 | tf_op jit(solution)/shard_map/ppermute | solution.py:594
  183.5 4.0 %collective-permute-start.25 = (bf16[16,128]{1,0:T(8,128)(2,1)S(1)}, bf16[16,128]{1,0:T(8,128)(2,1)S(1)}, u32[]{:S(2)}, u32[]{:S(2)}) collective-permute-start(bf16[16,128]{1,0:T(8,128)(2,1)S(1)} %get-tuple-element.156.refs_0_), channel_id=1, source_target_pairs={{0,2},{1,3},{2,0},{3,1},{4,6},{5,7},{6,4},{7,5},{8,10},{9,11},{10,... | collective-permute-start | bytes 12296 | tf_op jit(solution)/shard_map/ppermute | solution.py:594
  185.0 3.7 %collective-permute-start.24 = (bf16[16,128]{1,0:T(8,128)(2,1)S(1)}, bf16[16,128]{1,0:T(8,128)(2,1)S(1)}, u32[]{:S(2)}, u32[]{:S(2)}) collective-permute-start(bf16[16,128]{1,0:T(8,128)(2,1)S(1)} %get-tuple-element.156.refs_0_), channel_id=1, source_target_pairs={{0,1},{1,2},{2,3},{3,0},{4,5},{5,6},{6,7},{7,4},{8,9},{9,10},{10,1... | collective-permute-start | bytes 12296 | tf_op jit(solution)/shard_map/ppermute | solution.py:594
  188.7 2.5 %collective-permute-start.29 = (bf16[16,128]{1,0:T(8,128)(2,1)S(1)}, bf16[16,128]{1,0:T(8,128)(2,1)S(1)}, u32[]{:S(2)}, u32[]{:S(2)}) collective-permute-start(bf16[16,128]{1,0:T(8,128)(2,1)S(1)} %sum_over.2.refs_0_.refs_4_), channel_id=1, source_target_pairs={{0,12},{1,13},{2,14},{3,15},{4,0},{5,1},{6,2},{7,3},{8,4},{9,5},{1... | collective-permute-start | bytes 12296 | tf_op jit(solution)/shard_map/ppermute | solution.py:594
  189.3 4.0 %collective-permute-start.28 = (bf16[16,128]{1,0:T(8,128)(2,1)S(1)}, bf16[16,128]{1,0:T(8,128)(2,1)S(1)}, u32[]{:S(2)}, u32[]{:S(2)}) collective-permute-start(bf16[16,128]{1,0:T(8,128)(2,1)S(1)} %sum_over.2.refs_0_.refs_4_), channel_id=1, source_target_pairs={{0,8},{1,9},{2,10},{3,11},{4,12},{5,13},{6,14},{7,15},{8,0},{9,1},... | collective-permute-start | bytes 12296 | tf_op jit(solution)/shard_map/ppermute | solution.py:594
  190.4 3.7 %collective-permute-start.27 = (bf16[16,128]{1,0:T(8,128)(2,1)S(1)}, bf16[16,128]{1,0:T(8,128)(2,1)S(1)}, u32[]{:S(2)}, u32[]{:S(2)}) collective-permute-start(bf16[16,128]{1,0:T(8,128)(2,1)S(1)} %sum_over.2.refs_0_.refs_4_), channel_id=1, source_target_pairs={{0,4},{1,5},{2,6},{3,7},{4,8},{5,9},{6,10},{7,11},{8,12},{9,13},{1... | collective-permute-start | bytes 12296 | tf_op jit(solution)/shard_map/ppermute | solution.py:594
  194.1 3.0 %collective-permute-start.32 = (bf16[16,128]{1,0:T(8,128)(2,1)S(1)}, bf16[16,128]{1,0:T(8,128)(2,1)S(1)}, u32[]{:S(2)}, u32[]{:S(2)}) collective-permute-start(bf16[16,128]{1,0:T(8,128)(2,1)S(1)} %sum_over.3.refs_0_.refs_4_), channel_id=1, source_target_pairs={{0,96},{16,112},{32,0},{48,16},{64,32},{80,48},{96,64},{112,80},{1... | collective-permute-start | bytes 12296 | tf_op jit(solution)/shard_map/ppermute | solution.py:415
  196.3 4.0 %collective-permute-start.31 = (bf16[16,128]{1,0:T(8,128)(2,1)S(1)}, bf16[16,128]{1,0:T(8,128)(2,1)S(1)}, u32[]{:S(2)}, u32[]{:S(2)}) collective-permute-start(bf16[16,128]{1,0:T(8,128)(2,1)S(1)} %sum_over.3.refs_0_.refs_4_), channel_id=1, source_target_pairs={{0,64},{16,80},{32,96},{48,112},{64,0},{80,16},{96,32},{112,48},{1... | collective-permute-start | bytes 12296 | tf_op jit(solution)/shard_map/ppermute | solution.py:415
  196.8 3.7 %collective-permute-start.30 = (bf16[16,128]{1,0:T(8,128)(2,1)S(1)}, bf16[16,128]{1,0:T(8,128)(2,1)S(1)}, u32[]{:S(2)}, u32[]{:S(2)}) collective-permute-start(bf16[16,128]{1,0:T(8,128)(2,1)S(1)} %sum_over.3.refs_0_.refs_4_), channel_id=1, source_target_pairs={{0,32},{16,48},{32,64},{48,80},{64,96},{80,112},{96,0},{112,16},{1... | collective-permute-start | bytes 12296 | tf_op jit(solution)/shard_map/ppermute | solution.py:415
  200.4 5.6 %collective-permute-start.33 = (bf16[4,16,128]{2,1,0:T(8,128)(2,1)S(1)}, bf16[4,16,128]{2,1,0:T(8,128)(2,1)S(1)}, u32[]{:S(2)}, u32[]{:S(2)}) collective-permute-start(bf16[4,16,128]{2,1,0:T(8,128)(2,1)S(1)} %stack.9.refs_2_), channel_id=1, source_target_pairs={{0,16},{16,0},{32,48},{48,32},{64,80},{80,64},{96,112},{112,96},{1... | collective-permute-start | bytes 49160 | tf_op jit(solution)/shard_map/ppermute | solution.py:426

commit v10 on v9

--- a/solution.py
+++ b/solution.py
@@ -805,14 +805,14 @@
     take = lambda count: [refs.pop(0) for _ in range(count)]
     (state,) = take(1)
     if final:
-        branch, column, other = take(3)
+        (dots,) = take(1)
     zs = take(wanted[-1] + 1)
     _, krylov = take(2)
     if final:
         (hess_out,) = take(1)
     result, left = take(2)
     if final:
-        after, ups = take(2)
+        (after,) = take(1)
     else:
         after = state
     if not held:
@@ -850,8 +850,7 @@
     begin, run = windowed(parts, parts, fetch, work)
     begin()
     if final:
-        in_order(branch, column, other, ups)
-        grams = [row / points for row in from_branches(ups, 0)]
+        grams = [row / points for row in joined(dots[...].astype(F32))]
         after[...] = state[...]
         coefficients(STEPS, grams, state, after)
     run()
@@ -878,14 +877,10 @@
     outs = [(shape, F32, HBM)]
     args, specs = [state], [VMEM]
     if final:
-        args += products
-        specs += [SMEM, VMEM, VMEM]
-        column = products[1].shape
+        args.append(products)
+        specs.append(VMEM)
         outs.append(((STEPS + 1, STEPS, tall[2]), F32, FREE))
-        scratch += [
-            pltpu.VMEM(state.shape, F32),
-            pltpu.VMEM((2 * column[0],) + column[1:], BF16),
-        ]
+        scratch.append(pltpu.VMEM(state.shape, F32))
     args += zs[:count]
     specs += [VMEM if held else HBM] * count
     args.append(before)
@@ -966,13 +961,14 @@
         out = stage(k, points, wanted, branch, zs[0], basis, transfer, later)
         state = out["state"]
         zs = zs + [out["z"]]
-    low = 4 if inner % 4 == 0 else inner
     held = held[-STEPS:] + [out["z"]]
     krylov = vectors(state, held, [STEPS - 1], krylov, 2)[0]
-    summed = sum_over(out["send"], "inner", 1, low, krylov, AFTER)
-    summed = sum_over(summed, "inner", low, inner // low, summed, AFTER_VMEM)
-    column, other, _ = over_branches(summed, outer, summed, lambda column: None)
-    products = [branch, column, other]
+    products, last, pin = out["send"], krylov, AFTER
+    strides = [("inner", 1 << i) for i in range(inner.bit_length() - 1)]
+    strides += [("outer", 2 << i) for i in range(outer.bit_length() - 2)] + [("outer", 1)]
+    for axis, stride in strides:
+        products = sum_over(products, axis, stride, 2, last, pin)
+        last, pin = products, AFTER_VMEM
     krylov, hessenberg = vectors(state, held, [STEPS], krylov, 2, products, points)
     return krylov.reshape(STEPS + 1, *rhs.shape), hessenberg
 

time: 209 us -> 214 us (1.024)
  waiting for transfers between devices: 32.3 us -> 37.2 us
    ppermute x6 -> x7, waiting for transfers between devices: 5.44 us -> 14.6 us  [sum_over(): lax.ppermute(dots, axis, [(i, moved(i, j)) for i in range(size)])]
    ppermute x6 -> x7, starting transfers between devices: 4.54 us -> 11.8 us  [sum_over(): lax.ppermute(dots, axis, [(i, moved(i, j)) for i in range(size)])]
    ppermute x5 -> x4, starting transfers between devices: 16.8 us -> 12.1 us  [over_branches(): other = lax.ppermute(column, 'outer', [(o, o ^ 1) for o in range(outer)])]
    ppermute x15 -> x12, waiting for transfers between devices: 3.56 us -> 0.14 us  [over_branches(): lax.ppermute(summed, 'outer', shift)]
    ppermute x15 -> x12, starting transfers between devices: 15.8 us -> 12.8 us  [over_branches(): lax.ppermute(summed, 'outer', shift)]
    pallas_call x33 -> x37, Pallas kernels: 94.1 us -> 94.1 us  [call(): pl.pallas_call(kernel, in_specs=list(in_specs), out_specs=[spec for _, _,...]
  transfers between devices with their start and end apart: 38 -> 35, of which waited for: 12 -> 10; matrix products, arithmetic and copies ran while one was open for 0% -> 0% of each run, Pallas kernels for 35% -> 34%
where the time goes in v10:
time: 214 us; the launch traced here: 213 us
  Pallas kernels  94.1 us (44%)
  starting transfers between devices  80.1 us (37%)
  waiting for transfers between devices  37.2 us (17%)
    pallas_call x37, Pallas kernels, call(): pl.pallas_call(kernel, in_specs=list(in_specs), out_specs=[spec for _, _,...  94.1 us
    all_to_all x4, starting transfers between devices, exchange(): return lax.all_to_all(array, axis, split_axis=0, concat_axis=0, tiled=True)  25.2 us
    all_to_all x4, waiting for transfers between devices, exchange(): return lax.all_to_all(array, axis, split_axis=0, concat_axis=0, tiled=True)  22.4 us
    ppermute x7, waiting for transfers between devices, sum_over(): lax.ppermute(dots, axis, [(i, moved(i, j)) for i in range(size)])  14.6 us
    ppermute x4, starting transfers between devices, shards(): before = lax.ppermute(out['high'], 'inner', up_pairs)  13.1 us
    ppermute x12, starting transfers between devices, over_branches(): lax.ppermute(summed, 'outer', shift)  12.8 us
    ppermute x4, starting transfers between devices, over_branches(): other = lax.ppermute(column, 'outer', [(o, o ^ 1) for o in range(outer)])  12.1 us
    ppermute x7, starting transfers between devices, sum_over(): lax.ppermute(dots, axis, [(i, moved(i, j)) for i in range(size)])  11.8 us
  transfers between devices with their start and end apart: 35, of which 10 were waited for; matrix products, arithmetic and copies ran while one was open for 0% of the time, Pallas kernels for 34%

profile of v10, /device:TPU:1, one launch (start us, length us, event | category | flops | bytes accessed | tf_op | source)
XLA Modules:
  0.0 212.6 jit_solution(17960321649245984409)
XLA Ops:
  0.6 4.3 %stage0.1 = (f32[64,128]{1,0:T(8,128)S(1)}, bf16[16,336,128]{2,1,0:T(8,128)(2,1)}, bf16[8,256,128]{2,1,0:T(8,128)(2,1)}, bf16[2,256,128]{2,1,0:T(8,128)(2,1)S(1)}, bf16[2,256,128]{2,1,0:T(8,128)(2,1)S(1)}) custom-call(s32[4,16]{1,0:T(4,128)} %bitcast.13, s32[1]{0:T(128)} %bitcast.2.refs_1_.branch, f32[8,256,128]{2,1,0:T(8,128)} %bitcast.7, ...), custom_call_target="tpu_custom_call" | custom-call | flops 134217728 | bytes 4194304 | tf_op jit(solution)/shard_map/stage0/pallas_call | solution.py:118
  4.9 8.6 %all-to-all-start = ((bf16[16,336,128]{2,1,0:T(8,128)(2,1)}), bf16[16,336,128]{2,1,0:T(8,128)(2,1)S(1)}, u32[]{:S(2)}, u32[]{:S(2)}) async-start(bf16[16,336,128]{2,1,0:T(8,128)(2,1)} %get-tuple-element.81), calls=%async_computation | async-start | bytes 2752512 | tf_op jit(solution)/shard_map/all_to_all | solution.py:928
  13.5 3.3 %collective-permute-start.4 = (bf16[2,256,128]{2,1,0:T(8,128)(2,1)S(1)}, bf16[2,256,128]{2,1,0:T(8,128)(2,1)S(1)}, u32[]{:S(2)}, u32[]{:S(2)}) collective-permute-start(bf16[2,256,128]{2,1,0:T(8,128)(2,1)S(1)} %get-tuple-element.88), channel_id=1, source_target_pairs={{0,1},{1,2},{2,3},{3,4},{4,5},{5,6},{6,7},{7,8},{8,9},{9,10},{10,1... | collective-permute-start | bytes 393224 | tf_op jit(solution)/shard_map/ppermute | solution.py:939
  16.8 1.3 collective-permute-start.5
  18.1 9.6 %pack.1 = (bf16[16,512,256]{2,1,0:T(8,128)(2,1)}, s32[256]{0:T(256)S(1)}, bf16[8,256,64]{2,1,0:T(8,128)(2,1)}, bf16[64,512]{1,0:T(8,128)(2,1)}, bf16[64,512]{1,0:T(8,128)(2,1)}) custom-call(s32[1]{0:T(128)} %bitcast.2.refs_1_.branch, s32[8,48]{1,0:T(8,128)} %mask_ref.1, s32[8,48]{1,0:T(8,128)} %slot_ref.1, s32[8,8]{1,0:T(8,128)} %index_ref.1, ...), custom_call_target="tpu_custom_call" | custom-call | bytes 10485760 | tf_op jit(solution)/shard_map/pack/pallas_call | solution.py:118
  27.7 6.7 %near_field.4.refs_0_ = f32[8,256,128]{2,1,0:T(8,128)} custom-call(s32[256]{0:T(256)S(1)} %get-tuple-element.82.index_ref, bf16[8,8,256,256]{3,2,1,0:T(8,128)(2,1)} %blocks_ref.9, bf16[8,256,128]{2,1,0:T(8,128)(2,1)} %get-tuple-element.83.own_ref, bf16[16,512,256]{2,1,0:T(8,128)(2,1)} %get-tuple-element.84.refs_0_.packed_ref), custom_call_target="tpu_custom_call" | custom-call | flops 1073741824 | bytes 8388608 | tf_op jit(solution)/shard_map/near_field/pallas_call | solution.py:118
  34.5 2.5 %collective-permute-start.2 = (bf16[80,128]{1,0:T(8,128)(2,1)S(1)}, bf16[80,128]{1,0:T(8,128)(2,1)S(1)}, u32[]{:S(2)}, u32[]{:S(2)}) collective-permute-start(bf16[80,128]{1,0:T(8,128)(2,1)S(1)} %gather_sum.4.refs_1_.refs_0_), channel_id=1, source_target_pairs={{0,96},{16,112},{32,0},{48,16},{64,32},{80,48},{96,64},{112,80},{1... | collective-permute-start | bytes 61448 | tf_op jit(solution)/shard_map/ppermute | solution.py:415
  38.2 4.3 %far_field.4 = (f32[512,128]{1,0:T(8,128)S(1)}, bf16[64,256,256]{2,1,0:T(8,128)(2,1)S(1)}, f32[8,256,128]{2,1,0:T(8,128)S(1)}) custom-call(s32[256]{0:T(256)S(1)} %get-tuple-element.82.index_ref, bf16[16,336,128]{2,1,0:T(8,128)(2,1)S(1)} %all-to-all-done.recv, bf16[16,512,256]{2,1,0:T(8,128)(2,1)} %get-tuple-element.84.refs_0_.packed_ref, ...), custom_call_target="tpu_custom_call" | custom-call | flops 536870912 | bytes 4194304 | tf_op jit(solution)/shard_map/far_field/pallas_call | solution.py:118
  42.5 2.5 %collective-permute-start.3 = (bf16[4,80,128]{2,1,0:T(8,128)(2,1)S(1)}, bf16[4,80,128]{2,1,0:T(8,128)(2,1)S(1)}, u32[]{:S(2)}, u32[]{:S(2)}) collective-permute-start(bf16[4,80,128]{2,1,0:T(8,128)(2,1)S(1)} %stack.4.refs_6_.refs_2_), channel_id=1, source_target_pairs={{0,16},{16,0},{32,48},{48,32},{64,80},{80,64},{96,112},{112,96},{1... | collective-permute-start | bytes 245768 | tf_op jit(solution)/shard_map/ppermute | solution.py:426
  45.0 2.2 %halo_part.4 = (f32[8,256,128]{2,1,0:T(8,128)S(1)}, bf16[8,64,256]{2,1,0:T(8,128)(2,1)S(1)}, bf16[8,256,64]{2,1,0:T(8,128)(2,1)S(1)}, bf16[8,64,64]{2,1,0:T(8,12...) custom-call(s32[256]{0:T(256)S(1)} %get-tuple-element.82.index_ref, ...), custom_call_target="tpu_custom_call", output_to_operand_aliasing={{0}: (4, {})} | custom-call | flops 268435456 | bytes 2097152 | tf_op jit(solution)/shard_map/halo_part/pallas_call | solution.py:118
  47.2 4.6 %stage1.1 = (f32[8,256,128]{2,1,0:T(8,128)}, f32[64,128]{1,0:T(8,128)S(1)}, bf16[16,336,128]{2,1,0:T(8,128)(2,1)}, bf16[8,256,128]{2,1,0:T(8,128)(2,1)}, bf16[2,...) custom-call(s32[4,16]{1,0:T(4,128)} %bitcast.14, s32[1]{0:T(128)} %bitcast.2.refs_1_.branch, ...), custom_call_target="tpu_custom_call" | custom-call | flops 134217728 | bytes 5242880 | tf_op jit(solution)/shard_map/stage1/pallas_call | solution.py:118
  51.8 7.8 %all-to-all-start.1 = ((bf16[16,336,128]{2,1,0:T(8,128)(2,1)}), bf16[16,336,128]{2,1,0:T(8,128)(2,1)S(1)}, u32[]{:S(2)}, u32[]{:S(2)}) async-start(bf16[16,336,128]{2,1,0:T(8,128)(2,1)} %get-tuple-element.101), calls=%async_computation.1 | async-start | bytes 2752512 | tf_op jit(solution)/shard_map/all_to_all | solution.py:928
  59.6 3.3 %collective-permute-start.10 = (bf16[2,256,128]{2,1,0:T(8,128)(2,1)S(1)}, bf16[2,256,128]{2,1,0:T(8,128)(2,1)S(1)}, u32[]{:S(2)}, u32[]{:S(2)}) collective-permute-start(bf16[2,256,128]{2,1,0:T(8,128)(2,1)S(1)} %get-tuple-element.106), channel_id=1, source_target_pairs={{0,1},{1,2},{2,3},{3,4},{4,5},{5,6},{6,7},{7,8},{8,9},{9,10},{10,1... | collective-permute-start | bytes 393224 | tf_op jit(solution)/shard_map/ppermute | solution.py:939
  64.2 6.7 %near_field.5._.refs_0_ = f32[8,256,128]{2,1,0:T(8,128)} custom-call(s32[256]{0:T(256)S(1)} %get-tuple-element.82.index_ref, bf16[8,8,256,256]{3,2,1,0:T(8,128)(2,1)} %blocks_ref.9, bf16[8,256,128]{2,1,0:T(8,128)(2,1)} %get-tuple-element.102.own_ref), custom_call_target="tpu_custom_call" | custom-call | flops 1073741824 | bytes 8388608 | tf_op jit(solution)/shard_map/near_field/pallas_call | solution.py:118
  71.0 4.2 %choose.1.refs_0_.blocks_ref = bf16[64,256,256]{2,1,0:T(8,128)(2,1)} custom-call(s32[256]{0:T(256)S(1)} %get-tuple-element.82.index_ref, bf16[8,8,256,256]{3,2,1,0:T(8,128)(2,1)} %blocks_ref.9, f32[8,256,128]{2,1,0:T(8,128)} %near_field.5._.refs_0_), custom_call_target="tpu_custom_call" | custom-call | bytes 5242880 | tf_op jit(solution)/shard_map/choose/pallas_call | solution.py:118
  75.1 5.9 %all-to-all-done.1.recv = bf16[16,336,128]{2,1,0:T(8,128)(2,1)S(1)} async-done(((bf16[16,336,128]{2,1,0:T(8,128)(2,1)}), bf16[16,336,128]{2,1,0:T(8,128)(2,1)S(1)}, u32[]{:S(2)}, u32[]{:S(2)}) %all-to-all-start.1) | async-done | bytes 1376288 | tf_op jit(solution)/shard_map/all_to_all | solution.py:928
  81.1 1.9 collective-permute-start.8
  84.2 3.8 %far_field.5 = (f32[512,128]{1,0:T(8,128)S(1)}, bf16[64,256,256]{2,1,0:T(8,128)(2,1)S(1)}, f32[8,256,128]{2,1,0:T(8,128)S(1)}) custom-call(s32[256]{0:T(256)S(1)} %get-tuple-element.82.index_ref, bf16[16,336,128]{2,1,0:T(8,128)(2,1)S(1)} %all-to-all-done.1.recv, bf16[16,512,256]{2,1,0:T(8,128)(2,1)} %get-tuple-element.84.refs_0_.packed_ref, ...), custom_call_target="tpu_custom_call" | custom-call | flops 536870912 | bytes 4194304 | tf_op jit(solution)/shard_map/far_field/pallas_call | solution.py:118
  88.1 3.2 %collective-permute-start.9 = (bf16[4,80,128]{2,1,0:T(8,128)(2,1)S(1)}, bf16[4,80,128]{2,1,0:T(8,128)(2,1)S(1)}, u32[]{:S(2)}, u32[]{:S(2)}) collective-permute-start(bf16[4,80,128]{2,1,0:T(8,128)(2,1)S(1)} %stack.5.refs_7_.refs_2_), channel_id=1, source_target_pairs={{0,16},{16,0},{32,48},{48,32},{64,80},{80,64},{96,112},{112,96},{1... | collective-permute-start | bytes 245768 | tf_op jit(solution)/shard_map/ppermute | solution.py:426
  91.3 2.5 %halo_part.5 = (f32[8,256,128]{2,1,0:T(8,128)S(1)}, bf16[8,64,256]{2,1,0:T(8,128)(2,1)S(1)}, bf16[8,256,64]{2,1,0:T(8,128)(2,1)S(1)}, bf16[8,64,64]{2,1,0:T(8,12...) custom-call(s32[256]{0:T(256)S(1)} %get-tuple-element.82.index_ref, ...), custom_call_target="tpu_custom_call", output_to_operand_aliasing={{0}: (4, {})} | custom-call | flops 268435456 | bytes 2097152 | tf_op jit(solution)/shard_map/halo_part/pallas_call | solution.py:118
  93.7 4.7 %stage2.1 = (f32[8,256,128]{2,1,0:T(8,128)}, f32[64,128]{1,0:T(8,128)S(1)}, bf16[16,336,128]{2,1,0:T(8,128)(2,1)}, bf16[8,256,128]{2,1,0:T(8,128)(2,1)}, bf16[2,...) custom-call(s32[4,16]{1,0:T(4,128)} %bitcast.15, s32[1]{0:T(128)} %bitcast.2.refs_1_.branch, ...), custom_call_target="tpu_custom_call" | custom-call | flops 134217728 | bytes 6291456 | tf_op jit(solution)/shard_map/stage2/pallas_call | solution.py:118
  98.4 4.3 %all-to-all-start.2 = ((bf16[16,336,128]{2,1,0:T(8,128)(2,1)}), bf16[16,336,128]{2,1,0:T(8,128)(2,1)S(1)}, u32[]{:S(2)}, u32[]{:S(2)}) async-start(bf16[16,336,128]{2,1,0:T(8,128)(2,1)} %get-tuple-element.118), calls=%async_computation.2 | async-start | bytes 2752512 | tf_op jit(solution)/shard_map/all_to_all | solution.py:928
  102.8 3.3 %collective-permute-start.16 = (bf16[2,256,128]{2,1,0:T(8,128)(2,1)S(1)}, bf16[2,256,128]{2,1,0:T(8,128)(2,1)S(1)}, u32[]{:S(2)}, u32[]{:S(2)}) collective-permute-start(bf16[2,256,128]{2,1,0:T(8,128)(2,1)S(1)} %get-tuple-element.123), channel_id=1, source_target_pairs={{0,1},{1,2},{2,3},{3,4},{4,5},{5,6},{6,7},{7,8},{8,9},{9,10},{10,1... | collective-permute-start | bytes 393224 | tf_op jit(solution)/shard_map/ppermute | solution.py:939
  107.3 6.7 %near_field.6.refs_0_ = f32[8,256,128]{2,1,0:T(8,128)} custom-call(s32[256]{0:T(256)S(1)} %get-tuple-element.82.index_ref, bf16[8,8,256,256]{3,2,1,0:T(8,128)(2,1)} %blocks_ref.9, bf16[8,256,128]{2,1,0:T(8,128)(2,1)} %get-tuple-element.119.own_ref), custom_call_target="tpu_custom_call" | custom-call | flops 1073741824 | bytes 8388608 | tf_op jit(solution)/shard_map/near_field/pallas_call | solution.py:118
  114.1 10.1 %all-to-all-done.2.recv = bf16[16,336,128]{2,1,0:T(8,128)(2,1)S(1)} async-done(((bf16[16,336,128]{2,1,0:T(8,128)(2,1)}), bf16[16,336,128]{2,1,0:T(8,128)(2,1)S(1)}, u32[]{:S(2)}, u32[]{:S(2)}) %all-to-all-start.2) | async-done | bytes 1376288 | tf_op jit(solution)/shard_map/all_to_all | solution.py:928
  124.2 1.9 collective-permute-start.14
  127.0 3.8 %far_field.6 = (f32[512,128]{1,0:T(8,128)S(1)}, bf16[64,256,256]{2,1,0:T(8,128)(2,1)S(1)}, f32[8,256,128]{2,1,0:T(8,128)S(1)}) custom-call(s32[256]{0:T(256)S(1)} %get-tuple-element.82.index_ref, bf16[16,336,128]{2,1,0:T(8,128)(2,1)S(1)} %all-to-all-done.2.recv, bf16[16,512,256]{2,1,0:T(8,128)(2,1)} %get-tuple-element.84.refs_0_.packed_ref, ...), custom_call_target="tpu_custom_call" | custom-call | flops 536870912 | bytes 4194304 | tf_op jit(solution)/shard_map/far_field/pallas_call | solution.py:118
  130.8 3.2 %collective-permute-start.15 = (bf16[4,80,128]{2,1,0:T(8,128)(2,1)S(1)}, bf16[4,80,128]{2,1,0:T(8,128)(2,1)S(1)}, u32[]{:S(2)}, u32[]{:S(2)}) collective-permute-start(bf16[4,80,128]{2,1,0:T(8,128)(2,1)S(1)} %stack.6.refs_8_.refs_2_), channel_id=1, source_target_pairs={{0,16},{16,0},{32,48},{48,32},{64,80},{80,64},{96,112},{112,96},{1... | collective-permute-start | bytes 245768 | tf_op jit(solution)/shard_map/ppermute | solution.py:426
  134.0 2.8 %halo_part.6 = (f32[8,256,128]{2,1,0:T(8,128)S(1)}, bf16[8,64,256]{2,1,0:T(8,128)(2,1)S(1)}, bf16[8,256,64]{2,1,0:T(8,128)(2,1)S(1)}, bf16[8,64,64]{2,1,0:T(8,12...) custom-call(s32[256]{0:T(256)S(1)} %get-tuple-element.82.index_ref, ...), custom_call_target="tpu_custom_call", output_to_operand_aliasing={{0}: (4, {})} | custom-call | flops 268435456 | bytes 2097152 | tf_op jit(solution)/shard_map/halo_part/pallas_call | solution.py:118
  136.8 4.8 %stage3.1 = (f32[8,256,128]{2,1,0:T(8,128)}, f32[64,128]{1,0:T(8,128)S(1)}, bf16[16,336,128]{2,1,0:T(8,128)(2,1)}, bf16[8,256,128]{2,1,0:T(8,128)(2,1)}, bf16[2,...) custom-call(s32[4,16]{1,0:T(4,128)} %bitcast.16, s32[1]{0:T(128)} %bitcast.2.refs_1_.branch, ...), custom_call_target="tpu_custom_call" | custom-call | flops 134217728 | bytes 7340032 | tf_op jit(solution)/shard_map/stage3/pallas_call | solution.py:118
  141.6 4.4 %all-to-all-start.3 = ((bf16[16,336,128]{2,1,0:T(8,128)(2,1)}), bf16[16,336,128]{2,1,0:T(8,128)(2,1)S(1)}, u32[]{:S(2)}, u32[]{:S(2)}) async-start(bf16[16,336,128]{2,1,0:T(8,128)(2,1)} %get-tuple-element.136), calls=%async_computation.3 | async-start | bytes 2752512 | tf_op jit(solution)/shard_map/all_to_all | solution.py:928
  146.0 3.3 %collective-permute-start.22 = (bf16[2,256,128]{2,1,0:T(8,128)(2,1)S(1)}, bf16[2,256,128]{2,1,0:T(8,128)(2,1)S(1)}, u32[]{:S(2)}, u32[]{:S(2)}) collective-permute-start(bf16[2,256,128]{2,1,0:T(8,128)(2,1)S(1)} %get-tuple-element.141), channel_id=1, source_target_pairs={{0,1},{1,2},{2,3},{3,4},{4,5},{5,6},{6,7},{7,8},{8,9},{9,10},{10,1... | collective-permute-start | bytes 393224 | tf_op jit(solution)/shard_map/ppermute | solution.py:939
  150.6 6.7 %near_field.7.refs_4_.refs_0_ = f32[8,256,128]{2,1,0:T(8,128)} custom-call(s32[256]{0:T(256)S(1)} %get-tuple-element.82.index_ref, bf16[8,8,256,256]{3,2,1,0:T(8,128)(2,1)} %blocks_ref.9, bf16[8,256,128]{2,1,0:T(8,128)(2,1)} %get-tuple-element.138.own_ref), custom_call_target="tpu_custom_call" | custom-call | flops 1073741824 | bytes 8388608 | tf_op jit(solution)/shard_map/near_field/pallas_call | solution.py:118
  157.3 3.5 %vectors.2.refs_0_.refs_5_ = f32[5,8,256,128]{3,2,1,0:T(8,128)} custom-call(f32[64,128]{1,0:T(8,128)S(1)} %get-tuple-element.137.refs_0_.refs_4_, f32[8,256,128]{2,1,0:T(8,128)} %bitcast.11, f32[8,256,128]{2,1,0:T(8,128)} %get-tuple-element.109.refs_6_.refs_2_, f32[8,256,128]{2,1,0:T(8,128)} %get-tuple-element.126.refs_7_.refs_3_, ...), custom_call_target="tpu_custom_call" | custom-call | flops 8388608 | bytes 6291456 | tf_op jit(solution)/shard_map/vectors/pallas_call | solution.py:118
  160.9 6.5 %all-to-all-done.3.recv = bf16[16,336,128]{2,1,0:T(8,128)(2,1)S(1)} async-done(((bf16[16,336,128]{2,1,0:T(8,128)(2,1)}), bf16[16,336,128]{2,1,0:T(8,128)(2,1)S(1)}, u32[]{:S(2)}, u32[]{:S(2)}) %all-to-all-start.3) | async-done | bytes 1376288 | tf_op jit(solution)/shard_map/all_to_all | solution.py:928
  167.4 2.0 collective-permute-start.20
  170.7 3.8 %far_field.7 = (f32[512,128]{1,0:T(8,128)S(1)}, bf16[64,256,256]{2,1,0:T(8,128)(2,1)S(1)}, f32[8,256,128]{2,1,0:T(8,128)S(1)}) custom-call(s32[256]{0:T(256)S(1)} %get-tuple-element.82.index_ref, bf16[16,336,128]{2,1,0:T(8,128)(2,1)S(1)} %all-to-all-done.3.recv, bf16[16,512,256]{2,1,0:T(8,128)(2,1)} %get-tuple-element.84.refs_0_.packed_ref, ...), custom_call_target="tpu_custom_call" | custom-call | flops 536870912 | bytes 4194304 | tf_op jit(solution)/shard_map/far_field/pallas_call | solution.py:118
  174.5 3.2 %collective-permute-start.21 = (bf16[4,80,128]{2,1,0:T(8,128)(2,1)S(1)}, bf16[4,80,128]{2,1,0:T(8,128)(2,1)S(1)}, u32[]{:S(2)}, u32[]{:S(2)}) collective-permute-start(bf16[4,80,128]{2,1,0:T(8,128)(2,1)S(1)} %stack.7.refs_9_.refs_2_), channel_id=1, source_target_pairs={{0,16},{16,0},{32,48},{48,32},{64,80},{80,64},{96,112},{112,96},{1... | collective-permute-start | bytes 245768 | tf_op jit(solution)/shard_map/ppermute | solution.py:426
  177.7 3.1 %halo_part.7 = (f32[8,256,128]{2,1,0:T(8,128)S(1)}, bf16[8,64,256]{2,1,0:T(8,128)(2,1)S(1)}, bf16[8,256,64]{2,1,0:T(8,128)(2,1)S(1)}, bf16[8,64,64]{2,1,0:T(8,12...) custom-call(s32[256]{0:T(256)S(1)} %get-tuple-element.82.index_ref, ...), custom_call_target="tpu_custom_call", output_to_operand_aliasing={{0}: (4, {})} | custom-call | flops 268435456 | bytes 2097152 | tf_op jit(solution)/shard_map/halo_part/pallas_call | solution.py:118
  180.9 2.0 stage4.1
  185.9 3.6 %collective-permute-done.25.refs_1_ = bf16[16,128]{1,0:T(8,128)(2,1)S(1)} collective-permute-done((bf16[16,128]{1,0:T(8,128)(2,1)S(1)}, bf16[16,128]{1,0:T(8,128)(2,1)S(1)}, u32[]{:S(2)}, u32[]{:S(2)}) %collective-permute-start.25) | collective-permute-done | bytes 4128 | tf_op jit(solution)/shard_map/ppermute | solution.py:594
  189.6 2.4 %collective-permute-done.26.refs_1_ = bf16[16,128]{1,0:T(8,128)(2,1)S(1)} collective-permute-done((bf16[16,128]{1,0:T(8,128)(2,1)S(1)}, bf16[16,128]{1,0:T(8,128)(2,1)S(1)}, u32[]{:S(2)}, u32[]{:S(2)}) %collective-permute-start.26) | collective-permute-done | bytes 4128 | tf_op jit(solution)/shard_map/ppermute | solution.py:594
  193.0 3.1 %collective-permute-done.27.refs_1_ = bf16[16,128]{1,0:T(8,128)(2,1)S(1)} collective-permute-done((bf16[16,128]{1,0:T(8,128)(2,1)S(1)}, bf16[16,128]{1,0:T(8,128)(2,1)S(1)}, u32[]{:S(2)}, u32[]{:S(2)}) %collective-permute-start.27) | collective-permute-done | bytes 4128 | tf_op jit(solution)/shard_map/ppermute | solution.py:594
  197.2 1.5 collective-permute-done.28.refs_1_
  198.7 2.0 collective-permute-start.29
  200.7 2.1 collective-permute-done.29.refs_1_
  202.8 7.0 %collective-permute-start.30 = (bf16[16,128]{1,0:T(8,128)(2,1)S(1)}, bf16[16,128]{1,0:T(8,128)(2,1)S(1)}, u32[]{:S(2)}, u32[]{:S(2)}) collective-permute-start(bf16[16,128]{1,0:T(8,128)(2,1)S(1)} %sum_over.12.refs_0_.refs_2_), channel_id=1, source_target_pairs={{0,16},{16,0},{32,48},{48,32},{64,80},{80,64},{96,112},{112,96},{1... | collective-permute-start | bytes 12296 | tf_op jit(solution)/shard_map/ppermute | solution.py:594
  210.6 1.8 last_vector.1
  (59 shorter events, 14.8 us)
Async XLA Ops:
  4.9 29.5 %all-to-all-start = ((bf16[16,336,128]{2,1,0:T(8,128)(2,1)}), bf16[16,336,128]{2,1,0:T(8,128)(2,1)S(1)}, u32[]{:S(2)}, u32[]{:S(2)}) async-start(bf16[16,336,128]{2,1,0:T(8,128)(2,1)} %get-tuple-element.81), calls=%async_computation | async-start | bytes 2752512 | tf_op jit(solution)/shard_map/all_to_all | solution.py:928
  13.5 31.5 %collective-permute-start.4 = (bf16[2,256,128]{2,1,0:T(8,128)(2,1)S(1)}, bf16[2,256,128]{2,1,0:T(8,128)(2,1)S(1)}, u32[]{:S(2)}, u32[]{:S(2)}) collective-permute-start(bf16[2,256,128]{2,1,0:T(8,128)(2,1)S(1)} %get-tuple-element.88), channel_id=1, source_target_pairs={{0,1},{1,2},{2,3},{3,4},{4,5},{5,6},{6,7},{7,8},{8,9},{9,10},{10,1... | collective-permute-start | bytes 393224 | tf_op jit(solution)/shard_map/ppermute | solution.py:939
  16.8 28.2 %collective-permute-start.5 = (bf16[2,256,128]{2,1,0:T(8,128)(2,1)S(1)}, bf16[2,256,128]{2,1,0:T(8,128)(2,1)S(1)}, u32[]{:S(2)}, u32[]{:S(2)}) collective-permute-start(bf16[2,256,128]{2,1,0:T(8,128)(2,1)S(1)} %get-tuple-element.89), channel_id=1, source_target_pairs={{1,0},{2,1},{3,2},{4,3},{5,4},{6,5},{7,6},{8,7},{9,8},{10,9},{11,1... | collective-permute-start | bytes 393224 | tf_op jit(solution)/shard_map/ppermute | solution.py:940
  34.5 8.0 %collective-permute-start.2 = (bf16[80,128]{1,0:T(8,128)(2,1)S(1)}, bf16[80,128]{1,0:T(8,128)(2,1)S(1)}, u32[]{:S(2)}, u32[]{:S(2)}) collective-permute-start(bf16[80,128]{1,0:T(8,128)(2,1)S(1)} %gather_sum.4.refs_1_.refs_0_), channel_id=1, source_target_pairs={{0,96},{16,112},{32,0},{48,16},{64,32},{80,48},{96,64},{112,80},{1... | collective-permute-start | bytes 61448 | tf_op jit(solution)/shard_map/ppermute | solution.py:415
  37.0 5.5 %collective-permute-start.1 = (bf16[80,128]{1,0:T(8,128)(2,1)S(1)}, bf16[80,128]{1,0:T(8,128)(2,1)S(1)}, u32[]{:S(2)}, u32[]{:S(2)}) collective-permute-start(bf16[80,128]{1,0:T(8,128)(2,1)S(1)} %gather_sum.4.refs_1_.refs_0_), channel_id=1, source_target_pairs={{0,64},{16,80},{32,96},{48,112},{64,0},{80,16},{96,32},{112,48},{1... | collective-permute-start | bytes 61448 | tf_op jit(solution)/shard_map/ppermute | solution.py:415
  37.6 5.0 %collective-permute-start = (bf16[80,128]{1,0:T(8,128)(2,1)S(1)}, bf16[80,128]{1,0:T(8,128)(2,1)S(1)}, u32[]{:S(2)}, u32[]{:S(2)}) collective-permute-start(bf16[80,128]{1,0:T(8,128)(2,1)S(1)} %gather_sum.4.refs_1_.refs_0_), channel_id=1, source_target_pairs={{0,32},{16,48},{32,64},{48,80},{64,96},{80,112},{96,0},{112,16},{1... | collective-permute-start | bytes 61448 | tf_op jit(solution)/shard_map/ppermute | solution.py:415
  42.5 4.7 %collective-permute-start.3 = (bf16[4,80,128]{2,1,0:T(8,128)(2,1)S(1)}, bf16[4,80,128]{2,1,0:T(8,128)(2,1)S(1)}, u32[]{:S(2)}, u32[]{:S(2)}) collective-permute-start(bf16[4,80,128]{2,1,0:T(8,128)(2,1)S(1)} %stack.4.refs_6_.refs_2_), channel_id=1, source_target_pairs={{0,16},{16,0},{32,48},{48,32},{64,80},{80,64},{96,112},{112,96},{1... | collective-permute-start | bytes 245768 | tf_op jit(solution)/shard_map/ppermute | solution.py:426
  51.8 29.2 %all-to-all-start.1 = ((bf16[16,336,128]{2,1,0:T(8,128)(2,1)}), bf16[16,336,128]{2,1,0:T(8,128)(2,1)S(1)}, u32[]{:S(2)}, u32[]{:S(2)}) async-start(bf16[16,336,128]{2,1,0:T(8,128)(2,1)} %get-tuple-element.101), calls=%async_computation.1 | async-start | bytes 2752512 | tf_op jit(solution)/shard_map/all_to_all | solution.py:928
  59.6 31.6 %collective-permute-start.10 = (bf16[2,256,128]{2,1,0:T(8,128)(2,1)S(1)}, bf16[2,256,128]{2,1,0:T(8,128)(2,1)S(1)}, u32[]{:S(2)}, u32[]{:S(2)}) collective-permute-start(bf16[2,256,128]{2,1,0:T(8,128)(2,1)S(1)} %get-tuple-element.106), channel_id=1, source_target_pairs={{0,1},{1,2},{2,3},{3,4},{4,5},{5,6},{6,7},{7,8},{8,9},{9,10},{10,1... | collective-permute-start | bytes 393224 | tf_op jit(solution)/shard_map/ppermute | solution.py:939
  62.9 28.3 %collective-permute-start.11 = (bf16[2,256,128]{2,1,0:T(8,128)(2,1)S(1)}, bf16[2,256,128]{2,1,0:T(8,128)(2,1)S(1)}, u32[]{:S(2)}, u32[]{:S(2)}) collective-permute-start(bf16[2,256,128]{2,1,0:T(8,128)(2,1)S(1)} %get-tuple-element.107), channel_id=1, source_target_pairs={{1,0},{2,1},{3,2},{4,3},{5,4},{6,5},{7,6},{8,7},{9,8},{10,9},{11,1... | collective-permute-start | bytes 393224 | tf_op jit(solution)/shard_map/ppermute | solution.py:940
  81.1 6.9 %collective-permute-start.8 = (bf16[80,128]{1,0:T(8,128)(2,1)S(1)}, bf16[80,128]{1,0:T(8,128)(2,1)S(1)}, u32[]{:S(2)}, u32[]{:S(2)}) collective-permute-start(bf16[80,128]{1,0:T(8,128)(2,1)S(1)} %gather_sum.5.refs_1_.refs_0_), channel_id=1, source_target_pairs={{0,96},{16,112},{32,0},{48,16},{64,32},{80,48},{96,64},{112,80},{1... | collective-permute-start | bytes 61448 | tf_op jit(solution)/shard_map/ppermute | solution.py:415
  83.0 5.0 %collective-permute-start.7 = (bf16[80,128]{1,0:T(8,128)(2,1)S(1)}, bf16[80,128]{1,0:T(8,128)(2,1)S(1)}, u32[]{:S(2)}, u32[]{:S(2)}) collective-permute-start(bf16[80,128]{1,0:T(8,128)(2,1)S(1)} %gather_sum.5.refs_1_.refs_0_), channel_id=1, source_target_pairs={{0,64},{16,80},{32,96},{48,112},{64,0},{80,16},{96,32},{112,48},{1... | collective-permute-start | bytes 61448 | tf_op jit(solution)/shard_map/ppermute | solution.py:415
  84.2 3.8 %collective-permute-start.6 = (bf16[80,128]{1,0:T(8,128)(2,1)S(1)}, bf16[80,128]{1,0:T(8,128)(2,1)S(1)}, u32[]{:S(2)}, u32[]{:S(2)}) collective-permute-start(bf16[80,128]{1,0:T(8,128)(2,1)S(1)} %gather_sum.5.refs_1_.refs_0_), channel_id=1, source_target_pairs={{0,32},{16,48},{32,64},{48,80},{64,96},{80,112},{96,0},{112,16},{1... | collective-permute-start | bytes 61448 | tf_op jit(solution)/shard_map/ppermute | solution.py:415
  88.1 5.7 %collective-permute-start.9 = (bf16[4,80,128]{2,1,0:T(8,128)(2,1)S(1)}, bf16[4,80,128]{2,1,0:T(8,128)(2,1)S(1)}, u32[]{:S(2)}, u32[]{:S(2)}) collective-permute-start(bf16[4,80,128]{2,1,0:T(8,128)(2,1)S(1)} %stack.5.refs_7_.refs_2_), channel_id=1, source_target_pairs={{0,16},{16,0},{32,48},{48,32},{64,80},{80,64},{96,112},{112,96},{1... | collective-permute-start | bytes 245768 | tf_op jit(solution)/shard_map/ppermute | solution.py:426
  98.4 25.7 %all-to-all-start.2 = ((bf16[16,336,128]{2,1,0:T(8,128)(2,1)}), bf16[16,336,128]{2,1,0:T(8,128)(2,1)S(1)}, u32[]{:S(2)}, u32[]{:S(2)}) async-start(bf16[16,336,128]{2,1,0:T(8,128)(2,1)} %get-tuple-element.118), calls=%async_computation.2 | async-start | bytes 2752512 | tf_op jit(solution)/shard_map/all_to_all | solution.py:928
  102.8 31.3 %collective-permute-start.16 = (bf16[2,256,128]{2,1,0:T(8,128)(2,1)S(1)}, bf16[2,256,128]{2,1,0:T(8,128)(2,1)S(1)}, u32[]{:S(2)}, u32[]{:S(2)}) collective-permute-start(bf16[2,256,128]{2,1,0:T(8,128)(2,1)S(1)} %get-tuple-element.123), channel_id=1, source_target_pairs={{0,1},{1,2},{2,3},{3,4},{4,5},{5,6},{6,7},{7,8},{8,9},{9,10},{10,1... | collective-permute-start | bytes 393224 | tf_op jit(solution)/shard_map/ppermute | solution.py:939
  106.0 28.0 %collective-permute-start.17 = (bf16[2,256,128]{2,1,0:T(8,128)(2,1)S(1)}, bf16[2,256,128]{2,1,0:T(8,128)(2,1)S(1)}, u32[]{:S(2)}, u32[]{:S(2)}) collective-permute-start(bf16[2,256,128]{2,1,0:T(8,128)(2,1)S(1)} %get-tuple-element.124), channel_id=1, source_target_pairs={{1,0},{2,1},{3,2},{4,3},{5,4},{6,5},{7,6},{8,7},{9,8},{10,9},{11,1... | collective-permute-start | bytes 393224 | tf_op jit(solution)/shard_map/ppermute | solution.py:940
  124.2 6.5 %collective-permute-start.14 = (bf16[80,128]{1,0:T(8,128)(2,1)S(1)}, bf16[80,128]{1,0:T(8,128)(2,1)S(1)}, u32[]{:S(2)}, u32[]{:S(2)}) collective-permute-start(bf16[80,128]{1,0:T(8,128)(2,1)S(1)} %gather_sum.6.refs_1_.refs_0_), channel_id=1, source_target_pairs={{0,96},{16,112},{32,0},{48,16},{64,32},{80,48},{96,64},{112,80},{1... | collective-permute-start | bytes 61448 | tf_op jit(solution)/shard_map/ppermute | solution.py:415
  126.1 4.6 %collective-permute-start.13 = (bf16[80,128]{1,0:T(8,128)(2,1)S(1)}, bf16[80,128]{1,0:T(8,128)(2,1)S(1)}, u32[]{:S(2)}, u32[]{:S(2)}) collective-permute-start(bf16[80,128]{1,0:T(8,128)(2,1)S(1)} %gather_sum.6.refs_1_.refs_0_), channel_id=1, source_target_pairs={{0,64},{16,80},{32,96},{48,112},{64,0},{80,16},{96,32},{112,48},{1... | collective-permute-start | bytes 61448 | tf_op jit(solution)/shard_map/ppermute | solution.py:415
  127.0 3.8 %collective-permute-start.12 = (bf16[80,128]{1,0:T(8,128)(2,1)S(1)}, bf16[80,128]{1,0:T(8,128)(2,1)S(1)}, u32[]{:S(2)}, u32[]{:S(2)}) collective-permute-start(bf16[80,128]{1,0:T(8,128)(2,1)S(1)} %gather_sum.6.refs_1_.refs_0_), channel_id=1, source_target_pairs={{0,32},{16,48},{32,64},{48,80},{64,96},{80,112},{96,0},{112,16},{1... | collective-permute-start | bytes 61448 | tf_op jit(solution)/shard_map/ppermute | solution.py:415
  130.8 6.0 %collective-permute-start.15 = (bf16[4,80,128]{2,1,0:T(8,128)(2,1)S(1)}, bf16[4,80,128]{2,1,0:T(8,128)(2,1)S(1)}, u32[]{:S(2)}, u32[]{:S(2)}) collective-permute-start(bf16[4,80,128]{2,1,0:T(8,128)(2,1)S(1)} %stack.6.refs_8_.refs_2_), channel_id=1, source_target_pairs={{0,16},{16,0},{32,48},{48,32},{64,80},{80,64},{96,112},{112,96},{1... | collective-permute-start | bytes 245768 | tf_op jit(solution)/shard_map/ppermute | solution.py:426
  141.6 25.7 %all-to-all-start.3 = ((bf16[16,336,128]{2,1,0:T(8,128)(2,1)}), bf16[16,336,128]{2,1,0:T(8,128)(2,1)S(1)}, u32[]{:S(2)}, u32[]{:S(2)}) async-start(bf16[16,336,128]{2,1,0:T(8,128)(2,1)} %get-tuple-element.136), calls=%async_computation.3 | async-start | bytes 2752512 | tf_op jit(solution)/shard_map/all_to_all | solution.py:928
  146.0 31.7 %collective-permute-start.22 = (bf16[2,256,128]{2,1,0:T(8,128)(2,1)S(1)}, bf16[2,256,128]{2,1,0:T(8,128)(2,1)S(1)}, u32[]{:S(2)}, u32[]{:S(2)}) collective-permute-start(bf16[2,256,128]{2,1,0:T(8,128)(2,1)S(1)} %get-tuple-element.141), channel_id=1, source_target_pairs={{0,1},{1,2},{2,3},{3,4},{4,5},{5,6},{6,7},{7,8},{8,9},{9,10},{10,1... | collective-permute-start | bytes 393224 | tf_op jit(solution)/shard_map/ppermute | solution.py:939
  149.3 28.4 %collective-permute-start.23 = (bf16[2,256,128]{2,1,0:T(8,128)(2,1)S(1)}, bf16[2,256,128]{2,1,0:T(8,128)(2,1)S(1)}, u32[]{:S(2)}, u32[]{:S(2)}) collective-permute-start(bf16[2,256,128]{2,1,0:T(8,128)(2,1)S(1)} %get-tuple-element.142), channel_id=1, source_target_pairs={{1,0},{2,1},{3,2},{4,3},{5,4},{6,5},{7,6},{8,7},{9,8},{10,9},{11,1... | collective-permute-start | bytes 393224 | tf_op jit(solution)/shard_map/ppermute | solution.py:940
  167.4 7.0 %collective-permute-start.20 = (bf16[80,128]{1,0:T(8,128)(2,1)S(1)}, bf16[80,128]{1,0:T(8,128)(2,1)S(1)}, u32[]{:S(2)}, u32[]{:S(2)}) collective-permute-start(bf16[80,128]{1,0:T(8,128)(2,1)S(1)} %gather_sum.7.refs_1_.refs_0_), channel_id=1, source_target_pairs={{0,96},{16,112},{32,0},{48,16},{64,32},{80,48},{96,64},{112,80},{1... | collective-permute-start | bytes 61448 | tf_op jit(solution)/shard_map/ppermute | solution.py:415
  169.5 5.0 %collective-permute-start.19 = (bf16[80,128]{1,0:T(8,128)(2,1)S(1)}, bf16[80,128]{1,0:T(8,128)(2,1)S(1)}, u32[]{:S(2)}, u32[]{:S(2)}) collective-permute-start(bf16[80,128]{1,0:T(8,128)(2,1)S(1)} %gather_sum.7.refs_1_.refs_0_), channel_id=1, source_target_pairs={{0,64},{16,80},{32,96},{48,112},{64,0},{80,16},{96,32},{112,48},{1... | collective-permute-start | bytes 61448 | tf_op jit(solution)/shard_map/ppermute | solution.py:415
  170.7 3.8 %collective-permute-start.18 = (bf16[80,128]{1,0:T(8,128)(2,1)S(1)}, bf16[80,128]{1,0:T(8,128)(2,1)S(1)}, u32[]{:S(2)}, u32[]{:S(2)}) collective-permute-start(bf16[80,128]{1,0:T(8,128)(2,1)S(1)} %gather_sum.7.refs_1_.refs_0_), channel_id=1, source_target_pairs={{0,32},{16,48},{32,64},{48,80},{64,96},{80,112},{96,0},{112,16},{1... | collective-permute-start | bytes 61448 | tf_op jit(solution)/shard_map/ppermute | solution.py:415
  174.5 6.3 %collective-permute-start.21 = (bf16[4,80,128]{2,1,0:T(8,128)(2,1)S(1)}, bf16[4,80,128]{2,1,0:T(8,128)(2,1)S(1)}, u32[]{:S(2)}, u32[]{:S(2)}) collective-permute-start(bf16[4,80,128]{2,1,0:T(8,128)(2,1)S(1)} %stack.7.refs_9_.refs_2_), channel_id=1, source_target_pairs={{0,16},{16,0},{32,48},{48,32},{64,80},{80,64},{96,112},{112,96},{1... | collective-permute-start | bytes 245768 | tf_op jit(solution)/shard_map/ppermute | solution.py:426
  182.9 2.5 %collective-permute-start.24 = (bf16[16,128]{1,0:T(8,128)(2,1)S(1)}, bf16[16,128]{1,0:T(8,128)(2,1)S(1)}, u32[]{:S(2)}, u32[]{:S(2)}) collective-permute-start(bf16[16,128]{1,0:T(8,128)(2,1)S(1)} %get-tuple-element.156.refs_0_), channel_id=1, source_target_pairs={{0,1},{1,0},{2,3},{3,2},{4,5},{5,4},{6,7},{7,6},{8,9},{9,8},{10,11... | collective-permute-start | bytes 12296 | tf_op jit(solution)/shard_map/ppermute | solution.py:594
  185.4 4.0 %collective-permute-start.25 = (bf16[16,128]{1,0:T(8,128)(2,1)S(1)}, bf16[16,128]{1,0:T(8,128)(2,1)S(1)}, u32[]{:S(2)}, u32[]{:S(2)}) collective-permute-start(bf16[16,128]{1,0:T(8,128)(2,1)S(1)} %sum_over.7.refs_0_.refs_2_), channel_id=1, source_target_pairs={{0,2},{1,3},{2,0},{3,1},{4,6},{5,7},{6,4},{7,5},{8,10},{9,11},{10,... | collective-permute-start | bytes 12296 | tf_op jit(solution)/shard_map/ppermute | solution.py:594
  189.5 2.5 %collective-permute-start.26 = (bf16[16,128]{1,0:T(8,128)(2,1)S(1)}, bf16[16,128]{1,0:T(8,128)(2,1)S(1)}, u32[]{:S(2)}, u32[]{:S(2)}) collective-permute-start(bf16[16,128]{1,0:T(8,128)(2,1)S(1)} %sum_over.8.refs_0_.refs_2_), channel_id=1, source_target_pairs={{0,4},{1,5},{2,6},{3,7},{4,0},{5,1},{6,2},{7,3},{8,12},{9,13},{10,... | collective-permute-start | bytes 12296 | tf_op jit(solution)/shard_map/ppermute | solution.py:594
  192.1 4.0 %collective-permute-start.27 = (bf16[16,128]{1,0:T(8,128)(2,1)S(1)}, bf16[16,128]{1,0:T(8,128)(2,1)S(1)}, u32[]{:S(2)}, u32[]{:S(2)}) collective-permute-start(bf16[16,128]{1,0:T(8,128)(2,1)S(1)} %sum_over.9.refs_0_.refs_2_), channel_id=1, source_target_pairs={{0,8},{1,9},{2,10},{3,11},{4,12},{5,13},{6,14},{7,15},{8,0},{9,1},... | collective-permute-start | bytes 12296 | tf_op jit(solution)/shard_map/ppermute | solution.py:594
  196.1 2.5 %collective-permute-start.28 = (bf16[16,128]{1,0:T(8,128)(2,1)S(1)}, bf16[16,128]{1,0:T(8,128)(2,1)S(1)}, u32[]{:S(2)}, u32[]{:S(2)}) collective-permute-start(bf16[16,128]{1,0:T(8,128)(2,1)S(1)} %sum_over.10.refs_0_.refs_2_), channel_id=1, source_target_pairs={{0,32},{16,48},{32,0},{48,16},{64,96},{80,112},{96,64},{112,80},{1... | collective-permute-start | bytes 12296 | tf_op jit(solution)/shard_map/ppermute | solution.py:594
  198.7 4.0 %collective-permute-start.29 = (bf16[16,128]{1,0:T(8,128)(2,1)S(1)}, bf16[16,128]{1,0:T(8,128)(2,1)S(1)}, u32[]{:S(2)}, u32[]{:S(2)}) collective-permute-start(bf16[16,128]{1,0:T(8,128)(2,1)S(1)} %sum_over.11.refs_0_.refs_2_), channel_id=1, source_target_pairs={{0,64},{16,80},{32,96},{48,112},{64,0},{80,16},{96,32},{112,48},{1... | collective-permute-start | bytes 12296 | tf_op jit(solution)/shard_map/ppermute | solution.py:594
  202.8 7.8 %collective-permute-start.30 = (bf16[16,128]{1,0:T(8,128)(2,1)S(1)}, bf16[16,128]{1,0:T(8,128)(2,1)S(1)}, u32[]{:S(2)}, u32[]{:S(2)}) collective-permute-start(bf16[16,128]{1,0:T(8,128)(2,1)S(1)} %sum_over.12.refs_0_.refs_2_), channel_id=1, source_target_pairs={{0,16},{16,0},{32,48},{48,32},{64,80},{80,64},{96,112},{112,96},{1... | collective-permute-start | bytes 12296 | tf_op jit(solution)/shard_map/ppermute | solution.py:594
